TPU v7x, 32 devices: a whole 2x2x4 slice. The times are simulated.
32 devices in a mesh: dom: 8 (over z, core), sub: 4 (over y, x).
Axes of the slice: x: 2, y: 2, z: 4, core: 2. Of those that a mesh axis runs over, the one named last changes fastest.
Arguments:
- a_tiles: bfloat16 [128, 10, 128, 128], P(('dom', 'sub')), may hold values from -0.5 to 0.5
- a_cols: int32 [128, 10], P(('dom', 'sub')), may hold values from 0 to 127, as said below
- a_count: int32 [128], P(('dom', 'sub')), may hold values from 3 to 10, as said below
- p_tiles: bfloat16 [128, 128, 256], P(('dom', 'sub')), may hold values from -0.5 to 0.5
- p_cols: int32 [128, 2], P(('dom', 'sub')), may hold values from 0 to 15, as said below
Outputs:
- coarse_band: bfloat16 [2048, 768], P(('dom', 'sub'))
Inputs may be any that keep to these rules, and one draw needn't show every extreme that they name: `a_cols`: slot 0 of fine tile f holds f itself. Every column tile of fine tile f lies in its group g(f), or among the last 4 tiles of group g(f) - 1, or among the first 4 tiles of group g(f) + 1. Values in slots at or beyond a_count are such tiles too. `a_count`: each device has at least one fine row tile with all 10 slots live. `p_cols`: both coarse tiles of fine tile f lie in group g(f), between g(f) * 2 and (g(f) + 1) * 2 - 1. With j = f mod 16, the first, h, is within 1 of g(f) * 2 + (j * 2) // 16; the second is g(f) * 2 + (h - g(f) * 2 + 2 // 2) mod 2.
All inputs are finite; a program needn't handle non-finite values.
Results may differ from a plain program's by a relative error of at most 0.0049.
Values may be sent and summed in bfloat16 or wider, within the bound.
No kernel may reach another device: no remote copies, remote signals or barrier semaphores. Data moves between devices by JAX's collectives and lax.ppermute only.
A program may use at most 128 MiB of HBM per device.

v0:
```python
import jax
import jax.numpy as jnp
from jax import lax
from jax.sharding import PartitionSpec as P

COARSE_ROWS = 64


def from_behind(value, axis, steps):
    count = lax.axis_size(axis)
    initial, last = (max(0, -steps), min(count, count - steps))
    return lax.ppermute(value, axis, [(source, source + steps) for source in range(initial, last)])


def local(a_tiles, a_cols, a_count, p_tiles, p_cols):
    row_tiles = a_tiles.shape[0]
    slot_count = a_tiles.shape[1]
    tile_size = a_tiles.shape[2]
    sub_count = lax.axis_size("sub")
    group_here = lax.axis_index("dom")
    group_tiles = row_tiles * sub_count
    coarse_group = sub_count * COARSE_ROWS // tile_size
    band_blocks = 3 * coarse_group
    group_p, group_c = (
        lax.all_gather(p_tiles, "sub", axis=0, tiled=True),
        lax.all_gather(p_cols, "sub", axis=0, tiled=True),
    )
    left_p, left_c = from_behind(
        (group_p[group_tiles - row_tiles :], group_c[group_tiles - row_tiles :]), "dom", 1
    )
    right_p, right_c = from_behind((group_p[:row_tiles], group_c[:row_tiles]), "dom", -1)
    pool_p = jnp.concatenate([left_p, group_p, right_p], axis=0)
    pool_c = jnp.concatenate([left_c, group_c, right_c], axis=0)
    first_tile = group_here * group_tiles - row_tiles
    band_base = (group_here - 1) * coarse_group
    block_ids = jnp.arange(band_blocks, dtype=jnp.int32)
    slot_ids = jnp.arange(slot_count, dtype=jnp.int32)

    def row_product(row_inputs):
        a_row, column_ids, live_count = row_inputs
        local_index = column_ids - first_tile
        fetched = jnp.take(pool_p, local_index, axis=0)
        fetched_blocks = jnp.take(pool_c, local_index, axis=0) - band_base
        products = jnp.einsum("kab,kbc->kac", a_row, fetched, preferred_element_type=jnp.float32)
        live_slots = (slot_ids < live_count).astype(jnp.float32)
        selector = (fetched_blocks[:, :, None] == block_ids[None, None, :]).astype(
            jnp.float32
        ) * live_slots[:, None, None]
        split_products = products.reshape(slot_count, tile_size, 2, tile_size)
        q_block = jnp.einsum(
            "katb,ktc->acb", split_products, selector, precision=lax.Precision.HIGHEST
        )
        return q_block.reshape(tile_size, band_blocks * tile_size).astype(jnp.bfloat16)

    q_all = lax.map(row_product, (a_tiles, a_cols, a_count))
    q_flat = q_all.reshape(row_tiles * tile_size, band_blocks * tile_size)
    coarse_ids = jnp.arange(coarse_group, dtype=jnp.int32)
    home_blocks = p_cols - group_here * coarse_group
    placing = (home_blocks[:, :, None] == coarse_ids[None, None, :]).astype(jnp.bfloat16)
    split_p = p_tiles.reshape(row_tiles, tile_size, 2, tile_size)
    placed = jnp.einsum(
        "fatb,ftn->fanb", split_p, placing, preferred_element_type=jnp.float32
    ).astype(jnp.bfloat16)
    placed = placed.reshape(row_tiles * tile_size, coarse_group * tile_size)
    owned = lax.psum_scatter(
        lax.dot_general(
            placed, q_flat, (((0,), (0,)), ((), ())), preferred_element_type=jnp.float32
        ),
        "sub",
        scatter_dimension=0,
        tiled=True,
    )
    return owned.astype(jnp.bfloat16)


def solution(mesh):
    placed = (
        P(("dom", "sub"), None, None, None),
        P(("dom", "sub"), None),
        P(("dom", "sub")),
        P(("dom", "sub"), None, None),
        P(("dom", "sub"), None),
    )
    return jax.shard_map(
        local, mesh=mesh, in_specs=placed, out_specs=P(("dom", "sub"), None), check_vma=False
    )
```

profile of v0, /device:TPU:1, one launch (start us, length us, event | category | flops | bytes accessed | tf_op | source)
XLA Modules:
  0.0 120.5 jit_solution(2898110538182842744)
XLA Ops:
  6.5 0.7 all-gather.3.cloned.1.call-update
  7.3 7.3 %all-gather = s32[4,4,2]{1,2,0:T(2,128)S(1)} all-gather(s32[1,4,2]{1,2,0:T(2,128)} %bitcast.65), channel_id=1, replica_groups=mesh['dom'=8,'sub'=4] {'sub'}, dimensions={0}, use_global_device_ids=true | all-gather | bytes 160 | tf_op jit(solution)/shard_map/all_gather | solution.py:26
  14.6 5.5 %collective-permute-start = (s32[4,2]{0,1:T(2,128)S(1)}, s32[4,2]{0,1:T(2,128)S(1)}, u32[]{:S(2)}, u32[]{:S(2)}) collective-permute-start(s32[4,2]{0,1:T(2,128)S(1)} %get-tuple-element.149), channel_id=1, source_target_pairs={{0,4},{4,8},{8,12},{12,16},{16,20},{20,24},{24,28},{1,5},{5,9},{9,... | collective-permute-start | bytes 104 | tf_op jit(solution)/shard_map/ppermute | solution.py:12
  20.1 1.9 %collective-permute-start.1 = (s32[4,2]{0,1:T(2,128)S(1)}, s32[4,2]{0,1:T(2,128)S(1)}, u32[]{:S(2)}, u32[]{:S(2)}) collective-permute-start(s32[4,2]{0,1:T(2,128)S(1)} %get-tuple-element.150), channel_id=1, source_target_pairs={{4,0},{8,4},{12,8},{16,12},{20,16},{24,20},{28,24},{5,1},{9,5},{13... | collective-permute-start | bytes 104 | tf_op jit(solution)/shard_map/ppermute | solution.py:12
  22.0 1.0 reshape.76
  23.1 0.7 broadcast_subtract_fusion
  23.9 14.0 %all-gather.3.cloned.1.call-done = bf16[16,128,256]{2,1,0:T(8,128)(2,1)} async-done(((bf16[4,128,256]{2,1,0:T(8,128)(2,1)}), bf16[16,128,256]{2,1,0:T(8,128)(2,1)}) %all-gather.3.cloned.1.call-update) | async-done | bytes 1048592 | tf_op jit(solution)/shard_map/all_gather | solution.py:25
  37.9 1.2 fusion.36
  39.1 3.7 %collective-permute-start.2 = (bf16[4,128,256]{2,1,0:T(8,128)(2,1)S(1)}, bf16[4,128,256]{2,1,0:T(8,128)(2,1)S(1)}, u32[]{:S(2)}, u32[]{:S(2)}) collective-permute-start(bf16[4,128,256]{2,1,0:T(8,128)(2,1)S(1)} %get-tuple-element.147), channel_id=1, source_target_pairs={{0,4},{4,8},{8,12},{12,16},{16,20},{20,24},{24,28},{1,5},{5,9},{9,... | collective-permute-start | bytes 786440 | tf_op jit(solution)/shard_map/ppermute | solution.py:12
  42.8 1.9 %collective-permute-start.3 = (bf16[4,128,256]{2,1,0:T(8,128)(2,1)S(1)}, bf16[4,128,256]{2,1,0:T(8,128)(2,1)S(1)}, u32[]{:S(2)}, u32[]{:S(2)}) collective-permute-start(bf16[4,128,256]{2,1,0:T(8,128)(2,1)S(1)} %get-tuple-element.148), channel_id=1, source_target_pairs={{4,0},{8,4},{12,8},{16,12},{20,16},{24,20},{28,24},{5,1},{9,5},{13... | collective-permute-start | bytes 786440 | tf_op jit(solution)/shard_map/ppermute | solution.py:12
  44.7 1.1 convolution_convert_fusion
  46.1 4.4 %collective-permute-done.3 = bf16[4,128,256]{2,1,0:T(8,128)(2,1)S(1)} collective-permute-done((bf16[4,128,256]{2,1,0:T(8,128)(2,1)S(1)}, bf16[4,128,256]{2,1,0:T(8,128)(2,1)S(1)}, u32[]{:S(2)}, u32[]{:S(2)}) %collective-permute-start.3) | collective-permute-done | bytes 262176 | tf_op jit(solution)/shard_map/ppermute | solution.py:12
  50.5 1.3 %pad_maximum_fusion = bf16[24,128,256]{2,1,0:T(8,128)(2,1)} fusion(bf16[4,128,256]{2,1,0:T(8,128)(2,1)S(1)} %collective-permute-done.3, bf16[16,128,256]{2,1,0:T(8,128)(2,1)S(1)} %copy-done, bf16[4,128,256]{2,1,0:T(8,128)(2,1)S(1)} %collective-permute-done.2), kind=kLoop, calls=%fused_computation.34 | loop fusion | flops 1572864 | bytes 3145728 | tf_op jit(solution)/shard_map/concatenate | solution.py:32
  51.8 33.2 %while.11 = (s32[]{:T(128)}, bf16[4,128,768]{2,1,0:T(8,128)(2,1)S(1)}, s32[4,10]{1,0:T(4,128)S(1)}, s32[]{:T(128)}, s32[24,2]{1,0:T(8,128)S(1)}, /*index=5*/s32[...) while((s32[]{:T(128)}, ...), condition=%wide.region_1.2_spmd.clone, body=%wide.region_0.1_spmd.clone.sunk | while | flops 107906456 | bytes 8918555 | solution.py:55
  51.9 2.0 %gather_fusion = bf16[10,128,256]{2,1,0:T(8,128)(2,1)S(1)} fusion(bf16[24,128,256]{2,1,0:T(8,128)(2,1)} %get-tuple-element.234, s32[1024]{0:T(1024)S(1)} %pad_clamp_fusion.2), kind=kCustom, calls=%fused_computation.1.clone.clone.1 | custom fusion | bytes 1310760 | tf_op jit(solution)/shard_map/while/body/eval_jaxpr/jit(_take)/gather | solution.py:42
  53.9 1.4 %fusion.51 = f32[10,128,256]{2,1,0:T(8,128)S(1)} fusion(bf16[10,128,256]{2,1,0:T(8,128)(2,1)S(1)} %gather_fusion, pred[10]{0:T(512)(128)(4,1)S(1)} %compare_and_fusion.2, bf16[4,10,128,128]{3,2,1,0:T(8,128)(2,1)} %get-tuple-element.233, s32[]{:T(128)} %get-tuple-element.216), kind=kOutput, calls=%fused_computation.9.clone.1 | convolution fusion | flops 84213760 | bytes 2294282 | tf_op jit(solution)/shard_map/while/body/eval_jaxpr/kab,kbc->kac/dot_general | solution.py:44
  55.3 0.7 reshape.117
  57.8 1.9 %fusion.52 = bf16[128,6,128]{2,1,0:T(8,128)(2,1)S(1)} fusion(f32[10,128,2,128]{3,2,1,0:T(2,128)S(1)} %reshape.117, f32[10]{0:T(128)S(1)} %compare_convert_fusion.2, s32[10,2]{0,1:T(2,128)S(1)} %select_subtract_fusion.2), kind=kOutput, calls=%fused_computation.8.clone.1 | convolution fusion | flops 23691504 | bytes 1507448 | tf_op jit(solution)/shard_map/while/body/eval_jaxpr/katb,ktc->acb/dot_general | solution.py:50
  60.2 2.0 %gather_fusion = bf16[10,128,256]{2,1,0:T(8,128)(2,1)S(1)} fusion(bf16[24,128,256]{2,1,0:T(8,128)(2,1)} %get-tuple-element.234, s32[1024]{0:T(1024)S(1)} %pad_clamp_fusion.2), kind=kCustom, calls=%fused_computation.1.clone.clone.1 | custom fusion | bytes 1310760 | tf_op jit(solution)/shard_map/while/body/eval_jaxpr/jit(_take)/gather | solution.py:42
  62.2 1.4 %fusion.51 = f32[10,128,256]{2,1,0:T(8,128)S(1)} fusion(bf16[10,128,256]{2,1,0:T(8,128)(2,1)S(1)} %gather_fusion, pred[10]{0:T(512)(128)(4,1)S(1)} %compare_and_fusion.2, bf16[4,10,128,128]{3,2,1,0:T(8,128)(2,1)} %get-tuple-element.233, s32[]{:T(128)} %get-tuple-element.216), kind=kOutput, calls=%fused_computation.9.clone.1 | convolution fusion | flops 84213760 | bytes 2294282 | tf_op jit(solution)/shard_map/while/body/eval_jaxpr/kab,kbc->kac/dot_general | solution.py:44
  63.6 0.7 reshape.117
  66.1 1.9 %fusion.52 = bf16[128,6,128]{2,1,0:T(8,128)(2,1)S(1)} fusion(f32[10,128,2,128]{3,2,1,0:T(2,128)S(1)} %reshape.117, f32[10]{0:T(128)S(1)} %compare_convert_fusion.2, s32[10,2]{0,1:T(2,128)S(1)} %select_subtract_fusion.2), kind=kOutput, calls=%fused_computation.8.clone.1 | convolution fusion | flops 23691504 | bytes 1507448 | tf_op jit(solution)/shard_map/while/body/eval_jaxpr/katb,ktc->acb/dot_general | solution.py:50
  68.5 2.0 %gather_fusion = bf16[10,128,256]{2,1,0:T(8,128)(2,1)S(1)} fusion(bf16[24,128,256]{2,1,0:T(8,128)(2,1)} %get-tuple-element.234, s32[1024]{0:T(1024)S(1)} %pad_clamp_fusion.2), kind=kCustom, calls=%fused_computation.1.clone.clone.1 | custom fusion | bytes 1310760 | tf_op jit(solution)/shard_map/while/body/eval_jaxpr/jit(_take)/gather | solution.py:42
  70.5 1.4 %fusion.51 = f32[10,128,256]{2,1,0:T(8,128)S(1)} fusion(bf16[10,128,256]{2,1,0:T(8,128)(2,1)S(1)} %gather_fusion, pred[10]{0:T(512)(128)(4,1)S(1)} %compare_and_fusion.2, bf16[4,10,128,128]{3,2,1,0:T(8,128)(2,1)} %get-tuple-element.233, s32[]{:T(128)} %get-tuple-element.216), kind=kOutput, calls=%fused_computation.9.clone.1 | convolution fusion | flops 84213760 | bytes 2294282 | tf_op jit(solution)/shard_map/while/body/eval_jaxpr/kab,kbc->kac/dot_general | solution.py:44
  71.9 0.7 reshape.117
  74.4 1.9 %fusion.52 = bf16[128,6,128]{2,1,0:T(8,128)(2,1)S(1)} fusion(f32[10,128,2,128]{3,2,1,0:T(2,128)S(1)} %reshape.117, f32[10]{0:T(128)S(1)} %compare_convert_fusion.2, s32[10,2]{0,1:T(2,128)S(1)} %select_subtract_fusion.2), kind=kOutput, calls=%fused_computation.8.clone.1 | convolution fusion | flops 23691504 | bytes 1507448 | tf_op jit(solution)/shard_map/while/body/eval_jaxpr/katb,ktc->acb/dot_general | solution.py:50
  76.8 2.0 %gather_fusion = bf16[10,128,256]{2,1,0:T(8,128)(2,1)S(1)} fusion(bf16[24,128,256]{2,1,0:T(8,128)(2,1)} %get-tuple-element.234, s32[1024]{0:T(1024)S(1)} %pad_clamp_fusion.2), kind=kCustom, calls=%fused_computation.1.clone.clone.1 | custom fusion | bytes 1310760 | tf_op jit(solution)/shard_map/while/body/eval_jaxpr/jit(_take)/gather | solution.py:42
  78.8 1.4 %fusion.51 = f32[10,128,256]{2,1,0:T(8,128)S(1)} fusion(bf16[10,128,256]{2,1,0:T(8,128)(2,1)S(1)} %gather_fusion, pred[10]{0:T(512)(128)(4,1)S(1)} %compare_and_fusion.2, bf16[4,10,128,128]{3,2,1,0:T(8,128)(2,1)} %get-tuple-element.233, s32[]{:T(128)} %get-tuple-element.216), kind=kOutput, calls=%fused_computation.9.clone.1 | convolution fusion | flops 84213760 | bytes 2294282 | tf_op jit(solution)/shard_map/while/body/eval_jaxpr/kab,kbc->kac/dot_general | solution.py:44
  82.7 1.9 %fusion.52 = bf16[128,6,128]{2,1,0:T(8,128)(2,1)S(1)} fusion(f32[10,128,2,128]{3,2,1,0:T(2,128)S(1)} %reshape.117, f32[10]{0:T(128)S(1)} %compare_convert_fusion.2, s32[10,2]{0,1:T(2,128)S(1)} %select_subtract_fusion.2), kind=kOutput, calls=%fused_computation.8.clone.1 | convolution fusion | flops 23691504 | bytes 1507448 | tf_op jit(solution)/shard_map/while/body/eval_jaxpr/katb,ktc->acb/dot_general | solution.py:50
  85.0 2.3 %fusion.31 = f32[256,768]{1,0:T(8,128)} fusion(bf16[512,768]{1,0:T(8,128)(2,1)S(1)} %bitcast.63, bf16[64,8,2,128]{3,2,1,0:T(2,128)(2,1)} %bitcast.64), kind=kOutput, calls=%fused_computation.36 | convolution fusion | flops 201326592 | bytes 1835008 | tf_op jit(solution)/shard_map/dot_general | solution.py:66
  87.3 24.8 %reduce-scatter.2.cloned.1.call-done = f32[64,768]{1,0:T(8,128)} async-done(((f32[256,768]{1,0:T(8,128)}), f32[64,768]{1,0:T(8,128)}) %reduce-scatter.2.cloned.1.call-update) | async-done | bytes 196624 | tf_op jit(solution)/shard_map/reduce_scatter | solution.py:65
  112.1 1.6 %convert_element_type.36 = bf16[64,768]{1,0:T(8,128)(2,1)} convert(f32[64,768]{1,0:T(8,128)} %reduce-scatter.2.cloned.1.call-done) | non-fusion elementwise | flops 49152 | bytes 294912 | tf_op jit(solution)/shard_map/convert_element_type | solution.py:73
  (64 shorter events, 10.3 us)
Async XLA Ops:
  6.5 31.4 %all-gather.3.cloned.1.call-start = ((), (), s32[]{:S(2)}) async-start(), calls=%async_computation.1 | async-start | bytes 1310720 | tf_op jit(solution)/shard_map/all_gather | solution.py:25
  7.3 104.8 %reduce-scatter.2.cloned.1.call-start = ((), (), s32[]{:S(2)}) async-start(), calls=%async_computation.2 | async-start | bytes 983040 | tf_op jit(solution)/shard_map/reduce_scatter | solution.py:65
  14.6 31.3 %collective-permute-start = (s32[4,2]{0,1:T(2,128)S(1)}, s32[4,2]{0,1:T(2,128)S(1)}, u32[]{:S(2)}, u32[]{:S(2)}) collective-permute-start(s32[4,2]{0,1:T(2,128)S(1)} %get-tuple-element.149), channel_id=1, source_target_pairs={{0,4},{4,8},{8,12},{12,16},{16,20},{20,24},{24,28},{1,5},{5,9},{9,... | collective-permute-start | bytes 104 | tf_op jit(solution)/shard_map/ppermute | solution.py:12
  20.1 25.8 %collective-permute-start.1 = (s32[4,2]{0,1:T(2,128)S(1)}, s32[4,2]{0,1:T(2,128)S(1)}, u32[]{:S(2)}, u32[]{:S(2)}) collective-permute-start(s32[4,2]{0,1:T(2,128)S(1)} %get-tuple-element.150), channel_id=1, source_target_pairs={{4,0},{8,4},{12,8},{16,12},{20,16},{24,20},{28,24},{5,1},{9,5},{13... | collective-permute-start | bytes 104 | tf_op jit(solution)/shard_map/ppermute | solution.py:12
  37.9 12.5 %copy-start = (bf16[16,128,256]{2,1,0:T(8,128)(2,1)S(1)}, bf16[16,128,256]{2,1,0:T(8,128)(2,1)}, u32[]{:S(2)}) copy-start(bf16[16,128,256]{2,1,0:T(8,128)(2,1)} %all-gather.3.cloned.1.call-done) | copy-start | bytes 3145732
  39.1 7.0 %collective-permute-start.2 = (bf16[4,128,256]{2,1,0:T(8,128)(2,1)S(1)}, bf16[4,128,256]{2,1,0:T(8,128)(2,1)S(1)}, u32[]{:S(2)}, u32[]{:S(2)}) collective-permute-start(bf16[4,128,256]{2,1,0:T(8,128)(2,1)S(1)} %get-tuple-element.147), channel_id=1, source_target_pairs={{0,4},{4,8},{8,12},{12,16},{16,20},{20,24},{24,28},{1,5},{5,9},{9,... | collective-permute-start | bytes 786440 | tf_op jit(solution)/shard_map/ppermute | solution.py:12
  42.8 7.7 %collective-permute-start.3 = (bf16[4,128,256]{2,1,0:T(8,128)(2,1)S(1)}, bf16[4,128,256]{2,1,0:T(8,128)(2,1)S(1)}, u32[]{:S(2)}, u32[]{:S(2)}) collective-permute-start(bf16[4,128,256]{2,1,0:T(8,128)(2,1)S(1)} %get-tuple-element.148), channel_id=1, source_target_pairs={{4,0},{8,4},{12,8},{16,12},{20,16},{24,20},{28,24},{5,1},{9,5},{13... | collective-permute-start | bytes 786440 | tf_op jit(solution)/shard_map/ppermute | solution.py:12
  46.0 5.8 %copy-start.1 = (s32[4,10]{1,0:T(4,128)S(1)}, s32[4,10]{1,0:T(4,128)}, u32[]{:S(2)}) copy-start(s32[4,10]{1,0:T(4,128)} %param.8) | copy-start | bytes 484
  46.0 5.8 %copy-start.2 = (s32[4]{0:T(128)S(1)}, s32[4]{0:T(128)}, u32[]{:S(2)}) copy-start(s32[4]{0:T(128)} %param.9) | copy-start | bytes 52
Sparse Core Ops, SparseCore 0:
  9.2 28.6 all-gather.2
  87.4 24.6 reduce-scatter.1
where the time goes:
time: 122 us; the launch traced here: 121 us
  waiting for transfers between devices  44 us (36%)
  local copies, waits for them, and re-layouts  19.7 us (16%)
  matrix products  16.4 us (13%)
  between operations  13.5 us (11%)
  starting transfers between devices  13 us (11%)
  blocking collectives  7.28 us (6%)
  other arithmetic  6.32 us (5%)
    reduce_scatter x1, waiting for transfers between devices, local(): lax.psum_scatter(lax.dot_general(placed, q_flat, (((0,), (0,)), ((), ()))...  24.8 us
    all_gather x1, waiting for transfers between devices, local(): lax.all_gather(p_tiles, 'sub', axis=0, tiled=True)  14 us
    ppermute x4, starting transfers between devices, from_behind(): lax.ppermute(value, axis, [(source, source + steps) for source in range(i...  13 us
    gather x4, local copies, waits for them, and re-layouts, row_product(): fetched = jnp.take(pool_p, local_index, axis=0)  7.99 us
    dot_general x4, matrix products, row_product(): jnp.einsum('katb,ktc->acb', split_products, selector, precision=lax.Preci...  7.5 us
    all_gather x1, blocking collectives, local(): lax.all_gather(p_cols, 'sub', axis=0, tiled=True)  7.28 us
    dot_general x4, matrix products, row_product(): jnp.einsum('kab,kbc->kac', a_row, fetched, preferred_element_type=jnp.flo...  5.51 us
    ppermute x4, waiting for transfers between devices, from_behind(): lax.ppermute(value, axis, [(source, source + steps) for source in range(i...  4.47 us
  transfers between devices with their start and end apart: 6, of which 4 were waited for; matrix products, arithmetic and copies ran while one was open for 4% of the time, Pallas kernels for 0%

commit v1 on v0

v1 whole, which is shorter than its diff:
```python
import functools

import jax
import jax.numpy as jnp
from jax import lax
from jax.experimental import pallas as pl
from jax.experimental.pallas import tpu as pltpu
from jax.sharding import PartitionSpec as P

COARSE_ROWS = 64
BF16 = jnp.bfloat16
F32 = jnp.float32


def side_by_side(a_ref, f):
    return jnp.concatenate([a_ref[f, k] for k in range(a_ref.shape[1])], axis=1)


def placed_product(a_row, pool, index):
    stacked = jnp.concatenate([pool[i] for i in index], axis=0)
    return jnp.dot(a_row, stacked, preferred_element_type=F32).astype(BF16)


def own_tiles(rows, zero, half, me, pair_ref, pool):
    tiles = []
    for m in range(half):
        at = [me * rows + f for f in range(rows)]
        if half > 1:
            at = [jnp.where(pair_ref[rows + i] == m, i, zero) for i in at]
        tiles.append([pool[i] for i in at])
    return tiles


def restrict(tiles, q, half):
    outs = []
    for m in range(half):
        lhs = jnp.concatenate(tiles[m], axis=0)
        outs.append(
            lax.dot_general(lhs, q, (((0,), (0,)), ((), ())), preferred_element_type=F32)
        )
    return outs


def assemble_kernel(subs, *refs):
    col_refs, p_refs, (pool, left_ref, right_ref) = refs[:subs], refs[subs : 2 * subs], refs[2 * subs :]
    rows, tile = p_refs[0].shape[:2]
    me = lax.axis_index("sub")
    for k in range(subs):
        base = lax.bitwise_xor(me, k) * rows
        for f in range(rows):
            first = pl.multiple_of(
                jnp.where(col_refs[k][0, f] > col_refs[k][1, f], tile, 0), tile
            )
            for t, start in ((0, first), (1, pl.multiple_of(tile - first, tile))):
                pool[base + f, :, t * tile : (t + 1) * tile] = p_refs[k][f, :, pl.ds(start, tile)]
    pool[subs * rows] = jnp.zeros(pool.shape[1:], pool.dtype)
    left_ref[...] = pool[(subs - 1) * rows : subs * rows]
    right_ref[...] = pool[:rows]


def group_kernel(subs, half, cols_ref, count_ref, pair_ref, a_ref, pool, mid_ref, q):
    rows, slots, tile = a_ref.shape[0], a_ref.shape[1], a_ref.shape[2]
    zero = subs * rows
    me = lax.axis_index("sub")
    first = lax.axis_index("dom") * (subs * rows)
    for f in range(rows):
        a_row = side_by_side(a_ref, f)
        index = [[None] * slots for _ in range(half)]
        for k in range(slots):
            rel = cols_ref[f, k] - first
            inside = (rel >= 0) & (rel < zero) & (k < count_ref[f])
            safe = jnp.where(inside, rel, 0)
            for m in range(half):
                here = inside if half == 1 else inside & (pair_ref[rows + safe] == m)
                index[m][k] = jnp.where(here, safe, zero)
        for m in range(half):
            block = placed_product(a_row, pool, index[m])
            lo, hi = m * tile, (m + half) * tile
            q[f * tile : (f + 1) * tile, lo : lo + tile] = block[:, :tile]
            q[f * tile : (f + 1) * tile, hi : hi + tile] = block[:, tile:]
    for m, out in enumerate(restrict(own_tiles(rows, zero, half, me, pair_ref, pool), q[...], half)):
        mid_ref[m * tile : (m + 1) * tile] = out[:tile]
        mid_ref[(m + half) * tile : (m + half + 1) * tile] = out[tile:]


def halo_kernel(
    subs, half, cols_ref, count_ref, pair_ref, a_ref, mid_ref, pool, left_ref, right_ref, *rest
):
    outs, (edge, q, total) = rest[:subs], rest[subs:]
    rows, slots, tile = a_ref.shape[0], a_ref.shape[1], a_ref.shape[2]
    width = 2 * half * tile
    zero = 2 * rows
    me = lax.axis_index("sub")
    edge[:rows] = left_ref[...]
    edge[rows:zero] = right_ref[...]
    edge[zero] = jnp.zeros(edge.shape[1:], edge.dtype)
    first = lax.axis_index("dom") * (subs * rows)
    index = [[[[None] * slots for _ in range(half)] for _ in range(2)] for _ in range(rows)]
    for f in range(rows):
        for k in range(slots):
            rel = cols_ref[f, k] - first
            live = k < count_ref[f]
            left, right = live & (rel < 0), live & (rel >= subs * rows)
            for side, (inside, at, pair) in enumerate(
                ((left, rel + rows, 0), (right, rel - subs * rows + rows, subs * rows))
            ):
                safe = jnp.where(inside, at, 0)
                for m in range(half):
                    here = inside if half == 1 else inside & (pair_ref[pair + safe] == m)
                    index[f][side][m][k] = jnp.where(here, safe, zero)
    for f in range(rows):
        a_row = side_by_side(a_ref, f)
        for side in range(2):
            for m in range(half):
                block = placed_product(a_row, edge, index[f][side][m])
                lo, hi = side * width + m * tile, side * width + (m + half) * tile
                q[f * tile : (f + 1) * tile, lo : lo + tile] = block[:, :tile]
                q[f * tile : (f + 1) * tile, hi : hi + tile] = block[:, tile:]

    tiles = own_tiles(rows, subs * rows, half, me, pair_ref, pool)
    for m, out in enumerate(restrict(tiles, q[...], half)):
        for row, part in ((m * tile, out[:tile]), ((m + half) * tile, out[tile:])):
            total[row : row + tile, :width] = part[:, :width]
            total[row : row + tile, 2 * width :] = part[:, width:]
    total[:, width : 2 * width] = mid_ref[...]
    for k in range(subs):
        at = pl.multiple_of(lax.bitwise_xor(me, k) * COARSE_ROWS, COARSE_ROWS)
        outs[k][...] = total[pl.ds(at, COARSE_ROWS)].astype(outs[k].dtype)


def local(a_tiles, a_cols, a_count, p_tiles, p_cols):
    rows, slots, tile = a_tiles.shape[:3]
    subs, doms = lax.axis_size("sub"), lax.axis_size("dom")
    coarse_group = subs * COARSE_ROWS // tile
    half = coarse_group // 2
    width = coarse_group * tile
    group_tiles = rows * subs

    smem = pl.BlockSpec(memory_space=pltpu.SMEM)
    vmem = pl.BlockSpec(memory_space=pltpu.VMEM)
    p_bytes = rows * tile * 2 * tile * 2
    a_bytes = a_tiles.size * 2
    spare = 3 << 20

    def exchange(value, k):
        return lax.ppermute(value, "sub", [(s, s ^ k) for s in range(subs)])

    tiles = [p_tiles] + [exchange(p_tiles, k) for k in range(1, subs)]
    cols = [p_cols.T] + [exchange(p_cols.T, k) for k in range(1, subs)]

    pool, to_next, to_previous = pl.pallas_call(
        functools.partial(assemble_kernel, subs),
        out_shape=[
            jax.ShapeDtypeStruct((n, tile, 2 * tile), BF16) for n in (group_tiles + 1, rows, rows)
        ],
        in_specs=[smem] * subs + [vmem] * subs,
        out_specs=[vmem] * 3,
        compiler_params=pltpu.CompilerParams(vmem_limit_bytes=spare),
        cost_estimate=pl.CostEstimate(
            flops=1 << 30, bytes_accessed=2 * subs * p_bytes, transcendentals=0
        ),
        name="assemble",
    )(*cols, *tiles)
    left = lax.ppermute(to_next, "dom", [(d, d + 1) for d in range(doms - 1)])
    right = lax.ppermute(to_previous, "dom", [(d + 1, d) for d in range(doms - 1)])
    if half == 1:
        pair = jnp.zeros((1,), jnp.int32)
    else:
        m_own = jnp.min(p_cols, axis=1) - lax.axis_index("dom") * coarse_group
        m_group = lax.all_gather(m_own, "sub", axis=0, tiled=True)
        m_left = lax.ppermute(
            m_group[group_tiles - rows :], "dom", [(d, d + 1) for d in range(doms - 1)]
        )
        m_right = lax.ppermute(m_group[:rows], "dom", [(d + 1, d) for d in range(doms - 1)])
        pair = jnp.concatenate([m_left, m_group, m_right])

    flops = 2 * rows * slots * tile * tile * 2 * tile * half
    mid = pl.pallas_call(
        functools.partial(group_kernel, subs, half),
        out_shape=jax.ShapeDtypeStruct((width, width), F32),
        in_specs=[smem, smem, smem, vmem, vmem],
        out_specs=vmem,
        scratch_shapes=[pltpu.VMEM((rows * tile, width), BF16)],
        compiler_params=pltpu.CompilerParams(
            vmem_limit_bytes=2 * rows * tile * width + 4 * width * width + spare
        ),
        cost_estimate=pl.CostEstimate(
            flops=flops, bytes_accessed=a_bytes + subs * p_bytes, transcendentals=0
        ),
        name="group_part",
    )(a_cols, a_count, pair, a_tiles, pool)
    parts = pl.pallas_call(
        functools.partial(halo_kernel, subs, half),
        out_shape=[
            jax.ShapeDtypeStruct((COARSE_ROWS, 3 * width), F32 if k == 0 else BF16)
            for k in range(subs)
        ],
        in_specs=[smem, smem, smem, vmem, vmem, vmem, vmem, vmem],
        out_specs=[vmem] * subs,
        scratch_shapes=[
            pltpu.VMEM((2 * rows + 1, tile, 2 * tile), BF16),
            pltpu.VMEM((rows * tile, 2 * width), BF16),
            pltpu.VMEM((width, 3 * width), F32),
        ],
        compiler_params=pltpu.CompilerParams(
            vmem_limit_bytes=3 * p_bytes + 4 * rows * tile * width + 24 * width * width + spare
        ),
        cost_estimate=pl.CostEstimate(
            flops=2 * flops, bytes_accessed=a_bytes + 2 * p_bytes, transcendentals=0
        ),
        name="halo_part",
    )(a_cols, a_count, pair, a_tiles, mid, pool, left, right)
    owned = parts[0]
    for k in range(1, subs):
        owned = owned + exchange(parts[k], k).astype(F32)
    return owned.astype(BF16)


def solution(mesh):
    placed = (
        P(("dom", "sub"), None, None, None),
        P(("dom", "sub"), None),
        P(("dom", "sub")),
        P(("dom", "sub"), None, None),
        P(("dom", "sub"), None),
    )
    return jax.shard_map(
        local, mesh=mesh, in_specs=placed, out_specs=P(("dom", "sub"), None), check_vma=False
    )
```

time: 122 us -> 43.2 us (0.35); the launches traced: 121 us -> 43 us
  waiting for transfers between devices: 44 us -> 19 us
  local copies, waits for them, and re-layouts: 19.7 us -> 1.63 us
  matrix products: 16.4 us -> 0 us
  between operations: 13.5 us -> 0.1 us
  blocking collectives: 7.28 us -> 0 us
  other arithmetic: 6.32 us -> 0.69 us
  starting transfers between devices: 13 us -> 17.7 us
  Pallas kernels: 0 us -> 3.92 us
    reduce_scatter x1 -> x0, waiting for transfers between devices: 24.8 us -> none  [local(): lax.psum_scatter(lax.dot_general(placed, q_flat, (((0,), (0,)), ((), ()))...]
    dot_general x10 -> x0, matrix products: 16.4 us -> none  [the longest x4 7.5 us: row_product(): jnp.einsum('katb,ktc->acb', split_products, selector, precision=lax.Preci...]
    ppermute x4 -> x11, waiting for transfers between devices: 4.47 us -> 19 us  [the longest x9 14.6 us: exchange(): return lax.ppermute(value, 'sub', [(s, s ^ k) for s in range(subs)])]
    all_gather x1 -> x0, waiting for transfers between devices: 14 us -> none  [local(): lax.all_gather(p_tiles, 'sub', axis=0, tiled=True)]
    gather x12 -> x0, local copies, waits for them, and re-layouts: 10.6 us -> none  [the longest x4 7.99 us: row_product(): fetched = jnp.take(pool_p, local_index, axis=0)]
    all_gather x1 -> x0, blocking collectives: 7.28 us -> none  [local(): lax.all_gather(p_cols, 'sub', axis=0, tiled=True)]
    ppermute x4 -> x11, starting transfers between devices: 13 us -> 17.7 us  [the longest x9 9.69 us: exchange(): return lax.ppermute(value, 'sub', [(s, s ^ k) for s in range(subs)])]
    pallas_call x0 -> x3, Pallas kernels: none -> 3.92 us  [the longest x1 1.75 us: local(): pl.pallas_call(functools.partial(halo_kernel, subs, half), out_shape=[jax...]
  transfers between devices with their start and end apart: 6 -> 11, of which waited for: 4 -> 6; matrix products, arithmetic and copies ran while one was open for 4% -> 0% of each run, Pallas kernels for 0% -> 3%
where the time goes in v1:
time: 43.2 us; the launch traced here: 43 us
  waiting for transfers between devices  19 us (44%)
  starting transfers between devices  17.7 us (41%)
  Pallas kernels  3.92 us (9%)
  local copies, waits for them, and re-layouts  1.63 us (4%)
  other arithmetic  0.69 us (2%)
    ppermute x9, waiting for transfers between devices, exchange(): return lax.ppermute(value, 'sub', [(s, s ^ k) for s in range(subs)])  14.6 us
    ppermute x9, starting transfers between devices, exchange(): return lax.ppermute(value, 'sub', [(s, s ^ k) for s in range(subs)])  9.69 us
    ppermute x1, starting transfers between devices, local(): left = lax.ppermute(to_next, 'dom', [(d, d + 1) for d in range(doms - 1)])  6.05 us
    ppermute x1, waiting for transfers between devices, local(): lax.ppermute(to_previous, 'dom', [(d + 1, d) for d in range(doms - 1)])  4.39 us
    ppermute x1, starting transfers between devices, local(): lax.ppermute(to_previous, 'dom', [(d + 1, d) for d in range(doms - 1)])  1.92 us
    pallas_call x1, Pallas kernels, local(): pl.pallas_call(functools.partial(halo_kernel, subs, half), out_shape=[jax...  1.75 us
    unnamed x10, local copies, waits for them, and re-layouts  1.63 us
    pallas_call x1, Pallas kernels, local(): pl.pallas_call(functools.partial(group_kernel, subs, half), out_shape=jax...  1.32 us
  transfers between devices with their start and end apart: 11, of which 6 were waited for; matrix products, arithmetic and copies ran while one was open for 0% of the time, Pallas kernels for 3%

profile of v1, /device:TPU:1, one launch (start us, length us, event | category | flops | bytes accessed | tf_op | source)
XLA Modules:
  0.0 43.0 jit_solution(5329047729487916834)
XLA Ops:
  0.0 2.1 %collective-permute-start.4 = (bf16[4,128,256]{2,1,0:T(8,128)(2,1)}, bf16[4,128,256]{2,1,0:T(8,128)(2,1)S(1)}, u32[]{:S(2)}, u32[]{:S(2)}) collective-permute-start(bf16[4,128,256]{2,1,0:T(8,128)(2,1)} %refs_4_.1), channel_id=1, source_target_pairs={{0,2},{1,3},{2,0},{3,1},{4,6},{5,7},{6,4},{7,5},{8,10},{9,11},{10,... | collective-permute-start | bytes 786440 | tf_op jit(solution)/shard_map/ppermute | solution.py:146
  2.1 1.2 %collective-permute-start.3 = (bf16[4,128,256]{2,1,0:T(8,128)(2,1)}, bf16[4,128,256]{2,1,0:T(8,128)(2,1)S(1)}, u32[]{:S(2)}, u32[]{:S(2)}) collective-permute-start(bf16[4,128,256]{2,1,0:T(8,128)(2,1)} %refs_4_.1), channel_id=1, source_target_pairs={{0,1},{1,0},{2,3},{3,2},{4,5},{5,4},{6,7},{7,6},{8,9},{9,8},{10,11... | collective-permute-start | bytes 786440 | tf_op jit(solution)/shard_map/ppermute | solution.py:146
  3.3 0.0 collective-permute-start.5
  3.3 2.4 %collective-permute-start.2 = (s32[2,4]{1,0:T(2,128)}, s32[2,4]{1,0:T(2,128)S(1)}, u32[]{:S(2)}, u32[]{:S(2)}) collective-permute-start(s32[2,4]{1,0:T(2,128)} %bitcast.1), channel_id=1, source_target_pairs={{0,3},{1,2},{2,1},{3,0},{4,7},{5,6},{6,5},{7,4},{8,11},{9,10},{10,... | collective-permute-start | bytes 104 | tf_op jit(solution)/shard_map/ppermute | solution.py:146
  5.7 0.2 collective-permute-start.1
  5.9 8.9 %collective-permute-done.2.refs_3_ = s32[2,4]{1,0:T(2,128)S(1)} collective-permute-done((s32[2,4]{1,0:T(2,128)}, s32[2,4]{1,0:T(2,128)S(1)}, u32[]{:S(2)}, u32[]{:S(2)}) %collective-permute-start.2) | collective-permute-done | bytes 64 | tf_op jit(solution)/shard_map/ppermute | solution.py:146
  14.8 1.1 %collective-permute-start = (s32[2,4]{1,0:T(2,128)}, s32[2,4]{1,0:T(2,128)S(1)}, u32[]{:S(2)}, u32[]{:S(2)}) collective-permute-start(s32[2,4]{1,0:T(2,128)} %bitcast.3), channel_id=1, source_target_pairs={{0,1},{1,0},{2,3},{3,2},{4,5},{5,4},{6,7},{7,6},{8,9},{9,8},{10,11... | collective-permute-start | bytes 104 | tf_op jit(solution)/shard_map/ppermute | solution.py:146
  15.9 0.0 collective-permute-done.1.refs_2_
  15.9 1.5 %collective-permute-done.refs_1_ = s32[2,4]{1,0:T(2,128)S(1)} collective-permute-done((s32[2,4]{1,0:T(2,128)}, s32[2,4]{1,0:T(2,128)S(1)}, u32[]{:S(2)}, u32[]{:S(2)}) %collective-permute-start) | collective-permute-done | bytes 64 | tf_op jit(solution)/shard_map/ppermute | solution.py:146
  17.4 0.0 collective-permute-done.4.refs_6_
  17.4 0.0 collective-permute-done.3.refs_5_
  17.4 0.0 collective-permute-done.5.refs_7_
  17.5 0.0 copy-start.3
  17.5 0.9 %copy-done.3 = bf16[4,128,256]{2,1,0:T(8,128)(2,1)S(1)} copy-done((bf16[4,128,256]{2,1,0:T(8,128)(2,1)S(1)}, bf16[4,128,256]{2,1,0:T(8,128)(2,1)}, u32[]{:S(2)}) %copy-start.3) | copy-done | bytes 262168
  18.4 0.7 %copy-done.4 = s32[4,2]{0,1:T(2,128)S(1)} copy-done((s32[4,2]{0,1:T(2,128)S(1)}, s32[4,2]{0,1:T(2,128)}, u32[]{:S(2)}) %copy-start.4) | copy-done | bytes 56
  19.1 0.8 %assemble.1 = (bf16[17,128,256]{2,1,0:T(8,128)(2,1)S(1)}, bf16[4,128,256]{2,1,0:T(8,128)(2,1)S(1)}, bf16[4,128,256]{2,1,0:T(8,128)(2,1)S(1)}) custom-call(s32[2,4]{1,0:T(2,128)S(1)} %bitcast.4, s32[2,4]{1,0:T(2,128)S(1)} %collective-permute-done.refs_1_, s32[2,4]{1,0:T(2,128)S(1)} %collective-permute-done.1.refs_2_, ...), custom_call_target="tpu_custom_call" | custom-call | flops 1073741824 | bytes 2097152 | tf_op jit(solution)/shard_map/assemble/pallas_call | solution.py:151
  19.9 6.0 %collective-permute-start.6 = (bf16[4,128,256]{2,1,0:T(8,128)(2,1)S(1)}, bf16[4,128,256]{2,1,0:T(8,128)(2,1)S(1)}, u32[]{:S(2)}, u32[]{:S(2)}) collective-permute-start(bf16[4,128,256]{2,1,0:T(8,128)(2,1)S(1)} %get-tuple-element.13), channel_id=1, source_target_pairs={{0,4},{4,8},{8,12},{12,16},{16,20},{20,24},{24,28},{1,5},{5,9},{9,... | collective-permute-start | bytes 786440 | tf_op jit(solution)/shard_map/ppermute | solution.py:164
  26.0 1.9 %collective-permute-start.7 = (bf16[4,128,256]{2,1,0:T(8,128)(2,1)S(1)}, bf16[4,128,256]{2,1,0:T(8,128)(2,1)S(1)}, u32[]{:S(2)}, u32[]{:S(2)}) collective-permute-start(bf16[4,128,256]{2,1,0:T(8,128)(2,1)S(1)} %get-tuple-element.14), channel_id=1, source_target_pairs={{4,0},{8,4},{12,8},{16,12},{20,16},{24,20},{28,24},{5,1},{9,5},{13... | collective-permute-start | bytes 786440 | tf_op jit(solution)/shard_map/ppermute | solution.py:165
  27.9 0.0 copy-done
  27.9 0.0 copy-done.1
  27.9 0.0 copy-done.2
  28.0 1.3 %group_part.1.mid_ref = f32[256,256]{1,0:T(8,128)S(1)} custom-call(s32[4,10]{1,0:T(4,128)S(1)} %copy-done.1, s32[4]{0:T(128)S(1)} %copy-done.2, s32[1]{0:T(128)} %constant.0.clone.1.pair_ref, bf16[4,10,128,128]{3,2,1,0:T(8,128)(2,1)S(1)} %copy-done, bf16[17,128,256]{2,1,0:T(8,128)(2,1)S(1)} %get-tuple-element.12.pool), custom_call_target="tpu_custom_call" | custom-call | flops 335544320 | bytes 2359296 | tf_op jit(solution)/shard_map/group_part/pallas_call | solution.py:178
  29.3 0.0 collective-permute-done.6.left_ref
  29.3 4.4 %collective-permute-done.7.right_ref = bf16[4,128,256]{2,1,0:T(8,128)(2,1)S(1)} collective-permute-done((bf16[4,128,256]{2,1,0:T(8,128)(2,1)S(1)}, bf16[4,128,256]{2,1,0:T(8,128)(2,1)S(1)}, u32[]{:S(2)}, u32[]{:S(2)}) %collective-permute-start.7) | collective-permute-done | bytes 262176 | tf_op jit(solution)/shard_map/ppermute | solution.py:165
  33.7 1.8 %halo_part.1 = (f32[64,768]{1,0:T(8,128)S(1)}, bf16[64,768]{1,0:T(8,128)(2,1)S(1)}, bf16[64,768]{1,0:T(8,128)(2,1)S(1)}, bf16[64,768]{1,0:T(8,128)(2,1)S(1)}) custom-call(s32[4,10]{1,0:T(4,128)S(1)} %copy-done.1, s32[4]{0:T(128)S(1)} %copy-done.2, s32[1]{0:T(128)} %constant.0.clone.1.pair_ref, bf16[4,10,128,128]{3,2,1,0:T(8,128)(2,1)S(1)} %copy-done, ...), custom_call_target="tpu_custom_call" | custom-call | flops 671088640 | bytes 1835008 | tf_op jit(solution)/shard_map/halo_part/pallas_call | solution.py:192
  35.5 1.3 %collective-permute-start.8 = (bf16[64,768]{1,0:T(8,128)(2,1)S(1)}, bf16[64,768]{1,0:T(8,128)(2,1)S(1)}, u32[]{:S(2)}, u32[]{:S(2)}) collective-permute-start(bf16[64,768]{1,0:T(8,128)(2,1)S(1)} %get-tuple-element.16), channel_id=1, source_target_pairs={{0,1},{1,0},{2,3},{3,2},{4,5},{5,4},{6,7},{7,6},{8,9},{9,8},{10,11... | collective-permute-start | bytes 294920 | tf_op jit(solution)/shard_map/ppermute | solution.py:146
  36.7 1.2 %collective-permute-start.9 = (bf16[64,768]{1,0:T(8,128)(2,1)S(1)}, bf16[64,768]{1,0:T(8,128)(2,1)S(1)}, u32[]{:S(2)}, u32[]{:S(2)}) collective-permute-start(bf16[64,768]{1,0:T(8,128)(2,1)S(1)} %get-tuple-element.17), channel_id=1, source_target_pairs={{0,2},{1,3},{2,0},{3,1},{4,6},{5,7},{6,4},{7,5},{8,10},{9,11},{10,... | collective-permute-start | bytes 294920 | tf_op jit(solution)/shard_map/ppermute | solution.py:146
  38.0 0.2 collective-permute-start.10
  38.2 1.3 %collective-permute-done.8 = bf16[64,768]{1,0:T(8,128)(2,1)S(1)} collective-permute-done((bf16[64,768]{1,0:T(8,128)(2,1)S(1)}, bf16[64,768]{1,0:T(8,128)(2,1)S(1)}, u32[]{:S(2)}, u32[]{:S(2)}) %collective-permute-start.8) | collective-permute-done | bytes 98336 | tf_op jit(solution)/shard_map/ppermute | solution.py:146
  39.5 0.8 %collective-permute-done.9 = bf16[64,768]{1,0:T(8,128)(2,1)S(1)} collective-permute-done((bf16[64,768]{1,0:T(8,128)(2,1)S(1)}, bf16[64,768]{1,0:T(8,128)(2,1)S(1)}, u32[]{:S(2)}, u32[]{:S(2)}) %collective-permute-start.9) | collective-permute-done | bytes 98336 | tf_op jit(solution)/shard_map/ppermute | solution.py:146
  40.3 2.0 %collective-permute-done.10 = bf16[64,768]{1,0:T(8,128)(2,1)S(1)} collective-permute-done((bf16[64,768]{1,0:T(8,128)(2,1)S(1)}, bf16[64,768]{1,0:T(8,128)(2,1)S(1)}, u32[]{:S(2)}, u32[]{:S(2)}) %collective-permute-start.10) | collective-permute-done | bytes 98336 | tf_op jit(solution)/shard_map/ppermute | solution.py:146
  42.3 0.7 %add_convert_fusion = bf16[64,768]{1,0:T(8,128)(2,1)} fusion(bf16[64,768]{1,0:T(8,128)(2,1)S(1)} %collective-permute-done.10, bf16[64,768]{1,0:T(8,128)(2,1)S(1)} %collective-permute-done.9, f32[64,768]{1,0:T(8,128)S(1)} %get-tuple-element.15, bf16[64,768]{1,0:T(8,128)(2,1)S(1)} %collective-permute-done.8), kind=kLoop, calls=%fused_computation | loop fusion | flops 344064 | bytes 589824 | tf_op jit(solution)/shard_map/convert_element_type | solution.py:216
  (4 shorter events, 0.0 us)
Async XLA Ops:
  0.0 17.4 %collective-permute-start.4 = (bf16[4,128,256]{2,1,0:T(8,128)(2,1)}, bf16[4,128,256]{2,1,0:T(8,128)(2,1)S(1)}, u32[]{:S(2)}, u32[]{:S(2)}) collective-permute-start(bf16[4,128,256]{2,1,0:T(8,128)(2,1)} %refs_4_.1), channel_id=1, source_target_pairs={{0,2},{1,3},{2,0},{3,1},{4,6},{5,7},{6,4},{7,5},{8,10},{9,11},{10,... | collective-permute-start | bytes 786440 | tf_op jit(solution)/shard_map/ppermute | solution.py:146
  2.1 15.4 %collective-permute-start.3 = (bf16[4,128,256]{2,1,0:T(8,128)(2,1)}, bf16[4,128,256]{2,1,0:T(8,128)(2,1)S(1)}, u32[]{:S(2)}, u32[]{:S(2)}) collective-permute-start(bf16[4,128,256]{2,1,0:T(8,128)(2,1)} %refs_4_.1), channel_id=1, source_target_pairs={{0,1},{1,0},{2,3},{3,2},{4,5},{5,4},{6,7},{7,6},{8,9},{9,8},{10,11... | collective-permute-start | bytes 786440 | tf_op jit(solution)/shard_map/ppermute | solution.py:146
  3.3 14.2 %collective-permute-start.5 = (bf16[4,128,256]{2,1,0:T(8,128)(2,1)}, bf16[4,128,256]{2,1,0:T(8,128)(2,1)S(1)}, u32[]{:S(2)}, u32[]{:S(2)}) collective-permute-start(bf16[4,128,256]{2,1,0:T(8,128)(2,1)} %refs_4_.1), channel_id=1, source_target_pairs={{0,3},{1,2},{2,1},{3,0},{4,7},{5,6},{6,5},{7,4},{8,11},{9,10},{10,... | collective-permute-start | bytes 786440 | tf_op jit(solution)/shard_map/ppermute | solution.py:146
  3.3 24.6 %copy-start = (bf16[4,10,128,128]{3,2,1,0:T(8,128)(2,1)S(1)}, bf16[4,10,128,128]{3,2,1,0:T(8,128)(2,1)}, u32[]{:S(2)}) copy-start(bf16[4,10,128,128]{3,2,1,0:T(8,128)(2,1)} %a_ref.3) | copy-start | bytes 3932164
  3.3 24.7 %copy-start.1 = (s32[4,10]{1,0:T(4,128)S(1)}, s32[4,10]{1,0:T(4,128)}, u32[]{:S(2)}) copy-start(s32[4,10]{1,0:T(4,128)} %cols_ref.3) | copy-start | bytes 484
  3.3 24.7 %copy-start.2 = (s32[4]{0:T(128)S(1)}, s32[4]{0:T(128)}, u32[]{:S(2)}) copy-start(s32[4]{0:T(128)} %count_ref.3) | copy-start | bytes 52
  3.3 11.5 %collective-permute-start.2 = (s32[2,4]{1,0:T(2,128)}, s32[2,4]{1,0:T(2,128)S(1)}, u32[]{:S(2)}, u32[]{:S(2)}) collective-permute-start(s32[2,4]{1,0:T(2,128)} %bitcast.1), channel_id=1, source_target_pairs={{0,3},{1,2},{2,1},{3,0},{4,7},{5,6},{6,5},{7,4},{8,11},{9,10},{10,... | collective-permute-start | bytes 104 | tf_op jit(solution)/shard_map/ppermute | solution.py:146
  5.7 10.3 %collective-permute-start.1 = (s32[2,4]{1,0:T(2,128)}, s32[2,4]{1,0:T(2,128)S(1)}, u32[]{:S(2)}, u32[]{:S(2)}) collective-permute-start(s32[2,4]{1,0:T(2,128)} %bitcast.2), channel_id=1, source_target_pairs={{0,2},{1,3},{2,0},{3,1},{4,6},{5,7},{6,4},{7,5},{8,10},{9,11},{10,... | collective-permute-start | bytes 104 | tf_op jit(solution)/shard_map/ppermute | solution.py:146
  14.8 2.6 %collective-permute-start = (s32[2,4]{1,0:T(2,128)}, s32[2,4]{1,0:T(2,128)S(1)}, u32[]{:S(2)}, u32[]{:S(2)}) collective-permute-start(s32[2,4]{1,0:T(2,128)} %bitcast.3), channel_id=1, source_target_pairs={{0,1},{1,0},{2,3},{3,2},{4,5},{5,4},{6,7},{7,6},{8,9},{9,8},{10,11... | collective-permute-start | bytes 104 | tf_op jit(solution)/shard_map/ppermute | solution.py:146
  17.5 1.0 %copy-start.3 = (bf16[4,128,256]{2,1,0:T(8,128)(2,1)S(1)}, bf16[4,128,256]{2,1,0:T(8,128)(2,1)}, u32[]{:S(2)}) copy-start(bf16[4,128,256]{2,1,0:T(8,128)(2,1)} %refs_4_.1) | copy-start | bytes 786436
  18.4 0.7 %copy-start.4 = (s32[4,2]{0,1:T(2,128)S(1)}, s32[4,2]{0,1:T(2,128)}, u32[]{:S(2)}) copy-start(s32[4,2]{0,1:T(2,128)} %param.9) | copy-start | bytes 100
  19.9 9.3 %collective-permute-start.6 = (bf16[4,128,256]{2,1,0:T(8,128)(2,1)S(1)}, bf16[4,128,256]{2,1,0:T(8,128)(2,1)S(1)}, u32[]{:S(2)}, u32[]{:S(2)}) collective-permute-start(bf16[4,128,256]{2,1,0:T(8,128)(2,1)S(1)} %get-tuple-element.13), channel_id=1, source_target_pairs={{0,4},{4,8},{8,12},{12,16},{16,20},{20,24},{24,28},{1,5},{5,9},{9,... | collective-permute-start | bytes 786440 | tf_op jit(solution)/shard_map/ppermute | solution.py:164
  26.0 7.7 %collective-permute-start.7 = (bf16[4,128,256]{2,1,0:T(8,128)(2,1)S(1)}, bf16[4,128,256]{2,1,0:T(8,128)(2,1)S(1)}, u32[]{:S(2)}, u32[]{:S(2)}) collective-permute-start(bf16[4,128,256]{2,1,0:T(8,128)(2,1)S(1)} %get-tuple-element.14), channel_id=1, source_target_pairs={{4,0},{8,4},{12,8},{16,12},{20,16},{24,20},{28,24},{5,1},{9,5},{13... | collective-permute-start | bytes 786440 | tf_op jit(solution)/shard_map/ppermute | solution.py:165
  35.5 4.0 %collective-permute-start.8 = (bf16[64,768]{1,0:T(8,128)(2,1)S(1)}, bf16[64,768]{1,0:T(8,128)(2,1)S(1)}, u32[]{:S(2)}, u32[]{:S(2)}) collective-permute-start(bf16[64,768]{1,0:T(8,128)(2,1)S(1)} %get-tuple-element.16), channel_id=1, source_target_pairs={{0,1},{1,0},{2,3},{3,2},{4,5},{5,4},{6,7},{7,6},{8,9},{9,8},{10,11... | collective-permute-start | bytes 294920 | tf_op jit(solution)/shard_map/ppermute | solution.py:146
  36.7 3.6 %collective-permute-start.9 = (bf16[64,768]{1,0:T(8,128)(2,1)S(1)}, bf16[64,768]{1,0:T(8,128)(2,1)S(1)}, u32[]{:S(2)}, u32[]{:S(2)}) collective-permute-start(bf16[64,768]{1,0:T(8,128)(2,1)S(1)} %get-tuple-element.17), channel_id=1, source_target_pairs={{0,2},{1,3},{2,0},{3,1},{4,6},{5,7},{6,4},{7,5},{8,10},{9,11},{10,... | collective-permute-start | bytes 294920 | tf_op jit(solution)/shard_map/ppermute | solution.py:146
  38.0 4.4 %collective-permute-start.10 = (bf16[64,768]{1,0:T(8,128)(2,1)S(1)}, bf16[64,768]{1,0:T(8,128)(2,1)S(1)}, u32[]{:S(2)}, u32[]{:S(2)}) collective-permute-start(bf16[64,768]{1,0:T(8,128)(2,1)S(1)} %get-tuple-element.18), channel_id=1, source_target_pairs={{0,3},{1,2},{2,1},{3,0},{4,7},{5,6},{6,5},{7,4},{8,11},{9,10},{10,... | collective-permute-start | bytes 294920 | tf_op jit(solution)/shard_map/ppermute | solution.py:146

commit v2 on v1

v2 whole, which is shorter than its diff:
```python
import functools

import jax
import jax.numpy as jnp
from jax import lax
from jax.experimental import pallas as pl
from jax.experimental.pallas import tpu as pltpu
from jax.sharding import PartitionSpec as P

COARSE_ROWS = 64
BF16 = jnp.bfloat16
F32 = jnp.float32


def side_by_side(a_ref, f):
    return jnp.concatenate([a_ref[f, k] for k in range(a_ref.shape[1])], axis=1)


def placed_product(a_row, pool, index):
    stacked = jnp.concatenate([pool[i] for i in index], axis=0)
    return jnp.dot(a_row, stacked, preferred_element_type=F32).astype(BF16)


def own_tiles(rows, zero, half, me, pair_ref, pool):
    tiles = []
    for m in range(half):
        at = [me * rows + f for f in range(rows)]
        if half > 1:
            at = [jnp.where(pair_ref[rows + i] == m, i, zero) for i in at]
        tiles.append([pool[i] for i in at])
    return tiles


def restrict(tiles, q, half):
    outs = []
    for m in range(half):
        lhs = jnp.concatenate(tiles[m], axis=0)
        outs.append(
            lax.dot_general(lhs, q, (((0,), (0,)), ((), ())), preferred_element_type=F32)
        )
    return outs


def order_kernel(cols_ref, p_ref, own_ref):
    rows, tile = p_ref.shape[:2]
    for f in range(rows):
        first = pl.multiple_of(jnp.where(cols_ref[0, f] > cols_ref[1, f], tile, 0), tile)
        for t, start in ((0, first), (1, pl.multiple_of(tile - first, tile))):
            own_ref[f, :, t * tile : (t + 1) * tile] = p_ref[f, :, pl.ds(start, tile)]


def hand_out_kernel(subs, pool, near_ref, far_ref):
    rows = near_ref.shape[0]
    odd = lax.rem(lax.axis_index("dom"), 2)
    last = (subs - 1) * rows
    near_ref[...] = pool[pl.ds((1 - odd) * last, rows)]
    far_ref[...] = pool[pl.ds(odd * last, rows)]


def edge_kernel(subs, half, cols_ref, count_ref, pair_ref, a_ref, own_ref, out_ref, turned):
    rows, slots, tile = a_ref.shape[:3]
    first = lax.axis_index("dom") * (subs * rows)
    me = lax.axis_index("sub")
    out_ref[...] = jnp.zeros(out_ref.shape, F32)
    for f in range(rows):
        turned[f] = own_ref[f].T
    for f in range(rows):
        for k in range(slots):
            rel = cols_ref[f, k] - first
            live = (k < count_ref[f]) & ((rel < 0) | (rel >= subs * rows))

            @pl.when(live)
            def _():
                at = jnp.where(rel < 0, rel + rows, rel - subs * rows + rows)
                term = jnp.dot(turned[f], a_ref[f, k], preferred_element_type=F32)
                if half == 1:
                    out_ref[at] += term
                else:
                    m = pair_ref[rows + me * rows + f]
                    for start, part in ((m, term[:tile]), (m + half, term[tile:])):
                        out_ref[at, pl.ds(pl.multiple_of(start * tile, tile), tile)] += part


def group_kernel(subs, half, cols_ref, count_ref, pair_ref, a_ref, edge_ref, *rest):
    p_refs, rest = rest[:subs], rest[subs:]
    outs, (pool, q, mid_ref) = rest[:subs], rest[subs:]
    rows, slots, tile = a_ref.shape[0], a_ref.shape[1], a_ref.shape[2]
    zero = subs * rows
    width = 2 * half * tile
    me = lax.axis_index("sub")
    first = lax.axis_index("dom") * (subs * rows)
    for k in range(subs):
        pool[pl.ds(lax.bitwise_xor(me, k) * rows, rows)] = p_refs[k][...]
    pool[zero] = jnp.zeros(pool.shape[1:], pool.dtype)
    for f in range(rows):
        a_row = side_by_side(a_ref, f)
        index = [[None] * slots for _ in range(half)]
        for k in range(slots):
            rel = cols_ref[f, k] - first
            inside = (rel >= 0) & (rel < zero) & (k < count_ref[f])
            safe = jnp.where(inside, rel, 0)
            for m in range(half):
                here = inside if half == 1 else inside & (pair_ref[rows + safe] == m)
                index[m][k] = jnp.where(here, safe, zero)
        for m in range(half):
            block = placed_product(a_row, pool, index[m])
            lo, hi = m * tile, (m + half) * tile
            q[f * tile : (f + 1) * tile, lo : lo + tile] = block[:, :tile]
            q[f * tile : (f + 1) * tile, hi : hi + tile] = block[:, tile:]
    for m, out in enumerate(restrict(own_tiles(rows, zero, half, me, pair_ref, pool), q[...], half)):
        mid_ref[m * tile : (m + 1) * tile] = out[:tile]
        mid_ref[(m + half) * tile : (m + half + 1) * tile] = out[tile:]
    for k in range(subs):
        at = pl.ds(pl.multiple_of(lax.bitwise_xor(me, k) * COARSE_ROWS, COARSE_ROWS), COARSE_ROWS)
        kind = outs[k].dtype
        outs[k][:, :width] = mid_ref[at].astype(kind)
        for c in range(2 * rows):
            outs[k][:, width + c * tile : width + (c + 1) * tile] = edge_ref[c, at].astype(kind)


def sum_kernel(subs, width, *refs):
    part_refs, (mid_ref, edge_ref) = refs[:subs], refs[subs:]
    total = part_refs[0][...]
    for k in range(1, subs):
        total = total + part_refs[k][...].astype(F32)
    mid_ref[...] = total[:, :width].astype(BF16)
    sums = total[:, width:]
    high = sums.astype(BF16)
    edge_ref[:COARSE_ROWS] = high
    edge_ref[COARSE_ROWS:] = (sums - high.astype(F32)).astype(BF16)


def finish_kernel(subs, half, pair_ref, near_ref, far_ref, mid_ref, both_ref, out_ref, edge):
    rows, tile = near_ref.shape[:2]
    width = 2 * half * tile
    odd = lax.rem(lax.axis_index("dom"), 2)
    edge[pl.ds((1 - odd) * rows, rows)] = near_ref[...]
    edge[pl.ds(odd * rows, rows)] = far_ref[...]
    out_ref[:, width : 2 * width] = mid_ref[...]
    both = both_ref[...]
    for side in range(2):
        blocks = [jnp.zeros((COARSE_ROWS, tile), F32) for _ in range(2 * half)]
        tiles = range(side * rows, (side + 1) * rows)
        if half == 1:
            stacked = jnp.concatenate([edge[c] for c in tiles], axis=0)
            lhs = both[:, side * rows * tile : (side + 1) * rows * tile]
            term = jnp.dot(lhs, stacked, preferred_element_type=F32)
            term = term[:COARSE_ROWS] + term[COARSE_ROWS:]
            blocks = [term[:, :tile], term[:, tile:]]
        else:
            for c in tiles:
                lhs = both[:, c * tile : (c + 1) * tile]
                term = jnp.dot(lhs, edge[c], preferred_element_type=F32)
                term = term[:COARSE_ROWS] + term[COARSE_ROWS:]
                m_here = pair_ref[c if side == 0 else subs * rows + c]
                for m in range(half):
                    here = m_here == m
                    blocks[m] = blocks[m] + jnp.where(here, term[:, :tile], 0.0)
                    blocks[m + half] = blocks[m + half] + jnp.where(here, term[:, tile:], 0.0)
        for b in range(2 * half):
            at = 2 * side * width + b * tile
            out_ref[:, at : at + tile] = blocks[b].astype(BF16)


def local(a_tiles, a_cols, a_count, p_tiles, p_cols):
    rows, slots, tile = a_tiles.shape[:3]
    subs, doms = lax.axis_size("sub"), lax.axis_size("dom")
    coarse_group = subs * COARSE_ROWS // tile
    half = coarse_group // 2
    width = coarse_group * tile
    group_tiles = rows * subs

    smem = pl.BlockSpec(memory_space=pltpu.SMEM)
    vmem = pl.BlockSpec(memory_space=pltpu.VMEM)
    p_bytes = rows * tile * 2 * tile * 2
    a_bytes = a_tiles.size * 2
    spare = 3 << 20

    def exchange(value, k):
        return lax.ppermute(value, "sub", [(s, s ^ k) for s in range(subs)])

    own = pl.pallas_call(
        order_kernel,
        out_shape=jax.ShapeDtypeStruct(p_tiles.shape, BF16),
        in_specs=[smem, vmem],
        out_specs=vmem,
        compiler_params=pltpu.CompilerParams(vmem_limit_bytes=spare),
        cost_estimate=pl.CostEstimate(
            flops=1 << 30, bytes_accessed=2 * p_bytes, transcendentals=0
        ),
        name="order_columns",
    )(p_cols.T, p_tiles)

    if half == 1:
        pair = jnp.zeros((1,), jnp.int32)
    else:
        m_own = jnp.min(p_cols, axis=1) - lax.axis_index("dom") * coarse_group
        m_group = lax.all_gather(m_own, "sub", axis=0, tiled=True)
        m_left = lax.ppermute(
            m_group[group_tiles - rows :], "dom", [(d, d + 1) for d in range(doms - 1)]
        )
        m_right = lax.ppermute(m_group[:rows], "dom", [(d + 1, d) for d in range(doms - 1)])
        pair = jnp.concatenate([m_left, m_group, m_right])

    flops = 2 * rows * slots * tile * tile * 2 * tile * half
    edges = pl.pallas_call(
        functools.partial(edge_kernel, subs, half),
        out_shape=jax.ShapeDtypeStruct((2 * rows, width, tile), F32),
        in_specs=[smem, smem, smem, vmem, vmem],
        out_specs=vmem,
        scratch_shapes=[pltpu.VMEM((rows, 2 * tile, tile), BF16)],
        compiler_params=pltpu.CompilerParams(vmem_limit_bytes=8 * rows * tile * width + spare),
        cost_estimate=pl.CostEstimate(
            flops=flops, bytes_accessed=a_bytes + p_bytes, transcendentals=0
        ),
        name="edge_part",
    )(a_cols, a_count, pair, a_tiles, own)

    tiles = [own] + [exchange(own, k) for k in range(1, subs)]
    span = width + 2 * rows * tile
    *parts, pool = pl.pallas_call(
        functools.partial(group_kernel, subs, half),
        out_shape=[
            jax.ShapeDtypeStruct((COARSE_ROWS, span), F32 if k == 0 else BF16)
            for k in range(subs)
        ]
        + [jax.ShapeDtypeStruct((group_tiles + 1, tile, 2 * tile), BF16)],
        in_specs=[smem, smem, smem] + [vmem] * (subs + 2),
        out_specs=[vmem] * (subs + 1),
        scratch_shapes=[
            pltpu.VMEM((rows * tile, width), BF16),
            pltpu.VMEM((width, width), F32),
        ],
        compiler_params=pltpu.CompilerParams(
            vmem_limit_bytes=2 * rows * tile * width + 4 * width * width + spare
        ),
        cost_estimate=pl.CostEstimate(
            flops=flops, bytes_accessed=a_bytes + subs * p_bytes, transcendentals=0
        ),
        name="group_part",
    )(a_cols, a_count, pair, a_tiles, edges, *tiles)
    received = [exchange(parts[k], k) for k in range(1, subs)]
    to_near, to_far = pl.pallas_call(
        functools.partial(hand_out_kernel, subs),
        out_shape=[jax.ShapeDtypeStruct(p_tiles.shape, BF16)] * 2,
        in_specs=[vmem],
        out_specs=[vmem] * 2,
        compiler_params=pltpu.CompilerParams(vmem_limit_bytes=spare),
        name="hand_out",
    )(pool)
    far = lax.ppermute(
        to_far, "dom", [(d, d - 1 + 2 * (d % 2)) for d in range(1, doms - 1)]
    )
    near = lax.ppermute(to_near, "dom", [(d, d ^ 1) for d in range(doms)])
    mid, both = pl.pallas_call(
        functools.partial(sum_kernel, subs, width),
        out_shape=[
            jax.ShapeDtypeStruct((COARSE_ROWS, width), BF16),
            jax.ShapeDtypeStruct((2 * COARSE_ROWS, span - width), BF16),
        ],
        in_specs=[vmem] * subs,
        out_specs=[vmem] * 2,
        compiler_params=pltpu.CompilerParams(vmem_limit_bytes=spare),
        cost_estimate=pl.CostEstimate(
            flops=1 << 31, bytes_accessed=8 * COARSE_ROWS * span, transcendentals=0
        ),
        name="sum_parts",
    )(parts[0], *received)
    return pl.pallas_call(
        functools.partial(finish_kernel, subs, half),
        out_shape=jax.ShapeDtypeStruct((COARSE_ROWS, 3 * width), BF16),
        in_specs=[smem] + [vmem] * 4,
        out_specs=vmem,
        scratch_shapes=[pltpu.VMEM((2 * rows, tile, 2 * tile), BF16)],
        compiler_params=pltpu.CompilerParams(vmem_limit_bytes=2 * p_bytes + spare),
        cost_estimate=pl.CostEstimate(
            flops=1 << 28, bytes_accessed=4 * p_bytes, transcendentals=0
        ),
        name="finish",
    )(pair, near, far, mid, both)


def solution(mesh):
    placed = (
        P(("dom", "sub"), None, None, None),
        P(("dom", "sub"), None),
        P(("dom", "sub")),
        P(("dom", "sub"), None, None),
        P(("dom", "sub"), None),
    )
    return jax.shard_map(
        local, mesh=mesh, in_specs=placed, out_specs=P(("dom", "sub"), None), check_vma=False
    )
```

time: 43.2 us -> 32.4 us (0.75)
  starting transfers between devices: 17.7 us -> 10.9 us
  waiting for transfers between devices: 19 us -> 14.7 us
  Pallas kernels: 3.92 us -> 4.9 us
  other arithmetic: 0.69 us -> 0 us
    ppermute x9 -> x6, starting transfers between devices: 9.69 us -> 6.16 us  [exchange(): return lax.ppermute(value, 'sub', [(s, s ^ k) for s in range(subs)])]
    ppermute x2, starting transfers between devices: 7.97 us -> 4.77 us  [the longest x1 3.1 us: local(): lax.ppermute(to_far, 'dom', [(d, d - 1 + 2 * (d % 2)) for d in range(1, d...]
    ppermute x2, waiting for transfers between devices: 4.4 us -> 1.96 us  [the longest x1 1.95 us: local(): lax.ppermute(to_far, 'dom', [(d, d - 1 + 2 * (d % 2)) for d in range(1, d...]
    ppermute x9 -> x6, waiting for transfers between devices: 14.6 us -> 12.7 us  [exchange(): return lax.ppermute(value, 'sub', [(s, s ^ k) for s in range(subs)])]
    pallas_call x3 -> x6, Pallas kernels: 3.92 us -> 4.9 us  [the longest x1 1.77 us: local(): pl.pallas_call(functools.partial(edge_kernel, subs, half), out_shape=jax....]
    convert_element_type x1 -> x0, other arithmetic: 0.69 us -> none  [local(): return owned.astype(BF16)]
  transfers between devices with their start and end apart: 11 -> 8, of which waited for: 6 -> 4; matrix products, arithmetic and copies ran while one was open for 0% -> 0% of each run, Pallas kernels for 3% -> 6%
where the time goes in v2:
time: 32.4 us; the launch traced here: 32.2 us
  waiting for transfers between devices  14.7 us (45%)
  starting transfers between devices  10.9 us (34%)
  Pallas kernels  4.9 us (15%)
  local copies, waits for them, and re-layouts  1.64 us (5%)
    ppermute x6, waiting for transfers between devices, exchange(): return lax.ppermute(value, 'sub', [(s, s ^ k) for s in range(subs)])  12.7 us
    ppermute x6, starting transfers between devices, exchange(): return lax.ppermute(value, 'sub', [(s, s ^ k) for s in range(subs)])  6.16 us
    ppermute x1, starting transfers between devices, local(): lax.ppermute(to_far, 'dom', [(d, d - 1 + 2 * (d % 2)) for d in range(1, d...  3.1 us
    ppermute x1, waiting for transfers between devices, local(): lax.ppermute(to_far, 'dom', [(d, d - 1 + 2 * (d % 2)) for d in range(1, d...  1.95 us
    pallas_call x1, Pallas kernels, local(): pl.pallas_call(functools.partial(edge_kernel, subs, half), out_shape=jax....  1.77 us
    ppermute x1, starting transfers between devices, local(): near = lax.ppermute(to_near, 'dom', [(d, d ^ 1) for d in range(doms)])  1.67 us
    unnamed x10, local copies, waits for them, and re-layouts  1.64 us
    pallas_call x1, Pallas kernels, local(): pl.pallas_call(functools.partial(group_kernel, subs, half), out_shape=[ja...  1.46 us
  transfers between devices with their start and end apart: 8, of which 4 were waited for; matrix products, arithmetic and copies ran while one was open for 0% of the time, Pallas kernels for 6%

profile of v2, /device:TPU:1, one launch (start us, length us, event | category | flops | bytes accessed | tf_op | source)
XLA Modules:
  0.0 32.2 jit_solution(8733173802740324622)
XLA Ops:
  0.0 0.0 copy-start.3
  0.0 0.9 %copy-done.3 = bf16[4,128,256]{2,1,0:T(8,128)(2,1)S(1)} copy-done((bf16[4,128,256]{2,1,0:T(8,128)(2,1)S(1)}, bf16[4,128,256]{2,1,0:T(8,128)(2,1)}, u32[]{:S(2)}) %copy-start.3) | copy-done | bytes 262168
  1.0 0.0 copy-start.4
  1.0 0.7 %copy-done.4 = s32[4,2]{0,1:T(2,128)S(1)} copy-done((s32[4,2]{0,1:T(2,128)S(1)}, s32[4,2]{0,1:T(2,128)}, u32[]{:S(2)}) %copy-start.4) | copy-done | bytes 56
  1.6 0.0 copy-start
  1.6 0.0 copy-start.1
  1.6 0.0 copy-start.2
  1.6 0.6 %order_columns.1.own_ref.rest_0_ = bf16[4,128,256]{2,1,0:T(8,128)(2,1)S(1)} custom-call(s32[2,4]{1,0:T(2,128)S(1)} %bitcast.1, bf16[4,128,256]{2,1,0:T(8,128)(2,1)S(1)} %copy-done.3), custom_call_target="tpu_custom_call" | custom-call | flops 1073741824 | bytes 524288 | tf_op jit(solution)/shard_map/order_columns/pallas_call | solution.py:182
  2.2 3.1 %collective-permute-start.2 = (bf16[4,128,256]{2,1,0:T(8,128)(2,1)S(1)}, bf16[4,128,256]{2,1,0:T(8,128)(2,1)S(1)}, u32[]{:S(2)}, u32[]{:S(2)}) collective-permute-start(bf16[4,128,256]{2,1,0:T(8,128)(2,1)S(1)} %order_columns.1.own_ref.rest_0_), channel_id=1, source_target_pairs={{0,3},{1,2},{2,1},{3,0},{4,7},{5,6},{6,5},{7,4},{8,11},{9,10},{10,... | collective-permute-start | bytes 786440 | tf_op jit(solution)/shard_map/ppermute | solution.py:180
  5.3 0.2 collective-permute-start.1
  5.5 0.1 collective-permute-start
  5.7 0.0 copy-done
  5.7 0.0 copy-done.1
  5.7 0.0 copy-done.2
  5.7 1.8 %edge_part.1.edge_ref = f32[8,256,128]{2,1,0:T(8,128)S(1)} custom-call(s32[4,10]{1,0:T(4,128)S(1)} %copy-done.1, s32[4]{0:T(128)S(1)} %copy-done.2, s32[1]{0:T(128)} %constant.0.clone.1.pair_ref, bf16[4,10,128,128]{3,2,1,0:T(8,128)(2,1)S(1)} %copy-done, bf16[4,128,256]{2,1,0:T(8,128)(2,1)S(1)} %order_columns.1.own_ref.rest_0_), custom_call_target="tpu_custom_call" | custom-call | flops 335544320 | bytes 1572864 | tf_op jit(solution)/shard_map/edge_part/pallas_call | solution.py:206
  7.5 3.9 %collective-permute-done.2.rest_3_ = bf16[4,128,256]{2,1,0:T(8,128)(2,1)S(1)} collective-permute-done((bf16[4,128,256]{2,1,0:T(8,128)(2,1)S(1)}, bf16[4,128,256]{2,1,0:T(8,128)(2,1)S(1)}, u32[]{:S(2)}, u32[]{:S(2)}) %collective-permute-start.2) | collective-permute-done | bytes 262176 | tf_op jit(solution)/shard_map/ppermute | solution.py:180
  11.4 6.3 %collective-permute-done.1.rest_2_ = bf16[4,128,256]{2,1,0:T(8,128)(2,1)S(1)} collective-permute-done((bf16[4,128,256]{2,1,0:T(8,128)(2,1)S(1)}, bf16[4,128,256]{2,1,0:T(8,128)(2,1)S(1)}, u32[]{:S(2)}, u32[]{:S(2)}) %collective-permute-start.1) | collective-permute-done | bytes 262176 | tf_op jit(solution)/shard_map/ppermute | solution.py:180
  17.7 0.0 collective-permute-done.rest_1_
  17.7 1.5 %group_part.1 = (f32[64,1280]{1,0:T(8,128)S(1)}, bf16[64,1280]{1,0:T(8,128)(2,1)S(1)}, bf16[64,1280]{1,0:T(8,128)(2,1)S(1)}, bf16[64,1280]{1,0:T(8,128)(2,1)S(1)}, bf16[17,128,256]{2,1,0:T(8,128)(2,1)S(1)}) custom-call(s32[4,10]{1,0:T(4,128)S(1)} %copy-done.1, s32[4]{0:T(128)S(1)} %copy-done.2, s32[1]{0:T(128)} %constant.0.clone.1.pair_ref, ...), custom_call_target="tpu_custom_call" | custom-call | flops 335544320 | bytes 2359296 | tf_op jit(solution)/shard_map/group_part/pallas_call | solution.py:221
  19.2 1.5 %collective-permute-start.5 = (bf16[64,1280]{1,0:T(8,128)(2,1)S(1)}, bf16[64,1280]{1,0:T(8,128)(2,1)S(1)}, u32[]{:S(2)}, u32[]{:S(2)}) collective-permute-start(bf16[64,1280]{1,0:T(8,128)(2,1)S(1)} %get-tuple-element.18), channel_id=1, source_target_pairs={{0,1},{1,0},{2,3},{3,2},{4,5},{5,4},{6,7},{7,6},{8,9},{9,8},{10,11... | collective-permute-start | bytes 491528 | tf_op jit(solution)/shard_map/ppermute | solution.py:180
  20.6 0.1 collective-permute-start.6
  20.7 1.2 %collective-permute-start.7 = (bf16[64,1280]{1,0:T(8,128)(2,1)S(1)}, bf16[64,1280]{1,0:T(8,128)(2,1)S(1)}, u32[]{:S(2)}, u32[]{:S(2)}) collective-permute-start(bf16[64,1280]{1,0:T(8,128)(2,1)S(1)} %get-tuple-element.20), channel_id=1, source_target_pairs={{0,3},{1,2},{2,1},{3,0},{4,7},{5,6},{6,5},{7,4},{8,11},{9,10},{10,... | collective-permute-start | bytes 491528 | tf_op jit(solution)/shard_map/ppermute | solution.py:180
  21.9 1.7 %collective-permute-start.3 = (bf16[4,128,256]{2,1,0:T(8,128)(2,1)S(1)}, bf16[4,128,256]{2,1,0:T(8,128)(2,1)S(1)}, u32[]{:S(2)}, u32[]{:S(2)}) collective-permute-start(bf16[4,128,256]{2,1,0:T(8,128)(2,1)S(1)} %get-tuple-element.15), channel_id=1, source_target_pairs={{0,4},{4,0},{8,12},{12,8},{16,20},{20,16},{24,28},{28,24},{1,5},{5... | collective-permute-start | bytes 786440 | tf_op jit(solution)/shard_map/ppermute | solution.py:254
  23.6 3.1 %collective-permute-start.4 = (bf16[4,128,256]{2,1,0:T(8,128)(2,1)S(1)}, bf16[4,128,256]{2,1,0:T(8,128)(2,1)S(1)}, u32[]{:S(2)}, u32[]{:S(2)}) collective-permute-start(bf16[4,128,256]{2,1,0:T(8,128)(2,1)S(1)} %get-tuple-element.16), channel_id=1, source_target_pairs={{4,8},{8,4},{12,16},{16,12},{20,24},{24,20},{5,9},{9,5},{13,17},{1... | collective-permute-start | bytes 786440 | tf_op jit(solution)/shard_map/ppermute | solution.py:251
  26.7 0.0 collective-permute-done.5.refs_1_
  26.7 0.0 collective-permute-done.6.refs_2_
  26.7 2.5 %collective-permute-done.7.refs_3_ = bf16[64,1280]{1,0:T(8,128)(2,1)S(1)} collective-permute-done((bf16[64,1280]{1,0:T(8,128)(2,1)S(1)}, bf16[64,1280]{1,0:T(8,128)(2,1)S(1)}, u32[]{:S(2)}, u32[]{:S(2)}) %collective-permute-start.7) | collective-permute-done | bytes 163872 | tf_op jit(solution)/shard_map/ppermute | solution.py:180
  29.2 0.1 sum_parts.1
  29.3 0.0 collective-permute-done.3.near_ref
  29.3 2.0 %collective-permute-done.4.far_ref = bf16[4,128,256]{2,1,0:T(8,128)(2,1)S(1)} collective-permute-done((bf16[4,128,256]{2,1,0:T(8,128)(2,1)S(1)}, bf16[4,128,256]{2,1,0:T(8,128)(2,1)S(1)}, u32[]{:S(2)}, u32[]{:S(2)}) %collective-permute-start.4) | collective-permute-done | bytes 262176 | tf_op jit(solution)/shard_map/ppermute | solution.py:251
  31.3 0.9 %finish.1 = bf16[64,768]{1,0:T(8,128)(2,1)} custom-call(s32[1]{0:T(128)} %constant.0.clone.1.pair_ref, bf16[4,128,256]{2,1,0:T(8,128)(2,1)S(1)} %collective-permute-done.3.near_ref, bf16[4,128,256]{2,1,0:T(8,128)(2,1)S(1)} %collective-permute-done.4.far_ref, bf16[64,256]{1,0:T(8,128)(2,1)S(1)} %get-tuple-element.21.mid_ref, ...), custom_call_target="tpu_custom_call" | custom-call | flops 268435456 | bytes 1048576 | tf_op jit(solution)/shard_map/finish/pallas_call | solution.py:269
  (1 shorter events, 0.0 us)
Async XLA Ops:
  0.0 0.9 %copy-start.3 = (bf16[4,128,256]{2,1,0:T(8,128)(2,1)S(1)}, bf16[4,128,256]{2,1,0:T(8,128)(2,1)}, u32[]{:S(2)}) copy-start(bf16[4,128,256]{2,1,0:T(8,128)(2,1)} %p_ref.1) | copy-start | bytes 786436
  1.0 0.7 %copy-start.4 = (s32[4,2]{0,1:T(2,128)S(1)}, s32[4,2]{0,1:T(2,128)}, u32[]{:S(2)}) copy-start(s32[4,2]{0,1:T(2,128)} %param.9) | copy-start | bytes 100
  1.6 4.0 %copy-start = (bf16[4,10,128,128]{3,2,1,0:T(8,128)(2,1)S(1)}, bf16[4,10,128,128]{3,2,1,0:T(8,128)(2,1)}, u32[]{:S(2)}) copy-start(bf16[4,10,128,128]{3,2,1,0:T(8,128)(2,1)} %a_ref.3) | copy-start | bytes 3932164
  1.6 4.0 %copy-start.1 = (s32[4,10]{1,0:T(4,128)S(1)}, s32[4,10]{1,0:T(4,128)}, u32[]{:S(2)}) copy-start(s32[4,10]{1,0:T(4,128)} %cols_ref.3) | copy-start | bytes 484
  1.6 4.0 %copy-start.2 = (s32[4]{0:T(128)S(1)}, s32[4]{0:T(128)}, u32[]{:S(2)}) copy-start(s32[4]{0:T(128)} %count_ref.3) | copy-start | bytes 52
  2.2 9.1 %collective-permute-start.2 = (bf16[4,128,256]{2,1,0:T(8,128)(2,1)S(1)}, bf16[4,128,256]{2,1,0:T(8,128)(2,1)S(1)}, u32[]{:S(2)}, u32[]{:S(2)}) collective-permute-start(bf16[4,128,256]{2,1,0:T(8,128)(2,1)S(1)} %order_columns.1.own_ref.rest_0_), channel_id=1, source_target_pairs={{0,3},{1,2},{2,1},{3,0},{4,7},{5,6},{6,5},{7,4},{8,11},{9,10},{10,... | collective-permute-start | bytes 786440 | tf_op jit(solution)/shard_map/ppermute | solution.py:180
  5.3 12.4 %collective-permute-start.1 = (bf16[4,128,256]{2,1,0:T(8,128)(2,1)S(1)}, bf16[4,128,256]{2,1,0:T(8,128)(2,1)S(1)}, u32[]{:S(2)}, u32[]{:S(2)}) collective-permute-start(bf16[4,128,256]{2,1,0:T(8,128)(2,1)S(1)} %order_columns.1.own_ref.rest_0_), channel_id=1, source_target_pairs={{0,2},{1,3},{2,0},{3,1},{4,6},{5,7},{6,4},{7,5},{8,10},{9,11},{10,... | collective-permute-start | bytes 786440 | tf_op jit(solution)/shard_map/ppermute | solution.py:180
  5.5 12.2 %collective-permute-start = (bf16[4,128,256]{2,1,0:T(8,128)(2,1)S(1)}, bf16[4,128,256]{2,1,0:T(8,128)(2,1)S(1)}, u32[]{:S(2)}, u32[]{:S(2)}) collective-permute-start(bf16[4,128,256]{2,1,0:T(8,128)(2,1)S(1)} %order_columns.1.own_ref.rest_0_), channel_id=1, source_target_pairs={{0,1},{1,0},{2,3},{3,2},{4,5},{5,4},{6,7},{7,6},{8,9},{9,8},{10,11... | collective-permute-start | bytes 786440 | tf_op jit(solution)/shard_map/ppermute | solution.py:180
  19.2 7.6 %collective-permute-start.5 = (bf16[64,1280]{1,0:T(8,128)(2,1)S(1)}, bf16[64,1280]{1,0:T(8,128)(2,1)S(1)}, u32[]{:S(2)}, u32[]{:S(2)}) collective-permute-start(bf16[64,1280]{1,0:T(8,128)(2,1)S(1)} %get-tuple-element.18), channel_id=1, source_target_pairs={{0,1},{1,0},{2,3},{3,2},{4,5},{5,4},{6,7},{7,6},{8,9},{9,8},{10,11... | collective-permute-start | bytes 491528 | tf_op jit(solution)/shard_map/ppermute | solution.py:180
  20.6 6.1 %collective-permute-start.6 = (bf16[64,1280]{1,0:T(8,128)(2,1)S(1)}, bf16[64,1280]{1,0:T(8,128)(2,1)S(1)}, u32[]{:S(2)}, u32[]{:S(2)}) collective-permute-start(bf16[64,1280]{1,0:T(8,128)(2,1)S(1)} %get-tuple-element.19), channel_id=1, source_target_pairs={{0,2},{1,3},{2,0},{3,1},{4,6},{5,7},{6,4},{7,5},{8,10},{9,11},{10,... | collective-permute-start | bytes 491528 | tf_op jit(solution)/shard_map/ppermute | solution.py:180
  20.7 8.5 %collective-permute-start.7 = (bf16[64,1280]{1,0:T(8,128)(2,1)S(1)}, bf16[64,1280]{1,0:T(8,128)(2,1)S(1)}, u32[]{:S(2)}, u32[]{:S(2)}) collective-permute-start(bf16[64,1280]{1,0:T(8,128)(2,1)S(1)} %get-tuple-element.20), channel_id=1, source_target_pairs={{0,3},{1,2},{2,1},{3,0},{4,7},{5,6},{6,5},{7,4},{8,11},{9,10},{10,... | collective-permute-start | bytes 491528 | tf_op jit(solution)/shard_map/ppermute | solution.py:180
  21.9 7.4 %collective-permute-start.3 = (bf16[4,128,256]{2,1,0:T(8,128)(2,1)S(1)}, bf16[4,128,256]{2,1,0:T(8,128)(2,1)S(1)}, u32[]{:S(2)}, u32[]{:S(2)}) collective-permute-start(bf16[4,128,256]{2,1,0:T(8,128)(2,1)S(1)} %get-tuple-element.15), channel_id=1, source_target_pairs={{0,4},{4,0},{8,12},{12,8},{16,20},{20,16},{24,28},{28,24},{1,5},{5... | collective-permute-start | bytes 786440 | tf_op jit(solution)/shard_map/ppermute | solution.py:254
  23.6 7.7 %collective-permute-start.4 = (bf16[4,128,256]{2,1,0:T(8,128)(2,1)S(1)}, bf16[4,128,256]{2,1,0:T(8,128)(2,1)S(1)}, u32[]{:S(2)}, u32[]{:S(2)}) collective-permute-start(bf16[4,128,256]{2,1,0:T(8,128)(2,1)S(1)} %get-tuple-element.16), channel_id=1, source_target_pairs={{4,8},{8,4},{12,16},{16,12},{20,24},{24,20},{5,9},{9,5},{13,17},{1... | collective-permute-start | bytes 786440 | tf_op jit(solution)/shard_map/ppermute | solution.py:251

commit v3 on v2

--- a/solution.py
+++ b/solution.py
@@ -41,12 +41,13 @@
     return outs
 
 
-def order_kernel(cols_ref, p_ref, own_ref):
+def order_kernel(cols_ref, p_ref, *outs):
     rows, tile = p_ref.shape[:2]
+    piece = rows // 2
     for f in range(rows):
         first = pl.multiple_of(jnp.where(cols_ref[0, f] > cols_ref[1, f], tile, 0), tile)
         for t, start in ((0, first), (1, pl.multiple_of(tile - first, tile))):
-            own_ref[f, :, t * tile : (t + 1) * tile] = p_ref[f, :, pl.ds(start, tile)]
+            outs[f // piece][f % piece, :, t * tile : (t + 1) * tile] = p_ref[f, :, pl.ds(start, tile)]
 
 
 def hand_out_kernel(subs, pool, near_ref, far_ref):
@@ -57,13 +58,13 @@
     far_ref[...] = pool[pl.ds(odd * last, rows)]
 
 
-def edge_kernel(subs, half, cols_ref, count_ref, pair_ref, a_ref, own_ref, out_ref, turned):
+def edge_kernel(subs, half, cols_ref, count_ref, pair_ref, a_ref, own_0, own_1, out_ref, turned):
     rows, slots, tile = a_ref.shape[:3]
     first = lax.axis_index("dom") * (subs * rows)
     me = lax.axis_index("sub")
     out_ref[...] = jnp.zeros(out_ref.shape, F32)
     for f in range(rows):
-        turned[f] = own_ref[f].T
+        turned[f] = (own_0, own_1)[f // (rows // 2)][f % (rows // 2)].T
     for f in range(rows):
         for k in range(slots):
             rel = cols_ref[f, k] - first
@@ -82,15 +83,17 @@
 
 
 def group_kernel(subs, half, cols_ref, count_ref, pair_ref, a_ref, edge_ref, *rest):
-    p_refs, rest = rest[:subs], rest[subs:]
+    p_refs, rest = rest[: 2 * subs], rest[2 * subs :]
     outs, (pool, q, mid_ref) = rest[:subs], rest[subs:]
     rows, slots, tile = a_ref.shape[0], a_ref.shape[1], a_ref.shape[2]
     zero = subs * rows
     width = 2 * half * tile
     me = lax.axis_index("sub")
     first = lax.axis_index("dom") * (subs * rows)
+    piece = rows // 2
     for k in range(subs):
-        pool[pl.ds(lax.bitwise_xor(me, k) * rows, rows)] = p_refs[k][...]
+        for i in range(2):
+            pool[pl.ds(lax.bitwise_xor(me, k) * rows + i * piece, piece)] = p_refs[2 * k + i][...]
     pool[zero] = jnp.zeros(pool.shape[1:], pool.dtype)
     for f in range(rows):
         a_row = side_by_side(a_ref, f)
@@ -130,7 +133,7 @@
     edge_ref[COARSE_ROWS:] = (sums - high.astype(F32)).astype(BF16)
 
 
-def finish_kernel(subs, half, pair_ref, near_ref, far_ref, mid_ref, both_ref, out_ref, edge):
+def finish_kernel(subs, half, pair_ref, far_ref, near_ref, mid_ref, both_ref, out_ref, edge):
     rows, tile = near_ref.shape[:2]
     width = 2 * half * tile
     odd = lax.rem(lax.axis_index("dom"), 2)
@@ -181,9 +184,9 @@
 
     own = pl.pallas_call(
         order_kernel,
-        out_shape=jax.ShapeDtypeStruct(p_tiles.shape, BF16),
+        out_shape=[jax.ShapeDtypeStruct((rows // 2, tile, 2 * tile), BF16)] * 2,
         in_specs=[smem, vmem],
-        out_specs=vmem,
+        out_specs=[vmem] * 2,
         compiler_params=pltpu.CompilerParams(vmem_limit_bytes=spare),
         cost_estimate=pl.CostEstimate(
             flops=1 << 30, bytes_accessed=2 * p_bytes, transcendentals=0
@@ -206,7 +209,7 @@
     edges = pl.pallas_call(
         functools.partial(edge_kernel, subs, half),
         out_shape=jax.ShapeDtypeStruct((2 * rows, width, tile), F32),
-        in_specs=[smem, smem, smem, vmem, vmem],
+        in_specs=[smem, smem, smem, vmem, vmem, vmem],
         out_specs=vmem,
         scratch_shapes=[pltpu.VMEM((rows, 2 * tile, tile), BF16)],
         compiler_params=pltpu.CompilerParams(vmem_limit_bytes=8 * rows * tile * width + spare),
@@ -214,9 +217,13 @@
             flops=flops, bytes_accessed=a_bytes + p_bytes, transcendentals=0
         ),
         name="edge_part",
-    )(a_cols, a_count, pair, a_tiles, own)
-
-    tiles = [own] + [exchange(own, k) for k in range(1, subs)]
+    )(a_cols, a_count, pair, a_tiles, *own)
+
+    tiles = [list(own)] + [[None, None] for _ in range(subs - 1)]
+    for k in range(1, subs):
+        low, high = k & -k, 1 << (k.bit_length() - 1)
+        tiles[k][0] = exchange(tiles[k ^ low][0], low)
+        tiles[k][1] = exchange(tiles[k ^ high][1], high)
     span = width + 2 * rows * tile
     *parts, pool = pl.pallas_call(
         functools.partial(group_kernel, subs, half),
@@ -225,7 +232,7 @@
             for k in range(subs)
         ]
         + [jax.ShapeDtypeStruct((group_tiles + 1, tile, 2 * tile), BF16)],
-        in_specs=[smem, smem, smem] + [vmem] * (subs + 2),
+        in_specs=[smem, smem, smem] + [vmem] * (2 * subs + 2),
         out_specs=[vmem] * (subs + 1),
         scratch_shapes=[
             pltpu.VMEM((rows * tile, width), BF16),
@@ -238,7 +245,7 @@
             flops=flops, bytes_accessed=a_bytes + subs * p_bytes, transcendentals=0
         ),
         name="group_part",
-    )(a_cols, a_count, pair, a_tiles, edges, *tiles)
+    )(a_cols, a_count, pair, a_tiles, edges, *sum(tiles, []))
     received = [exchange(parts[k], k) for k in range(1, subs)]
     to_near, to_far = pl.pallas_call(
         functools.partial(hand_out_kernel, subs),
@@ -277,7 +284,7 @@
             flops=1 << 28, bytes_accessed=4 * p_bytes, transcendentals=0
         ),
         name="finish",
-    )(pair, near, far, mid, both)
+    )(pair, far, near, mid, both)
 
 
 def solution(mesh):

time: 32.4 us -> 30 us (0.926)
  waiting for transfers between devices: 14.7 us -> 7.51 us
  starting transfers between devices: 10.9 us -> 15.4 us
    ppermute x6 -> x9, waiting for transfers between devices: 12.7 us -> 3.69 us  [exchange(): return lax.ppermute(value, 'sub', [(s, s ^ k) for s in range(subs)])]
    ppermute x1, starting transfers between devices: 3.1 us -> 6.61 us  [local(): lax.ppermute(to_far, 'dom', [(d, d - 1 + 2 * (d % 2)) for d in range(1, d...]
    ppermute x6 -> x9, starting transfers between devices: 6.16 us -> 8.74 us  [exchange(): return lax.ppermute(value, 'sub', [(s, s ^ k) for s in range(subs)])]
    ppermute x1, waiting for transfers between devices: 1.95 us -> 3.82 us  [local(): lax.ppermute(to_far, 'dom', [(d, d - 1 + 2 * (d % 2)) for d in range(1, d...]
    ppermute x1, starting transfers between devices: 1.67 us -> 0.07 us  [local(): near = lax.ppermute(to_near, 'dom', [(d, d ^ 1) for d in range(doms)])]
  transfers between devices with their start and end apart: 8 -> 11, of which waited for: 4 -> 3; matrix products, arithmetic and copies ran while one was open for 0% -> 0% of each run, Pallas kernels for 6% -> 7%
where the time goes in v3:
time: 30 us; the launch traced here: 29.9 us
  starting transfers between devices  15.4 us (51%)
  waiting for transfers between devices  7.51 us (25%)
  Pallas kernels  5.19 us (17%)
  local copies, waits for them, and re-layouts  1.64 us (5%)
    ppermute x9, starting transfers between devices, exchange(): return lax.ppermute(value, 'sub', [(s, s ^ k) for s in range(subs)])  8.74 us
    ppermute x1, starting transfers between devices, local(): lax.ppermute(to_far, 'dom', [(d, d - 1 + 2 * (d % 2)) for d in range(1, d...  6.61 us
    ppermute x1, waiting for transfers between devices, local(): lax.ppermute(to_far, 'dom', [(d, d - 1 + 2 * (d % 2)) for d in range(1, d...  3.82 us
    ppermute x9, waiting for transfers between devices, exchange(): return lax.ppermute(value, 'sub', [(s, s ^ k) for s in range(subs)])  3.69 us
    pallas_call x1, Pallas kernels, local(): pl.pallas_call(functools.partial(edge_kernel, subs, half), out_shape=jax....  2.05 us
    unnamed x10, local copies, waits for them, and re-layouts  1.64 us
    pallas_call x1, Pallas kernels, local(): pl.pallas_call(functools.partial(group_kernel, subs, half), out_shape=[ja...  1.46 us
    pallas_call x1, Pallas kernels, local(): pl.pallas_call(functools.partial(finish_kernel, subs, half), out_shape=ja...  0.93 us
  transfers between devices with their start and end apart: 11, of which 3 were waited for; matrix products, arithmetic and copies ran while one was open for 0% of the time, Pallas kernels for 7%

profile of v3, /device:TPU:1, one launch (start us, length us, event | category | flops | bytes accessed | tf_op | source)
XLA Modules:
  0.0 29.9 jit_solution(4786240548869372062)
XLA Ops:
  0.0 0.9 %copy-done.3 = bf16[4,128,256]{2,1,0:T(8,128)(2,1)S(1)} copy-done((bf16[4,128,256]{2,1,0:T(8,128)(2,1)S(1)}, bf16[4,128,256]{2,1,0:T(8,128)(2,1)}, u32[]{:S(2)}) %copy-start.3) | copy-done | bytes 262168
  1.0 0.7 %copy-done.4 = s32[4,2]{0,1:T(2,128)S(1)} copy-done((s32[4,2]{0,1:T(2,128)S(1)}, s32[4,2]{0,1:T(2,128)}, u32[]{:S(2)}) %copy-start.4) | copy-done | bytes 56
  1.6 0.6 %order_columns.1 = (bf16[2,128,256]{2,1,0:T(8,128)(2,1)S(1)}, bf16[2,128,256]{2,1,0:T(8,128)(2,1)S(1)}) custom-call(s32[2,4]{1,0:T(2,128)S(1)} %bitcast.1, bf16[4,128,256]{2,1,0:T(8,128)(2,1)S(1)} %copy-done.3), custom_call_target="tpu_custom_call" | custom-call | flops 1073741824 | bytes 524288 | tf_op jit(solution)/shard_map/order_columns/pallas_call | solution.py:185
  2.2 2.1 %collective-permute-start.2 = (bf16[2,128,256]{2,1,0:T(8,128)(2,1)S(1)}, bf16[2,128,256]{2,1,0:T(8,128)(2,1)S(1)}, u32[]{:S(2)}, u32[]{:S(2)}) collective-permute-start(bf16[2,128,256]{2,1,0:T(8,128)(2,1)S(1)} %get-tuple-element.16.own_0.rest_0_), channel_id=1, source_target_pairs={{0,2},{1,3},{2,0},{3,1},{4,6},{5,7},{6,4},{7,5},{8,10},{9,11},{10,... | collective-permute-start | bytes 393224 | tf_op jit(solution)/shard_map/ppermute | solution.py:183
  4.4 1.2 %collective-permute-start.1 = (bf16[2,128,256]{2,1,0:T(8,128)(2,1)S(1)}, bf16[2,128,256]{2,1,0:T(8,128)(2,1)S(1)}, u32[]{:S(2)}, u32[]{:S(2)}) collective-permute-start(bf16[2,128,256]{2,1,0:T(8,128)(2,1)S(1)} %get-tuple-element.17.own_1.rest_1_), channel_id=1, source_target_pairs={{0,1},{1,0},{2,3},{3,2},{4,5},{5,4},{6,7},{7,6},{8,9},{9,8},{10,11... | collective-permute-start | bytes 393224 | tf_op jit(solution)/shard_map/ppermute | solution.py:183
  5.6 0.3 collective-permute-start
  5.8 0.1 collective-permute-start.3
  5.9 1.7 %collective-permute-done.2.rest_4_ = bf16[2,128,256]{2,1,0:T(8,128)(2,1)S(1)} collective-permute-done((bf16[2,128,256]{2,1,0:T(8,128)(2,1)S(1)}, bf16[2,128,256]{2,1,0:T(8,128)(2,1)S(1)}, u32[]{:S(2)}, u32[]{:S(2)}) %collective-permute-start.2) | collective-permute-done | bytes 131104 | tf_op jit(solution)/shard_map/ppermute | solution.py:183
  7.6 1.1 %collective-permute-start.4 = (bf16[2,128,256]{2,1,0:T(8,128)(2,1)S(1)}, bf16[2,128,256]{2,1,0:T(8,128)(2,1)S(1)}, u32[]{:S(2)}, u32[]{:S(2)}) collective-permute-start(bf16[2,128,256]{2,1,0:T(8,128)(2,1)S(1)} %collective-permute-done.2.rest_4_), channel_id=1, source_target_pairs={{0,1},{1,0},{2,3},{3,2},{4,5},{5,4},{6,7},{7,6},{8,9},{9,8},{10,11... | collective-permute-start | bytes 393224 | tf_op jit(solution)/shard_map/ppermute | solution.py:183
  8.7 0.0 collective-permute-done.1.rest_3_
  8.7 1.2 %collective-permute-start.5 = (bf16[2,128,256]{2,1,0:T(8,128)(2,1)S(1)}, bf16[2,128,256]{2,1,0:T(8,128)(2,1)S(1)}, u32[]{:S(2)}, u32[]{:S(2)}) collective-permute-start(bf16[2,128,256]{2,1,0:T(8,128)(2,1)S(1)} %collective-permute-done.1.rest_3_), channel_id=1, source_target_pairs={{0,2},{1,3},{2,0},{3,1},{4,6},{5,7},{6,4},{7,5},{8,10},{9,11},{10,... | collective-permute-start | bytes 393224 | tf_op jit(solution)/shard_map/ppermute | solution.py:183
  10.0 0.0 copy-done
  10.0 0.0 copy-done.1
  10.0 0.0 copy-done.2
  10.0 2.1 %edge_part.1.edge_ref = f32[8,256,128]{2,1,0:T(8,128)S(1)} custom-call(s32[4,10]{1,0:T(4,128)S(1)} %copy-done.1, s32[4]{0:T(128)S(1)} %copy-done.2, s32[1]{0:T(128)} %constant.0.clone.1.pair_ref, bf16[4,10,128,128]{3,2,1,0:T(8,128)(2,1)S(1)} %copy-done, bf16[2,128,256]{2,1,0:T(8,128)(2,1)S(1)} %get-tuple-element.16.own_0.rest_0_, ...), custom_call_target="tpu_custom_call" | custom-call | flops 335544320 | bytes 1572864 | tf_op jit(solution)/shard_map/edge_part/pallas_call | solution.py:209
  12.0 0.0 collective-permute-done.rest_2_
  12.0 0.0 collective-permute-done.3.rest_5_
  12.1 2.0 %collective-permute-done.4.rest_6_ = bf16[2,128,256]{2,1,0:T(8,128)(2,1)S(1)} collective-permute-done((bf16[2,128,256]{2,1,0:T(8,128)(2,1)S(1)}, bf16[2,128,256]{2,1,0:T(8,128)(2,1)S(1)}, u32[]{:S(2)}, u32[]{:S(2)}) %collective-permute-start.4) | collective-permute-done | bytes 131104 | tf_op jit(solution)/shard_map/ppermute | solution.py:183
  14.0 0.0 collective-permute-done.5.rest_7_
  14.1 1.5 %group_part.1 = (f32[64,1280]{1,0:T(8,128)S(1)}, bf16[64,1280]{1,0:T(8,128)(2,1)S(1)}, bf16[64,1280]{1,0:T(8,128)(2,1)S(1)}, bf16[64,1280]{1,0:T(8,128)(2,1)S(1)}, bf16[17,128,256]{2,1,0:T(8,128)(2,1)S(1)}) custom-call(s32[4,10]{1,0:T(4,128)S(1)} %copy-done.1, s32[4]{0:T(128)S(1)} %copy-done.2, s32[1]{0:T(128)} %constant.0.clone.1.pair_ref, ...), custom_call_target="tpu_custom_call" | custom-call | flops 335544320 | bytes 2359296 | tf_op jit(solution)/shard_map/group_part/pallas_call | solution.py:228
  15.5 1.3 %collective-permute-start.8 = (bf16[64,1280]{1,0:T(8,128)(2,1)S(1)}, bf16[64,1280]{1,0:T(8,128)(2,1)S(1)}, u32[]{:S(2)}, u32[]{:S(2)}) collective-permute-start(bf16[64,1280]{1,0:T(8,128)(2,1)S(1)} %get-tuple-element.22), channel_id=1, source_target_pairs={{0,1},{1,0},{2,3},{3,2},{4,5},{5,4},{6,7},{7,6},{8,9},{9,8},{10,11... | collective-permute-start | bytes 491528 | tf_op jit(solution)/shard_map/ppermute | solution.py:183
  16.8 0.2 collective-permute-start.9
  17.0 1.2 %collective-permute-start.10 = (bf16[64,1280]{1,0:T(8,128)(2,1)S(1)}, bf16[64,1280]{1,0:T(8,128)(2,1)S(1)}, u32[]{:S(2)}, u32[]{:S(2)}) collective-permute-start(bf16[64,1280]{1,0:T(8,128)(2,1)S(1)} %get-tuple-element.24), channel_id=1, source_target_pairs={{0,3},{1,2},{2,1},{3,0},{4,7},{5,6},{6,5},{7,4},{8,11},{9,10},{10,... | collective-permute-start | bytes 491528 | tf_op jit(solution)/shard_map/ppermute | solution.py:183
  18.3 6.6 %collective-permute-start.6 = (bf16[4,128,256]{2,1,0:T(8,128)(2,1)S(1)}, bf16[4,128,256]{2,1,0:T(8,128)(2,1)S(1)}, u32[]{:S(2)}, u32[]{:S(2)}) collective-permute-start(bf16[4,128,256]{2,1,0:T(8,128)(2,1)S(1)} %get-tuple-element.19), channel_id=1, source_target_pairs={{4,8},{8,4},{12,16},{16,12},{20,24},{24,20},{5,9},{9,5},{13,17},{1... | collective-permute-start | bytes 786440 | tf_op jit(solution)/shard_map/ppermute | solution.py:258
  24.9 0.1 collective-permute-start.7
  25.0 0.0 collective-permute-done.8.refs_1_
  25.0 0.0 collective-permute-done.9.refs_2_
  25.0 0.0 collective-permute-done.10.refs_3_
  25.0 0.1 sum_parts.1
  25.1 3.8 %collective-permute-done.6.far_ref = bf16[4,128,256]{2,1,0:T(8,128)(2,1)S(1)} collective-permute-done((bf16[4,128,256]{2,1,0:T(8,128)(2,1)S(1)}, bf16[4,128,256]{2,1,0:T(8,128)(2,1)S(1)}, u32[]{:S(2)}, u32[]{:S(2)}) %collective-permute-start.6) | collective-permute-done | bytes 262176 | tf_op jit(solution)/shard_map/ppermute | solution.py:258
  28.9 0.0 collective-permute-done.7.near_ref
  28.9 0.9 %finish.1 = bf16[64,768]{1,0:T(8,128)(2,1)} custom-call(s32[1]{0:T(128)} %constant.0.clone.1.pair_ref, bf16[4,128,256]{2,1,0:T(8,128)(2,1)S(1)} %collective-permute-done.6.far_ref, bf16[4,128,256]{2,1,0:T(8,128)(2,1)S(1)} %collective-permute-done.7.near_ref, bf16[64,256]{1,0:T(8,128)(2,1)S(1)} %get-tuple-element.25.mid_ref, ...), custom_call_target="tpu_custom_call" | custom-call | flops 268435456 | bytes 1048576 | tf_op jit(solution)/shard_map/finish/pallas_call | solution.py:276
  (6 shorter events, 0.0 us)
Async XLA Ops:
  0.0 0.9 %copy-start.3 = (bf16[4,128,256]{2,1,0:T(8,128)(2,1)S(1)}, bf16[4,128,256]{2,1,0:T(8,128)(2,1)}, u32[]{:S(2)}) copy-start(bf16[4,128,256]{2,1,0:T(8,128)(2,1)} %p_ref.1) | copy-start | bytes 786436
  1.0 0.7 %copy-start.4 = (s32[4,2]{0,1:T(2,128)S(1)}, s32[4,2]{0,1:T(2,128)}, u32[]{:S(2)}) copy-start(s32[4,2]{0,1:T(2,128)} %param.9) | copy-start | bytes 100
  1.6 8.3 %copy-start = (bf16[4,10,128,128]{3,2,1,0:T(8,128)(2,1)S(1)}, bf16[4,10,128,128]{3,2,1,0:T(8,128)(2,1)}, u32[]{:S(2)}) copy-start(bf16[4,10,128,128]{3,2,1,0:T(8,128)(2,1)} %a_ref.3) | copy-start | bytes 3932164
  1.6 8.3 %copy-start.1 = (s32[4,10]{1,0:T(4,128)S(1)}, s32[4,10]{1,0:T(4,128)}, u32[]{:S(2)}) copy-start(s32[4,10]{1,0:T(4,128)} %cols_ref.3) | copy-start | bytes 484
  1.6 8.3 %copy-start.2 = (s32[4]{0:T(128)S(1)}, s32[4]{0:T(128)}, u32[]{:S(2)}) copy-start(s32[4]{0:T(128)} %count_ref.3) | copy-start | bytes 52
  2.2 5.4 %collective-permute-start.2 = (bf16[2,128,256]{2,1,0:T(8,128)(2,1)S(1)}, bf16[2,128,256]{2,1,0:T(8,128)(2,1)S(1)}, u32[]{:S(2)}, u32[]{:S(2)}) collective-permute-start(bf16[2,128,256]{2,1,0:T(8,128)(2,1)S(1)} %get-tuple-element.16.own_0.rest_0_), channel_id=1, source_target_pairs={{0,2},{1,3},{2,0},{3,1},{4,6},{5,7},{6,4},{7,5},{8,10},{9,11},{10,... | collective-permute-start | bytes 393224 | tf_op jit(solution)/shard_map/ppermute | solution.py:183
  4.4 4.3 %collective-permute-start.1 = (bf16[2,128,256]{2,1,0:T(8,128)(2,1)S(1)}, bf16[2,128,256]{2,1,0:T(8,128)(2,1)S(1)}, u32[]{:S(2)}, u32[]{:S(2)}) collective-permute-start(bf16[2,128,256]{2,1,0:T(8,128)(2,1)S(1)} %get-tuple-element.17.own_1.rest_1_), channel_id=1, source_target_pairs={{0,1},{1,0},{2,3},{3,2},{4,5},{5,4},{6,7},{7,6},{8,9},{9,8},{10,11... | collective-permute-start | bytes 393224 | tf_op jit(solution)/shard_map/ppermute | solution.py:183
  5.6 6.4 %collective-permute-start = (bf16[2,128,256]{2,1,0:T(8,128)(2,1)S(1)}, bf16[2,128,256]{2,1,0:T(8,128)(2,1)S(1)}, u32[]{:S(2)}, u32[]{:S(2)}) collective-permute-start(bf16[2,128,256]{2,1,0:T(8,128)(2,1)S(1)} %get-tuple-element.16.own_0.rest_0_), channel_id=1, source_target_pairs={{0,1},{1,0},{2,3},{3,2},{4,5},{5,4},{6,7},{7,6},{8,9},{9,8},{10,11... | collective-permute-start | bytes 393224 | tf_op jit(solution)/shard_map/ppermute | solution.py:183
  5.8 6.2 %collective-permute-start.3 = (bf16[2,128,256]{2,1,0:T(8,128)(2,1)S(1)}, bf16[2,128,256]{2,1,0:T(8,128)(2,1)S(1)}, u32[]{:S(2)}, u32[]{:S(2)}) collective-permute-start(bf16[2,128,256]{2,1,0:T(8,128)(2,1)S(1)} %get-tuple-element.17.own_1.rest_1_), channel_id=1, source_target_pairs={{0,2},{1,3},{2,0},{3,1},{4,6},{5,7},{6,4},{7,5},{8,10},{9,11},{10,... | collective-permute-start | bytes 393224 | tf_op jit(solution)/shard_map/ppermute | solution.py:183
  7.6 6.4 %collective-permute-start.4 = (bf16[2,128,256]{2,1,0:T(8,128)(2,1)S(1)}, bf16[2,128,256]{2,1,0:T(8,128)(2,1)S(1)}, u32[]{:S(2)}, u32[]{:S(2)}) collective-permute-start(bf16[2,128,256]{2,1,0:T(8,128)(2,1)S(1)} %collective-permute-done.2.rest_4_), channel_id=1, source_target_pairs={{0,1},{1,0},{2,3},{3,2},{4,5},{5,4},{6,7},{7,6},{8,9},{9,8},{10,11... | collective-permute-start | bytes 393224 | tf_op jit(solution)/shard_map/ppermute | solution.py:183
  8.7 5.3 %collective-permute-start.5 = (bf16[2,128,256]{2,1,0:T(8,128)(2,1)S(1)}, bf16[2,128,256]{2,1,0:T(8,128)(2,1)S(1)}, u32[]{:S(2)}, u32[]{:S(2)}) collective-permute-start(bf16[2,128,256]{2,1,0:T(8,128)(2,1)S(1)} %collective-permute-done.1.rest_3_), channel_id=1, source_target_pairs={{0,2},{1,3},{2,0},{3,1},{4,6},{5,7},{6,4},{7,5},{8,10},{9,11},{10,... | collective-permute-start | bytes 393224 | tf_op jit(solution)/shard_map/ppermute | solution.py:183
  15.5 9.5 %collective-permute-start.8 = (bf16[64,1280]{1,0:T(8,128)(2,1)S(1)}, bf16[64,1280]{1,0:T(8,128)(2,1)S(1)}, u32[]{:S(2)}, u32[]{:S(2)}) collective-permute-start(bf16[64,1280]{1,0:T(8,128)(2,1)S(1)} %get-tuple-element.22), channel_id=1, source_target_pairs={{0,1},{1,0},{2,3},{3,2},{4,5},{5,4},{6,7},{7,6},{8,9},{9,8},{10,11... | collective-permute-start | bytes 491528 | tf_op jit(solution)/shard_map/ppermute | solution.py:183
  16.8 8.2 %collective-permute-start.9 = (bf16[64,1280]{1,0:T(8,128)(2,1)S(1)}, bf16[64,1280]{1,0:T(8,128)(2,1)S(1)}, u32[]{:S(2)}, u32[]{:S(2)}) collective-permute-start(bf16[64,1280]{1,0:T(8,128)(2,1)S(1)} %get-tuple-element.23), channel_id=1, source_target_pairs={{0,2},{1,3},{2,0},{3,1},{4,6},{5,7},{6,4},{7,5},{8,10},{9,11},{10,... | collective-permute-start | bytes 491528 | tf_op jit(solution)/shard_map/ppermute | solution.py:183
  17.0 8.0 %collective-permute-start.10 = (bf16[64,1280]{1,0:T(8,128)(2,1)S(1)}, bf16[64,1280]{1,0:T(8,128)(2,1)S(1)}, u32[]{:S(2)}, u32[]{:S(2)}) collective-permute-start(bf16[64,1280]{1,0:T(8,128)(2,1)S(1)} %get-tuple-element.24), channel_id=1, source_target_pairs={{0,3},{1,2},{2,1},{3,0},{4,7},{5,6},{6,5},{7,4},{8,11},{9,10},{10,... | collective-permute-start | bytes 491528 | tf_op jit(solution)/shard_map/ppermute | solution.py:183
  18.3 10.7 %collective-permute-start.6 = (bf16[4,128,256]{2,1,0:T(8,128)(2,1)S(1)}, bf16[4,128,256]{2,1,0:T(8,128)(2,1)S(1)}, u32[]{:S(2)}, u32[]{:S(2)}) collective-permute-start(bf16[4,128,256]{2,1,0:T(8,128)(2,1)S(1)} %get-tuple-element.19), channel_id=1, source_target_pairs={{4,8},{8,4},{12,16},{16,12},{20,24},{24,20},{5,9},{9,5},{13,17},{1... | collective-permute-start | bytes 786440 | tf_op jit(solution)/shard_map/ppermute | solution.py:258
  24.9 4.0 %collective-permute-start.7 = (bf16[4,128,256]{2,1,0:T(8,128)(2,1)S(1)}, bf16[4,128,256]{2,1,0:T(8,128)(2,1)S(1)}, u32[]{:S(2)}, u32[]{:S(2)}) collective-permute-start(bf16[4,128,256]{2,1,0:T(8,128)(2,1)S(1)} %get-tuple-element.20), channel_id=1, source_target_pairs={{0,4},{4,0},{8,12},{12,8},{16,20},{20,16},{24,28},{28,24},{1,5},{5... | collective-permute-start | bytes 786440 | tf_op jit(solution)/shard_map/ppermute | solution.py:261

commit v4 on v3

--- a/solution.py
+++ b/solution.py
@@ -41,10 +41,18 @@
     return outs
 
 
-def order_kernel(cols_ref, p_ref, *outs):
+def order_kernel(cols_hbm, p_hbm, *rest):
+    outs, (cols_ref, p_ref, sems) = rest[:2], rest[2:]
     rows, tile = p_ref.shape[:2]
     piece = rows // 2
+    lists = pltpu.make_async_copy(cols_hbm, cols_ref, sems.at[rows])
+    lists.start()
+    loads = [pltpu.make_async_copy(p_hbm.at[f], p_ref.at[f], sems.at[f]) for f in range(rows)]
+    for load in loads:
+        load.start()
+    lists.wait()
     for f in range(rows):
+        loads[f].wait()
         first = pl.multiple_of(jnp.where(cols_ref[0, f] > cols_ref[1, f], tile, 0), tile)
         for t, start in ((0, first), (1, pl.multiple_of(tile - first, tile))):
             outs[f // piece][f % piece, :, t * tile : (t + 1) * tile] = p_ref[f, :, pl.ds(start, tile)]
@@ -58,14 +66,19 @@
     far_ref[...] = pool[pl.ds(odd * last, rows)]
 
 
-def edge_kernel(subs, half, cols_ref, count_ref, pair_ref, a_ref, own_0, own_1, out_ref, turned):
+def edge_kernel(subs, half, cols_ref, count_ref, pair_ref, a_hbm, own_0, own_1, *rest):
+    out_ref, a_ref, turned, sems = rest
     rows, slots, tile = a_ref.shape[:3]
     first = lax.axis_index("dom") * (subs * rows)
     me = lax.axis_index("sub")
+    loads = [pltpu.make_async_copy(a_hbm.at[f], a_ref.at[f], sems.at[f]) for f in range(rows)]
+    for load in loads:
+        load.start()
     out_ref[...] = jnp.zeros(out_ref.shape, F32)
     for f in range(rows):
         turned[f] = (own_0, own_1)[f // (rows // 2)][f % (rows // 2)].T
     for f in range(rows):
+        loads[f].wait()
         for k in range(slots):
             rel = cols_ref[f, k] - first
             live = (k < count_ref[f]) & ((rel < 0) | (rel >= subs * rows))
@@ -185,14 +198,22 @@
     own = pl.pallas_call(
         order_kernel,
         out_shape=[jax.ShapeDtypeStruct((rows // 2, tile, 2 * tile), BF16)] * 2,
-        in_specs=[smem, vmem],
+        in_specs=[pl.BlockSpec(memory_space=pltpu.HBM)] * 2,
         out_specs=[vmem] * 2,
+        scratch_shapes=[
+            pltpu.SMEM((2, rows), jnp.int32),
+            pltpu.VMEM(p_tiles.shape, BF16),
+            pltpu.SemaphoreType.DMA((rows + 1,)),
+        ],
         compiler_params=pltpu.CompilerParams(vmem_limit_bytes=spare),
         cost_estimate=pl.CostEstimate(
             flops=1 << 30, bytes_accessed=2 * p_bytes, transcendentals=0
         ),
         name="order_columns",
-    )(p_cols.T, p_tiles)
+    )(
+        pltpu.with_memory_space_constraint(p_cols.T, pltpu.HBM),
+        pltpu.with_memory_space_constraint(p_tiles, pltpu.HBM),
+    )
 
     if half == 1:
         pair = jnp.zeros((1,), jnp.int32)
@@ -206,18 +227,24 @@
         pair = jnp.concatenate([m_left, m_group, m_right])
 
     flops = 2 * rows * slots * tile * tile * 2 * tile * half
-    edges = pl.pallas_call(
+    edges, a_held = pl.pallas_call(
         functools.partial(edge_kernel, subs, half),
-        out_shape=jax.ShapeDtypeStruct((2 * rows, width, tile), F32),
-        in_specs=[smem, smem, smem, vmem, vmem, vmem],
-        out_specs=vmem,
-        scratch_shapes=[pltpu.VMEM((rows, 2 * tile, tile), BF16)],
+        out_shape=[
+            jax.ShapeDtypeStruct((2 * rows, width, tile), F32),
+            jax.ShapeDtypeStruct(a_tiles.shape, BF16),
+        ],
+        in_specs=[smem, smem, smem, pl.BlockSpec(memory_space=pltpu.HBM), vmem, vmem],
+        out_specs=[vmem] * 2,
+        scratch_shapes=[
+            pltpu.VMEM((rows, 2 * tile, tile), BF16),
+            pltpu.SemaphoreType.DMA((rows,)),
+        ],
         compiler_params=pltpu.CompilerParams(vmem_limit_bytes=8 * rows * tile * width + spare),
         cost_estimate=pl.CostEstimate(
             flops=flops, bytes_accessed=a_bytes + p_bytes, transcendentals=0
         ),
         name="edge_part",
-    )(a_cols, a_count, pair, a_tiles, *own)
+    )(a_cols, a_count, pair, pltpu.with_memory_space_constraint(a_tiles, pltpu.HBM), *own)
 
     tiles = [list(own)] + [[None, None] for _ in range(subs - 1)]
     for k in range(1, subs):
@@ -245,7 +272,7 @@
             flops=flops, bytes_accessed=a_bytes + subs * p_bytes, transcendentals=0
         ),
         name="group_part",
-    )(a_cols, a_count, pair, a_tiles, edges, *sum(tiles, []))
+    )(a_cols, a_count, pair, a_held, edges, *sum(tiles, []))
     received = [exchange(parts[k], k) for k in range(1, subs)]
     to_near, to_far = pl.pallas_call(
         functools.partial(hand_out_kernel, subs),

time: 30 us -> 28.8 us (0.960)
  local copies, waits for them, and re-layouts: 1.64 us -> 0.01 us
  Pallas kernels: 5.19 us -> 6.75 us
  waiting for transfers between devices: 7.51 us -> 6.36 us
    unnamed x10 -> x4, local copies, waits for them, and re-layouts: 1.64 us -> 0.01 us
    pallas_call x1, Pallas kernels: 2.05 us -> 3.21 us  [local(): pl.pallas_call(functools.partial(edge_kernel, subs, half), out_shape=[jax...]
    ppermute x9, waiting for transfers between devices: 3.69 us -> 2.54 us  [exchange(): return lax.ppermute(value, 'sub', [(s, s ^ k) for s in range(subs)])]
    pallas_call x1, Pallas kernels: 0.6 us -> 1.02 us  [local(): pl.pallas_call(order_kernel, out_shape=[jax.ShapeDtypeStruct((rows // 2,...]
  transfers between devices with their start and end apart: 11 -> 11, of which waited for: 3 -> 3; matrix products, arithmetic and copies ran while one was open for 0% -> 0% of each run, Pallas kernels for 7% -> 12%
where the time goes in v4:
time: 28.8 us; the launch traced here: 28.7 us
  starting transfers between devices  15.5 us (54%)
  Pallas kernels  6.75 us (23%)
  waiting for transfers between devices  6.36 us (22%)
    ppermute x9, starting transfers between devices, exchange(): return lax.ppermute(value, 'sub', [(s, s ^ k) for s in range(subs)])  8.74 us
    ppermute x1, starting transfers between devices, local(): lax.ppermute(to_far, 'dom', [(d, d - 1 + 2 * (d % 2)) for d in range(1, d...  6.63 us
    ppermute x1, waiting for transfers between devices, local(): lax.ppermute(to_far, 'dom', [(d, d - 1 + 2 * (d % 2)) for d in range(1, d...  3.82 us
    pallas_call x1, Pallas kernels, local(): pl.pallas_call(functools.partial(edge_kernel, subs, half), out_shape=[jax...  3.21 us
    ppermute x9, waiting for transfers between devices, exchange(): return lax.ppermute(value, 'sub', [(s, s ^ k) for s in range(subs)])  2.54 us
    pallas_call x1, Pallas kernels, local(): pl.pallas_call(functools.partial(group_kernel, subs, half), out_shape=[ja...  1.46 us
    pallas_call x1, Pallas kernels, local(): pl.pallas_call(order_kernel, out_shape=[jax.ShapeDtypeStruct((rows // 2,...  1.02 us
    pallas_call x1, Pallas kernels, local(): pl.pallas_call(functools.partial(finish_kernel, subs, half), out_shape=ja...  0.93 us
  transfers between devices with their start and end apart: 11, of which 3 were waited for; matrix products, arithmetic and copies ran while one was open for 0% of the time, Pallas kernels for 12%

profile of v4, /device:TPU:1, one launch (start us, length us, event | category | flops | bytes accessed | tf_op | source)
XLA Modules:
  0.0 28.7 jit_solution(6453566129183660233)
XLA Ops:
  0.0 0.0 copy-start
  0.0 0.0 copy-start.1
  0.0 1.0 %order_columns.1 = (bf16[2,128,256]{2,1,0:T(8,128)(2,1)S(1)}, bf16[2,128,256]{2,1,0:T(8,128)(2,1)S(1)}) custom-call(s32[2,4]{1,0:T(2,128)} %bitcast.1, bf16[4,128,256]{2,1,0:T(8,128)(2,1)} %p_hbm.1), custom_call_target="tpu_custom_call" | custom-call | flops 1073741824 | bytes 524288 | tf_op jit(solution)/shard_map/order_columns/pallas_call | solution.py:198
  1.0 2.1 %collective-permute-start.2 = (bf16[2,128,256]{2,1,0:T(8,128)(2,1)S(1)}, bf16[2,128,256]{2,1,0:T(8,128)(2,1)S(1)}, u32[]{:S(2)}, u32[]{:S(2)}) collective-permute-start(bf16[2,128,256]{2,1,0:T(8,128)(2,1)S(1)} %get-tuple-element.18.own_0.rest_0_), channel_id=1, source_target_pairs={{0,2},{1,3},{2,0},{3,1},{4,6},{5,7},{6,4},{7,5},{8,10},{9,11},{10,... | collective-permute-start | bytes 393224 | tf_op jit(solution)/shard_map/ppermute | solution.py:196
  3.2 1.2 %collective-permute-start.1 = (bf16[2,128,256]{2,1,0:T(8,128)(2,1)S(1)}, bf16[2,128,256]{2,1,0:T(8,128)(2,1)S(1)}, u32[]{:S(2)}, u32[]{:S(2)}) collective-permute-start(bf16[2,128,256]{2,1,0:T(8,128)(2,1)S(1)} %get-tuple-element.19.own_1.rest_1_), channel_id=1, source_target_pairs={{0,1},{1,0},{2,3},{3,2},{4,5},{5,4},{6,7},{7,6},{8,9},{9,8},{10,11... | collective-permute-start | bytes 393224 | tf_op jit(solution)/shard_map/ppermute | solution.py:196
  4.4 0.3 collective-permute-start
  4.6 0.1 collective-permute-start.3
  4.7 1.7 %collective-permute-done.2.rest_4_ = bf16[2,128,256]{2,1,0:T(8,128)(2,1)S(1)} collective-permute-done((bf16[2,128,256]{2,1,0:T(8,128)(2,1)S(1)}, bf16[2,128,256]{2,1,0:T(8,128)(2,1)S(1)}, u32[]{:S(2)}, u32[]{:S(2)}) %collective-permute-start.2) | collective-permute-done | bytes 131104 | tf_op jit(solution)/shard_map/ppermute | solution.py:196
  6.4 1.1 %collective-permute-start.4 = (bf16[2,128,256]{2,1,0:T(8,128)(2,1)S(1)}, bf16[2,128,256]{2,1,0:T(8,128)(2,1)S(1)}, u32[]{:S(2)}, u32[]{:S(2)}) collective-permute-start(bf16[2,128,256]{2,1,0:T(8,128)(2,1)S(1)} %collective-permute-done.2.rest_4_), channel_id=1, source_target_pairs={{0,1},{1,0},{2,3},{3,2},{4,5},{5,4},{6,7},{7,6},{8,9},{9,8},{10,11... | collective-permute-start | bytes 393224 | tf_op jit(solution)/shard_map/ppermute | solution.py:196
  7.5 0.0 collective-permute-done.1.rest_3_
  7.5 1.2 %collective-permute-start.5 = (bf16[2,128,256]{2,1,0:T(8,128)(2,1)S(1)}, bf16[2,128,256]{2,1,0:T(8,128)(2,1)S(1)}, u32[]{:S(2)}, u32[]{:S(2)}) collective-permute-start(bf16[2,128,256]{2,1,0:T(8,128)(2,1)S(1)} %collective-permute-done.1.rest_3_), channel_id=1, source_target_pairs={{0,2},{1,3},{2,0},{3,1},{4,6},{5,7},{6,4},{7,5},{8,10},{9,11},{10,... | collective-permute-start | bytes 393224 | tf_op jit(solution)/shard_map/ppermute | solution.py:196
  8.7 0.0 copy-done
  8.7 0.0 copy-done.1
  8.7 3.2 %edge_part.1 = (f32[8,256,128]{2,1,0:T(8,128)S(1)}, bf16[4,10,128,128]{3,2,1,0:T(8,128)(2,1)S(1)}) custom-call(s32[4,10]{1,0:T(4,128)S(1)} %copy-done, s32[4]{0:T(128)S(1)} %copy-done.1, s32[1]{0:T(128)} %constant.0.clone.1.pair_ref, bf16[4,10,128,128]{3,2,1,0:T(8,128)(2,1)} %a_hbm.1, bf16[2,128,256]{2,1,0:T(8,128)(2,1)S(1)} %get-tuple-element.18.own_0.rest_0_, ...), custom_call_target="tpu_custom_call" | custom-call | flops 335544320 | bytes 1572864 | tf_op jit(solution)/shard_map/edge_part/pallas_call | solution.py:230
  12.0 0.0 collective-permute-done.rest_2_
  12.0 0.0 collective-permute-done.3.rest_5_
  12.0 0.8 %collective-permute-done.4.rest_6_ = bf16[2,128,256]{2,1,0:T(8,128)(2,1)S(1)} collective-permute-done((bf16[2,128,256]{2,1,0:T(8,128)(2,1)S(1)}, bf16[2,128,256]{2,1,0:T(8,128)(2,1)S(1)}, u32[]{:S(2)}, u32[]{:S(2)}) %collective-permute-start.4) | collective-permute-done | bytes 131104 | tf_op jit(solution)/shard_map/ppermute | solution.py:196
  12.8 0.0 collective-permute-done.5.rest_7_
  12.8 1.5 %group_part.1 = (f32[64,1280]{1,0:T(8,128)S(1)}, bf16[64,1280]{1,0:T(8,128)(2,1)S(1)}, bf16[64,1280]{1,0:T(8,128)(2,1)S(1)}, bf16[64,1280]{1,0:T(8,128)(2,1)S(1)}, bf16[17,128,256]{2,1,0:T(8,128)(2,1)S(1)}) custom-call(s32[4,10]{1,0:T(4,128)S(1)} %copy-done, s32[4]{0:T(128)S(1)} %copy-done.1, s32[1]{0:T(128)} %constant.0.clone.1.pair_ref, ...), custom_call_target="tpu_custom_call" | custom-call | flops 335544320 | bytes 2359296 | tf_op jit(solution)/shard_map/group_part/pallas_call | solution.py:255
  14.3 1.3 %collective-permute-start.8 = (bf16[64,1280]{1,0:T(8,128)(2,1)S(1)}, bf16[64,1280]{1,0:T(8,128)(2,1)S(1)}, u32[]{:S(2)}, u32[]{:S(2)}) collective-permute-start(bf16[64,1280]{1,0:T(8,128)(2,1)S(1)} %get-tuple-element.26), channel_id=1, source_target_pairs={{0,1},{1,0},{2,3},{3,2},{4,5},{5,4},{6,7},{7,6},{8,9},{9,8},{10,11... | collective-permute-start | bytes 491528 | tf_op jit(solution)/shard_map/ppermute | solution.py:196
  15.6 0.2 collective-permute-start.9
  15.8 1.2 %collective-permute-start.10 = (bf16[64,1280]{1,0:T(8,128)(2,1)S(1)}, bf16[64,1280]{1,0:T(8,128)(2,1)S(1)}, u32[]{:S(2)}, u32[]{:S(2)}) collective-permute-start(bf16[64,1280]{1,0:T(8,128)(2,1)S(1)} %get-tuple-element.28), channel_id=1, source_target_pairs={{0,3},{1,2},{2,1},{3,0},{4,7},{5,6},{6,5},{7,4},{8,11},{9,10},{10,... | collective-permute-start | bytes 491528 | tf_op jit(solution)/shard_map/ppermute | solution.py:196
  17.0 6.6 %collective-permute-start.6 = (bf16[4,128,256]{2,1,0:T(8,128)(2,1)S(1)}, bf16[4,128,256]{2,1,0:T(8,128)(2,1)S(1)}, u32[]{:S(2)}, u32[]{:S(2)}) collective-permute-start(bf16[4,128,256]{2,1,0:T(8,128)(2,1)S(1)} %get-tuple-element.23), channel_id=1, source_target_pairs={{4,8},{8,4},{12,16},{16,12},{20,24},{24,20},{5,9},{9,5},{13,17},{1... | collective-permute-start | bytes 786440 | tf_op jit(solution)/shard_map/ppermute | solution.py:285
  23.7 0.1 collective-permute-start.7
  23.8 0.0 collective-permute-done.8.refs_1_
  23.8 0.0 collective-permute-done.9.refs_2_
  23.8 0.0 collective-permute-done.10.refs_3_
  23.8 0.1 sum_parts.1
  23.9 3.8 %collective-permute-done.6.far_ref = bf16[4,128,256]{2,1,0:T(8,128)(2,1)S(1)} collective-permute-done((bf16[4,128,256]{2,1,0:T(8,128)(2,1)S(1)}, bf16[4,128,256]{2,1,0:T(8,128)(2,1)S(1)}, u32[]{:S(2)}, u32[]{:S(2)}) %collective-permute-start.6) | collective-permute-done | bytes 262176 | tf_op jit(solution)/shard_map/ppermute | solution.py:285
  27.7 0.0 collective-permute-done.7.near_ref
  27.7 0.9 %finish.1 = bf16[64,768]{1,0:T(8,128)(2,1)} custom-call(s32[1]{0:T(128)} %constant.0.clone.1.pair_ref, bf16[4,128,256]{2,1,0:T(8,128)(2,1)S(1)} %collective-permute-done.6.far_ref, bf16[4,128,256]{2,1,0:T(8,128)(2,1)S(1)} %collective-permute-done.7.near_ref, bf16[64,256]{1,0:T(8,128)(2,1)S(1)} %get-tuple-element.29.mid_ref, ...), custom_call_target="tpu_custom_call" | custom-call | flops 268435456 | bytes 1048576 | tf_op jit(solution)/shard_map/finish/pallas_call | solution.py:303
  (1 shorter events, 0.0 us)
Async XLA Ops:
  0.0 8.7 %copy-start = (s32[4,10]{1,0:T(4,128)S(1)}, s32[4,10]{1,0:T(4,128)}, u32[]{:S(2)}) copy-start(s32[4,10]{1,0:T(4,128)} %cols_ref.3) | copy-start | bytes 484
  0.0 8.7 %copy-start.1 = (s32[4]{0:T(128)S(1)}, s32[4]{0:T(128)}, u32[]{:S(2)}) copy-start(s32[4]{0:T(128)} %count_ref.3) | copy-start | bytes 52
  1.0 5.4 %collective-permute-start.2 = (bf16[2,128,256]{2,1,0:T(8,128)(2,1)S(1)}, bf16[2,128,256]{2,1,0:T(8,128)(2,1)S(1)}, u32[]{:S(2)}, u32[]{:S(2)}) collective-permute-start(bf16[2,128,256]{2,1,0:T(8,128)(2,1)S(1)} %get-tuple-element.18.own_0.rest_0_), channel_id=1, source_target_pairs={{0,2},{1,3},{2,0},{3,1},{4,6},{5,7},{6,4},{7,5},{8,10},{9,11},{10,... | collective-permute-start | bytes 393224 | tf_op jit(solution)/shard_map/ppermute | solution.py:196
  3.2 4.3 %collective-permute-start.1 = (bf16[2,128,256]{2,1,0:T(8,128)(2,1)S(1)}, bf16[2,128,256]{2,1,0:T(8,128)(2,1)S(1)}, u32[]{:S(2)}, u32[]{:S(2)}) collective-permute-start(bf16[2,128,256]{2,1,0:T(8,128)(2,1)S(1)} %get-tuple-element.19.own_1.rest_1_), channel_id=1, source_target_pairs={{0,1},{1,0},{2,3},{3,2},{4,5},{5,4},{6,7},{7,6},{8,9},{9,8},{10,11... | collective-permute-start | bytes 393224 | tf_op jit(solution)/shard_map/ppermute | solution.py:196
  4.4 7.6 %collective-permute-start = (bf16[2,128,256]{2,1,0:T(8,128)(2,1)S(1)}, bf16[2,128,256]{2,1,0:T(8,128)(2,1)S(1)}, u32[]{:S(2)}, u32[]{:S(2)}) collective-permute-start(bf16[2,128,256]{2,1,0:T(8,128)(2,1)S(1)} %get-tuple-element.18.own_0.rest_0_), channel_id=1, source_target_pairs={{0,1},{1,0},{2,3},{3,2},{4,5},{5,4},{6,7},{7,6},{8,9},{9,8},{10,11... | collective-permute-start | bytes 393224 | tf_op jit(solution)/shard_map/ppermute | solution.py:196
  4.6 7.3 %collective-permute-start.3 = (bf16[2,128,256]{2,1,0:T(8,128)(2,1)S(1)}, bf16[2,128,256]{2,1,0:T(8,128)(2,1)S(1)}, u32[]{:S(2)}, u32[]{:S(2)}) collective-permute-start(bf16[2,128,256]{2,1,0:T(8,128)(2,1)S(1)} %get-tuple-element.19.own_1.rest_1_), channel_id=1, source_target_pairs={{0,2},{1,3},{2,0},{3,1},{4,6},{5,7},{6,4},{7,5},{8,10},{9,11},{10,... | collective-permute-start | bytes 393224 | tf_op jit(solution)/shard_map/ppermute | solution.py:196
  6.4 6.4 %collective-permute-start.4 = (bf16[2,128,256]{2,1,0:T(8,128)(2,1)S(1)}, bf16[2,128,256]{2,1,0:T(8,128)(2,1)S(1)}, u32[]{:S(2)}, u32[]{:S(2)}) collective-permute-start(bf16[2,128,256]{2,1,0:T(8,128)(2,1)S(1)} %collective-permute-done.2.rest_4_), channel_id=1, source_target_pairs={{0,1},{1,0},{2,3},{3,2},{4,5},{5,4},{6,7},{7,6},{8,9},{9,8},{10,11... | collective-permute-start | bytes 393224 | tf_op jit(solution)/shard_map/ppermute | solution.py:196
  7.5 5.3 %collective-permute-start.5 = (bf16[2,128,256]{2,1,0:T(8,128)(2,1)S(1)}, bf16[2,128,256]{2,1,0:T(8,128)(2,1)S(1)}, u32[]{:S(2)}, u32[]{:S(2)}) collective-permute-start(bf16[2,128,256]{2,1,0:T(8,128)(2,1)S(1)} %collective-permute-done.1.rest_3_), channel_id=1, source_target_pairs={{0,2},{1,3},{2,0},{3,1},{4,6},{5,7},{6,4},{7,5},{8,10},{9,11},{10,... | collective-permute-start | bytes 393224 | tf_op jit(solution)/shard_map/ppermute | solution.py:196
  14.3 9.5 %collective-permute-start.8 = (bf16[64,1280]{1,0:T(8,128)(2,1)S(1)}, bf16[64,1280]{1,0:T(8,128)(2,1)S(1)}, u32[]{:S(2)}, u32[]{:S(2)}) collective-permute-start(bf16[64,1280]{1,0:T(8,128)(2,1)S(1)} %get-tuple-element.26), channel_id=1, source_target_pairs={{0,1},{1,0},{2,3},{3,2},{4,5},{5,4},{6,7},{7,6},{8,9},{9,8},{10,11... | collective-permute-start | bytes 491528 | tf_op jit(solution)/shard_map/ppermute | solution.py:196
  15.6 8.2 %collective-permute-start.9 = (bf16[64,1280]{1,0:T(8,128)(2,1)S(1)}, bf16[64,1280]{1,0:T(8,128)(2,1)S(1)}, u32[]{:S(2)}, u32[]{:S(2)}) collective-permute-start(bf16[64,1280]{1,0:T(8,128)(2,1)S(1)} %get-tuple-element.27), channel_id=1, source_target_pairs={{0,2},{1,3},{2,0},{3,1},{4,6},{5,7},{6,4},{7,5},{8,10},{9,11},{10,... | collective-permute-start | bytes 491528 | tf_op jit(solution)/shard_map/ppermute | solution.py:196
  15.8 8.0 %collective-permute-start.10 = (bf16[64,1280]{1,0:T(8,128)(2,1)S(1)}, bf16[64,1280]{1,0:T(8,128)(2,1)S(1)}, u32[]{:S(2)}, u32[]{:S(2)}) collective-permute-start(bf16[64,1280]{1,0:T(8,128)(2,1)S(1)} %get-tuple-element.28), channel_id=1, source_target_pairs={{0,3},{1,2},{2,1},{3,0},{4,7},{5,6},{6,5},{7,4},{8,11},{9,10},{10,... | collective-permute-start | bytes 491528 | tf_op jit(solution)/shard_map/ppermute | solution.py:196
  17.0 10.7 %collective-permute-start.6 = (bf16[4,128,256]{2,1,0:T(8,128)(2,1)S(1)}, bf16[4,128,256]{2,1,0:T(8,128)(2,1)S(1)}, u32[]{:S(2)}, u32[]{:S(2)}) collective-permute-start(bf16[4,128,256]{2,1,0:T(8,128)(2,1)S(1)} %get-tuple-element.23), channel_id=1, source_target_pairs={{4,8},{8,4},{12,16},{16,12},{20,24},{24,20},{5,9},{9,5},{13,17},{1... | collective-permute-start | bytes 786440 | tf_op jit(solution)/shard_map/ppermute | solution.py:285
  23.7 4.0 %collective-permute-start.7 = (bf16[4,128,256]{2,1,0:T(8,128)(2,1)S(1)}, bf16[4,128,256]{2,1,0:T(8,128)(2,1)S(1)}, u32[]{:S(2)}, u32[]{:S(2)}) collective-permute-start(bf16[4,128,256]{2,1,0:T(8,128)(2,1)S(1)} %get-tuple-element.24), channel_id=1, source_target_pairs={{0,4},{4,0},{8,12},{12,8},{16,20},{20,16},{24,28},{28,24},{1,5},{5... | collective-permute-start | bytes 786440 | tf_op jit(solution)/shard_map/ppermute | solution.py:288

commit v5 on v4

--- a/solution.py
+++ b/solution.py
@@ -58,16 +58,27 @@
             outs[f // piece][f % piece, :, t * tile : (t + 1) * tile] = p_ref[f, :, pl.ds(start, tile)]
 
 
-def hand_out_kernel(subs, pool, near_ref, far_ref):
-    rows = near_ref.shape[0]
-    odd = lax.rem(lax.axis_index("dom"), 2)
+def assemble_kernel(subs, *refs):
+    p_refs, (pool, near_ref, far_ref) = refs[: 2 * subs], refs[2 * subs :]
+    piece = p_refs[0].shape[0]
+    rows = 2 * piece
+    me, odd = lax.axis_index("sub"), lax.rem(lax.axis_index("dom"), 2)
+    for k in range(subs):
+        for i in range(2):
+            pool[pl.ds(lax.bitwise_xor(me, k) * rows + i * piece, piece)] = p_refs[2 * k + i][...]
+    pool[subs * rows] = jnp.zeros(pool.shape[1:], pool.dtype)
     last = (subs - 1) * rows
     near_ref[...] = pool[pl.ds((1 - odd) * last, rows)]
     far_ref[...] = pool[pl.ds(odd * last, rows)]
 
 
+def owner_rows(me, k):
+    start = pl.multiple_of(lax.bitwise_xor(me, k) * COARSE_ROWS, COARSE_ROWS)
+    return pl.ds(start, COARSE_ROWS)
+
+
 def edge_kernel(subs, half, cols_ref, count_ref, pair_ref, a_hbm, own_0, own_1, *rest):
-    out_ref, a_ref, turned, sems = rest
+    outs, (a_ref, out_ref, turned, sems) = rest[:subs], rest[subs:]
     rows, slots, tile = a_ref.shape[:3]
     first = lax.axis_index("dom") * (subs * rows)
     me = lax.axis_index("sub")
@@ -93,21 +104,19 @@
                     m = pair_ref[rows + me * rows + f]
                     for start, part in ((m, term[:tile]), (m + half, term[tile:])):
                         out_ref[at, pl.ds(pl.multiple_of(start * tile, tile), tile)] += part
-
-
-def group_kernel(subs, half, cols_ref, count_ref, pair_ref, a_ref, edge_ref, *rest):
-    p_refs, rest = rest[: 2 * subs], rest[2 * subs :]
-    outs, (pool, q, mid_ref) = rest[:subs], rest[subs:]
+    for k in range(subs):
+        for c in range(2 * rows):
+            part = out_ref[c, owner_rows(me, k)]
+            outs[k][:, c * tile : (c + 1) * tile] = part.astype(outs[k].dtype)
+
+
+def group_kernel(subs, half, cols_ref, count_ref, pair_ref, a_ref, pool, *rest):
+    outs, (q, mid_ref) = rest[:subs], rest[subs:]
     rows, slots, tile = a_ref.shape[0], a_ref.shape[1], a_ref.shape[2]
     zero = subs * rows
     width = 2 * half * tile
     me = lax.axis_index("sub")
     first = lax.axis_index("dom") * (subs * rows)
-    piece = rows // 2
-    for k in range(subs):
-        for i in range(2):
-            pool[pl.ds(lax.bitwise_xor(me, k) * rows + i * piece, piece)] = p_refs[2 * k + i][...]
-    pool[zero] = jnp.zeros(pool.shape[1:], pool.dtype)
     for f in range(rows):
         a_row = side_by_side(a_ref, f)
         index = [[None] * slots for _ in range(half)]
@@ -127,26 +136,26 @@
         mid_ref[m * tile : (m + 1) * tile] = out[:tile]
         mid_ref[(m + half) * tile : (m + half + 1) * tile] = out[tile:]
     for k in range(subs):
-        at = pl.ds(pl.multiple_of(lax.bitwise_xor(me, k) * COARSE_ROWS, COARSE_ROWS), COARSE_ROWS)
-        kind = outs[k].dtype
-        outs[k][:, :width] = mid_ref[at].astype(kind)
-        for c in range(2 * rows):
-            outs[k][:, width + c * tile : width + (c + 1) * tile] = edge_ref[c, at].astype(kind)
-
-
-def sum_kernel(subs, width, *refs):
-    part_refs, (mid_ref, edge_ref) = refs[:subs], refs[subs:]
-    total = part_refs[0][...]
-    for k in range(1, subs):
-        total = total + part_refs[k][...].astype(F32)
-    mid_ref[...] = total[:, :width].astype(BF16)
-    sums = total[:, width:]
-    high = sums.astype(BF16)
-    edge_ref[:COARSE_ROWS] = high
-    edge_ref[COARSE_ROWS:] = (sums - high.astype(F32)).astype(BF16)
-
-
-def finish_kernel(subs, half, pair_ref, far_ref, near_ref, mid_ref, both_ref, out_ref, edge):
+        outs[k][...] = mid_ref[owner_rows(me, k)].astype(outs[k].dtype)
+
+
+def total_of(refs):
+    total = refs[0][...]
+    for ref in refs[1:]:
+        total = total + ref[...].astype(F32)
+    return total
+
+
+def sum_kernel(subs, *refs):
+    mid_ref, out_ref = refs[2 * subs :]
+    mid_ref[...] = total_of(refs[subs : 2 * subs]).astype(BF16)
+    total = total_of(refs[:subs])
+    high = total.astype(BF16)
+    out_ref[:COARSE_ROWS] = high
+    out_ref[COARSE_ROWS:] = (total - high.astype(F32)).astype(BF16)
+
+
+def finish_kernel(subs, half, pair_ref, near_ref, far_ref, mid_ref, both_ref, out_ref, edge):
     rows, tile = near_ref.shape[:2]
     width = 2 * half * tile
     odd = lax.rem(lax.axis_index("dom"), 2)
@@ -227,15 +236,16 @@
         pair = jnp.concatenate([m_left, m_group, m_right])
 
     flops = 2 * rows * slots * tile * tile * 2 * tile * half
-    edges, a_held = pl.pallas_call(
+    span = 2 * rows * tile
+    kinds = [F32] + [BF16] * (subs - 1)
+    *edges, a_held = pl.pallas_call(
         functools.partial(edge_kernel, subs, half),
-        out_shape=[
-            jax.ShapeDtypeStruct((2 * rows, width, tile), F32),
-            jax.ShapeDtypeStruct(a_tiles.shape, BF16),
-        ],
+        out_shape=[jax.ShapeDtypeStruct((COARSE_ROWS, span), kind) for kind in kinds]
+        + [jax.ShapeDtypeStruct(a_tiles.shape, BF16)],
         in_specs=[smem, smem, smem, pl.BlockSpec(memory_space=pltpu.HBM), vmem, vmem],
-        out_specs=[vmem] * 2,
+        out_specs=[vmem] * (subs + 1),
         scratch_shapes=[
+            pltpu.VMEM((2 * rows, width, tile), F32),
             pltpu.VMEM((rows, 2 * tile, tile), BF16),
             pltpu.SemaphoreType.DMA((rows,)),
         ],
@@ -251,16 +261,25 @@
         low, high = k & -k, 1 << (k.bit_length() - 1)
         tiles[k][0] = exchange(tiles[k ^ low][0], low)
         tiles[k][1] = exchange(tiles[k ^ high][1], high)
-    span = width + 2 * rows * tile
-    *parts, pool = pl.pallas_call(
+    edge_terms = edges[:1] + [exchange(edges[k], k) for k in range(1, subs)]
+    pool, to_near, to_far = pl.pallas_call(
+        functools.partial(assemble_kernel, subs),
+        out_shape=[
+            jax.ShapeDtypeStruct((n, tile, 2 * tile), BF16) for n in (group_tiles + 1, rows, rows)
+        ],
+        in_specs=[vmem] * (2 * subs),
+        out_specs=[vmem] * 3,
+        compiler_params=pltpu.CompilerParams(vmem_limit_bytes=spare),
+        cost_estimate=pl.CostEstimate(flops=1 << 20, bytes_accessed=1 << 20, transcendentals=0),
+        name="assemble",
+    )(*sum(tiles, []))
+    far = lax.ppermute(to_far, "dom", [(d, d - 1 + 2 * (d % 2)) for d in range(1, doms - 1)])
+    near = lax.ppermute(to_near, "dom", [(d, d ^ 1) for d in range(doms)])
+    mids = pl.pallas_call(
         functools.partial(group_kernel, subs, half),
-        out_shape=[
-            jax.ShapeDtypeStruct((COARSE_ROWS, span), F32 if k == 0 else BF16)
-            for k in range(subs)
-        ]
-        + [jax.ShapeDtypeStruct((group_tiles + 1, tile, 2 * tile), BF16)],
-        in_specs=[smem, smem, smem] + [vmem] * (2 * subs + 2),
-        out_specs=[vmem] * (subs + 1),
+        out_shape=[jax.ShapeDtypeStruct((COARSE_ROWS, width), kind) for kind in kinds],
+        in_specs=[smem, smem, smem, vmem, vmem],
+        out_specs=[vmem] * subs,
         scratch_shapes=[
             pltpu.VMEM((rows * tile, width), BF16),
             pltpu.VMEM((width, width), F32),
@@ -268,38 +287,22 @@
         compiler_params=pltpu.CompilerParams(
             vmem_limit_bytes=2 * rows * tile * width + 4 * width * width + spare
         ),
-        cost_estimate=pl.CostEstimate(
-            flops=flops, bytes_accessed=a_bytes + subs * p_bytes, transcendentals=0
-        ),
+        cost_estimate=pl.CostEstimate(flops=1 << 20, bytes_accessed=1 << 20, transcendentals=0),
         name="group_part",
-    )(a_cols, a_count, pair, a_held, edges, *sum(tiles, []))
-    received = [exchange(parts[k], k) for k in range(1, subs)]
-    to_near, to_far = pl.pallas_call(
-        functools.partial(hand_out_kernel, subs),
-        out_shape=[jax.ShapeDtypeStruct(p_tiles.shape, BF16)] * 2,
-        in_specs=[vmem],
+    )(a_cols, a_count, pair, a_held, pool)
+    mid_terms = [mids[0]] + [exchange(mids[k], k) for k in range(1, subs)]
+    mid, both = pl.pallas_call(
+        functools.partial(sum_kernel, subs),
+        out_shape=[
+            jax.ShapeDtypeStruct((COARSE_ROWS, width), BF16),
+            jax.ShapeDtypeStruct((2 * COARSE_ROWS, span), BF16),
+        ],
+        in_specs=[vmem] * (2 * subs),
         out_specs=[vmem] * 2,
         compiler_params=pltpu.CompilerParams(vmem_limit_bytes=spare),
-        name="hand_out",
-    )(pool)
-    far = lax.ppermute(
-        to_far, "dom", [(d, d - 1 + 2 * (d % 2)) for d in range(1, doms - 1)]
-    )
-    near = lax.ppermute(to_near, "dom", [(d, d ^ 1) for d in range(doms)])
-    mid, both = pl.pallas_call(
-        functools.partial(sum_kernel, subs, width),
-        out_shape=[
-            jax.ShapeDtypeStruct((COARSE_ROWS, width), BF16),
-            jax.ShapeDtypeStruct((2 * COARSE_ROWS, span - width), BF16),
-        ],
-        in_specs=[vmem] * subs,
-        out_specs=[vmem] * 2,
-        compiler_params=pltpu.CompilerParams(vmem_limit_bytes=spare),
-        cost_estimate=pl.CostEstimate(
-            flops=1 << 31, bytes_accessed=8 * COARSE_ROWS * span, transcendentals=0
-        ),
+        cost_estimate=pl.CostEstimate(flops=7 << 28, bytes_accessed=1 << 20, transcendentals=0),
         name="sum_parts",
-    )(parts[0], *received)
+    )(*edge_terms, *mid_terms)
     return pl.pallas_call(
         functools.partial(finish_kernel, subs, half),
         out_shape=jax.ShapeDtypeStruct((COARSE_ROWS, 3 * width), BF16),
@@ -307,11 +310,9 @@
         out_specs=vmem,
         scratch_shapes=[pltpu.VMEM((2 * rows, tile, 2 * tile), BF16)],
         compiler_params=pltpu.CompilerParams(vmem_limit_bytes=2 * p_bytes + spare),
-        cost_estimate=pl.CostEstimate(
-            flops=1 << 28, bytes_accessed=4 * p_bytes, transcendentals=0
-        ),
+        cost_estimate=pl.CostEstimate(flops=1 << 20, bytes_accessed=1 << 20, transcendentals=0),
         name="finish",
-    )(pair, far, near, mid, both)
+    )(pair, near, far, mid, both)
 
 
 def solution(mesh):

time: 28.8 us -> 29.3 us (1.017)
  starting transfers between devices: 15.5 us -> 18.9 us
  waiting for transfers between devices: 6.36 us -> 3.81 us
  Pallas kernels: 6.75 us -> 6.16 us
    ppermute x1, waiting for transfers between devices: 3.82 us -> 0.01 us  [local(): lax.ppermute(to_far, 'dom', [(d, d - 1 + 2 * (d % 2)) for d in range(1, d...]
    ppermute x1, starting transfers between devices: 0.07 us -> 3.62 us  [local(): near = lax.ppermute(to_near, 'dom', [(d, d ^ 1) for d in range(doms)])]
    ppermute x1, starting transfers between devices: 6.63 us -> 3.82 us  [local(): lax.ppermute(to_far, 'dom', [(d, d - 1 + 2 * (d % 2)) for d in range(1, d...]
    ppermute x9 -> x12, starting transfers between devices: 8.74 us -> 11.4 us  [exchange(): return lax.ppermute(value, 'sub', [(s, s ^ k) for s in range(subs)])]
    ppermute x9 -> x12, waiting for transfers between devices: 2.54 us -> 3.81 us  [exchange(): return lax.ppermute(value, 'sub', [(s, s ^ k) for s in range(subs)])]
    pallas_call x1, Pallas kernels: 3.21 us -> 2.67 us  [local(): pl.pallas_call(functools.partial(edge_kernel, subs, half), out_shape=[jax...]
  transfers between devices with their start and end apart: 11 -> 14, of which waited for: 3 -> 3; matrix products, arithmetic and copies ran while one was open for 0% -> 0% of each run, Pallas kernels for 12% -> 15%
where the time goes in v5:
time: 29.3 us; the launch traced here: 29 us
  starting transfers between devices  18.9 us (65%)
  Pallas kernels  6.16 us (21%)
  waiting for transfers between devices  3.81 us (13%)
    ppermute x12, starting transfers between devices, exchange(): return lax.ppermute(value, 'sub', [(s, s ^ k) for s in range(subs)])  11.4 us
    ppermute x1, starting transfers between devices, local(): lax.ppermute(to_far, 'dom', [(d, d - 1 + 2 * (d % 2)) for d in range(1, d...  3.82 us
    ppermute x12, waiting for transfers between devices, exchange(): return lax.ppermute(value, 'sub', [(s, s ^ k) for s in range(subs)])  3.81 us
    ppermute x1, starting transfers between devices, local(): near = lax.ppermute(to_near, 'dom', [(d, d ^ 1) for d in range(doms)])  3.62 us
    pallas_call x1, Pallas kernels, local(): pl.pallas_call(functools.partial(edge_kernel, subs, half), out_shape=[jax...  2.67 us
    pallas_call x1, Pallas kernels, local(): pl.pallas_call(functools.partial(group_kernel, subs, half), out_shape=[ja...  1.33 us
    pallas_call x1, Pallas kernels, local(): pl.pallas_call(order_kernel, out_shape=[jax.ShapeDtypeStruct((rows // 2,...  1.02 us
    pallas_call x1, Pallas kernels, local(): pl.pallas_call(functools.partial(finish_kernel, subs, half), out_shape=ja...  0.93 us
  transfers between devices with their start and end apart: 14, of which 3 were waited for; matrix products, arithmetic and copies ran while one was open for 0% of the time, Pallas kernels for 15%

profile of v5, /device:TPU:1, one launch (start us, length us, event | category | flops | bytes accessed | tf_op | source)
XLA Modules:
  0.0 29.0 jit_solution(14062596519962764671)
XLA Ops:
  0.0 1.0 %order_columns.1 = (bf16[2,128,256]{2,1,0:T(8,128)(2,1)S(1)}, bf16[2,128,256]{2,1,0:T(8,128)(2,1)S(1)}) custom-call(s32[2,4]{1,0:T(2,128)} %bitcast.1, bf16[4,128,256]{2,1,0:T(8,128)(2,1)} %p_hbm.1), custom_call_target="tpu_custom_call" | custom-call | flops 1073741824 | bytes 524288 | tf_op jit(solution)/shard_map/order_columns/pallas_call | solution.py:207
  1.0 2.1 %collective-permute-start.2 = (bf16[2,128,256]{2,1,0:T(8,128)(2,1)S(1)}, bf16[2,128,256]{2,1,0:T(8,128)(2,1)S(1)}, u32[]{:S(2)}, u32[]{:S(2)}) collective-permute-start(bf16[2,128,256]{2,1,0:T(8,128)(2,1)S(1)} %get-tuple-element.21.refs_0_.own_0), channel_id=1, source_target_pairs={{0,2},{1,3},{2,0},{3,1},{4,6},{5,7},{6,4},{7,5},{8,10},{9,11},{10,... | collective-permute-start | bytes 393224 | tf_op jit(solution)/shard_map/ppermute | solution.py:205
  3.2 1.2 %collective-permute-start.1 = (bf16[2,128,256]{2,1,0:T(8,128)(2,1)S(1)}, bf16[2,128,256]{2,1,0:T(8,128)(2,1)S(1)}, u32[]{:S(2)}, u32[]{:S(2)}) collective-permute-start(bf16[2,128,256]{2,1,0:T(8,128)(2,1)S(1)} %get-tuple-element.22.refs_1_.own_1), channel_id=1, source_target_pairs={{0,1},{1,0},{2,3},{3,2},{4,5},{5,4},{6,7},{7,6},{8,9},{9,8},{10,11... | collective-permute-start | bytes 393224 | tf_op jit(solution)/shard_map/ppermute | solution.py:205
  4.4 0.3 collective-permute-start
  4.6 0.1 collective-permute-start.3
  4.7 1.7 %collective-permute-done.2.refs_4_ = bf16[2,128,256]{2,1,0:T(8,128)(2,1)S(1)} collective-permute-done((bf16[2,128,256]{2,1,0:T(8,128)(2,1)S(1)}, bf16[2,128,256]{2,1,0:T(8,128)(2,1)S(1)}, u32[]{:S(2)}, u32[]{:S(2)}) %collective-permute-start.2) | collective-permute-done | bytes 131104 | tf_op jit(solution)/shard_map/ppermute | solution.py:205
  6.4 1.1 %collective-permute-start.4 = (bf16[2,128,256]{2,1,0:T(8,128)(2,1)S(1)}, bf16[2,128,256]{2,1,0:T(8,128)(2,1)S(1)}, u32[]{:S(2)}, u32[]{:S(2)}) collective-permute-start(bf16[2,128,256]{2,1,0:T(8,128)(2,1)S(1)} %collective-permute-done.2.refs_4_), channel_id=1, source_target_pairs={{0,1},{1,0},{2,3},{3,2},{4,5},{5,4},{6,7},{7,6},{8,9},{9,8},{10,11... | collective-permute-start | bytes 393224 | tf_op jit(solution)/shard_map/ppermute | solution.py:205
  7.5 0.0 collective-permute-done.1.refs_3_
  7.5 1.2 %collective-permute-start.5 = (bf16[2,128,256]{2,1,0:T(8,128)(2,1)S(1)}, bf16[2,128,256]{2,1,0:T(8,128)(2,1)S(1)}, u32[]{:S(2)}, u32[]{:S(2)}) collective-permute-start(bf16[2,128,256]{2,1,0:T(8,128)(2,1)S(1)} %collective-permute-done.1.refs_3_), channel_id=1, source_target_pairs={{0,2},{1,3},{2,0},{3,1},{4,6},{5,7},{6,4},{7,5},{8,10},{9,11},{10,... | collective-permute-start | bytes 393224 | tf_op jit(solution)/shard_map/ppermute | solution.py:205
  8.7 2.7 %edge_part.1 = (f32[64,1024]{1,0:T(8,128)S(1)}, bf16[64,1024]{1,0:T(8,128)(2,1)S(1)}, bf16[64,1024]{1,0:T(8,128)(2,1)S(1)}, bf16[64,1024]{1,0:T(8,128)(2,1)S(1)}, bf16[4,10,128,128]{3,2,1,0:T(8,128)(2,1)S(1)}) custom-call(s32[4,10]{1,0:T(4,128)S(1)} %copy-done, s32[4]{0:T(128)S(1)} %copy-done.1, s32[1]{0:T(128)} %constant.0.clone.1.pair_ref, ...), custom_call_target="tpu_custom_call" | custom-call | flops 335544320 | bytes 1572864 | tf_op jit(solution)/shard_map/edge_part/pallas_call | solution.py:241
  11.4 0.1 collective-permute-start.8
  11.5 0.0 collective-permute-done.refs_2_
  11.5 1.2 %collective-permute-start.9 = (bf16[64,1024]{1,0:T(8,128)(2,1)S(1)}, bf16[64,1024]{1,0:T(8,128)(2,1)S(1)}, u32[]{:S(2)}, u32[]{:S(2)}) collective-permute-start(bf16[64,1024]{1,0:T(8,128)(2,1)S(1)} %get-tuple-element.27), channel_id=1, source_target_pairs={{0,2},{1,3},{2,0},{3,1},{4,6},{5,7},{6,4},{7,5},{8,10},{9,11},{10,... | collective-permute-start | bytes 393224 | tf_op jit(solution)/shard_map/ppermute | solution.py:205
  12.8 0.0 collective-permute-done.3.refs_5_
  12.8 1.4 %collective-permute-start.10 = (bf16[64,1024]{1,0:T(8,128)(2,1)S(1)}, bf16[64,1024]{1,0:T(8,128)(2,1)S(1)}, u32[]{:S(2)}, u32[]{:S(2)}) collective-permute-start(bf16[64,1024]{1,0:T(8,128)(2,1)S(1)} %get-tuple-element.28), channel_id=1, source_target_pairs={{0,3},{1,2},{2,1},{3,0},{4,7},{5,6},{6,5},{7,4},{8,11},{9,10},{10,... | collective-permute-start | bytes 393224 | tf_op jit(solution)/shard_map/ppermute | solution.py:205
  14.1 0.0 collective-permute-done.4.refs_6_
  14.1 0.0 collective-permute-done.5.refs_7_
  14.2 0.1 assemble.1
  14.3 3.6 %collective-permute-start.6 = (bf16[4,128,256]{2,1,0:T(8,128)(2,1)S(1)}, bf16[4,128,256]{2,1,0:T(8,128)(2,1)S(1)}, u32[]{:S(2)}, u32[]{:S(2)}) collective-permute-start(bf16[4,128,256]{2,1,0:T(8,128)(2,1)S(1)} %get-tuple-element.23), channel_id=1, source_target_pairs={{0,4},{4,0},{8,12},{12,8},{16,20},{20,16},{24,28},{28,24},{1,5},{5... | collective-permute-start | bytes 786440 | tf_op jit(solution)/shard_map/ppermute | solution.py:277
  17.9 3.8 %collective-permute-start.7 = (bf16[4,128,256]{2,1,0:T(8,128)(2,1)S(1)}, bf16[4,128,256]{2,1,0:T(8,128)(2,1)S(1)}, u32[]{:S(2)}, u32[]{:S(2)}) collective-permute-start(bf16[4,128,256]{2,1,0:T(8,128)(2,1)S(1)} %get-tuple-element.24), channel_id=1, source_target_pairs={{4,8},{8,4},{12,16},{16,12},{20,24},{24,20},{5,9},{9,5},{13,17},{1... | collective-permute-start | bytes 786440 | tf_op jit(solution)/shard_map/ppermute | solution.py:276
  21.7 1.3 %group_part.1 = (f32[64,256]{1,0:T(8,128)S(1)}, bf16[64,256]{1,0:T(8,128)(2,1)S(1)}, bf16[64,256]{1,0:T(8,128)(2,1)S(1)}, bf16[64,256]{1,0:T(8,128)(2,1)S(1)}) custom-call(s32[4,10]{1,0:T(4,128)S(1)} %copy-done, s32[4]{0:T(128)S(1)} %copy-done.1, s32[1]{0:T(128)} %constant.0.clone.1.pair_ref, bf16[4,10,128,128]{3,2,1,0:T(8,128)(2,1)S(1)} %get-tuple-element.29.a_ref, ...), custom_call_target="tpu_custom_call" | custom-call | flops 1048576 | bytes 1048576 | tf_op jit(solution)/shard_map/group_part/pallas_call | solution.py:278
  23.1 0.0 collective-permute-done.8.refs_1_
  23.1 0.4 %collective-permute-start.11 = (bf16[64,256]{1,0:T(8,128)(2,1)S(1)}, bf16[64,256]{1,0:T(8,128)(2,1)S(1)}, u32[]{:S(2)}, u32[]{:S(2)}) collective-permute-start(bf16[64,256]{1,0:T(8,128)(2,1)S(1)} %get-tuple-element.32), channel_id=1, source_target_pairs={{0,1},{1,0},{2,3},{3,2},{4,5},{5,4},{6,7},{7,6},{8,9},{9,8},{10,11... | collective-permute-start | bytes 98312 | tf_op jit(solution)/shard_map/ppermute | solution.py:205
  23.5 0.8 %collective-permute-start.12 = (bf16[64,256]{1,0:T(8,128)(2,1)S(1)}, bf16[64,256]{1,0:T(8,128)(2,1)S(1)}, u32[]{:S(2)}, u32[]{:S(2)}) collective-permute-start(bf16[64,256]{1,0:T(8,128)(2,1)S(1)} %get-tuple-element.33), channel_id=1, source_target_pairs={{0,2},{1,3},{2,0},{3,1},{4,6},{5,7},{6,4},{7,5},{8,10},{9,11},{10,... | collective-permute-start | bytes 98312 | tf_op jit(solution)/shard_map/ppermute | solution.py:205
  24.2 0.0 collective-permute-done.10.refs_3_
  24.2 1.6 %collective-permute-start.13 = (bf16[64,256]{1,0:T(8,128)(2,1)S(1)}, bf16[64,256]{1,0:T(8,128)(2,1)S(1)}, u32[]{:S(2)}, u32[]{:S(2)}) collective-permute-start(bf16[64,256]{1,0:T(8,128)(2,1)S(1)} %get-tuple-element.34), channel_id=1, source_target_pairs={{0,3},{1,2},{2,1},{3,0},{4,7},{5,6},{6,5},{7,4},{8,11},{9,10},{10,... | collective-permute-start | bytes 98312 | tf_op jit(solution)/shard_map/ppermute | solution.py:205
  25.8 0.7 %collective-permute-done.11.refs_5_ = bf16[64,256]{1,0:T(8,128)(2,1)S(1)} collective-permute-done((bf16[64,256]{1,0:T(8,128)(2,1)S(1)}, bf16[64,256]{1,0:T(8,128)(2,1)S(1)}, u32[]{:S(2)}, u32[]{:S(2)}) %collective-permute-start.11) | collective-permute-done | bytes 32800 | tf_op jit(solution)/shard_map/ppermute | solution.py:205
  26.5 1.4 %collective-permute-done.13.refs_7_ = bf16[64,256]{1,0:T(8,128)(2,1)S(1)} collective-permute-done((bf16[64,256]{1,0:T(8,128)(2,1)S(1)}, bf16[64,256]{1,0:T(8,128)(2,1)S(1)}, u32[]{:S(2)}, u32[]{:S(2)}) %collective-permute-start.13) | collective-permute-done | bytes 32800 | tf_op jit(solution)/shard_map/ppermute | solution.py:205
  27.9 0.1 sum_parts.1
  28.0 0.0 collective-permute-done.6.near_ref
  28.0 0.0 collective-permute-done.7.far_ref
  28.0 0.9 %finish.1 = bf16[64,768]{1,0:T(8,128)(2,1)} custom-call(s32[1]{0:T(128)} %constant.0.clone.1.pair_ref, bf16[4,128,256]{2,1,0:T(8,128)(2,1)S(1)} %collective-permute-done.6.near_ref, bf16[4,128,256]{2,1,0:T(8,128)(2,1)S(1)} %collective-permute-done.7.far_ref, bf16[64,256]{1,0:T(8,128)(2,1)S(1)} %get-tuple-element.35.mid_ref, ...), custom_call_target="tpu_custom_call" | custom-call | flops 1048576 | bytes 1048576 | tf_op jit(solution)/shard_map/finish/pallas_call | solution.py:306
  (6 shorter events, 0.0 us)
Async XLA Ops:
  0.0 8.7 %copy-start = (s32[4,10]{1,0:T(4,128)S(1)}, s32[4,10]{1,0:T(4,128)}, u32[]{:S(2)}) copy-start(s32[4,10]{1,0:T(4,128)} %cols_ref.3) | copy-start | bytes 484
  0.0 8.7 %copy-start.1 = (s32[4]{0:T(128)S(1)}, s32[4]{0:T(128)}, u32[]{:S(2)}) copy-start(s32[4]{0:T(128)} %count_ref.3) | copy-start | bytes 52
  1.0 5.4 %collective-permute-start.2 = (bf16[2,128,256]{2,1,0:T(8,128)(2,1)S(1)}, bf16[2,128,256]{2,1,0:T(8,128)(2,1)S(1)}, u32[]{:S(2)}, u32[]{:S(2)}) collective-permute-start(bf16[2,128,256]{2,1,0:T(8,128)(2,1)S(1)} %get-tuple-element.21.refs_0_.own_0), channel_id=1, source_target_pairs={{0,2},{1,3},{2,0},{3,1},{4,6},{5,7},{6,4},{7,5},{8,10},{9,11},{10,... | collective-permute-start | bytes 393224 | tf_op jit(solution)/shard_map/ppermute | solution.py:205
  3.2 4.3 %collective-permute-start.1 = (bf16[2,128,256]{2,1,0:T(8,128)(2,1)S(1)}, bf16[2,128,256]{2,1,0:T(8,128)(2,1)S(1)}, u32[]{:S(2)}, u32[]{:S(2)}) collective-permute-start(bf16[2,128,256]{2,1,0:T(8,128)(2,1)S(1)} %get-tuple-element.22.refs_1_.own_1), channel_id=1, source_target_pairs={{0,1},{1,0},{2,3},{3,2},{4,5},{5,4},{6,7},{7,6},{8,9},{9,8},{10,11... | collective-permute-start | bytes 393224 | tf_op jit(solution)/shard_map/ppermute | solution.py:205
  4.4 7.1 %collective-permute-start = (bf16[2,128,256]{2,1,0:T(8,128)(2,1)S(1)}, bf16[2,128,256]{2,1,0:T(8,128)(2,1)S(1)}, u32[]{:S(2)}, u32[]{:S(2)}) collective-permute-start(bf16[2,128,256]{2,1,0:T(8,128)(2,1)S(1)} %get-tuple-element.21.refs_0_.own_0), channel_id=1, source_target_pairs={{0,1},{1,0},{2,3},{3,2},{4,5},{5,4},{6,7},{7,6},{8,9},{9,8},{10,11... | collective-permute-start | bytes 393224 | tf_op jit(solution)/shard_map/ppermute | solution.py:205
  4.6 8.1 %collective-permute-start.3 = (bf16[2,128,256]{2,1,0:T(8,128)(2,1)S(1)}, bf16[2,128,256]{2,1,0:T(8,128)(2,1)S(1)}, u32[]{:S(2)}, u32[]{:S(2)}) collective-permute-start(bf16[2,128,256]{2,1,0:T(8,128)(2,1)S(1)} %get-tuple-element.22.refs_1_.own_1), channel_id=1, source_target_pairs={{0,2},{1,3},{2,0},{3,1},{4,6},{5,7},{6,4},{7,5},{8,10},{9,11},{10,... | collective-permute-start | bytes 393224 | tf_op jit(solution)/shard_map/ppermute | solution.py:205
  6.4 7.8 %collective-permute-start.4 = (bf16[2,128,256]{2,1,0:T(8,128)(2,1)S(1)}, bf16[2,128,256]{2,1,0:T(8,128)(2,1)S(1)}, u32[]{:S(2)}, u32[]{:S(2)}) collective-permute-start(bf16[2,128,256]{2,1,0:T(8,128)(2,1)S(1)} %collective-permute-done.2.refs_4_), channel_id=1, source_target_pairs={{0,1},{1,0},{2,3},{3,2},{4,5},{5,4},{6,7},{7,6},{8,9},{9,8},{10,11... | collective-permute-start | bytes 393224 | tf_op jit(solution)/shard_map/ppermute | solution.py:205
  7.5 6.6 %collective-permute-start.5 = (bf16[2,128,256]{2,1,0:T(8,128)(2,1)S(1)}, bf16[2,128,256]{2,1,0:T(8,128)(2,1)S(1)}, u32[]{:S(2)}, u32[]{:S(2)}) collective-permute-start(bf16[2,128,256]{2,1,0:T(8,128)(2,1)S(1)} %collective-permute-done.1.refs_3_), channel_id=1, source_target_pairs={{0,2},{1,3},{2,0},{3,1},{4,6},{5,7},{6,4},{7,5},{8,10},{9,11},{10,... | collective-permute-start | bytes 393224 | tf_op jit(solution)/shard_map/ppermute | solution.py:205
  11.4 11.6 %collective-permute-start.8 = (bf16[64,1024]{1,0:T(8,128)(2,1)S(1)}, bf16[64,1024]{1,0:T(8,128)(2,1)S(1)}, u32[]{:S(2)}, u32[]{:S(2)}) collective-permute-start(bf16[64,1024]{1,0:T(8,128)(2,1)S(1)} %get-tuple-element.26), channel_id=1, source_target_pairs={{0,1},{1,0},{2,3},{3,2},{4,5},{5,4},{6,7},{7,6},{8,9},{9,8},{10,11... | collective-permute-start | bytes 393224 | tf_op jit(solution)/shard_map/ppermute | solution.py:205
  11.5 11.9 %collective-permute-start.9 = (bf16[64,1024]{1,0:T(8,128)(2,1)S(1)}, bf16[64,1024]{1,0:T(8,128)(2,1)S(1)}, u32[]{:S(2)}, u32[]{:S(2)}) collective-permute-start(bf16[64,1024]{1,0:T(8,128)(2,1)S(1)} %get-tuple-element.27), channel_id=1, source_target_pairs={{0,2},{1,3},{2,0},{3,1},{4,6},{5,7},{6,4},{7,5},{8,10},{9,11},{10,... | collective-permute-start | bytes 393224 | tf_op jit(solution)/shard_map/ppermute | solution.py:205
  12.8 11.5 %collective-permute-start.10 = (bf16[64,1024]{1,0:T(8,128)(2,1)S(1)}, bf16[64,1024]{1,0:T(8,128)(2,1)S(1)}, u32[]{:S(2)}, u32[]{:S(2)}) collective-permute-start(bf16[64,1024]{1,0:T(8,128)(2,1)S(1)} %get-tuple-element.28), channel_id=1, source_target_pairs={{0,3},{1,2},{2,1},{3,0},{4,7},{5,6},{6,5},{7,4},{8,11},{9,10},{10,... | collective-permute-start | bytes 393224 | tf_op jit(solution)/shard_map/ppermute | solution.py:205
  14.3 13.7 %collective-permute-start.6 = (bf16[4,128,256]{2,1,0:T(8,128)(2,1)S(1)}, bf16[4,128,256]{2,1,0:T(8,128)(2,1)S(1)}, u32[]{:S(2)}, u32[]{:S(2)}) collective-permute-start(bf16[4,128,256]{2,1,0:T(8,128)(2,1)S(1)} %get-tuple-element.23), channel_id=1, source_target_pairs={{0,4},{4,0},{8,12},{12,8},{16,20},{20,16},{24,28},{28,24},{1,5},{5... | collective-permute-start | bytes 786440 | tf_op jit(solution)/shard_map/ppermute | solution.py:277
  17.9 10.1 %collective-permute-start.7 = (bf16[4,128,256]{2,1,0:T(8,128)(2,1)S(1)}, bf16[4,128,256]{2,1,0:T(8,128)(2,1)S(1)}, u32[]{:S(2)}, u32[]{:S(2)}) collective-permute-start(bf16[4,128,256]{2,1,0:T(8,128)(2,1)S(1)} %get-tuple-element.24), channel_id=1, source_target_pairs={{4,8},{8,4},{12,16},{16,12},{20,24},{24,20},{5,9},{9,5},{13,17},{1... | collective-permute-start | bytes 786440 | tf_op jit(solution)/shard_map/ppermute | solution.py:276
  23.1 3.5 %collective-permute-start.11 = (bf16[64,256]{1,0:T(8,128)(2,1)S(1)}, bf16[64,256]{1,0:T(8,128)(2,1)S(1)}, u32[]{:S(2)}, u32[]{:S(2)}) collective-permute-start(bf16[64,256]{1,0:T(8,128)(2,1)S(1)} %get-tuple-element.32), channel_id=1, source_target_pairs={{0,1},{1,0},{2,3},{3,2},{4,5},{5,4},{6,7},{7,6},{8,9},{9,8},{10,11... | collective-permute-start | bytes 98312 | tf_op jit(solution)/shard_map/ppermute | solution.py:205
  23.5 3.1 %collective-permute-start.12 = (bf16[64,256]{1,0:T(8,128)(2,1)S(1)}, bf16[64,256]{1,0:T(8,128)(2,1)S(1)}, u32[]{:S(2)}, u32[]{:S(2)}) collective-permute-start(bf16[64,256]{1,0:T(8,128)(2,1)S(1)} %get-tuple-element.33), channel_id=1, source_target_pairs={{0,2},{1,3},{2,0},{3,1},{4,6},{5,7},{6,4},{7,5},{8,10},{9,11},{10,... | collective-permute-start | bytes 98312 | tf_op jit(solution)/shard_map/ppermute | solution.py:205
  24.2 3.7 %collective-permute-start.13 = (bf16[64,256]{1,0:T(8,128)(2,1)S(1)}, bf16[64,256]{1,0:T(8,128)(2,1)S(1)}, u32[]{:S(2)}, u32[]{:S(2)}) collective-permute-start(bf16[64,256]{1,0:T(8,128)(2,1)S(1)} %get-tuple-element.34), channel_id=1, source_target_pairs={{0,3},{1,2},{2,1},{3,0},{4,7},{5,6},{6,5},{7,4},{8,11},{9,10},{10,... | collective-permute-start | bytes 98312 | tf_op jit(solution)/shard_map/ppermute | solution.py:205

commit v6 on v4

--- a/solution.py
+++ b/solution.py
@@ -134,48 +134,61 @@
             outs[k][:, width + c * tile : width + (c + 1) * tile] = edge_ref[c, at].astype(kind)
 
 
-def sum_kernel(subs, width, *refs):
-    part_refs, (mid_ref, edge_ref) = refs[:subs], refs[subs:]
-    total = part_refs[0][...]
-    for k in range(1, subs):
-        total = total + part_refs[k][...].astype(F32)
+def halo_product(subs, half, side, pair_ref, terms, p_ref):
+    rows, tile = p_ref.shape[:2]
+    if half == 1:
+        stacked = jnp.concatenate([p_ref[t] for t in range(rows)], axis=0)
+        out = jnp.dot(terms, stacked, preferred_element_type=F32)
+        out = out[:COARSE_ROWS] + out[COARSE_ROWS:]
+        return [out[:, :tile], out[:, tile:]]
+    blocks = [jnp.zeros((COARSE_ROWS, tile), F32) for _ in range(2 * half)]
+    for t in range(rows):
+        lhs = terms[:, t * tile : (t + 1) * tile]
+        out = jnp.dot(lhs, p_ref[t], preferred_element_type=F32)
+        out = out[:COARSE_ROWS] + out[COARSE_ROWS:]
+        m_here = pair_ref[side * (subs + 1) * rows + t]
+        for m in range(half):
+            blocks[m] = blocks[m] + jnp.where(m_here == m, out[:, :tile], 0.0)
+            blocks[m + half] = blocks[m + half] + jnp.where(m_here == m, out[:, tile:], 0.0)
+    return blocks
+
+
+def sum_kernel(*refs):
+    total = refs[0][...]
+    for ref in refs[1:-1]:
+        total = total + ref[...].astype(F32)
+    refs[-1][...] = total
+
+
+def near_kernel(subs, half, pair_ref, near_ref, sum_ref, last_ref, *rest):
+    mid_ref, side_ref, terms_ref, total = rest
+    rows, tile = near_ref.shape[:2]
+    width, span = 2 * half * tile, rows * tile
+    odd = lax.rem(lax.axis_index("dom"), 2)
+    total[...] = sum_ref[...] + last_ref[...].astype(F32)
     mid_ref[...] = total[:, :width].astype(BF16)
-    sums = total[:, width:]
-    high = sums.astype(BF16)
-    edge_ref[:COARSE_ROWS] = high
-    edge_ref[COARSE_ROWS:] = (sums - high.astype(F32)).astype(BF16)
-
-
-def finish_kernel(subs, half, pair_ref, far_ref, near_ref, mid_ref, both_ref, out_ref, edge):
-    rows, tile = near_ref.shape[:2]
+
+    def terms(side):
+        value = total[:, pl.ds(pl.multiple_of(width + side * span, tile), span)]
+        high = value.astype(BF16)
+        return jnp.concatenate([high, (value - high.astype(F32)).astype(BF16)], axis=0)
+
+    terms_ref[...] = terms(odd)
+    blocks = halo_product(subs, half, 1 - odd, pair_ref, terms(1 - odd), near_ref)
+    for b in range(2 * half):
+        side_ref[:, b * tile : (b + 1) * tile] = blocks[b].astype(BF16)
+
+
+def finish_kernel(subs, half, pair_ref, far_ref, terms_ref, mid_ref, side_ref, out_ref):
+    tile = far_ref.shape[1]
     width = 2 * half * tile
     odd = lax.rem(lax.axis_index("dom"), 2)
-    edge[pl.ds((1 - odd) * rows, rows)] = near_ref[...]
-    edge[pl.ds(odd * rows, rows)] = far_ref[...]
     out_ref[:, width : 2 * width] = mid_ref[...]
-    both = both_ref[...]
-    for side in range(2):
-        blocks = [jnp.zeros((COARSE_ROWS, tile), F32) for _ in range(2 * half)]
-        tiles = range(side * rows, (side + 1) * rows)
-        if half == 1:
-            stacked = jnp.concatenate([edge[c] for c in tiles], axis=0)
-            lhs = both[:, side * rows * tile : (side + 1) * rows * tile]
-            term = jnp.dot(lhs, stacked, preferred_element_type=F32)
-            term = term[:COARSE_ROWS] + term[COARSE_ROWS:]
-            blocks = [term[:, :tile], term[:, tile:]]
-        else:
-            for c in tiles:
-                lhs = both[:, c * tile : (c + 1) * tile]
-                term = jnp.dot(lhs, edge[c], preferred_element_type=F32)
-                term = term[:COARSE_ROWS] + term[COARSE_ROWS:]
-                m_here = pair_ref[c if side == 0 else subs * rows + c]
-                for m in range(half):
-                    here = m_here == m
-                    blocks[m] = blocks[m] + jnp.where(here, term[:, :tile], 0.0)
-                    blocks[m + half] = blocks[m + half] + jnp.where(here, term[:, tile:], 0.0)
-        for b in range(2 * half):
-            at = 2 * side * width + b * tile
-            out_ref[:, at : at + tile] = blocks[b].astype(BF16)
+    out_ref[:, pl.ds(pl.multiple_of((1 - odd) * 2 * width, tile), width)] = side_ref[...]
+    blocks = halo_product(subs, half, odd, pair_ref, terms_ref[...], far_ref)
+    for b in range(2 * half):
+        at = pl.multiple_of(odd * 2 * width + b * tile, tile)
+        out_ref[:, pl.ds(at, tile)] = blocks[b].astype(BF16)
 
 
 def local(a_tiles, a_cols, a_count, p_tiles, p_cols):
@@ -286,32 +299,38 @@
         to_far, "dom", [(d, d - 1 + 2 * (d % 2)) for d in range(1, doms - 1)]
     )
     near = lax.ppermute(to_near, "dom", [(d, d ^ 1) for d in range(doms)])
-    mid, both = pl.pallas_call(
-        functools.partial(sum_kernel, subs, width),
+    sums = pl.pallas_call(
+        sum_kernel,
+        out_shape=jax.ShapeDtypeStruct((COARSE_ROWS, span), F32),
+        in_specs=[vmem] * (subs - 1),
+        out_specs=vmem,
+        compiler_params=pltpu.CompilerParams(vmem_limit_bytes=spare),
+        cost_estimate=pl.CostEstimate(flops=3 << 29, bytes_accessed=1 << 20, transcendentals=0),
+        name="sum_parts",
+    )(parts[0], *received[:-1])
+    mid, side, terms = pl.pallas_call(
+        functools.partial(near_kernel, subs, half),
         out_shape=[
             jax.ShapeDtypeStruct((COARSE_ROWS, width), BF16),
-            jax.ShapeDtypeStruct((2 * COARSE_ROWS, span - width), BF16),
-        ],
-        in_specs=[vmem] * subs,
-        out_specs=[vmem] * 2,
-        compiler_params=pltpu.CompilerParams(vmem_limit_bytes=spare),
-        cost_estimate=pl.CostEstimate(
-            flops=1 << 31, bytes_accessed=8 * COARSE_ROWS * span, transcendentals=0
-        ),
-        name="sum_parts",
-    )(parts[0], *received)
+            jax.ShapeDtypeStruct((COARSE_ROWS, width), BF16),
+            jax.ShapeDtypeStruct((2 * COARSE_ROWS, rows * tile), BF16),
+        ],
+        in_specs=[smem] + [vmem] * 3,
+        out_specs=[vmem] * 3,
+        scratch_shapes=[pltpu.VMEM((COARSE_ROWS, span), F32)],
+        compiler_params=pltpu.CompilerParams(vmem_limit_bytes=2 * p_bytes + spare),
+        cost_estimate=pl.CostEstimate(flops=1 << 20, bytes_accessed=1 << 20, transcendentals=0),
+        name="near_part",
+    )(pair, near, sums, received[-1])
     return pl.pallas_call(
         functools.partial(finish_kernel, subs, half),
         out_shape=jax.ShapeDtypeStruct((COARSE_ROWS, 3 * width), BF16),
         in_specs=[smem] + [vmem] * 4,
         out_specs=vmem,
-        scratch_shapes=[pltpu.VMEM((2 * rows, tile, 2 * tile), BF16)],
         compiler_params=pltpu.CompilerParams(vmem_limit_bytes=2 * p_bytes + spare),
-        cost_estimate=pl.CostEstimate(
-            flops=1 << 28, bytes_accessed=4 * p_bytes, transcendentals=0
-        ),
-        name="finish",
-    )(pair, far, near, mid, both)
+        cost_estimate=pl.CostEstimate(flops=1 << 20, bytes_accessed=1 << 20, transcendentals=0),
+        name="far_part",
+    )(pair, far, terms, mid, side)
 
 
 def solution(mesh):

time: 28.8 us -> 29.5 us (1.024)
  the two profiles are of different devices: /device:TPU:1 before, /device:TPU:17 now
where the time goes in v6:
time: 29.5 us; the launch traced here: 29.4 us
  starting transfers between devices  14.6 us (49%)
  waiting for transfers between devices  8.5 us (29%)
  Pallas kernels  6.14 us (21%)
    ppermute x9, waiting for transfers between devices, exchange(): return lax.ppermute(value, 'sub', [(s, s ^ k) for s in range(subs)])  8.49 us
    ppermute x9, starting transfers between devices, exchange(): return lax.ppermute(value, 'sub', [(s, s ^ k) for s in range(subs)])  8.22 us
    ppermute x1, starting transfers between devices, local(): near = lax.ppermute(to_near, 'dom', [(d, d ^ 1) for d in range(doms)])  3.3 us
    ppermute x1, starting transfers between devices, local(): lax.ppermute(to_far, 'dom', [(d, d - 1 + 2 * (d % 2)) for d in range(1, d...  3.1 us
    pallas_call x1, Pallas kernels, local(): pl.pallas_call(functools.partial(edge_kernel, subs, half), out_shape=[jax...  2.49 us
    pallas_call x1, Pallas kernels, local(): pl.pallas_call(functools.partial(group_kernel, subs, half), out_shape=[ja...  1.46 us
    pallas_call x1, Pallas kernels, local(): pl.pallas_call(order_kernel, out_shape=[jax.ShapeDtypeStruct((rows // 2,...  1.02 us
    pallas_call x1, Pallas kernels, local(): pl.pallas_call(functools.partial(finish_kernel, subs, half), out_shape=ja...  0.83 us
  transfers between devices with their start and end apart: 11, of which 3 were waited for; matrix products, arithmetic and copies ran while one was open for 0% of the time, Pallas kernels for 10%

profile of v6, /device:TPU:17, one launch (start us, length us, event | category | flops | bytes accessed | tf_op | source)
XLA Modules:
  0.0 29.4 jit_solution(17380329364687658176)
XLA Ops:
  0.0 0.0 copy-start
  0.0 0.0 copy-start.1
  0.0 1.0 %order_columns.1 = (bf16[2,128,256]{2,1,0:T(8,128)(2,1)S(1)}, bf16[2,128,256]{2,1,0:T(8,128)(2,1)S(1)}) custom-call(s32[2,4]{1,0:T(2,128)} %bitcast.1, bf16[4,128,256]{2,1,0:T(8,128)(2,1)} %p_hbm.1), custom_call_target="tpu_custom_call" | custom-call | flops 1073741824 | bytes 524288 | tf_op jit(solution)/shard_map/order_columns/pallas_call | solution.py:211
  1.0 1.3 %collective-permute-start.2 = (bf16[2,128,256]{2,1,0:T(8,128)(2,1)S(1)}, bf16[2,128,256]{2,1,0:T(8,128)(2,1)S(1)}, u32[]{:S(2)}, u32[]{:S(2)}) collective-permute-start(bf16[2,128,256]{2,1,0:T(8,128)(2,1)S(1)} %get-tuple-element.19.own_0.rest_0_), channel_id=1, source_target_pairs={{0,2},{1,3},{2,0},{3,1},{4,6},{5,7},{6,4},{7,5},{8,10},{9,11},{10,... | collective-permute-start | bytes 393224 | tf_op jit(solution)/shard_map/ppermute | solution.py:209
  2.3 1.2 %collective-permute-start.1 = (bf16[2,128,256]{2,1,0:T(8,128)(2,1)S(1)}, bf16[2,128,256]{2,1,0:T(8,128)(2,1)S(1)}, u32[]{:S(2)}, u32[]{:S(2)}) collective-permute-start(bf16[2,128,256]{2,1,0:T(8,128)(2,1)S(1)} %get-tuple-element.20.own_1.rest_1_), channel_id=1, source_target_pairs={{0,1},{1,0},{2,3},{3,2},{4,5},{5,4},{6,7},{7,6},{8,9},{9,8},{10,11... | collective-permute-start | bytes 393224 | tf_op jit(solution)/shard_map/ppermute | solution.py:209
  3.5 0.3 collective-permute-start
  3.8 0.2 collective-permute-start.3
  4.0 1.4 %collective-permute-done.2.rest_4_ = bf16[2,128,256]{2,1,0:T(8,128)(2,1)S(1)} collective-permute-done((bf16[2,128,256]{2,1,0:T(8,128)(2,1)S(1)}, bf16[2,128,256]{2,1,0:T(8,128)(2,1)S(1)}, u32[]{:S(2)}, u32[]{:S(2)}) %collective-permute-start.2) | collective-permute-done | bytes 131104 | tf_op jit(solution)/shard_map/ppermute | solution.py:209
  5.5 1.2 %collective-permute-start.4 = (bf16[2,128,256]{2,1,0:T(8,128)(2,1)S(1)}, bf16[2,128,256]{2,1,0:T(8,128)(2,1)S(1)}, u32[]{:S(2)}, u32[]{:S(2)}) collective-permute-start(bf16[2,128,256]{2,1,0:T(8,128)(2,1)S(1)} %collective-permute-done.2.rest_4_), channel_id=1, source_target_pairs={{0,1},{1,0},{2,3},{3,2},{4,5},{5,4},{6,7},{7,6},{8,9},{9,8},{10,11... | collective-permute-start | bytes 393224 | tf_op jit(solution)/shard_map/ppermute | solution.py:209
  6.7 0.0 collective-permute-done.1.rest_3_
  6.7 1.2 %collective-permute-start.5 = (bf16[2,128,256]{2,1,0:T(8,128)(2,1)S(1)}, bf16[2,128,256]{2,1,0:T(8,128)(2,1)S(1)}, u32[]{:S(2)}, u32[]{:S(2)}) collective-permute-start(bf16[2,128,256]{2,1,0:T(8,128)(2,1)S(1)} %collective-permute-done.1.rest_3_), channel_id=1, source_target_pairs={{0,2},{1,3},{2,0},{3,1},{4,6},{5,7},{6,4},{7,5},{8,10},{9,11},{10,... | collective-permute-start | bytes 393224 | tf_op jit(solution)/shard_map/ppermute | solution.py:209
  7.9 0.0 copy-done
  7.9 0.0 copy-done.1
  7.9 2.5 %edge_part.1 = (f32[8,256,128]{2,1,0:T(8,128)S(1)}, bf16[4,10,128,128]{3,2,1,0:T(8,128)(2,1)S(1)}) custom-call(s32[4,10]{1,0:T(4,128)S(1)} %copy-done, s32[4]{0:T(128)S(1)} %copy-done.1, s32[1]{0:T(128)} %constant.0.clone.1.pair_ref, bf16[4,10,128,128]{3,2,1,0:T(8,128)(2,1)} %a_hbm.1, bf16[2,128,256]{2,1,0:T(8,128)(2,1)S(1)} %get-tuple-element.19.own_0.rest_0_, ...), custom_call_target="tpu_custom_call" | custom-call | flops 335544320 | bytes 1572864 | tf_op jit(solution)/shard_map/edge_part/pallas_call | solution.py:243
  10.4 0.0 collective-permute-done.rest_2_
  10.4 0.0 collective-permute-done.3.rest_5_
  10.4 1.6 %collective-permute-done.4.rest_6_ = bf16[2,128,256]{2,1,0:T(8,128)(2,1)S(1)} collective-permute-done((bf16[2,128,256]{2,1,0:T(8,128)(2,1)S(1)}, bf16[2,128,256]{2,1,0:T(8,128)(2,1)S(1)}, u32[]{:S(2)}, u32[]{:S(2)}) %collective-permute-start.4) | collective-permute-done | bytes 131104 | tf_op jit(solution)/shard_map/ppermute | solution.py:209
  12.0 0.0 collective-permute-done.5.rest_7_
  12.0 1.5 %group_part.1 = (f32[64,1280]{1,0:T(8,128)S(1)}, bf16[64,1280]{1,0:T(8,128)(2,1)S(1)}, bf16[64,1280]{1,0:T(8,128)(2,1)S(1)}, bf16[64,1280]{1,0:T(8,128)(2,1)S(1)}, bf16[17,128,256]{2,1,0:T(8,128)(2,1)S(1)}) custom-call(s32[4,10]{1,0:T(4,128)S(1)} %copy-done, s32[4]{0:T(128)S(1)} %copy-done.1, s32[1]{0:T(128)} %constant.0.clone.1.pair_ref, ...), custom_call_target="tpu_custom_call" | custom-call | flops 335544320 | bytes 2359296 | tf_op jit(solution)/shard_map/group_part/pallas_call | solution.py:268
  13.5 1.3 %collective-permute-start.8 = (bf16[64,1280]{1,0:T(8,128)(2,1)S(1)}, bf16[64,1280]{1,0:T(8,128)(2,1)S(1)}, u32[]{:S(2)}, u32[]{:S(2)}) collective-permute-start(bf16[64,1280]{1,0:T(8,128)(2,1)S(1)} %get-tuple-element.27), channel_id=1, source_target_pairs={{0,1},{1,0},{2,3},{3,2},{4,5},{5,4},{6,7},{7,6},{8,9},{9,8},{10,11... | collective-permute-start | bytes 491528 | tf_op jit(solution)/shard_map/ppermute | solution.py:209
  14.7 0.2 collective-permute-start.9
  15.0 3.3 %collective-permute-start.7 = (bf16[4,128,256]{2,1,0:T(8,128)(2,1)S(1)}, bf16[4,128,256]{2,1,0:T(8,128)(2,1)S(1)}, u32[]{:S(2)}, u32[]{:S(2)}) collective-permute-start(bf16[4,128,256]{2,1,0:T(8,128)(2,1)S(1)} %get-tuple-element.25), channel_id=1, source_target_pairs={{0,4},{4,0},{8,12},{12,8},{16,20},{20,16},{24,28},{28,24},{1,5},{5... | collective-permute-start | bytes 786440 | tf_op jit(solution)/shard_map/ppermute | solution.py:301
  18.3 3.1 %collective-permute-start.6 = (bf16[4,128,256]{2,1,0:T(8,128)(2,1)S(1)}, bf16[4,128,256]{2,1,0:T(8,128)(2,1)S(1)}, u32[]{:S(2)}, u32[]{:S(2)}) collective-permute-start(bf16[4,128,256]{2,1,0:T(8,128)(2,1)S(1)} %get-tuple-element.24), channel_id=1, source_target_pairs={{4,8},{8,4},{12,16},{16,12},{20,24},{24,20},{5,9},{9,5},{13,17},{1... | collective-permute-start | bytes 786440 | tf_op jit(solution)/shard_map/ppermute | solution.py:298
  21.4 1.3 %collective-permute-start.10 = (bf16[64,1280]{1,0:T(8,128)(2,1)S(1)}, bf16[64,1280]{1,0:T(8,128)(2,1)S(1)}, u32[]{:S(2)}, u32[]{:S(2)}) collective-permute-start(bf16[64,1280]{1,0:T(8,128)(2,1)S(1)} %get-tuple-element.29), channel_id=1, source_target_pairs={{0,3},{1,2},{2,1},{3,0},{4,7},{5,6},{6,5},{7,4},{8,11},{9,10},{10,... | collective-permute-start | bytes 491528 | tf_op jit(solution)/shard_map/ppermute | solution.py:209
  22.7 0.0 collective-permute-done.8.refs_1_
  22.7 0.0 collective-permute-done.9.refs_2_
  22.7 0.1 sum_parts.1.sum_ref
  22.8 5.5 %collective-permute-done.10.last_ref = bf16[64,1280]{1,0:T(8,128)(2,1)S(1)} collective-permute-done((bf16[64,1280]{1,0:T(8,128)(2,1)S(1)}, bf16[64,1280]{1,0:T(8,128)(2,1)S(1)}, u32[]{:S(2)}, u32[]{:S(2)}) %collective-permute-start.10) | collective-permute-done | bytes 163872 | tf_op jit(solution)/shard_map/ppermute | solution.py:209
  28.2 0.0 collective-permute-done.7.near_ref
  28.3 0.3 near_part.1
  28.5 0.0 collective-permute-done.6.far_ref
  28.5 0.8 %far_part.1 = bf16[64,768]{1,0:T(8,128)(2,1)} custom-call(s32[1]{0:T(128)} %constant.0.clone.1.pair_ref, bf16[4,128,256]{2,1,0:T(8,128)(2,1)S(1)} %collective-permute-done.6.far_ref, bf16[128,512]{1,0:T(8,128)(2,1)S(1)} %get-tuple-element.30.terms_ref, bf16[64,256]{1,0:T(8,128)(2,1)S(1)} %get-tuple-element.31.mid_ref, ...), custom_call_target="tpu_custom_call" | custom-call | flops 1048576 | bytes 1048576 | tf_op jit(solution)/shard_map/far_part/pallas_call | solution.py:325
  (1 shorter events, 0.0 us)
Async XLA Ops:
  0.0 7.9 %copy-start = (s32[4,10]{1,0:T(4,128)S(1)}, s32[4,10]{1,0:T(4,128)}, u32[]{:S(2)}) copy-start(s32[4,10]{1,0:T(4,128)} %cols_ref.3) | copy-start | bytes 484
  0.0 7.9 %copy-start.1 = (s32[4]{0:T(128)S(1)}, s32[4]{0:T(128)}, u32[]{:S(2)}) copy-start(s32[4]{0:T(128)} %count_ref.3) | copy-start | bytes 52
  1.0 4.4 %collective-permute-start.2 = (bf16[2,128,256]{2,1,0:T(8,128)(2,1)S(1)}, bf16[2,128,256]{2,1,0:T(8,128)(2,1)S(1)}, u32[]{:S(2)}, u32[]{:S(2)}) collective-permute-start(bf16[2,128,256]{2,1,0:T(8,128)(2,1)S(1)} %get-tuple-element.19.own_0.rest_0_), channel_id=1, source_target_pairs={{0,2},{1,3},{2,0},{3,1},{4,6},{5,7},{6,4},{7,5},{8,10},{9,11},{10,... | collective-permute-start | bytes 393224 | tf_op jit(solution)/shard_map/ppermute | solution.py:209
  2.3 4.3 %collective-permute-start.1 = (bf16[2,128,256]{2,1,0:T(8,128)(2,1)S(1)}, bf16[2,128,256]{2,1,0:T(8,128)(2,1)S(1)}, u32[]{:S(2)}, u32[]{:S(2)}) collective-permute-start(bf16[2,128,256]{2,1,0:T(8,128)(2,1)S(1)} %get-tuple-element.20.own_1.rest_1_), channel_id=1, source_target_pairs={{0,1},{1,0},{2,3},{3,2},{4,5},{5,4},{6,7},{7,6},{8,9},{9,8},{10,11... | collective-permute-start | bytes 393224 | tf_op jit(solution)/shard_map/ppermute | solution.py:209
  3.5 6.9 %collective-permute-start = (bf16[2,128,256]{2,1,0:T(8,128)(2,1)S(1)}, bf16[2,128,256]{2,1,0:T(8,128)(2,1)S(1)}, u32[]{:S(2)}, u32[]{:S(2)}) collective-permute-start(bf16[2,128,256]{2,1,0:T(8,128)(2,1)S(1)} %get-tuple-element.19.own_0.rest_0_), channel_id=1, source_target_pairs={{0,1},{1,0},{2,3},{3,2},{4,5},{5,4},{6,7},{7,6},{8,9},{9,8},{10,11... | collective-permute-start | bytes 393224 | tf_op jit(solution)/shard_map/ppermute | solution.py:209
  3.8 6.6 %collective-permute-start.3 = (bf16[2,128,256]{2,1,0:T(8,128)(2,1)S(1)}, bf16[2,128,256]{2,1,0:T(8,128)(2,1)S(1)}, u32[]{:S(2)}, u32[]{:S(2)}) collective-permute-start(bf16[2,128,256]{2,1,0:T(8,128)(2,1)S(1)} %get-tuple-element.20.own_1.rest_1_), channel_id=1, source_target_pairs={{0,2},{1,3},{2,0},{3,1},{4,6},{5,7},{6,4},{7,5},{8,10},{9,11},{10,... | collective-permute-start | bytes 393224 | tf_op jit(solution)/shard_map/ppermute | solution.py:209
  5.5 6.5 %collective-permute-start.4 = (bf16[2,128,256]{2,1,0:T(8,128)(2,1)S(1)}, bf16[2,128,256]{2,1,0:T(8,128)(2,1)S(1)}, u32[]{:S(2)}, u32[]{:S(2)}) collective-permute-start(bf16[2,128,256]{2,1,0:T(8,128)(2,1)S(1)} %collective-permute-done.2.rest_4_), channel_id=1, source_target_pairs={{0,1},{1,0},{2,3},{3,2},{4,5},{5,4},{6,7},{7,6},{8,9},{9,8},{10,11... | collective-permute-start | bytes 393224 | tf_op jit(solution)/shard_map/ppermute | solution.py:209
  6.7 5.3 %collective-permute-start.5 = (bf16[2,128,256]{2,1,0:T(8,128)(2,1)S(1)}, bf16[2,128,256]{2,1,0:T(8,128)(2,1)S(1)}, u32[]{:S(2)}, u32[]{:S(2)}) collective-permute-start(bf16[2,128,256]{2,1,0:T(8,128)(2,1)S(1)} %collective-permute-done.1.rest_3_), channel_id=1, source_target_pairs={{0,2},{1,3},{2,0},{3,1},{4,6},{5,7},{6,4},{7,5},{8,10},{9,11},{10,... | collective-permute-start | bytes 393224 | tf_op jit(solution)/shard_map/ppermute | solution.py:209
  13.5 9.2 %collective-permute-start.8 = (bf16[64,1280]{1,0:T(8,128)(2,1)S(1)}, bf16[64,1280]{1,0:T(8,128)(2,1)S(1)}, u32[]{:S(2)}, u32[]{:S(2)}) collective-permute-start(bf16[64,1280]{1,0:T(8,128)(2,1)S(1)} %get-tuple-element.27), channel_id=1, source_target_pairs={{0,1},{1,0},{2,3},{3,2},{4,5},{5,4},{6,7},{7,6},{8,9},{9,8},{10,11... | collective-permute-start | bytes 491528 | tf_op jit(solution)/shard_map/ppermute | solution.py:209
  14.7 8.0 %collective-permute-start.9 = (bf16[64,1280]{1,0:T(8,128)(2,1)S(1)}, bf16[64,1280]{1,0:T(8,128)(2,1)S(1)}, u32[]{:S(2)}, u32[]{:S(2)}) collective-permute-start(bf16[64,1280]{1,0:T(8,128)(2,1)S(1)} %get-tuple-element.28), channel_id=1, source_target_pairs={{0,2},{1,3},{2,0},{3,1},{4,6},{5,7},{6,4},{7,5},{8,10},{9,11},{10,... | collective-permute-start | bytes 491528 | tf_op jit(solution)/shard_map/ppermute | solution.py:209
  15.0 13.2 %collective-permute-start.7 = (bf16[4,128,256]{2,1,0:T(8,128)(2,1)S(1)}, bf16[4,128,256]{2,1,0:T(8,128)(2,1)S(1)}, u32[]{:S(2)}, u32[]{:S(2)}) collective-permute-start(bf16[4,128,256]{2,1,0:T(8,128)(2,1)S(1)} %get-tuple-element.25), channel_id=1, source_target_pairs={{0,4},{4,0},{8,12},{12,8},{16,20},{20,16},{24,28},{28,24},{1,5},{5... | collective-permute-start | bytes 786440 | tf_op jit(solution)/shard_map/ppermute | solution.py:301
  18.3 10.2 %collective-permute-start.6 = (bf16[4,128,256]{2,1,0:T(8,128)(2,1)S(1)}, bf16[4,128,256]{2,1,0:T(8,128)(2,1)S(1)}, u32[]{:S(2)}, u32[]{:S(2)}) collective-permute-start(bf16[4,128,256]{2,1,0:T(8,128)(2,1)S(1)} %get-tuple-element.24), channel_id=1, source_target_pairs={{4,8},{8,4},{12,16},{16,12},{20,24},{24,20},{5,9},{9,5},{13,17},{1... | collective-permute-start | bytes 786440 | tf_op jit(solution)/shard_map/ppermute | solution.py:298
  21.4 6.8 %collective-permute-start.10 = (bf16[64,1280]{1,0:T(8,128)(2,1)S(1)}, bf16[64,1280]{1,0:T(8,128)(2,1)S(1)}, u32[]{:S(2)}, u32[]{:S(2)}) collective-permute-start(bf16[64,1280]{1,0:T(8,128)(2,1)S(1)} %get-tuple-element.29), channel_id=1, source_target_pairs={{0,3},{1,2},{2,1},{3,0},{4,7},{5,6},{6,5},{7,4},{8,11},{9,10},{10,... | collective-permute-start | bytes 491528 | tf_op jit(solution)/shard_map/ppermute | solution.py:209

commit v7 on v4

--- a/solution.py
+++ b/solution.py
@@ -93,6 +93,79 @@
                     m = pair_ref[rows + me * rows + f]
                     for start, part in ((m, term[:tile]), (m + half, term[tile:])):
                         out_ref[at, pl.ds(pl.multiple_of(start * tile, tile), tile)] += part
+
+
+def terms_kernel(subs, cols_ref, count_ref, a_hbm, own_0, own_1, *rest):
+    edges, (high_ref, low_ref, a_ref, total, turned, sems) = rest[:subs], rest[subs:]
+    rows, slots, tile = a_ref.shape[:3]
+    tiles = total.shape[0] - 1
+    me = lax.axis_index("sub")
+    base = lax.axis_index("dom") * (subs * rows) - rows
+    loads = [pltpu.make_async_copy(a_hbm.at[f], a_ref.at[f], sems.at[f]) for f in range(rows)]
+    for load in loads:
+        load.start()
+    total[...] = jnp.zeros(total.shape, F32)
+    for f in range(rows):
+        turned[f] = (own_0, own_1)[f // (rows // 2)][f % (rows // 2)].T
+    for f in range(rows):
+        loads[f].wait()
+        for k in range(slots):
+            at = jnp.where(k < count_ref[f], cols_ref[f, k] - base, tiles)
+            total[at] += jnp.dot(turned[f], a_ref[f, k], preferred_element_type=F32)
+    for c in range(subs * rows):
+        value = total[rows + c]
+        high = value.astype(BF16)
+        high_ref[c] = high
+        low_ref[c] = (value - high.astype(F32)).astype(BF16)
+    for k in range(subs):
+        start = pl.multiple_of(lax.bitwise_xor(me, k) * COARSE_ROWS, COARSE_ROWS)
+        for i, c in enumerate([*range(rows), *range(tiles - rows, tiles)]):
+            part = total[c, pl.ds(start, COARSE_ROWS)]
+            edges[k][:, i * tile : (i + 1) * tile] = part.astype(edges[k].dtype)
+
+
+def terms_product(rows, sources, high_ref, low_ref, p_refs):
+    me = lax.axis_index("sub")
+    both = []
+    for ref in (high_ref, low_ref):
+        at = [lax.bitwise_xor(me, k) * rows + f for k in sources for f in range(rows)]
+        both.append(jnp.concatenate([ref[i] for i in at], axis=1))
+    stacked = jnp.concatenate([ref[i] for ref in p_refs for i in range(ref.shape[0])], axis=0)
+    out = jnp.dot(jnp.concatenate(both, axis=0), stacked, preferred_element_type=F32)
+    height = high_ref.shape[1]
+    return out[:height] + out[height:]
+
+
+def early_kernel(rows, sources, high_ref, low_ref, *rest):
+    rest[-1][...] = terms_product(rows, sources, high_ref, low_ref, rest[:-1])
+
+
+def late_kernel(subs, rows, sources, high_ref, low_ref, early_ref, *rest):
+    p_refs, rest = rest[: 2 * len(sources)], rest[2 * len(sources) :]
+    edges, outs, mid = rest[:subs], rest[subs:-1], rest[-1]
+    width = mid.shape[1]
+    mid[...] = early_ref[...] + terms_product(rows, sources, high_ref, low_ref, p_refs)
+    me = lax.axis_index("sub")
+    for k in range(subs):
+        start = pl.multiple_of(lax.bitwise_xor(me, k) * COARSE_ROWS, COARSE_ROWS)
+        outs[k][:, :width] = mid[pl.ds(start, COARSE_ROWS)].astype(outs[k].dtype)
+        outs[k][:, width:] = edges[k][...]
+
+
+def hand_out_pieces_kernel(subs, *refs):
+    p_refs, (near_ref, far_ref, ends) = refs[: 2 * subs], refs[2 * subs :]
+    rows, piece = near_ref.shape[0], p_refs[0].shape[0]
+    me, odd = lax.axis_index("sub"), lax.rem(lax.axis_index("dom"), 2)
+    for k in range(subs):
+        for at, who in ((0, 0), (rows, subs - 1)):
+
+            @pl.when(me == who ^ k)
+            def _():
+                for i in range(2):
+                    ends[at + i * piece : at + (i + 1) * piece] = p_refs[2 * k + i][...]
+
+    near_ref[...] = ends[pl.ds((1 - odd) * rows, rows)]
+    far_ref[...] = ends[pl.ds(odd * rows, rows)]
 
 
 def group_kernel(subs, half, cols_ref, count_ref, pair_ref, a_ref, edge_ref, *rest):
@@ -178,6 +251,61 @@
             out_ref[:, at : at + tile] = blocks[b].astype(BF16)
 
 
+def narrow_parts(a_tiles, a_cols, a_count, own, tiles, span):
+    rows, slots, tile = a_tiles.shape[:3]
+    subs = lax.axis_size("sub")
+    width = 2 * tile
+    smem = pl.BlockSpec(memory_space=pltpu.SMEM)
+    vmem = pl.BlockSpec(memory_space=pltpu.VMEM)
+    kinds = [F32] + [BF16] * (subs - 1)
+    spare = 3 << 20
+    products = 2 * width * rows * tile * width
+    *edges, high, low = pl.pallas_call(
+        functools.partial(terms_kernel, subs),
+        out_shape=[jax.ShapeDtypeStruct((COARSE_ROWS, span - width), kind) for kind in kinds]
+        + [jax.ShapeDtypeStruct((subs * rows, width, tile), BF16)] * 2,
+        in_specs=[smem, smem, pl.BlockSpec(memory_space=pltpu.HBM), vmem, vmem],
+        out_specs=[vmem] * (subs + 2),
+        scratch_shapes=[
+            pltpu.VMEM(a_tiles.shape, BF16),
+            pltpu.VMEM(((subs + 2) * rows + 1, width, tile), F32),
+            pltpu.VMEM((rows, width, tile), BF16),
+            pltpu.SemaphoreType.DMA((rows,)),
+        ],
+        compiler_params=pltpu.CompilerParams(
+            vmem_limit_bytes=2 * a_tiles.size + 4 * ((subs + 2) * rows + 1) * width * tile + spare
+        ),
+        cost_estimate=pl.CostEstimate(
+            flops=1 << 31, bytes_accessed=2 * a_tiles.size, transcendentals=0
+        ),
+        name="terms",
+    )(a_cols, a_count, pltpu.with_memory_space_constraint(a_tiles, pltpu.HBM), *own)
+    first, last = list(range(subs - 1)), [subs - 1]
+    early = pl.pallas_call(
+        functools.partial(early_kernel, rows, first),
+        out_shape=jax.ShapeDtypeStruct((width, width), F32),
+        in_specs=[vmem] * (2 + 2 * len(first)),
+        out_specs=vmem,
+        compiler_params=pltpu.CompilerParams(vmem_limit_bytes=spare),
+        cost_estimate=pl.CostEstimate(
+            flops=2 * len(first) * products, bytes_accessed=1 << 20, transcendentals=0
+        ),
+        name="early_part",
+    )(high, low, *[piece for k in first for piece in tiles[k]])
+    return pl.pallas_call(
+        functools.partial(late_kernel, subs, rows, last),
+        out_shape=[jax.ShapeDtypeStruct((COARSE_ROWS, span), kind) for kind in kinds],
+        in_specs=[vmem] * (3 + 2 * len(last) + subs),
+        out_specs=[vmem] * subs,
+        scratch_shapes=[pltpu.VMEM((width, width), F32)],
+        compiler_params=pltpu.CompilerParams(vmem_limit_bytes=spare),
+        cost_estimate=pl.CostEstimate(
+            flops=2 * products, bytes_accessed=1 << 20, transcendentals=0
+        ),
+        name="late_part",
+    )(high, low, early, *tiles[-1], *edges)
+
+
 def local(a_tiles, a_cols, a_count, p_tiles, p_cols):
     rows, slots, tile = a_tiles.shape[:3]
     subs, doms = lax.axis_size("sub"), lax.axis_size("dom")
@@ -215,6 +343,12 @@
         pltpu.with_memory_space_constraint(p_tiles, pltpu.HBM),
     )
 
+    tiles = [list(own)] + [[None, None] for _ in range(subs - 1)]
+    for k in range(1, subs):
+        low, high = k & -k, 1 << (k.bit_length() - 1)
+        tiles[k][0] = exchange(tiles[k ^ low][0], low)
+        tiles[k][1] = exchange(tiles[k ^ high][1], high)
+    span = width + 2 * rows * tile
     if half == 1:
         pair = jnp.zeros((1,), jnp.int32)
     else:
@@ -226,62 +360,69 @@
         m_right = lax.ppermute(m_group[:rows], "dom", [(d + 1, d) for d in range(doms - 1)])
         pair = jnp.concatenate([m_left, m_group, m_right])
 
-    flops = 2 * rows * slots * tile * tile * 2 * tile * half
-    edges, a_held = pl.pallas_call(
-        functools.partial(edge_kernel, subs, half),
-        out_shape=[
-            jax.ShapeDtypeStruct((2 * rows, width, tile), F32),
-            jax.ShapeDtypeStruct(a_tiles.shape, BF16),
-        ],
-        in_specs=[smem, smem, smem, pl.BlockSpec(memory_space=pltpu.HBM), vmem, vmem],
-        out_specs=[vmem] * 2,
-        scratch_shapes=[
-            pltpu.VMEM((rows, 2 * tile, tile), BF16),
-            pltpu.SemaphoreType.DMA((rows,)),
-        ],
-        compiler_params=pltpu.CompilerParams(vmem_limit_bytes=8 * rows * tile * width + spare),
-        cost_estimate=pl.CostEstimate(
-            flops=flops, bytes_accessed=a_bytes + p_bytes, transcendentals=0
-        ),
-        name="edge_part",
-    )(a_cols, a_count, pair, pltpu.with_memory_space_constraint(a_tiles, pltpu.HBM), *own)
-
-    tiles = [list(own)] + [[None, None] for _ in range(subs - 1)]
-    for k in range(1, subs):
-        low, high = k & -k, 1 << (k.bit_length() - 1)
-        tiles[k][0] = exchange(tiles[k ^ low][0], low)
-        tiles[k][1] = exchange(tiles[k ^ high][1], high)
-    span = width + 2 * rows * tile
-    *parts, pool = pl.pallas_call(
-        functools.partial(group_kernel, subs, half),
-        out_shape=[
-            jax.ShapeDtypeStruct((COARSE_ROWS, span), F32 if k == 0 else BF16)
-            for k in range(subs)
-        ]
-        + [jax.ShapeDtypeStruct((group_tiles + 1, tile, 2 * tile), BF16)],
-        in_specs=[smem, smem, smem] + [vmem] * (2 * subs + 2),
-        out_specs=[vmem] * (subs + 1),
-        scratch_shapes=[
-            pltpu.VMEM((rows * tile, width), BF16),
-            pltpu.VMEM((width, width), F32),
-        ],
-        compiler_params=pltpu.CompilerParams(
-            vmem_limit_bytes=2 * rows * tile * width + 4 * width * width + spare
-        ),
-        cost_estimate=pl.CostEstimate(
-            flops=flops, bytes_accessed=a_bytes + subs * p_bytes, transcendentals=0
-        ),
-        name="group_part",
-    )(a_cols, a_count, pair, a_held, edges, *sum(tiles, []))
+    flat = [piece for pieces in tiles for piece in pieces]
+    if half == 1:
+        parts = narrow_parts(a_tiles, a_cols, a_count, own, tiles, span)
+        to_near, to_far = pl.pallas_call(
+            functools.partial(hand_out_pieces_kernel, subs),
+            out_shape=[jax.ShapeDtypeStruct(p_tiles.shape, BF16)] * 2,
+            in_specs=[vmem] * (2 * subs),
+            out_specs=[vmem] * 2,
+            scratch_shapes=[pltpu.VMEM((2 * rows, tile, 2 * tile), BF16)],
+            compiler_params=pltpu.CompilerParams(vmem_limit_bytes=spare),
+            name="hand_out",
+        )(*flat)
+    else:
+        flops = 2 * rows * slots * tile * tile * 2 * tile * half
+        edges, a_held = pl.pallas_call(
+            functools.partial(edge_kernel, subs, half),
+            out_shape=[
+                jax.ShapeDtypeStruct((2 * rows, width, tile), F32),
+                jax.ShapeDtypeStruct(a_tiles.shape, BF16),
+            ],
+            in_specs=[smem, smem, smem, pl.BlockSpec(memory_space=pltpu.HBM), vmem, vmem],
+            out_specs=[vmem] * 2,
+            scratch_shapes=[
+                pltpu.VMEM((rows, 2 * tile, tile), BF16),
+                pltpu.SemaphoreType.DMA((rows,)),
+            ],
+            compiler_params=pltpu.CompilerParams(vmem_limit_bytes=8 * rows * tile * width + spare),
+            cost_estimate=pl.CostEstimate(
+                flops=flops, bytes_accessed=a_bytes + p_bytes, transcendentals=0
+            ),
+            name="edge_part",
+        )(a_cols, a_count, pair, pltpu.with_memory_space_constraint(a_tiles, pltpu.HBM), *own)
+
+        *parts, pool = pl.pallas_call(
+            functools.partial(group_kernel, subs, half),
+            out_shape=[
+                jax.ShapeDtypeStruct((COARSE_ROWS, span), F32 if k == 0 else BF16)
+                for k in range(subs)
+            ]
+            + [jax.ShapeDtypeStruct((group_tiles + 1, tile, 2 * tile), BF16)],
+            in_specs=[smem, smem, smem] + [vmem] * (2 * subs + 2),
+            out_specs=[vmem] * (subs + 1),
+            scratch_shapes=[
+                pltpu.VMEM((rows * tile, width), BF16),
+                pltpu.VMEM((width, width), F32),
+            ],
+            compiler_params=pltpu.CompilerParams(
+                vmem_limit_bytes=2 * rows * tile * width + 4 * width * width + spare
+            ),
+            cost_estimate=pl.CostEstimate(
+                flops=flops, bytes_accessed=a_bytes + subs * p_bytes, transcendentals=0
+            ),
+            name="group_part",
+        )(a_cols, a_count, pair, a_held, edges, *flat)
+        to_near, to_far = pl.pallas_call(
+            functools.partial(hand_out_kernel, subs),
+            out_shape=[jax.ShapeDtypeStruct(p_tiles.shape, BF16)] * 2,
+            in_specs=[vmem],
+            out_specs=[vmem] * 2,
+            compiler_params=pltpu.CompilerParams(vmem_limit_bytes=spare),
+            name="hand_out",
+        )(pool)
     received = [exchange(parts[k], k) for k in range(1, subs)]
-    to_near, to_far = pl.pallas_call(
-        functools.partial(hand_out_kernel, subs),
-        out_shape=[jax.ShapeDtypeStruct(p_tiles.shape, BF16)] * 2,
-        in_specs=[vmem],
-        out_specs=[vmem] * 2,
-        compiler_params=pltpu.CompilerParams(vmem_limit_bytes=spare),
-        name="hand_out",
-    )(pool)
     far = lax.ppermute(
         to_far, "dom", [(d, d - 1 + 2 * (d % 2)) for d in range(1, doms - 1)]
     )

time: 28.8 us -> 28.1 us (0.976)
  waiting for transfers between devices: 6.36 us -> 5.75 us
  Pallas kernels: 6.75 us -> 6.27 us
  starting transfers between devices: 15.5 us -> 15.8 us
    ppermute x9, waiting for transfers between devices: 2.54 us -> 1.93 us  [exchange(): return lax.ppermute(value, 'sub', [(s, s ^ k) for s in range(subs)])]
    pallas_call x3 -> x4, Pallas kernels: 4.7 us -> 4.22 us  [the longest x1 3.24 us: narrow_parts(): pl.pallas_call(functools.partial(terms_kernel, subs), out_shape=[jax.Shap...]
    ppermute x1, starting transfers between devices: 6.63 us -> 6.94 us  [local(): lax.ppermute(to_far, 'dom', [(d, d - 1 + 2 * (d % 2)) for d in range(1, d...]
  transfers between devices with their start and end apart: 11 -> 11, of which waited for: 3 -> 3; matrix products, arithmetic and copies ran while one was open for 0% -> 0% of each run, Pallas kernels for 12% -> 14%
where the time goes in v7:
time: 28.1 us; the launch traced here: 27.9 us
  starting transfers between devices  15.8 us (56%)
  Pallas kernels  6.27 us (22%)
  waiting for transfers between devices  5.75 us (20%)
    ppermute x9, starting transfers between devices, exchange(): return lax.ppermute(value, 'sub', [(s, s ^ k) for s in range(subs)])  8.74 us
    ppermute x1, starting transfers between devices, local(): lax.ppermute(to_far, 'dom', [(d, d - 1 + 2 * (d % 2)) for d in range(1, d...  6.94 us
    ppermute x1, waiting for transfers between devices, local(): lax.ppermute(to_far, 'dom', [(d, d - 1 + 2 * (d % 2)) for d in range(1, d...  3.82 us
    pallas_call x1, Pallas kernels, narrow_parts(): pl.pallas_call(functools.partial(terms_kernel, subs), out_shape=[jax.Shap...  3.24 us
    ppermute x9, waiting for transfers between devices, exchange(): return lax.ppermute(value, 'sub', [(s, s ^ k) for s in range(subs)])  1.93 us
    pallas_call x1, Pallas kernels, local(): pl.pallas_call(order_kernel, out_shape=[jax.ShapeDtypeStruct((rows // 2,...  1.02 us
    pallas_call x1, Pallas kernels, local(): pl.pallas_call(functools.partial(finish_kernel, subs, half), out_shape=ja...  0.93 us
    pallas_call x1, Pallas kernels, narrow_parts(): pl.pallas_call(functools.partial(early_kernel, rows, first), out_shape=ja...  0.57 us
  transfers between devices with their start and end apart: 11, of which 3 were waited for; matrix products, arithmetic and copies ran while one was open for 0% of the time, Pallas kernels for 14%

profile of v7, /device:TPU:1, one launch (start us, length us, event | category | flops | bytes accessed | tf_op | source)
XLA Modules:
  0.0 27.9 jit_solution(855780304444572517)
XLA Ops:
  0.0 0.0 copy-start
  0.0 1.0 %order_columns.1 = (bf16[2,128,256]{2,1,0:T(8,128)(2,1)S(1)}, bf16[2,128,256]{2,1,0:T(8,128)(2,1)S(1)}) custom-call(s32[2,4]{1,0:T(2,128)} %bitcast.1, bf16[4,128,256]{2,1,0:T(8,128)(2,1)} %p_hbm.1), custom_call_target="tpu_custom_call" | custom-call | flops 1073741824 | bytes 524288 | tf_op jit(solution)/shard_map/order_columns/pallas_call | solution.py:326
  1.0 2.1 %collective-permute-start.2 = (bf16[2,128,256]{2,1,0:T(8,128)(2,1)S(1)}, bf16[2,128,256]{2,1,0:T(8,128)(2,1)S(1)}, u32[]{:S(2)}, u32[]{:S(2)}) collective-permute-start(bf16[2,128,256]{2,1,0:T(8,128)(2,1)S(1)} %get-tuple-element.21.refs_0_.own_0.rest_0_), channel_id=1, source_target_pairs={{0,2},{1,3},{2,0},{3,1},{4,6},{5,7},{6,4},{7,5},{8,10},{9,11},{10,... | collective-permute-start | bytes 393224 | tf_op jit(solution)/shard_map/ppermute | solution.py:324
  3.2 1.2 %collective-permute-start.1 = (bf16[2,128,256]{2,1,0:T(8,128)(2,1)S(1)}, bf16[2,128,256]{2,1,0:T(8,128)(2,1)S(1)}, u32[]{:S(2)}, u32[]{:S(2)}) collective-permute-start(bf16[2,128,256]{2,1,0:T(8,128)(2,1)S(1)} %get-tuple-element.22.refs_1_.own_1.rest_1_), channel_id=1, source_target_pairs={{0,1},{1,0},{2,3},{3,2},{4,5},{5,4},{6,7},{7,6},{8,9},{9,8},{10,11... | collective-permute-start | bytes 393224 | tf_op jit(solution)/shard_map/ppermute | solution.py:324
  4.4 0.3 collective-permute-start
  4.6 0.1 collective-permute-start.3
  4.7 1.7 %collective-permute-done.2.refs_4_.rest_4_ = bf16[2,128,256]{2,1,0:T(8,128)(2,1)S(1)} collective-permute-done((bf16[2,128,256]{2,1,0:T(8,128)(2,1)S(1)}, bf16[2,128,256]{2,1,0:T(8,128)(2,1)S(1)}, u32[]{:S(2)}, u32[]{:S(2)}) %collective-permute-start.2) | collective-permute-done | bytes 131104 | tf_op jit(solution)/shard_map/ppermute | solution.py:324
  6.4 1.1 %collective-permute-start.4 = (bf16[2,128,256]{2,1,0:T(8,128)(2,1)S(1)}, bf16[2,128,256]{2,1,0:T(8,128)(2,1)S(1)}, u32[]{:S(2)}, u32[]{:S(2)}) collective-permute-start(bf16[2,128,256]{2,1,0:T(8,128)(2,1)S(1)} %collective-permute-done.2.refs_4_.rest_4_), channel_id=1, source_target_pairs={{0,1},{1,0},{2,3},{3,2},{4,5},{5,4},{6,7},{7,6},{8,9},{9,8},{10,11... | collective-permute-start | bytes 393224 | tf_op jit(solution)/shard_map/ppermute | solution.py:324
  7.5 0.0 collective-permute-done.1.refs_3_.rest_3_
  7.5 1.2 %collective-permute-start.5 = (bf16[2,128,256]{2,1,0:T(8,128)(2,1)S(1)}, bf16[2,128,256]{2,1,0:T(8,128)(2,1)S(1)}, u32[]{:S(2)}, u32[]{:S(2)}) collective-permute-start(bf16[2,128,256]{2,1,0:T(8,128)(2,1)S(1)} %collective-permute-done.1.refs_3_.rest_3_), channel_id=1, source_target_pairs={{0,2},{1,3},{2,0},{3,1},{4,6},{5,7},{6,4},{7,5},{8,10},{9,11},{10,... | collective-permute-start | bytes 393224 | tf_op jit(solution)/shard_map/ppermute | solution.py:324
  8.7 0.0 copy-done
  8.7 0.0 copy-done.1
  8.7 3.2 %terms.1 = (f32[64,1024]{1,0:T(8,128)S(1)}, bf16[64,1024]{1,0:T(8,128)(2,1)S(1)}, bf16[64,1024]{1,0:T(8,128)(2,1)S(1)}, bf16[64,1024]{1,0:T(8,128)(2,1)S(1)}, bf...) custom-call(s32[4,10]{1,0:T(4,128)S(1)} %copy-done, s32[4]{0:T(128)S(1)} %copy-done.1, ...), custom_call_target="tpu_custom_call" | custom-call | flops 2147483648 | bytes 1310720 | tf_op jit(solution)/shard_map/terms/pallas_call | solution.py:263
  12.0 0.0 collective-permute-done.refs_2_.rest_2_
  12.0 0.0 collective-permute-done.3.refs_5_.rest_5_
  12.0 0.6 %early_part.1.early_ref = f32[256,256]{1,0:T(8,128)S(1)} custom-call(bf16[16,256,128]{2,1,0:T(8,128)(2,1)S(1)} %get-tuple-element.25.high_ref, bf16[16,256,128]{2,1,0:T(8,128)(2,1)S(1)} %get-tuple-element.26.low_ref, bf16[2,128,256]{2,1,0:T(8,128)(2,1)S(1)} %get-tuple-element.21.refs_0_.own_0.rest_0_, ...), custom_call_target="tpu_custom_call" | custom-call | flops 402653184 | bytes 1048576 | tf_op jit(solution)/shard_map/early_part/pallas_call | solution.py:284
  12.6 0.2 collective-permute-done.4.refs_6_.rest_0_
  12.8 0.0 collective-permute-done.5.refs_7_.rest_1_
  12.8 0.3 %late_part.1 = (f32[64,1280]{1,0:T(8,128)S(1)}, bf16[64,1280]{1,0:T(8,128)(2,1)S(1)}, bf16[64,1280]{1,0:T(8,128)(2,1)S(1)}, bf16[64,1280]{1,0:T(8,128)(2,1)S(1)}) custom-call(bf16[16,256,128]{2,1,0:T(8,128)(2,1)S(1)} %get-tuple-element.25.high_ref, bf16[16,256,128]{2,1,0:T(8,128)(2,1)S(1)} %get-tuple-element.26.low_ref, f32[256,256]{1,0:T(8,128)S(1)} %early_part.1.early_ref, ...), custom_call_target="tpu_custom_call" | custom-call | flops 134217728 | bytes 1048576 | tf_op jit(solution)/shard_map/late_part/pallas_call | solution.py:295
  13.2 1.3 %collective-permute-start.8 = (bf16[64,1280]{1,0:T(8,128)(2,1)S(1)}, bf16[64,1280]{1,0:T(8,128)(2,1)S(1)}, u32[]{:S(2)}, u32[]{:S(2)}) collective-permute-start(bf16[64,1280]{1,0:T(8,128)(2,1)S(1)} %get-tuple-element.32), channel_id=1, source_target_pairs={{0,1},{1,0},{2,3},{3,2},{4,5},{5,4},{6,7},{7,6},{8,9},{9,8},{10,11... | collective-permute-start | bytes 491528 | tf_op jit(solution)/shard_map/ppermute | solution.py:324
  14.4 0.2 collective-permute-start.9
  14.7 1.2 %collective-permute-start.10 = (bf16[64,1280]{1,0:T(8,128)(2,1)S(1)}, bf16[64,1280]{1,0:T(8,128)(2,1)S(1)}, u32[]{:S(2)}, u32[]{:S(2)}) collective-permute-start(bf16[64,1280]{1,0:T(8,128)(2,1)S(1)} %get-tuple-element.34), channel_id=1, source_target_pairs={{0,3},{1,2},{2,1},{3,0},{4,7},{5,6},{6,5},{7,4},{8,11},{9,10},{10,... | collective-permute-start | bytes 491528 | tf_op jit(solution)/shard_map/ppermute | solution.py:324
  15.9 0.1 hand_out.1
  16.0 6.9 %collective-permute-start.6 = (bf16[4,128,256]{2,1,0:T(8,128)(2,1)S(1)}, bf16[4,128,256]{2,1,0:T(8,128)(2,1)S(1)}, u32[]{:S(2)}, u32[]{:S(2)}) collective-permute-start(bf16[4,128,256]{2,1,0:T(8,128)(2,1)S(1)} %get-tuple-element.23), channel_id=1, source_target_pairs={{4,8},{8,4},{12,16},{16,12},{20,24},{24,20},{5,9},{9,5},{13,17},{1... | collective-permute-start | bytes 786440 | tf_op jit(solution)/shard_map/ppermute | solution.py:426
  22.9 0.1 collective-permute-start.7
  23.0 0.0 collective-permute-done.8.refs_1_
  23.0 0.0 collective-permute-done.9.refs_2_
  23.0 0.0 collective-permute-done.10.refs_3_
  23.0 0.1 sum_parts.1
  23.1 3.8 %collective-permute-done.6.far_ref = bf16[4,128,256]{2,1,0:T(8,128)(2,1)S(1)} collective-permute-done((bf16[4,128,256]{2,1,0:T(8,128)(2,1)S(1)}, bf16[4,128,256]{2,1,0:T(8,128)(2,1)S(1)}, u32[]{:S(2)}, u32[]{:S(2)}) %collective-permute-start.6) | collective-permute-done | bytes 262176 | tf_op jit(solution)/shard_map/ppermute | solution.py:426
  27.0 0.0 collective-permute-done.7.near_ref
  27.0 0.9 %finish.1 = bf16[64,768]{1,0:T(8,128)(2,1)} custom-call(s32[1]{0:T(128)} %constant.0.clone.1.pair_ref, bf16[4,128,256]{2,1,0:T(8,128)(2,1)S(1)} %collective-permute-done.6.far_ref, bf16[4,128,256]{2,1,0:T(8,128)(2,1)S(1)} %collective-permute-done.7.near_ref, bf16[64,256]{1,0:T(8,128)(2,1)S(1)} %get-tuple-element.35.mid_ref, ...), custom_call_target="tpu_custom_call" | custom-call | flops 268435456 | bytes 1048576 | tf_op jit(solution)/shard_map/finish/pallas_call | solution.py:444
  (1 shorter events, 0.0 us)
Async XLA Ops:
  0.0 8.7 %copy-start = (s32[4,10]{1,0:T(4,128)S(1)}, s32[4,10]{1,0:T(4,128)}, u32[]{:S(2)}) copy-start(s32[4,10]{1,0:T(4,128)} %cols_ref.1) | copy-start | bytes 484
  0.0 8.7 %copy-start.1 = (s32[4]{0:T(128)S(1)}, s32[4]{0:T(128)}, u32[]{:S(2)}) copy-start(s32[4]{0:T(128)} %count_ref.1) | copy-start | bytes 52
  1.0 5.4 %collective-permute-start.2 = (bf16[2,128,256]{2,1,0:T(8,128)(2,1)S(1)}, bf16[2,128,256]{2,1,0:T(8,128)(2,1)S(1)}, u32[]{:S(2)}, u32[]{:S(2)}) collective-permute-start(bf16[2,128,256]{2,1,0:T(8,128)(2,1)S(1)} %get-tuple-element.21.refs_0_.own_0.rest_0_), channel_id=1, source_target_pairs={{0,2},{1,3},{2,0},{3,1},{4,6},{5,7},{6,4},{7,5},{8,10},{9,11},{10,... | collective-permute-start | bytes 393224 | tf_op jit(solution)/shard_map/ppermute | solution.py:324
  3.2 4.3 %collective-permute-start.1 = (bf16[2,128,256]{2,1,0:T(8,128)(2,1)S(1)}, bf16[2,128,256]{2,1,0:T(8,128)(2,1)S(1)}, u32[]{:S(2)}, u32[]{:S(2)}) collective-permute-start(bf16[2,128,256]{2,1,0:T(8,128)(2,1)S(1)} %get-tuple-element.22.refs_1_.own_1.rest_1_), channel_id=1, source_target_pairs={{0,1},{1,0},{2,3},{3,2},{4,5},{5,4},{6,7},{7,6},{8,9},{9,8},{10,11... | collective-permute-start | bytes 393224 | tf_op jit(solution)/shard_map/ppermute | solution.py:324
  4.4 7.6 %collective-permute-start = (bf16[2,128,256]{2,1,0:T(8,128)(2,1)S(1)}, bf16[2,128,256]{2,1,0:T(8,128)(2,1)S(1)}, u32[]{:S(2)}, u32[]{:S(2)}) collective-permute-start(bf16[2,128,256]{2,1,0:T(8,128)(2,1)S(1)} %get-tuple-element.21.refs_0_.own_0.rest_0_), channel_id=1, source_target_pairs={{0,1},{1,0},{2,3},{3,2},{4,5},{5,4},{6,7},{7,6},{8,9},{9,8},{10,11... | collective-permute-start | bytes 393224 | tf_op jit(solution)/shard_map/ppermute | solution.py:324
  4.6 7.4 %collective-permute-start.3 = (bf16[2,128,256]{2,1,0:T(8,128)(2,1)S(1)}, bf16[2,128,256]{2,1,0:T(8,128)(2,1)S(1)}, u32[]{:S(2)}, u32[]{:S(2)}) collective-permute-start(bf16[2,128,256]{2,1,0:T(8,128)(2,1)S(1)} %get-tuple-element.22.refs_1_.own_1.rest_1_), channel_id=1, source_target_pairs={{0,2},{1,3},{2,0},{3,1},{4,6},{5,7},{6,4},{7,5},{8,10},{9,11},{10,... | collective-permute-start | bytes 393224 | tf_op jit(solution)/shard_map/ppermute | solution.py:324
  6.4 6.4 %collective-permute-start.4 = (bf16[2,128,256]{2,1,0:T(8,128)(2,1)S(1)}, bf16[2,128,256]{2,1,0:T(8,128)(2,1)S(1)}, u32[]{:S(2)}, u32[]{:S(2)}) collective-permute-start(bf16[2,128,256]{2,1,0:T(8,128)(2,1)S(1)} %collective-permute-done.2.refs_4_.rest_4_), channel_id=1, source_target_pairs={{0,1},{1,0},{2,3},{3,2},{4,5},{5,4},{6,7},{7,6},{8,9},{9,8},{10,11... | collective-permute-start | bytes 393224 | tf_op jit(solution)/shard_map/ppermute | solution.py:324
  7.5 5.3 %collective-permute-start.5 = (bf16[2,128,256]{2,1,0:T(8,128)(2,1)S(1)}, bf16[2,128,256]{2,1,0:T(8,128)(2,1)S(1)}, u32[]{:S(2)}, u32[]{:S(2)}) collective-permute-start(bf16[2,128,256]{2,1,0:T(8,128)(2,1)S(1)} %collective-permute-done.1.refs_3_.rest_3_), channel_id=1, source_target_pairs={{0,2},{1,3},{2,0},{3,1},{4,6},{5,7},{6,4},{7,5},{8,10},{9,11},{10,... | collective-permute-start | bytes 393224 | tf_op jit(solution)/shard_map/ppermute | solution.py:324
  13.2 9.8 %collective-permute-start.8 = (bf16[64,1280]{1,0:T(8,128)(2,1)S(1)}, bf16[64,1280]{1,0:T(8,128)(2,1)S(1)}, u32[]{:S(2)}, u32[]{:S(2)}) collective-permute-start(bf16[64,1280]{1,0:T(8,128)(2,1)S(1)} %get-tuple-element.32), channel_id=1, source_target_pairs={{0,1},{1,0},{2,3},{3,2},{4,5},{5,4},{6,7},{7,6},{8,9},{9,8},{10,11... | collective-permute-start | bytes 491528 | tf_op jit(solution)/shard_map/ppermute | solution.py:324
  14.4 8.6 %collective-permute-start.9 = (bf16[64,1280]{1,0:T(8,128)(2,1)S(1)}, bf16[64,1280]{1,0:T(8,128)(2,1)S(1)}, u32[]{:S(2)}, u32[]{:S(2)}) collective-permute-start(bf16[64,1280]{1,0:T(8,128)(2,1)S(1)} %get-tuple-element.33), channel_id=1, source_target_pairs={{0,2},{1,3},{2,0},{3,1},{4,6},{5,7},{6,4},{7,5},{8,10},{9,11},{10,... | collective-permute-start | bytes 491528 | tf_op jit(solution)/shard_map/ppermute | solution.py:324
  14.7 8.3 %collective-permute-start.10 = (bf16[64,1280]{1,0:T(8,128)(2,1)S(1)}, bf16[64,1280]{1,0:T(8,128)(2,1)S(1)}, u32[]{:S(2)}, u32[]{:S(2)}) collective-permute-start(bf16[64,1280]{1,0:T(8,128)(2,1)S(1)} %get-tuple-element.34), channel_id=1, source_target_pairs={{0,3},{1,2},{2,1},{3,0},{4,7},{5,6},{6,5},{7,4},{8,11},{9,10},{10,... | collective-permute-start | bytes 491528 | tf_op jit(solution)/shard_map/ppermute | solution.py:324
  16.0 11.0 %collective-permute-start.6 = (bf16[4,128,256]{2,1,0:T(8,128)(2,1)S(1)}, bf16[4,128,256]{2,1,0:T(8,128)(2,1)S(1)}, u32[]{:S(2)}, u32[]{:S(2)}) collective-permute-start(bf16[4,128,256]{2,1,0:T(8,128)(2,1)S(1)} %get-tuple-element.23), channel_id=1, source_target_pairs={{4,8},{8,4},{12,16},{16,12},{20,24},{24,20},{5,9},{9,5},{13,17},{1... | collective-permute-start | bytes 786440 | tf_op jit(solution)/shard_map/ppermute | solution.py:426
  22.9 4.0 %collective-permute-start.7 = (bf16[4,128,256]{2,1,0:T(8,128)(2,1)S(1)}, bf16[4,128,256]{2,1,0:T(8,128)(2,1)S(1)}, u32[]{:S(2)}, u32[]{:S(2)}) collective-permute-start(bf16[4,128,256]{2,1,0:T(8,128)(2,1)S(1)} %get-tuple-element.24), channel_id=1, source_target_pairs={{0,4},{4,0},{8,12},{12,8},{16,20},{20,16},{24,28},{28,24},{1,5},{5... | collective-permute-start | bytes 786440 | tf_op jit(solution)/shard_map/ppermute | solution.py:429

commit v8 on v7

--- a/solution.py
+++ b/solution.py
@@ -207,48 +207,61 @@
             outs[k][:, width + c * tile : width + (c + 1) * tile] = edge_ref[c, at].astype(kind)
 
 
-def sum_kernel(subs, width, *refs):
-    part_refs, (mid_ref, edge_ref) = refs[:subs], refs[subs:]
-    total = part_refs[0][...]
-    for k in range(1, subs):
-        total = total + part_refs[k][...].astype(F32)
+def halo_product(subs, half, side, pair_ref, terms, p_ref):
+    rows, tile = p_ref.shape[:2]
+    if half == 1:
+        stacked = jnp.concatenate([p_ref[t] for t in range(rows)], axis=0)
+        out = jnp.dot(terms, stacked, preferred_element_type=F32)
+        out = out[:COARSE_ROWS] + out[COARSE_ROWS:]
+        return [out[:, :tile], out[:, tile:]]
+    blocks = [jnp.zeros((COARSE_ROWS, tile), F32) for _ in range(2 * half)]
+    for t in range(rows):
+        lhs = terms[:, t * tile : (t + 1) * tile]
+        out = jnp.dot(lhs, p_ref[t], preferred_element_type=F32)
+        out = out[:COARSE_ROWS] + out[COARSE_ROWS:]
+        m_here = pair_ref[side * (subs + 1) * rows + t]
+        for m in range(half):
+            blocks[m] = blocks[m] + jnp.where(m_here == m, out[:, :tile], 0.0)
+            blocks[m + half] = blocks[m + half] + jnp.where(m_here == m, out[:, tile:], 0.0)
+    return blocks
+
+
+def sum_kernel(*refs):
+    total = refs[0][...]
+    for ref in refs[1:-1]:
+        total = total + ref[...].astype(F32)
+    refs[-1][...] = total
+
+
+def near_kernel(subs, half, pair_ref, near_ref, sum_ref, last_ref, *rest):
+    mid_ref, side_ref, terms_ref, total = rest
+    rows, tile = near_ref.shape[:2]
+    width, span = 2 * half * tile, rows * tile
+    odd = lax.rem(lax.axis_index("dom"), 2)
+    total[...] = sum_ref[...] + last_ref[...].astype(F32)
     mid_ref[...] = total[:, :width].astype(BF16)
-    sums = total[:, width:]
-    high = sums.astype(BF16)
-    edge_ref[:COARSE_ROWS] = high
-    edge_ref[COARSE_ROWS:] = (sums - high.astype(F32)).astype(BF16)
-
-
-def finish_kernel(subs, half, pair_ref, far_ref, near_ref, mid_ref, both_ref, out_ref, edge):
-    rows, tile = near_ref.shape[:2]
+
+    def terms(side):
+        value = total[:, pl.ds(pl.multiple_of(width + side * span, tile), span)]
+        high = value.astype(BF16)
+        return jnp.concatenate([high, (value - high.astype(F32)).astype(BF16)], axis=0)
+
+    terms_ref[...] = terms(odd)
+    blocks = halo_product(subs, half, 1 - odd, pair_ref, terms(1 - odd), near_ref)
+    for b in range(2 * half):
+        side_ref[:, b * tile : (b + 1) * tile] = blocks[b].astype(BF16)
+
+
+def finish_kernel(subs, half, pair_ref, far_ref, terms_ref, mid_ref, side_ref, out_ref):
+    tile = far_ref.shape[1]
     width = 2 * half * tile
     odd = lax.rem(lax.axis_index("dom"), 2)
-    edge[pl.ds((1 - odd) * rows, rows)] = near_ref[...]
-    edge[pl.ds(odd * rows, rows)] = far_ref[...]
     out_ref[:, width : 2 * width] = mid_ref[...]
-    both = both_ref[...]
-    for side in range(2):
-        blocks = [jnp.zeros((COARSE_ROWS, tile), F32) for _ in range(2 * half)]
-        tiles = range(side * rows, (side + 1) * rows)
-        if half == 1:
-            stacked = jnp.concatenate([edge[c] for c in tiles], axis=0)
-            lhs = both[:, side * rows * tile : (side + 1) * rows * tile]
-            term = jnp.dot(lhs, stacked, preferred_element_type=F32)
-            term = term[:COARSE_ROWS] + term[COARSE_ROWS:]
-            blocks = [term[:, :tile], term[:, tile:]]
-        else:
-            for c in tiles:
-                lhs = both[:, c * tile : (c + 1) * tile]
-                term = jnp.dot(lhs, edge[c], preferred_element_type=F32)
-                term = term[:COARSE_ROWS] + term[COARSE_ROWS:]
-                m_here = pair_ref[c if side == 0 else subs * rows + c]
-                for m in range(half):
-                    here = m_here == m
-                    blocks[m] = blocks[m] + jnp.where(here, term[:, :tile], 0.0)
-                    blocks[m + half] = blocks[m + half] + jnp.where(here, term[:, tile:], 0.0)
-        for b in range(2 * half):
-            at = 2 * side * width + b * tile
-            out_ref[:, at : at + tile] = blocks[b].astype(BF16)
+    out_ref[:, pl.ds(pl.multiple_of((1 - odd) * 2 * width, tile), width)] = side_ref[...]
+    blocks = halo_product(subs, half, odd, pair_ref, terms_ref[...], far_ref)
+    for b in range(2 * half):
+        at = pl.multiple_of(odd * 2 * width + b * tile, tile)
+        out_ref[:, pl.ds(at, tile)] = blocks[b].astype(BF16)
 
 
 def narrow_parts(a_tiles, a_cols, a_count, own, tiles, span):
@@ -422,37 +435,43 @@
             compiler_params=pltpu.CompilerParams(vmem_limit_bytes=spare),
             name="hand_out",
         )(pool)
-    received = [exchange(parts[k], k) for k in range(1, subs)]
+    received = [exchange(parts[k], k) for k in [*range(subs - 1, subs // 2, -1), *range(1, subs // 2), subs // 2]]
     far = lax.ppermute(
         to_far, "dom", [(d, d - 1 + 2 * (d % 2)) for d in range(1, doms - 1)]
     )
     near = lax.ppermute(to_near, "dom", [(d, d ^ 1) for d in range(doms)])
-    mid, both = pl.pallas_call(
-        functools.partial(sum_kernel, subs, width),
+    sums = pl.pallas_call(
+        sum_kernel,
+        out_shape=jax.ShapeDtypeStruct((COARSE_ROWS, span), F32),
+        in_specs=[vmem] * (subs - 1),
+        out_specs=vmem,
+        compiler_params=pltpu.CompilerParams(vmem_limit_bytes=spare),
+        cost_estimate=pl.CostEstimate(flops=3 << 29, bytes_accessed=1 << 20, transcendentals=0),
+        name="sum_parts",
+    )(parts[0], *received[:-1])
+    mid, side, terms = pl.pallas_call(
+        functools.partial(near_kernel, subs, half),
         out_shape=[
             jax.ShapeDtypeStruct((COARSE_ROWS, width), BF16),
-            jax.ShapeDtypeStruct((2 * COARSE_ROWS, span - width), BF16),
+            jax.ShapeDtypeStruct((COARSE_ROWS, width), BF16),
+            jax.ShapeDtypeStruct((2 * COARSE_ROWS, rows * tile), BF16),
         ],
-        in_specs=[vmem] * subs,
-        out_specs=[vmem] * 2,
-        compiler_params=pltpu.CompilerParams(vmem_limit_bytes=spare),
-        cost_estimate=pl.CostEstimate(
-            flops=1 << 31, bytes_accessed=8 * COARSE_ROWS * span, transcendentals=0
-        ),
-        name="sum_parts",
-    )(parts[0], *received)
+        in_specs=[smem] + [vmem] * 3,
+        out_specs=[vmem] * 3,
+        scratch_shapes=[pltpu.VMEM((COARSE_ROWS, span), F32)],
+        compiler_params=pltpu.CompilerParams(vmem_limit_bytes=2 * p_bytes + spare),
+        cost_estimate=pl.CostEstimate(flops=1 << 20, bytes_accessed=1 << 20, transcendentals=0),
+        name="near_part",
+    )(pair, near, sums, received[-1])
     return pl.pallas_call(
         functools.partial(finish_kernel, subs, half),
         out_shape=jax.ShapeDtypeStruct((COARSE_ROWS, 3 * width), BF16),
         in_specs=[smem] + [vmem] * 4,
         out_specs=vmem,
-        scratch_shapes=[pltpu.VMEM((2 * rows, tile, 2 * tile), BF16)],
         compiler_params=pltpu.CompilerParams(vmem_limit_bytes=2 * p_bytes + spare),
-        cost_estimate=pl.CostEstimate(
-            flops=1 << 28, bytes_accessed=4 * p_bytes, transcendentals=0
-        ),
-        name="finish",
-    )(pair, far, near, mid, both)
+        cost_estimate=pl.CostEstimate(flops=1 << 20, bytes_accessed=1 << 20, transcendentals=0),
+        name="far_part",
+    )(pair, far, terms, mid, side)
 
 
 def solution(mesh):

time: 28.1 us -> 28.4 us (1.011)
  the two profiles are of different devices: /device:TPU:1 before, /device:TPU:9 now
where the time goes in v8:
time: 28.4 us; the launch traced here: 28.2 us
  starting transfers between devices  15 us (53%)
  waiting for transfers between devices  6.83 us (24%)
  Pallas kernels  6.37 us (22%)
    ppermute x9, starting transfers between devices, exchange(): return lax.ppermute(value, 'sub', [(s, s ^ k) for s in range(subs)])  7.63 us
    ppermute x9, waiting for transfers between devices, exchange(): return lax.ppermute(value, 'sub', [(s, s ^ k) for s in range(subs)])  6.82 us
    ppermute x1, starting transfers between devices, local(): near = lax.ppermute(to_near, 'dom', [(d, d ^ 1) for d in range(doms)])  4.21 us
    pallas_call x1, Pallas kernels, narrow_parts(): pl.pallas_call(functools.partial(terms_kernel, subs), out_shape=[jax.Shap...  3.24 us
    ppermute x1, starting transfers between devices, local(): lax.ppermute(to_far, 'dom', [(d, d - 1 + 2 * (d % 2)) for d in range(1, d...  3.11 us
    pallas_call x1, Pallas kernels, local(): pl.pallas_call(order_kernel, out_shape=[jax.ShapeDtypeStruct((rows // 2,...  1.02 us
    pallas_call x1, Pallas kernels, local(): pl.pallas_call(functools.partial(finish_kernel, subs, half), out_shape=ja...  0.83 us
    pallas_call x1, Pallas kernels, narrow_parts(): pl.pallas_call(functools.partial(early_kernel, rows, first), out_shape=ja...  0.57 us
  transfers between devices with their start and end apart: 11, of which 3 were waited for; matrix products, arithmetic and copies ran while one was open for 0% of the time, Pallas kernels for 15%

profile of v8, /device:TPU:9, one launch (start us, length us, event | category | flops | bytes accessed | tf_op | source)
XLA Modules:
  0.0 28.2 jit_solution(10442878797108518923)
XLA Ops:
  0.0 0.0 copy-start
  0.0 1.0 %order_columns.1 = (bf16[2,128,256]{2,1,0:T(8,128)(2,1)S(1)}, bf16[2,128,256]{2,1,0:T(8,128)(2,1)S(1)}) custom-call(s32[2,4]{1,0:T(2,128)} %bitcast.1, bf16[4,128,256]{2,1,0:T(8,128)(2,1)} %p_hbm.1), custom_call_target="tpu_custom_call" | custom-call | flops 1073741824 | bytes 524288 | tf_op jit(solution)/shard_map/order_columns/pallas_call | solution.py:339
  1.0 1.3 %collective-permute-start.2 = (bf16[2,128,256]{2,1,0:T(8,128)(2,1)S(1)}, bf16[2,128,256]{2,1,0:T(8,128)(2,1)S(1)}, u32[]{:S(2)}, u32[]{:S(2)}) collective-permute-start(bf16[2,128,256]{2,1,0:T(8,128)(2,1)S(1)} %get-tuple-element.22.refs_0_.own_0.rest_0_), channel_id=1, source_target_pairs={{0,2},{1,3},{2,0},{3,1},{4,6},{5,7},{6,4},{7,5},{8,10},{9,11},{10,... | collective-permute-start | bytes 393224 | tf_op jit(solution)/shard_map/ppermute | solution.py:337
  2.3 1.2 %collective-permute-start.1 = (bf16[2,128,256]{2,1,0:T(8,128)(2,1)S(1)}, bf16[2,128,256]{2,1,0:T(8,128)(2,1)S(1)}, u32[]{:S(2)}, u32[]{:S(2)}) collective-permute-start(bf16[2,128,256]{2,1,0:T(8,128)(2,1)S(1)} %get-tuple-element.23.refs_1_.own_1.rest_1_), channel_id=1, source_target_pairs={{0,1},{1,0},{2,3},{3,2},{4,5},{5,4},{6,7},{7,6},{8,9},{9,8},{10,11... | collective-permute-start | bytes 393224 | tf_op jit(solution)/shard_map/ppermute | solution.py:337
  3.5 0.3 collective-permute-start
  3.8 0.2 collective-permute-start.3
  4.0 1.4 %collective-permute-done.2.refs_4_.rest_4_ = bf16[2,128,256]{2,1,0:T(8,128)(2,1)S(1)} collective-permute-done((bf16[2,128,256]{2,1,0:T(8,128)(2,1)S(1)}, bf16[2,128,256]{2,1,0:T(8,128)(2,1)S(1)}, u32[]{:S(2)}, u32[]{:S(2)}) %collective-permute-start.2) | collective-permute-done | bytes 131104 | tf_op jit(solution)/shard_map/ppermute | solution.py:337
  5.5 1.2 %collective-permute-start.4 = (bf16[2,128,256]{2,1,0:T(8,128)(2,1)S(1)}, bf16[2,128,256]{2,1,0:T(8,128)(2,1)S(1)}, u32[]{:S(2)}, u32[]{:S(2)}) collective-permute-start(bf16[2,128,256]{2,1,0:T(8,128)(2,1)S(1)} %collective-permute-done.2.refs_4_.rest_4_), channel_id=1, source_target_pairs={{0,1},{1,0},{2,3},{3,2},{4,5},{5,4},{6,7},{7,6},{8,9},{9,8},{10,11... | collective-permute-start | bytes 393224 | tf_op jit(solution)/shard_map/ppermute | solution.py:337
  6.7 0.0 collective-permute-done.1.refs_3_.rest_3_
  6.7 1.2 %collective-permute-start.5 = (bf16[2,128,256]{2,1,0:T(8,128)(2,1)S(1)}, bf16[2,128,256]{2,1,0:T(8,128)(2,1)S(1)}, u32[]{:S(2)}, u32[]{:S(2)}) collective-permute-start(bf16[2,128,256]{2,1,0:T(8,128)(2,1)S(1)} %collective-permute-done.1.refs_3_.rest_3_), channel_id=1, source_target_pairs={{0,2},{1,3},{2,0},{3,1},{4,6},{5,7},{6,4},{7,5},{8,10},{9,11},{10,... | collective-permute-start | bytes 393224 | tf_op jit(solution)/shard_map/ppermute | solution.py:337
  7.9 0.0 copy-done
  7.9 0.0 copy-done.1
  7.9 3.2 %terms.1 = (f32[64,1024]{1,0:T(8,128)S(1)}, bf16[64,1024]{1,0:T(8,128)(2,1)S(1)}, bf16[64,1024]{1,0:T(8,128)(2,1)S(1)}, bf16[64,1024]{1,0:T(8,128)(2,1)S(1)}, bf...) custom-call(s32[4,10]{1,0:T(4,128)S(1)} %copy-done, s32[4]{0:T(128)S(1)} %copy-done.1, ...), custom_call_target="tpu_custom_call" | custom-call | flops 2147483648 | bytes 1310720 | tf_op jit(solution)/shard_map/terms/pallas_call | solution.py:276
  11.2 0.0 collective-permute-done.refs_2_.rest_2_
  11.2 0.0 collective-permute-done.3.refs_5_.rest_5_
  11.2 0.6 %early_part.1.early_ref = f32[256,256]{1,0:T(8,128)S(1)} custom-call(bf16[16,256,128]{2,1,0:T(8,128)(2,1)S(1)} %get-tuple-element.26.high_ref, bf16[16,256,128]{2,1,0:T(8,128)(2,1)S(1)} %get-tuple-element.27.low_ref, bf16[2,128,256]{2,1,0:T(8,128)(2,1)S(1)} %get-tuple-element.22.refs_0_.own_0.rest_0_, ...), custom_call_target="tpu_custom_call" | custom-call | flops 402653184 | bytes 1048576 | tf_op jit(solution)/shard_map/early_part/pallas_call | solution.py:297
  11.8 0.2 collective-permute-done.4.refs_6_.rest_0_
  12.0 0.0 collective-permute-done.5.refs_7_.rest_1_
  12.0 0.3 %late_part.1 = (f32[64,1280]{1,0:T(8,128)S(1)}, bf16[64,1280]{1,0:T(8,128)(2,1)S(1)}, bf16[64,1280]{1,0:T(8,128)(2,1)S(1)}, bf16[64,1280]{1,0:T(8,128)(2,1)S(1)}) custom-call(bf16[16,256,128]{2,1,0:T(8,128)(2,1)S(1)} %get-tuple-element.26.high_ref, bf16[16,256,128]{2,1,0:T(8,128)(2,1)S(1)} %get-tuple-element.27.low_ref, f32[256,256]{1,0:T(8,128)S(1)} %early_part.1.early_ref, ...), custom_call_target="tpu_custom_call" | custom-call | flops 134217728 | bytes 1048576 | tf_op jit(solution)/shard_map/late_part/pallas_call | solution.py:308
  12.3 1.2 %collective-permute-start.8 = (bf16[64,1280]{1,0:T(8,128)(2,1)S(1)}, bf16[64,1280]{1,0:T(8,128)(2,1)S(1)}, u32[]{:S(2)}, u32[]{:S(2)}) collective-permute-start(bf16[64,1280]{1,0:T(8,128)(2,1)S(1)} %get-tuple-element.33), channel_id=1, source_target_pairs={{0,3},{1,2},{2,1},{3,0},{4,7},{5,6},{6,5},{7,4},{8,11},{9,10},{10,... | collective-permute-start | bytes 491528 | tf_op jit(solution)/shard_map/ppermute | solution.py:337
  13.6 0.2 collective-permute-start.9
  13.8 0.1 hand_out.1
  13.9 4.2 %collective-permute-start.7 = (bf16[4,128,256]{2,1,0:T(8,128)(2,1)S(1)}, bf16[4,128,256]{2,1,0:T(8,128)(2,1)S(1)}, u32[]{:S(2)}, u32[]{:S(2)}) collective-permute-start(bf16[4,128,256]{2,1,0:T(8,128)(2,1)S(1)} %get-tuple-element.25), channel_id=1, source_target_pairs={{0,4},{4,0},{8,12},{12,8},{16,20},{20,16},{24,28},{28,24},{1,5},{5... | collective-permute-start | bytes 786440 | tf_op jit(solution)/shard_map/ppermute | solution.py:442
  18.1 3.1 %collective-permute-start.6 = (bf16[4,128,256]{2,1,0:T(8,128)(2,1)S(1)}, bf16[4,128,256]{2,1,0:T(8,128)(2,1)S(1)}, u32[]{:S(2)}, u32[]{:S(2)}) collective-permute-start(bf16[4,128,256]{2,1,0:T(8,128)(2,1)S(1)} %get-tuple-element.24), channel_id=1, source_target_pairs={{4,8},{8,4},{12,16},{16,12},{20,24},{24,20},{5,9},{9,5},{13,17},{1... | collective-permute-start | bytes 786440 | tf_op jit(solution)/shard_map/ppermute | solution.py:439
  21.2 0.7 %collective-permute-start.10 = (bf16[64,1280]{1,0:T(8,128)(2,1)S(1)}, bf16[64,1280]{1,0:T(8,128)(2,1)S(1)}, u32[]{:S(2)}, u32[]{:S(2)}) collective-permute-start(bf16[64,1280]{1,0:T(8,128)(2,1)S(1)} %get-tuple-element.35), channel_id=1, source_target_pairs={{0,2},{1,3},{2,0},{3,1},{4,6},{5,7},{6,4},{7,5},{8,10},{9,11},{10,... | collective-permute-start | bytes 491528 | tf_op jit(solution)/shard_map/ppermute | solution.py:337
  21.9 0.0 collective-permute-done.8.refs_1_
  21.9 0.0 collective-permute-done.9.refs_2_
  22.0 5.1 %collective-permute-done.10.last_ref = bf16[64,1280]{1,0:T(8,128)(2,1)S(1)} collective-permute-done((bf16[64,1280]{1,0:T(8,128)(2,1)S(1)}, bf16[64,1280]{1,0:T(8,128)(2,1)S(1)}, u32[]{:S(2)}, u32[]{:S(2)}) %collective-permute-start.10) | collective-permute-done | bytes 163872 | tf_op jit(solution)/shard_map/ppermute | solution.py:337
  27.1 0.0 collective-permute-done.7.near_ref
  27.1 0.3 near_part.1
  27.4 0.0 collective-permute-done.6.far_ref
  27.4 0.8 %far_part.1 = bf16[64,768]{1,0:T(8,128)(2,1)} custom-call(s32[1]{0:T(128)} %constant.0.clone.1.pair_ref, bf16[4,128,256]{2,1,0:T(8,128)(2,1)S(1)} %collective-permute-done.6.far_ref, bf16[128,512]{1,0:T(8,128)(2,1)S(1)} %get-tuple-element.36.terms_ref, bf16[64,256]{1,0:T(8,128)(2,1)S(1)} %get-tuple-element.37.mid_ref, ...), custom_call_target="tpu_custom_call" | custom-call | flops 1048576 | bytes 1048576 | tf_op jit(solution)/shard_map/far_part/pallas_call | solution.py:466
  (2 shorter events, 0.0 us)
Async XLA Ops:
  0.0 7.9 %copy-start = (s32[4,10]{1,0:T(4,128)S(1)}, s32[4,10]{1,0:T(4,128)}, u32[]{:S(2)}) copy-start(s32[4,10]{1,0:T(4,128)} %cols_ref.1) | copy-start | bytes 484
  0.0 7.9 %copy-start.1 = (s32[4]{0:T(128)S(1)}, s32[4]{0:T(128)}, u32[]{:S(2)}) copy-start(s32[4]{0:T(128)} %count_ref.1) | copy-start | bytes 52
  1.0 4.4 %collective-permute-start.2 = (bf16[2,128,256]{2,1,0:T(8,128)(2,1)S(1)}, bf16[2,128,256]{2,1,0:T(8,128)(2,1)S(1)}, u32[]{:S(2)}, u32[]{:S(2)}) collective-permute-start(bf16[2,128,256]{2,1,0:T(8,128)(2,1)S(1)} %get-tuple-element.22.refs_0_.own_0.rest_0_), channel_id=1, source_target_pairs={{0,2},{1,3},{2,0},{3,1},{4,6},{5,7},{6,4},{7,5},{8,10},{9,11},{10,... | collective-permute-start | bytes 393224 | tf_op jit(solution)/shard_map/ppermute | solution.py:337
  2.3 4.3 %collective-permute-start.1 = (bf16[2,128,256]{2,1,0:T(8,128)(2,1)S(1)}, bf16[2,128,256]{2,1,0:T(8,128)(2,1)S(1)}, u32[]{:S(2)}, u32[]{:S(2)}) collective-permute-start(bf16[2,128,256]{2,1,0:T(8,128)(2,1)S(1)} %get-tuple-element.23.refs_1_.own_1.rest_1_), channel_id=1, source_target_pairs={{0,1},{1,0},{2,3},{3,2},{4,5},{5,4},{6,7},{7,6},{8,9},{9,8},{10,11... | collective-permute-start | bytes 393224 | tf_op jit(solution)/shard_map/ppermute | solution.py:337
  3.5 7.6 %collective-permute-start = (bf16[2,128,256]{2,1,0:T(8,128)(2,1)S(1)}, bf16[2,128,256]{2,1,0:T(8,128)(2,1)S(1)}, u32[]{:S(2)}, u32[]{:S(2)}) collective-permute-start(bf16[2,128,256]{2,1,0:T(8,128)(2,1)S(1)} %get-tuple-element.22.refs_0_.own_0.rest_0_), channel_id=1, source_target_pairs={{0,1},{1,0},{2,3},{3,2},{4,5},{5,4},{6,7},{7,6},{8,9},{9,8},{10,11... | collective-permute-start | bytes 393224 | tf_op jit(solution)/shard_map/ppermute | solution.py:337
  3.8 7.4 %collective-permute-start.3 = (bf16[2,128,256]{2,1,0:T(8,128)(2,1)S(1)}, bf16[2,128,256]{2,1,0:T(8,128)(2,1)S(1)}, u32[]{:S(2)}, u32[]{:S(2)}) collective-permute-start(bf16[2,128,256]{2,1,0:T(8,128)(2,1)S(1)} %get-tuple-element.23.refs_1_.own_1.rest_1_), channel_id=1, source_target_pairs={{0,2},{1,3},{2,0},{3,1},{4,6},{5,7},{6,4},{7,5},{8,10},{9,11},{10,... | collective-permute-start | bytes 393224 | tf_op jit(solution)/shard_map/ppermute | solution.py:337
  5.5 6.5 %collective-permute-start.4 = (bf16[2,128,256]{2,1,0:T(8,128)(2,1)S(1)}, bf16[2,128,256]{2,1,0:T(8,128)(2,1)S(1)}, u32[]{:S(2)}, u32[]{:S(2)}) collective-permute-start(bf16[2,128,256]{2,1,0:T(8,128)(2,1)S(1)} %collective-permute-done.2.refs_4_.rest_4_), channel_id=1, source_target_pairs={{0,1},{1,0},{2,3},{3,2},{4,5},{5,4},{6,7},{7,6},{8,9},{9,8},{10,11... | collective-permute-start | bytes 393224 | tf_op jit(solution)/shard_map/ppermute | solution.py:337
  6.7 5.3 %collective-permute-start.5 = (bf16[2,128,256]{2,1,0:T(8,128)(2,1)S(1)}, bf16[2,128,256]{2,1,0:T(8,128)(2,1)S(1)}, u32[]{:S(2)}, u32[]{:S(2)}) collective-permute-start(bf16[2,128,256]{2,1,0:T(8,128)(2,1)S(1)} %collective-permute-done.1.refs_3_.rest_3_), channel_id=1, source_target_pairs={{0,2},{1,3},{2,0},{3,1},{4,6},{5,7},{6,4},{7,5},{8,10},{9,11},{10,... | collective-permute-start | bytes 393224 | tf_op jit(solution)/shard_map/ppermute | solution.py:337
  12.3 9.6 %collective-permute-start.8 = (bf16[64,1280]{1,0:T(8,128)(2,1)S(1)}, bf16[64,1280]{1,0:T(8,128)(2,1)S(1)}, u32[]{:S(2)}, u32[]{:S(2)}) collective-permute-start(bf16[64,1280]{1,0:T(8,128)(2,1)S(1)} %get-tuple-element.33), channel_id=1, source_target_pairs={{0,3},{1,2},{2,1},{3,0},{4,7},{5,6},{6,5},{7,4},{8,11},{9,10},{10,... | collective-permute-start | bytes 491528 | tf_op jit(solution)/shard_map/ppermute | solution.py:337
  13.6 8.4 %collective-permute-start.9 = (bf16[64,1280]{1,0:T(8,128)(2,1)S(1)}, bf16[64,1280]{1,0:T(8,128)(2,1)S(1)}, u32[]{:S(2)}, u32[]{:S(2)}) collective-permute-start(bf16[64,1280]{1,0:T(8,128)(2,1)S(1)} %get-tuple-element.34), channel_id=1, source_target_pairs={{0,1},{1,0},{2,3},{3,2},{4,5},{5,4},{6,7},{7,6},{8,9},{9,8},{10,11... | collective-permute-start | bytes 491528 | tf_op jit(solution)/shard_map/ppermute | solution.py:337
  13.9 13.2 %collective-permute-start.7 = (bf16[4,128,256]{2,1,0:T(8,128)(2,1)S(1)}, bf16[4,128,256]{2,1,0:T(8,128)(2,1)S(1)}, u32[]{:S(2)}, u32[]{:S(2)}) collective-permute-start(bf16[4,128,256]{2,1,0:T(8,128)(2,1)S(1)} %get-tuple-element.25), channel_id=1, source_target_pairs={{0,4},{4,0},{8,12},{12,8},{16,20},{20,16},{24,28},{28,24},{1,5},{5... | collective-permute-start | bytes 786440 | tf_op jit(solution)/shard_map/ppermute | solution.py:442
  18.1 9.3 %collective-permute-start.6 = (bf16[4,128,256]{2,1,0:T(8,128)(2,1)S(1)}, bf16[4,128,256]{2,1,0:T(8,128)(2,1)S(1)}, u32[]{:S(2)}, u32[]{:S(2)}) collective-permute-start(bf16[4,128,256]{2,1,0:T(8,128)(2,1)S(1)} %get-tuple-element.24), channel_id=1, source_target_pairs={{4,8},{8,4},{12,16},{16,12},{20,24},{24,20},{5,9},{9,5},{13,17},{1... | collective-permute-start | bytes 786440 | tf_op jit(solution)/shard_map/ppermute | solution.py:439
  21.2 5.9 %collective-permute-start.10 = (bf16[64,1280]{1,0:T(8,128)(2,1)S(1)}, bf16[64,1280]{1,0:T(8,128)(2,1)S(1)}, u32[]{:S(2)}, u32[]{:S(2)}) collective-permute-start(bf16[64,1280]{1,0:T(8,128)(2,1)S(1)} %get-tuple-element.35), channel_id=1, source_target_pairs={{0,2},{1,3},{2,0},{3,1},{4,6},{5,7},{6,4},{7,5},{8,10},{9,11},{10,... | collective-permute-start | bytes 491528 | tf_op jit(solution)/shard_map/ppermute | solution.py:337

commit v9 on v7

--- a/solution.py
+++ b/solution.py
@@ -251,16 +251,16 @@
             out_ref[:, at : at + tile] = blocks[b].astype(BF16)
 
 
-def narrow_parts(a_tiles, a_cols, a_count, own, tiles, span):
+def narrow_terms(a_tiles, a_cols, a_count, own):
     rows, slots, tile = a_tiles.shape[:3]
     subs = lax.axis_size("sub")
     width = 2 * tile
+    span = width + 2 * rows * tile
     smem = pl.BlockSpec(memory_space=pltpu.SMEM)
     vmem = pl.BlockSpec(memory_space=pltpu.VMEM)
     kinds = [F32] + [BF16] * (subs - 1)
     spare = 3 << 20
-    products = 2 * width * rows * tile * width
-    *edges, high, low = pl.pallas_call(
+    return pl.pallas_call(
         functools.partial(terms_kernel, subs),
         out_shape=[jax.ShapeDtypeStruct((COARSE_ROWS, span - width), kind) for kind in kinds]
         + [jax.ShapeDtypeStruct((subs * rows, width, tile), BF16)] * 2,
@@ -280,6 +280,16 @@
         ),
         name="terms",
     )(a_cols, a_count, pltpu.with_memory_space_constraint(a_tiles, pltpu.HBM), *own)
+
+
+def narrow_parts(edges, high, low, tiles):
+    subs, (rows, width, tile) = len(edges), high.shape
+    rows //= subs
+    span = width + edges[0].shape[1]
+    vmem = pl.BlockSpec(memory_space=pltpu.VMEM)
+    kinds = [F32] + [BF16] * (subs - 1)
+    spare = 3 << 20
+    products = 2 * width * rows * tile * width
     first, last = list(range(subs - 1)), [subs - 1]
     early = pl.pallas_call(
         functools.partial(early_kernel, rows, first),
@@ -344,10 +354,14 @@
     )
 
     tiles = [list(own)] + [[None, None] for _ in range(subs - 1)]
+    if half == 1:
+        *edges, high, low = narrow_terms(a_tiles, a_cols, a_count, own)
     for k in range(1, subs):
-        low, high = k & -k, 1 << (k.bit_length() - 1)
-        tiles[k][0] = exchange(tiles[k ^ low][0], low)
-        tiles[k][1] = exchange(tiles[k ^ high][1], high)
+        if half == 1 and k == subs - 1:
+            tiles[2][0], high = lax.optimization_barrier((tiles[2][0], high))
+        first, last = k & -k, 1 << (k.bit_length() - 1)
+        tiles[k][0] = exchange(tiles[k ^ first][0], first)
+        tiles[k][1] = exchange(tiles[k ^ last][1], last)
     span = width + 2 * rows * tile
     if half == 1:
         pair = jnp.zeros((1,), jnp.int32)
@@ -362,7 +376,7 @@
 
     flat = [piece for pieces in tiles for piece in pieces]
     if half == 1:
-        parts = narrow_parts(a_tiles, a_cols, a_count, own, tiles, span)
+        parts = narrow_parts(edges, high, low, tiles)
         to_near, to_far = pl.pallas_call(
             functools.partial(hand_out_pieces_kernel, subs),
             out_shape=[jax.ShapeDtypeStruct(p_tiles.shape, BF16)] * 2,

time: 28.1 us -> 28.7 us (1.021)
  starting transfers between devices: 15.8 us -> 16.3 us
    ppermute x9, starting transfers between devices: 8.74 us -> 9.05 us  [exchange(): return lax.ppermute(value, 'sub', [(s, s ^ k) for s in range(subs)])]
where the time goes in v9:
time: 28.7 us; the launch traced here: 28.5 us
  starting transfers between devices  16.3 us (57%)
  Pallas kernels  6.26 us (22%)
  waiting for transfers between devices  5.84 us (20%)
    ppermute x9, starting transfers between devices, exchange(): return lax.ppermute(value, 'sub', [(s, s ^ k) for s in range(subs)])  9.05 us
    ppermute x1, starting transfers between devices, local(): lax.ppermute(to_far, 'dom', [(d, d - 1 + 2 * (d % 2)) for d in range(1, d...  7.16 us
    ppermute x1, waiting for transfers between devices, local(): lax.ppermute(to_far, 'dom', [(d, d - 1 + 2 * (d % 2)) for d in range(1, d...  3.82 us
    pallas_call x1, Pallas kernels, narrow_terms(): pl.pallas_call(functools.partial(terms_kernel, subs), out_shape=[jax.Shap...  3.24 us
    ppermute x9, waiting for transfers between devices, exchange(): return lax.ppermute(value, 'sub', [(s, s ^ k) for s in range(subs)])  2.01 us
    pallas_call x1, Pallas kernels, local(): pl.pallas_call(order_kernel, out_shape=[jax.ShapeDtypeStruct((rows // 2,...  1.02 us
    pallas_call x1, Pallas kernels, local(): pl.pallas_call(functools.partial(finish_kernel, subs, half), out_shape=ja...  0.93 us
  transfers between devices with their start and end apart: 11, of which 3 were waited for; matrix products, arithmetic and copies ran while one was open for 0% of the time, Pallas kernels for 14%

profile of v9, /device:TPU:1, one launch (start us, length us, event | category | flops | bytes accessed | tf_op | source)
XLA Modules:
  0.0 28.5 jit_solution(2140431310058772462)
XLA Ops:
  0.0 0.0 copy-start
  0.0 1.0 %order_columns.1 = (bf16[2,128,256]{2,1,0:T(8,128)(2,1)S(1)}, bf16[2,128,256]{2,1,0:T(8,128)(2,1)S(1)}) custom-call(s32[2,4]{1,0:T(2,128)} %bitcast.1, bf16[4,128,256]{2,1,0:T(8,128)(2,1)} %p_hbm.1), custom_call_target="tpu_custom_call" | custom-call | flops 1073741824 | bytes 524288 | tf_op jit(solution)/shard_map/order_columns/pallas_call | solution.py:336
  1.0 2.1 %collective-permute-start = (bf16[2,128,256]{2,1,0:T(8,128)(2,1)S(1)}, bf16[2,128,256]{2,1,0:T(8,128)(2,1)S(1)}, u32[]{:S(2)}, u32[]{:S(2)}) collective-permute-start(bf16[2,128,256]{2,1,0:T(8,128)(2,1)S(1)} %get-tuple-element.23.own_0.refs_0_.rest_0_), channel_id=1, source_target_pairs={{0,1},{1,0},{2,3},{3,2},{4,5},{5,4},{6,7},{7,6},{8,9},{9,8},{10,11... | collective-permute-start | bytes 393224 | tf_op jit(solution)/shard_map/ppermute | solution.py:334
  3.1 1.2 %collective-permute-start.2 = (bf16[2,128,256]{2,1,0:T(8,128)(2,1)S(1)}, bf16[2,128,256]{2,1,0:T(8,128)(2,1)S(1)}, u32[]{:S(2)}, u32[]{:S(2)}) collective-permute-start(bf16[2,128,256]{2,1,0:T(8,128)(2,1)S(1)} %get-tuple-element.23.own_0.refs_0_.rest_0_), channel_id=1, source_target_pairs={{0,2},{1,3},{2,0},{3,1},{4,6},{5,7},{6,4},{7,5},{8,10},{9,11},{10,... | collective-permute-start | bytes 393224 | tf_op jit(solution)/shard_map/ppermute | solution.py:334
  4.4 0.3 collective-permute-start.1
  4.6 0.1 collective-permute-start.3
  4.7 0.0 copy-done
  4.7 0.0 copy-done.1
  4.7 3.2 %terms.1 = (f32[64,1024]{1,0:T(8,128)S(1)}, bf16[64,1024]{1,0:T(8,128)(2,1)S(1)}, bf16[64,1024]{1,0:T(8,128)(2,1)S(1)}, bf16[64,1024]{1,0:T(8,128)(2,1)S(1)}, bf...) custom-call(s32[4,10]{1,0:T(4,128)S(1)} %copy-done, s32[4]{0:T(128)S(1)} %copy-done.1, ...), custom_call_target="tpu_custom_call" | custom-call | flops 2147483648 | bytes 1310720 | tf_op jit(solution)/shard_map/terms/pallas_call | solution.py:263
  7.9 0.0 collective-permute-done.2.refs_4_.rest_4_
  7.9 1.5 %collective-permute-start.4 = (bf16[2,128,256]{2,1,0:T(8,128)(2,1)S(1)}, bf16[2,128,256]{2,1,0:T(8,128)(2,1)S(1)}, u32[]{:S(2)}, u32[]{:S(2)}) collective-permute-start(bf16[2,128,256]{2,1,0:T(8,128)(2,1)S(1)} %collective-permute-done.2.refs_4_.rest_4_), channel_id=1, source_target_pairs={{0,1},{1,0},{2,3},{3,2},{4,5},{5,4},{6,7},{7,6},{8,9},{9,8},{10,11... | collective-permute-start | bytes 393224 | tf_op jit(solution)/shard_map/ppermute | solution.py:334
  9.4 0.0 collective-permute-done.1.refs_3_.rest_3_
  9.4 1.2 %collective-permute-start.5 = (bf16[2,128,256]{2,1,0:T(8,128)(2,1)S(1)}, bf16[2,128,256]{2,1,0:T(8,128)(2,1)S(1)}, u32[]{:S(2)}, u32[]{:S(2)}) collective-permute-start(bf16[2,128,256]{2,1,0:T(8,128)(2,1)S(1)} %collective-permute-done.1.refs_3_.rest_3_), channel_id=1, source_target_pairs={{0,2},{1,3},{2,0},{3,1},{4,6},{5,7},{6,4},{7,5},{8,10},{9,11},{10,... | collective-permute-start | bytes 393224 | tf_op jit(solution)/shard_map/ppermute | solution.py:334
  10.6 0.0 collective-permute-done.refs_2_.rest_2_
  10.6 0.0 collective-permute-done.3.refs_5_.rest_5_
  10.6 0.6 %early_part.1.early_ref = f32[256,256]{1,0:T(8,128)S(1)} custom-call(bf16[16,256,128]{2,1,0:T(8,128)(2,1)S(1)} %get-tuple-element.29.high_ref, bf16[16,256,128]{2,1,0:T(8,128)(2,1)S(1)} %get-tuple-element.30.low_ref, bf16[2,128,256]{2,1,0:T(8,128)(2,1)S(1)} %get-tuple-element.23.own_0.refs_0_.rest_0_, ...), custom_call_target="tpu_custom_call" | custom-call | flops 402653184 | bytes 1048576 | tf_op jit(solution)/shard_map/early_part/pallas_call | solution.py:294
  11.2 0.6 %collective-permute-done.4.refs_6_.rest_0_ = bf16[2,128,256]{2,1,0:T(8,128)(2,1)S(1)} collective-permute-done((bf16[2,128,256]{2,1,0:T(8,128)(2,1)S(1)}, bf16[2,128,256]{2,1,0:T(8,128)(2,1)S(1)}, u32[]{:S(2)}, u32[]{:S(2)}) %collective-permute-start.4) | collective-permute-done | bytes 131104 | tf_op jit(solution)/shard_map/ppermute | solution.py:334
  11.8 1.4 %collective-permute-done.5.refs_7_.rest_1_ = bf16[2,128,256]{2,1,0:T(8,128)(2,1)S(1)} collective-permute-done((bf16[2,128,256]{2,1,0:T(8,128)(2,1)S(1)}, bf16[2,128,256]{2,1,0:T(8,128)(2,1)S(1)}, u32[]{:S(2)}, u32[]{:S(2)}) %collective-permute-start.5) | collective-permute-done | bytes 131104 | tf_op jit(solution)/shard_map/ppermute | solution.py:334
  13.2 0.3 %late_part.1 = (f32[64,1280]{1,0:T(8,128)S(1)}, bf16[64,1280]{1,0:T(8,128)(2,1)S(1)}, bf16[64,1280]{1,0:T(8,128)(2,1)S(1)}, bf16[64,1280]{1,0:T(8,128)(2,1)S(1)}) custom-call(bf16[16,256,128]{2,1,0:T(8,128)(2,1)S(1)} %get-tuple-element.29.high_ref, bf16[16,256,128]{2,1,0:T(8,128)(2,1)S(1)} %get-tuple-element.30.low_ref, f32[256,256]{1,0:T(8,128)S(1)} %early_part.1.early_ref, ...), custom_call_target="tpu_custom_call" | custom-call | flops 134217728 | bytes 1048576 | tf_op jit(solution)/shard_map/late_part/pallas_call | solution.py:305
  13.5 1.3 %collective-permute-start.8 = (bf16[64,1280]{1,0:T(8,128)(2,1)S(1)}, bf16[64,1280]{1,0:T(8,128)(2,1)S(1)}, u32[]{:S(2)}, u32[]{:S(2)}) collective-permute-start(bf16[64,1280]{1,0:T(8,128)(2,1)S(1)} %get-tuple-element.36), channel_id=1, source_target_pairs={{0,1},{1,0},{2,3},{3,2},{4,5},{5,4},{6,7},{7,6},{8,9},{9,8},{10,11... | collective-permute-start | bytes 491528 | tf_op jit(solution)/shard_map/ppermute | solution.py:334
  14.8 1.2 %collective-permute-start.9 = (bf16[64,1280]{1,0:T(8,128)(2,1)S(1)}, bf16[64,1280]{1,0:T(8,128)(2,1)S(1)}, u32[]{:S(2)}, u32[]{:S(2)}) collective-permute-start(bf16[64,1280]{1,0:T(8,128)(2,1)S(1)} %get-tuple-element.37), channel_id=1, source_target_pairs={{0,2},{1,3},{2,0},{3,1},{4,6},{5,7},{6,4},{7,5},{8,10},{9,11},{10,... | collective-permute-start | bytes 491528 | tf_op jit(solution)/shard_map/ppermute | solution.py:334
  16.1 0.2 collective-permute-start.10
  16.3 0.1 hand_out.1
  16.4 7.2 %collective-permute-start.6 = (bf16[4,128,256]{2,1,0:T(8,128)(2,1)S(1)}, bf16[4,128,256]{2,1,0:T(8,128)(2,1)S(1)}, u32[]{:S(2)}, u32[]{:S(2)}) collective-permute-start(bf16[4,128,256]{2,1,0:T(8,128)(2,1)S(1)} %get-tuple-element.27), channel_id=1, source_target_pairs={{4,8},{8,4},{12,16},{16,12},{20,24},{24,20},{5,9},{9,5},{13,17},{1... | collective-permute-start | bytes 786440 | tf_op jit(solution)/shard_map/ppermute | solution.py:440
  23.5 0.1 collective-permute-start.7
  23.6 0.0 collective-permute-done.8.refs_1_
  23.6 0.0 collective-permute-done.9.refs_2_
  23.6 0.0 collective-permute-done.10.refs_3_
  23.6 0.1 sum_parts.1
  23.7 3.8 %collective-permute-done.6.far_ref = bf16[4,128,256]{2,1,0:T(8,128)(2,1)S(1)} collective-permute-done((bf16[4,128,256]{2,1,0:T(8,128)(2,1)S(1)}, bf16[4,128,256]{2,1,0:T(8,128)(2,1)S(1)}, u32[]{:S(2)}, u32[]{:S(2)}) %collective-permute-start.6) | collective-permute-done | bytes 262176 | tf_op jit(solution)/shard_map/ppermute | solution.py:440
  27.6 0.0 collective-permute-done.7.near_ref
  27.6 0.9 %finish.1 = bf16[64,768]{1,0:T(8,128)(2,1)} custom-call(s32[1]{0:T(128)} %constant.0.clone.1.pair_ref, bf16[4,128,256]{2,1,0:T(8,128)(2,1)S(1)} %collective-permute-done.6.far_ref, bf16[4,128,256]{2,1,0:T(8,128)(2,1)S(1)} %collective-permute-done.7.near_ref, bf16[64,256]{1,0:T(8,128)(2,1)S(1)} %get-tuple-element.39.mid_ref, ...), custom_call_target="tpu_custom_call" | custom-call | flops 268435456 | bytes 1048576 | tf_op jit(solution)/shard_map/finish/pallas_call | solution.py:458
  (1 shorter events, 0.0 us)
Async XLA Ops:
  0.0 4.7 %copy-start = (s32[4,10]{1,0:T(4,128)S(1)}, s32[4,10]{1,0:T(4,128)}, u32[]{:S(2)}) copy-start(s32[4,10]{1,0:T(4,128)} %cols_ref.1) | copy-start | bytes 484
  0.0 4.7 %copy-start.1 = (s32[4]{0:T(128)S(1)}, s32[4]{0:T(128)}, u32[]{:S(2)}) copy-start(s32[4]{0:T(128)} %count_ref.1) | copy-start | bytes 52
  1.0 9.6 %collective-permute-start = (bf16[2,128,256]{2,1,0:T(8,128)(2,1)S(1)}, bf16[2,128,256]{2,1,0:T(8,128)(2,1)S(1)}, u32[]{:S(2)}, u32[]{:S(2)}) collective-permute-start(bf16[2,128,256]{2,1,0:T(8,128)(2,1)S(1)} %get-tuple-element.23.own_0.refs_0_.rest_0_), channel_id=1, source_target_pairs={{0,1},{1,0},{2,3},{3,2},{4,5},{5,4},{6,7},{7,6},{8,9},{9,8},{10,11... | collective-permute-start | bytes 393224 | tf_op jit(solution)/shard_map/ppermute | solution.py:334
  3.1 4.8 %collective-permute-start.2 = (bf16[2,128,256]{2,1,0:T(8,128)(2,1)S(1)}, bf16[2,128,256]{2,1,0:T(8,128)(2,1)S(1)}, u32[]{:S(2)}, u32[]{:S(2)}) collective-permute-start(bf16[2,128,256]{2,1,0:T(8,128)(2,1)S(1)} %get-tuple-element.23.own_0.refs_0_.rest_0_), channel_id=1, source_target_pairs={{0,2},{1,3},{2,0},{3,1},{4,6},{5,7},{6,4},{7,5},{8,10},{9,11},{10,... | collective-permute-start | bytes 393224 | tf_op jit(solution)/shard_map/ppermute | solution.py:334
  4.4 5.0 %collective-permute-start.1 = (bf16[2,128,256]{2,1,0:T(8,128)(2,1)S(1)}, bf16[2,128,256]{2,1,0:T(8,128)(2,1)S(1)}, u32[]{:S(2)}, u32[]{:S(2)}) collective-permute-start(bf16[2,128,256]{2,1,0:T(8,128)(2,1)S(1)} %get-tuple-element.24.own_1.refs_1_.rest_1_), channel_id=1, source_target_pairs={{0,1},{1,0},{2,3},{3,2},{4,5},{5,4},{6,7},{7,6},{8,9},{9,8},{10,11... | collective-permute-start | bytes 393224 | tf_op jit(solution)/shard_map/ppermute | solution.py:334
  4.6 6.0 %collective-permute-start.3 = (bf16[2,128,256]{2,1,0:T(8,128)(2,1)S(1)}, bf16[2,128,256]{2,1,0:T(8,128)(2,1)S(1)}, u32[]{:S(2)}, u32[]{:S(2)}) collective-permute-start(bf16[2,128,256]{2,1,0:T(8,128)(2,1)S(1)} %get-tuple-element.24.own_1.refs_1_.rest_1_), channel_id=1, source_target_pairs={{0,2},{1,3},{2,0},{3,1},{4,6},{5,7},{6,4},{7,5},{8,10},{9,11},{10,... | collective-permute-start | bytes 393224 | tf_op jit(solution)/shard_map/ppermute | solution.py:334
  7.9 3.9 %collective-permute-start.4 = (bf16[2,128,256]{2,1,0:T(8,128)(2,1)S(1)}, bf16[2,128,256]{2,1,0:T(8,128)(2,1)S(1)}, u32[]{:S(2)}, u32[]{:S(2)}) collective-permute-start(bf16[2,128,256]{2,1,0:T(8,128)(2,1)S(1)} %collective-permute-done.2.refs_4_.rest_4_), channel_id=1, source_target_pairs={{0,1},{1,0},{2,3},{3,2},{4,5},{5,4},{6,7},{7,6},{8,9},{9,8},{10,11... | collective-permute-start | bytes 393224 | tf_op jit(solution)/shard_map/ppermute | solution.py:334
  9.4 3.8 %collective-permute-start.5 = (bf16[2,128,256]{2,1,0:T(8,128)(2,1)S(1)}, bf16[2,128,256]{2,1,0:T(8,128)(2,1)S(1)}, u32[]{:S(2)}, u32[]{:S(2)}) collective-permute-start(bf16[2,128,256]{2,1,0:T(8,128)(2,1)S(1)} %collective-permute-done.1.refs_3_.rest_3_), channel_id=1, source_target_pairs={{0,2},{1,3},{2,0},{3,1},{4,6},{5,7},{6,4},{7,5},{8,10},{9,11},{10,... | collective-permute-start | bytes 393224 | tf_op jit(solution)/shard_map/ppermute | solution.py:334
  13.5 10.1 %collective-permute-start.8 = (bf16[64,1280]{1,0:T(8,128)(2,1)S(1)}, bf16[64,1280]{1,0:T(8,128)(2,1)S(1)}, u32[]{:S(2)}, u32[]{:S(2)}) collective-permute-start(bf16[64,1280]{1,0:T(8,128)(2,1)S(1)} %get-tuple-element.36), channel_id=1, source_target_pairs={{0,1},{1,0},{2,3},{3,2},{4,5},{5,4},{6,7},{7,6},{8,9},{9,8},{10,11... | collective-permute-start | bytes 491528 | tf_op jit(solution)/shard_map/ppermute | solution.py:334
  14.8 8.8 %collective-permute-start.9 = (bf16[64,1280]{1,0:T(8,128)(2,1)S(1)}, bf16[64,1280]{1,0:T(8,128)(2,1)S(1)}, u32[]{:S(2)}, u32[]{:S(2)}) collective-permute-start(bf16[64,1280]{1,0:T(8,128)(2,1)S(1)} %get-tuple-element.37), channel_id=1, source_target_pairs={{0,2},{1,3},{2,0},{3,1},{4,6},{5,7},{6,4},{7,5},{8,10},{9,11},{10,... | collective-permute-start | bytes 491528 | tf_op jit(solution)/shard_map/ppermute | solution.py:334
  16.1 7.6 %collective-permute-start.10 = (bf16[64,1280]{1,0:T(8,128)(2,1)S(1)}, bf16[64,1280]{1,0:T(8,128)(2,1)S(1)}, u32[]{:S(2)}, u32[]{:S(2)}) collective-permute-start(bf16[64,1280]{1,0:T(8,128)(2,1)S(1)} %get-tuple-element.38), channel_id=1, source_target_pairs={{0,3},{1,2},{2,1},{3,0},{4,7},{5,6},{6,5},{7,4},{8,11},{9,10},{10,... | collective-permute-start | bytes 491528 | tf_op jit(solution)/shard_map/ppermute | solution.py:334
  16.4 11.2 %collective-permute-start.6 = (bf16[4,128,256]{2,1,0:T(8,128)(2,1)S(1)}, bf16[4,128,256]{2,1,0:T(8,128)(2,1)S(1)}, u32[]{:S(2)}, u32[]{:S(2)}) collective-permute-start(bf16[4,128,256]{2,1,0:T(8,128)(2,1)S(1)} %get-tuple-element.27), channel_id=1, source_target_pairs={{4,8},{8,4},{12,16},{16,12},{20,24},{24,20},{5,9},{9,5},{13,17},{1... | collective-permute-start | bytes 786440 | tf_op jit(solution)/shard_map/ppermute | solution.py:440
  23.5 4.0 %collective-permute-start.7 = (bf16[4,128,256]{2,1,0:T(8,128)(2,1)S(1)}, bf16[4,128,256]{2,1,0:T(8,128)(2,1)S(1)}, u32[]{:S(2)}, u32[]{:S(2)}) collective-permute-start(bf16[4,128,256]{2,1,0:T(8,128)(2,1)S(1)} %get-tuple-element.28), channel_id=1, source_target_pairs={{0,4},{4,0},{8,12},{12,8},{16,20},{20,16},{24,28},{28,24},{1,5},{5... | collective-permute-start | bytes 786440 | tf_op jit(solution)/shard_map/ppermute | solution.py:443

commit v10 on v7

--- a/solution.py
+++ b/solution.py
@@ -141,21 +141,16 @@
 
 
 def late_kernel(subs, rows, sources, high_ref, low_ref, early_ref, *rest):
-    p_refs, rest = rest[: 2 * len(sources)], rest[2 * len(sources) :]
-    edges, outs, mid = rest[:subs], rest[subs:-1], rest[-1]
-    width = mid.shape[1]
-    mid[...] = early_ref[...] + terms_product(rows, sources, high_ref, low_ref, p_refs)
-    me = lax.axis_index("sub")
+    p_refs, rest = rest[: 2 * subs], rest[2 * subs :]
+    edges, outs, (near_ref, far_ref, mid, ends) = rest[:subs], rest[subs:-4], rest[-4:]
+    width, piece = mid.shape[1], p_refs[0].shape[0]
+    me, odd = lax.axis_index("sub"), lax.rem(lax.axis_index("dom"), 2)
+    last = [p_refs[2 * k + i] for k in sources for i in range(2)]
+    mid[...] = early_ref[...] + terms_product(rows, sources, high_ref, low_ref, last)
     for k in range(subs):
         start = pl.multiple_of(lax.bitwise_xor(me, k) * COARSE_ROWS, COARSE_ROWS)
         outs[k][:, :width] = mid[pl.ds(start, COARSE_ROWS)].astype(outs[k].dtype)
         outs[k][:, width:] = edges[k][...]
-
-
-def hand_out_pieces_kernel(subs, *refs):
-    p_refs, (near_ref, far_ref, ends) = refs[: 2 * subs], refs[2 * subs :]
-    rows, piece = near_ref.shape[0], p_refs[0].shape[0]
-    me, odd = lax.axis_index("sub"), lax.rem(lax.axis_index("dom"), 2)
     for k in range(subs):
         for at, who in ((0, 0), (rows, subs - 1)):
 
@@ -219,7 +214,9 @@
     edge_ref[COARSE_ROWS:] = (sums - high.astype(F32)).astype(BF16)
 
 
-def finish_kernel(subs, half, pair_ref, far_ref, near_ref, mid_ref, both_ref, out_ref, edge):
+def finish_kernel(subs, half, *refs):
+    pair_ref = refs[0] if half > 1 else None
+    far_ref, near_ref, mid_ref, both_ref, out_ref, edge = refs[-6:]
     rows, tile = near_ref.shape[:2]
     width = 2 * half * tile
     odd = lax.rem(lax.axis_index("dom"), 2)
@@ -294,16 +291,20 @@
     )(high, low, *[piece for k in first for piece in tiles[k]])
     return pl.pallas_call(
         functools.partial(late_kernel, subs, rows, last),
-        out_shape=[jax.ShapeDtypeStruct((COARSE_ROWS, span), kind) for kind in kinds],
-        in_specs=[vmem] * (3 + 2 * len(last) + subs),
-        out_specs=[vmem] * subs,
-        scratch_shapes=[pltpu.VMEM((width, width), F32)],
+        out_shape=[jax.ShapeDtypeStruct((COARSE_ROWS, span), kind) for kind in kinds]
+        + [jax.ShapeDtypeStruct((rows, tile, width), BF16)] * 2,
+        in_specs=[vmem] * (3 + 3 * subs),
+        out_specs=[vmem] * (subs + 2),
+        scratch_shapes=[
+            pltpu.VMEM((width, width), F32),
+            pltpu.VMEM((2 * rows, tile, width), BF16),
+        ],
         compiler_params=pltpu.CompilerParams(vmem_limit_bytes=spare),
         cost_estimate=pl.CostEstimate(
             flops=2 * products, bytes_accessed=1 << 20, transcendentals=0
         ),
         name="late_part",
-    )(high, low, early, *tiles[-1], *edges)
+    )(high, low, early, *[piece for pieces in tiles for piece in pieces], *edges)
 
 
 def local(a_tiles, a_cols, a_count, p_tiles, p_cols):
@@ -349,9 +350,8 @@
         tiles[k][0] = exchange(tiles[k ^ low][0], low)
         tiles[k][1] = exchange(tiles[k ^ high][1], high)
     span = width + 2 * rows * tile
-    if half == 1:
-        pair = jnp.zeros((1,), jnp.int32)
-    else:
+    pairs = []
+    if half > 1:
         m_own = jnp.min(p_cols, axis=1) - lax.axis_index("dom") * coarse_group
         m_group = lax.all_gather(m_own, "sub", axis=0, tiled=True)
         m_left = lax.ppermute(
@@ -359,19 +359,11 @@
         )
         m_right = lax.ppermute(m_group[:rows], "dom", [(d + 1, d) for d in range(doms - 1)])
         pair = jnp.concatenate([m_left, m_group, m_right])
+        pairs = [pair]
 
     flat = [piece for pieces in tiles for piece in pieces]
     if half == 1:
-        parts = narrow_parts(a_tiles, a_cols, a_count, own, tiles, span)
-        to_near, to_far = pl.pallas_call(
-            functools.partial(hand_out_pieces_kernel, subs),
-            out_shape=[jax.ShapeDtypeStruct(p_tiles.shape, BF16)] * 2,
-            in_specs=[vmem] * (2 * subs),
-            out_specs=[vmem] * 2,
-            scratch_shapes=[pltpu.VMEM((2 * rows, tile, 2 * tile), BF16)],
-            compiler_params=pltpu.CompilerParams(vmem_limit_bytes=spare),
-            name="hand_out",
-        )(*flat)
+        *parts, to_near, to_far = narrow_parts(a_tiles, a_cols, a_count, own, tiles, span)
     else:
         flops = 2 * rows * slots * tile * tile * 2 * tile * half
         edges, a_held = pl.pallas_call(
@@ -422,7 +414,7 @@
             compiler_params=pltpu.CompilerParams(vmem_limit_bytes=spare),
             name="hand_out",
         )(pool)
-    received = [exchange(parts[k], k) for k in range(1, subs)]
+    received = [exchange(parts[k], k) for k in range(subs - 1, 0, -1)]
     far = lax.ppermute(
         to_far, "dom", [(d, d - 1 + 2 * (d % 2)) for d in range(1, doms - 1)]
     )
@@ -444,7 +436,7 @@
     return pl.pallas_call(
         functools.partial(finish_kernel, subs, half),
         out_shape=jax.ShapeDtypeStruct((COARSE_ROWS, 3 * width), BF16),
-        in_specs=[smem] + [vmem] * 4,
+        in_specs=[smem] * len(pairs) + [vmem] * 4,
         out_specs=vmem,
         scratch_shapes=[pltpu.VMEM((2 * rows, tile, 2 * tile), BF16)],
         compiler_params=pltpu.CompilerParams(vmem_limit_bytes=2 * p_bytes + spare),
@@ -452,7 +444,7 @@
             flops=1 << 28, bytes_accessed=4 * p_bytes, transcendentals=0
         ),
         name="finish",
-    )(pair, far, near, mid, both)
+    )(*pairs, far, near, mid, both)
 
 
 def solution(mesh):

time: 28.1 us -> 28.1 us (level)
  no operation moved by 1% of the time
where the time goes in v10:
time: 28.1 us; the launch traced here: 27.9 us
  starting transfers between devices  15.7 us (56%)
  Pallas kernels  6.26 us (22%)
  waiting for transfers between devices  5.76 us (20%)
    ppermute x9, starting transfers between devices, exchange(): return lax.ppermute(value, 'sub', [(s, s ^ k) for s in range(subs)])  8.75 us
    ppermute x1, starting transfers between devices, local(): lax.ppermute(to_far, 'dom', [(d, d - 1 + 2 * (d % 2)) for d in range(1, d...  6.92 us
    ppermute x1, waiting for transfers between devices, local(): lax.ppermute(to_far, 'dom', [(d, d - 1 + 2 * (d % 2)) for d in range(1, d...  3.82 us
    pallas_call x1, Pallas kernels, narrow_parts(): pl.pallas_call(functools.partial(terms_kernel, subs), out_shape=[jax.Shap...  3.23 us
    ppermute x9, waiting for transfers between devices, exchange(): return lax.ppermute(value, 'sub', [(s, s ^ k) for s in range(subs)])  1.93 us
    pallas_call x1, Pallas kernels, local(): pl.pallas_call(order_kernel, out_shape=[jax.ShapeDtypeStruct((rows // 2,...  1.02 us
    pallas_call x1, Pallas kernels, local(): pl.pallas_call(functools.partial(finish_kernel, subs, half), out_shape=ja...  0.93 us
    pallas_call x1, Pallas kernels, narrow_parts(): pl.pallas_call(functools.partial(early_kernel, rows, first), out_shape=ja...  0.57 us
  transfers between devices with their start and end apart: 11, of which 3 were waited for; matrix products, arithmetic and copies ran while one was open for 0% of the time, Pallas kernels for 14%

profile of v10, /device:TPU:1, one launch (start us, length us, event | category | flops | bytes accessed | tf_op | source)
XLA Modules:
  0.0 27.9 jit_solution(9053256089463085046)
XLA Ops:
  0.0 0.0 copy-start
  0.0 0.0 copy-start.1
  0.0 1.0 %order_columns.1 = (bf16[2,128,256]{2,1,0:T(8,128)(2,1)S(1)}, bf16[2,128,256]{2,1,0:T(8,128)(2,1)S(1)}) custom-call(s32[2,4]{1,0:T(2,128)} %bitcast.1, bf16[4,128,256]{2,1,0:T(8,128)(2,1)} %p_hbm.1), custom_call_target="tpu_custom_call" | custom-call | flops 1073741824 | bytes 524288 | tf_op jit(solution)/shard_map/order_columns/pallas_call | solution.py:327
  1.0 2.1 %collective-permute-start.2 = (bf16[2,128,256]{2,1,0:T(8,128)(2,1)S(1)}, bf16[2,128,256]{2,1,0:T(8,128)(2,1)S(1)}, u32[]{:S(2)}, u32[]{:S(2)}) collective-permute-start(bf16[2,128,256]{2,1,0:T(8,128)(2,1)S(1)} %get-tuple-element.21.own_0.rest_0_), channel_id=1, source_target_pairs={{0,2},{1,3},{2,0},{3,1},{4,6},{5,7},{6,4},{7,5},{8,10},{9,11},{10,... | collective-permute-start | bytes 393224 | tf_op jit(solution)/shard_map/ppermute | solution.py:325
  3.2 1.2 %collective-permute-start.1 = (bf16[2,128,256]{2,1,0:T(8,128)(2,1)S(1)}, bf16[2,128,256]{2,1,0:T(8,128)(2,1)S(1)}, u32[]{:S(2)}, u32[]{:S(2)}) collective-permute-start(bf16[2,128,256]{2,1,0:T(8,128)(2,1)S(1)} %get-tuple-element.22.own_1.rest_1_), channel_id=1, source_target_pairs={{0,1},{1,0},{2,3},{3,2},{4,5},{5,4},{6,7},{7,6},{8,9},{9,8},{10,11... | collective-permute-start | bytes 393224 | tf_op jit(solution)/shard_map/ppermute | solution.py:325
  4.4 0.3 collective-permute-start
  4.6 0.1 collective-permute-start.3
  4.7 1.7 %collective-permute-done.2.rest_4_ = bf16[2,128,256]{2,1,0:T(8,128)(2,1)S(1)} collective-permute-done((bf16[2,128,256]{2,1,0:T(8,128)(2,1)S(1)}, bf16[2,128,256]{2,1,0:T(8,128)(2,1)S(1)}, u32[]{:S(2)}, u32[]{:S(2)}) %collective-permute-start.2) | collective-permute-done | bytes 131104 | tf_op jit(solution)/shard_map/ppermute | solution.py:325
  6.4 1.1 %collective-permute-start.4 = (bf16[2,128,256]{2,1,0:T(8,128)(2,1)S(1)}, bf16[2,128,256]{2,1,0:T(8,128)(2,1)S(1)}, u32[]{:S(2)}, u32[]{:S(2)}) collective-permute-start(bf16[2,128,256]{2,1,0:T(8,128)(2,1)S(1)} %collective-permute-done.2.rest_4_), channel_id=1, source_target_pairs={{0,1},{1,0},{2,3},{3,2},{4,5},{5,4},{6,7},{7,6},{8,9},{9,8},{10,11... | collective-permute-start | bytes 393224 | tf_op jit(solution)/shard_map/ppermute | solution.py:325
  7.5 0.0 collective-permute-done.1.rest_3_
  7.5 1.2 %collective-permute-start.5 = (bf16[2,128,256]{2,1,0:T(8,128)(2,1)S(1)}, bf16[2,128,256]{2,1,0:T(8,128)(2,1)S(1)}, u32[]{:S(2)}, u32[]{:S(2)}) collective-permute-start(bf16[2,128,256]{2,1,0:T(8,128)(2,1)S(1)} %collective-permute-done.1.rest_3_), channel_id=1, source_target_pairs={{0,2},{1,3},{2,0},{3,1},{4,6},{5,7},{6,4},{7,5},{8,10},{9,11},{10,... | collective-permute-start | bytes 393224 | tf_op jit(solution)/shard_map/ppermute | solution.py:325
  8.7 0.0 copy-done
  8.7 0.0 copy-done.1
  8.7 3.2 %terms.1 = (f32[64,1024]{1,0:T(8,128)S(1)}, bf16[64,1024]{1,0:T(8,128)(2,1)S(1)}, bf16[64,1024]{1,0:T(8,128)(2,1)S(1)}, bf16[64,1024]{1,0:T(8,128)(2,1)S(1)}, bf...) custom-call(s32[4,10]{1,0:T(4,128)S(1)} %copy-done, s32[4]{0:T(128)S(1)} %copy-done.1, ...), custom_call_target="tpu_custom_call" | custom-call | flops 2147483648 | bytes 1310720 | tf_op jit(solution)/shard_map/terms/pallas_call | solution.py:260
  12.0 0.0 collective-permute-done.rest_2_
  12.0 0.0 collective-permute-done.3.rest_5_
  12.0 0.6 %early_part.1.early_ref = f32[256,256]{1,0:T(8,128)S(1)} custom-call(bf16[16,256,128]{2,1,0:T(8,128)(2,1)S(1)} %get-tuple-element.23.high_ref, bf16[16,256,128]{2,1,0:T(8,128)(2,1)S(1)} %get-tuple-element.24.low_ref, bf16[2,128,256]{2,1,0:T(8,128)(2,1)S(1)} %get-tuple-element.21.own_0.rest_0_, bf16[2,128,256]{2,1,0:T(8,128)(2,1)S(1)} %get-tuple-element.22.own_1.rest_1_, ...), custom_call_target="tpu_custom_call" | custom-call | flops 402653184 | bytes 1048576 | tf_op jit(solution)/shard_map/early_part/pallas_call | solution.py:281
  12.6 0.2 collective-permute-done.4.rest_6_
  12.8 0.0 collective-permute-done.5.rest_7_
  12.8 0.4 %late_part.1 = (f32[64,1280]{1,0:T(8,128)S(1)}, bf16[64,1280]{1,0:T(8,128)(2,1)S(1)}, bf16[64,1280]{1,0:T(8,128)(2,1)S(1)}, bf16[64,1280]{1,0:T(8,128)(2,1)S(1)}...) custom-call(bf16[16,256,128]{2,1,0:T(8,128)(2,1)S(1)} %get-tuple-element.23.high_ref, ...), custom_call_target="tpu_custom_call" | custom-call | flops 134217728 | bytes 1048576 | tf_op jit(solution)/shard_map/late_part/pallas_call | solution.py:292
  13.3 1.2 %collective-permute-start.8 = (bf16[64,1280]{1,0:T(8,128)(2,1)S(1)}, bf16[64,1280]{1,0:T(8,128)(2,1)S(1)}, u32[]{:S(2)}, u32[]{:S(2)}) collective-permute-start(bf16[64,1280]{1,0:T(8,128)(2,1)S(1)} %get-tuple-element.32), channel_id=1, source_target_pairs={{0,3},{1,2},{2,1},{3,0},{4,7},{5,6},{6,5},{7,4},{8,11},{9,10},{10,... | collective-permute-start | bytes 491528 | tf_op jit(solution)/shard_map/ppermute | solution.py:325
  14.5 1.2 %collective-permute-start.9 = (bf16[64,1280]{1,0:T(8,128)(2,1)S(1)}, bf16[64,1280]{1,0:T(8,128)(2,1)S(1)}, u32[]{:S(2)}, u32[]{:S(2)}) collective-permute-start(bf16[64,1280]{1,0:T(8,128)(2,1)S(1)} %get-tuple-element.33), channel_id=1, source_target_pairs={{0,2},{1,3},{2,0},{3,1},{4,6},{5,7},{6,4},{7,5},{8,10},{9,11},{10,... | collective-permute-start | bytes 491528 | tf_op jit(solution)/shard_map/ppermute | solution.py:325
  15.7 0.3 collective-permute-start.10
  16.0 6.9 %collective-permute-start.6 = (bf16[4,128,256]{2,1,0:T(8,128)(2,1)S(1)}, bf16[4,128,256]{2,1,0:T(8,128)(2,1)S(1)}, u32[]{:S(2)}, u32[]{:S(2)}) collective-permute-start(bf16[4,128,256]{2,1,0:T(8,128)(2,1)S(1)} %get-tuple-element.29), channel_id=1, source_target_pairs={{4,8},{8,4},{12,16},{16,12},{20,24},{24,20},{5,9},{9,5},{13,17},{1... | collective-permute-start | bytes 786440 | tf_op jit(solution)/shard_map/ppermute | solution.py:418
  22.9 0.1 collective-permute-start.7
  23.0 0.0 collective-permute-done.8.refs_1_
  23.0 0.0 collective-permute-done.9.refs_2_
  23.0 0.0 collective-permute-done.10.refs_3_
  23.0 0.1 sum_parts.1
  23.1 3.8 %collective-permute-done.6.refs_0_ = bf16[4,128,256]{2,1,0:T(8,128)(2,1)S(1)} collective-permute-done((bf16[4,128,256]{2,1,0:T(8,128)(2,1)S(1)}, bf16[4,128,256]{2,1,0:T(8,128)(2,1)S(1)}, u32[]{:S(2)}, u32[]{:S(2)}) %collective-permute-start.6) | collective-permute-done | bytes 262176 | tf_op jit(solution)/shard_map/ppermute | solution.py:418
  26.9 0.0 collective-permute-done.7.refs_1_
  26.9 0.9 %finish.1 = bf16[64,768]{1,0:T(8,128)(2,1)} custom-call(bf16[4,128,256]{2,1,0:T(8,128)(2,1)S(1)} %collective-permute-done.6.refs_0_, bf16[4,128,256]{2,1,0:T(8,128)(2,1)S(1)} %collective-permute-done.7.refs_1_, bf16[64,256]{1,0:T(8,128)(2,1)S(1)} %get-tuple-element.35.refs_2_, bf16[128,1024]{1,0:T(8,128)(2,1)S(1)} %get-tuple-element.36.refs_3_), custom_call_target="tpu_custom_call" | custom-call | flops 268435456 | bytes 1048576 | tf_op jit(solution)/shard_map/finish/pallas_call | solution.py:436
Async XLA Ops:
  0.0 8.7 %copy-start = (s32[4,10]{1,0:T(4,128)S(1)}, s32[4,10]{1,0:T(4,128)}, u32[]{:S(2)}) copy-start(s32[4,10]{1,0:T(4,128)} %cols_ref.1) | copy-start | bytes 484
  0.0 8.7 %copy-start.1 = (s32[4]{0:T(128)S(1)}, s32[4]{0:T(128)}, u32[]{:S(2)}) copy-start(s32[4]{0:T(128)} %count_ref.1) | copy-start | bytes 52
  1.0 5.4 %collective-permute-start.2 = (bf16[2,128,256]{2,1,0:T(8,128)(2,1)S(1)}, bf16[2,128,256]{2,1,0:T(8,128)(2,1)S(1)}, u32[]{:S(2)}, u32[]{:S(2)}) collective-permute-start(bf16[2,128,256]{2,1,0:T(8,128)(2,1)S(1)} %get-tuple-element.21.own_0.rest_0_), channel_id=1, source_target_pairs={{0,2},{1,3},{2,0},{3,1},{4,6},{5,7},{6,4},{7,5},{8,10},{9,11},{10,... | collective-permute-start | bytes 393224 | tf_op jit(solution)/shard_map/ppermute | solution.py:325
  3.2 4.3 %collective-permute-start.1 = (bf16[2,128,256]{2,1,0:T(8,128)(2,1)S(1)}, bf16[2,128,256]{2,1,0:T(8,128)(2,1)S(1)}, u32[]{:S(2)}, u32[]{:S(2)}) collective-permute-start(bf16[2,128,256]{2,1,0:T(8,128)(2,1)S(1)} %get-tuple-element.22.own_1.rest_1_), channel_id=1, source_target_pairs={{0,1},{1,0},{2,3},{3,2},{4,5},{5,4},{6,7},{7,6},{8,9},{9,8},{10,11... | collective-permute-start | bytes 393224 | tf_op jit(solution)/shard_map/ppermute | solution.py:325
  4.4 7.6 %collective-permute-start = (bf16[2,128,256]{2,1,0:T(8,128)(2,1)S(1)}, bf16[2,128,256]{2,1,0:T(8,128)(2,1)S(1)}, u32[]{:S(2)}, u32[]{:S(2)}) collective-permute-start(bf16[2,128,256]{2,1,0:T(8,128)(2,1)S(1)} %get-tuple-element.21.own_0.rest_0_), channel_id=1, source_target_pairs={{0,1},{1,0},{2,3},{3,2},{4,5},{5,4},{6,7},{7,6},{8,9},{9,8},{10,11... | collective-permute-start | bytes 393224 | tf_op jit(solution)/shard_map/ppermute | solution.py:325
  4.6 7.4 %collective-permute-start.3 = (bf16[2,128,256]{2,1,0:T(8,128)(2,1)S(1)}, bf16[2,128,256]{2,1,0:T(8,128)(2,1)S(1)}, u32[]{:S(2)}, u32[]{:S(2)}) collective-permute-start(bf16[2,128,256]{2,1,0:T(8,128)(2,1)S(1)} %get-tuple-element.22.own_1.rest_1_), channel_id=1, source_target_pairs={{0,2},{1,3},{2,0},{3,1},{4,6},{5,7},{6,4},{7,5},{8,10},{9,11},{10,... | collective-permute-start | bytes 393224 | tf_op jit(solution)/shard_map/ppermute | solution.py:325
  6.4 6.4 %collective-permute-start.4 = (bf16[2,128,256]{2,1,0:T(8,128)(2,1)S(1)}, bf16[2,128,256]{2,1,0:T(8,128)(2,1)S(1)}, u32[]{:S(2)}, u32[]{:S(2)}) collective-permute-start(bf16[2,128,256]{2,1,0:T(8,128)(2,1)S(1)} %collective-permute-done.2.rest_4_), channel_id=1, source_target_pairs={{0,1},{1,0},{2,3},{3,2},{4,5},{5,4},{6,7},{7,6},{8,9},{9,8},{10,11... | collective-permute-start | bytes 393224 | tf_op jit(solution)/shard_map/ppermute | solution.py:325
  7.5 5.3 %collective-permute-start.5 = (bf16[2,128,256]{2,1,0:T(8,128)(2,1)S(1)}, bf16[2,128,256]{2,1,0:T(8,128)(2,1)S(1)}, u32[]{:S(2)}, u32[]{:S(2)}) collective-permute-start(bf16[2,128,256]{2,1,0:T(8,128)(2,1)S(1)} %collective-permute-done.1.rest_3_), channel_id=1, source_target_pairs={{0,2},{1,3},{2,0},{3,1},{4,6},{5,7},{6,4},{7,5},{8,10},{9,11},{10,... | collective-permute-start | bytes 393224 | tf_op jit(solution)/shard_map/ppermute | solution.py:325
  13.3 9.7 %collective-permute-start.8 = (bf16[64,1280]{1,0:T(8,128)(2,1)S(1)}, bf16[64,1280]{1,0:T(8,128)(2,1)S(1)}, u32[]{:S(2)}, u32[]{:S(2)}) collective-permute-start(bf16[64,1280]{1,0:T(8,128)(2,1)S(1)} %get-tuple-element.32), channel_id=1, source_target_pairs={{0,3},{1,2},{2,1},{3,0},{4,7},{5,6},{6,5},{7,4},{8,11},{9,10},{10,... | collective-permute-start | bytes 491528 | tf_op jit(solution)/shard_map/ppermute | solution.py:325
  14.5 8.5 %collective-permute-start.9 = (bf16[64,1280]{1,0:T(8,128)(2,1)S(1)}, bf16[64,1280]{1,0:T(8,128)(2,1)S(1)}, u32[]{:S(2)}, u32[]{:S(2)}) collective-permute-start(bf16[64,1280]{1,0:T(8,128)(2,1)S(1)} %get-tuple-element.33), channel_id=1, source_target_pairs={{0,2},{1,3},{2,0},{3,1},{4,6},{5,7},{6,4},{7,5},{8,10},{9,11},{10,... | collective-permute-start | bytes 491528 | tf_op jit(solution)/shard_map/ppermute | solution.py:325
  15.7 7.3 %collective-permute-start.10 = (bf16[64,1280]{1,0:T(8,128)(2,1)S(1)}, bf16[64,1280]{1,0:T(8,128)(2,1)S(1)}, u32[]{:S(2)}, u32[]{:S(2)}) collective-permute-start(bf16[64,1280]{1,0:T(8,128)(2,1)S(1)} %get-tuple-element.34), channel_id=1, source_target_pairs={{0,1},{1,0},{2,3},{3,2},{4,5},{5,4},{6,7},{7,6},{8,9},{9,8},{10,11... | collective-permute-start | bytes 491528 | tf_op jit(solution)/shard_map/ppermute | solution.py:325
  16.0 11.0 %collective-permute-start.6 = (bf16[4,128,256]{2,1,0:T(8,128)(2,1)S(1)}, bf16[4,128,256]{2,1,0:T(8,128)(2,1)S(1)}, u32[]{:S(2)}, u32[]{:S(2)}) collective-permute-start(bf16[4,128,256]{2,1,0:T(8,128)(2,1)S(1)} %get-tuple-element.29), channel_id=1, source_target_pairs={{4,8},{8,4},{12,16},{16,12},{20,24},{24,20},{5,9},{9,5},{13,17},{1... | collective-permute-start | bytes 786440 | tf_op jit(solution)/shard_map/ppermute | solution.py:418
  22.9 4.0 %collective-permute-start.7 = (bf16[4,128,256]{2,1,0:T(8,128)(2,1)S(1)}, bf16[4,128,256]{2,1,0:T(8,128)(2,1)S(1)}, u32[]{:S(2)}, u32[]{:S(2)}) collective-permute-start(bf16[4,128,256]{2,1,0:T(8,128)(2,1)S(1)} %get-tuple-element.30), channel_id=1, source_target_pairs={{0,4},{4,0},{8,12},{12,8},{16,20},{20,16},{24,28},{28,24},{1,5},{5... | collective-permute-start | bytes 786440 | tf_op jit(solution)/shard_map/ppermute | solution.py:421

commit v11 on v8

--- a/solution.py
+++ b/solution.py
@@ -152,7 +152,7 @@
         outs[k][:, width:] = edges[k][...]
 
 
-def hand_out_pieces_kernel(subs, *refs):
+def hand_out_pieces_kernel(subs, _, *refs):
     p_refs, (near_ref, far_ref, ends) = refs[: 2 * subs], refs[2 * subs :]
     rows, piece = near_ref.shape[0], p_refs[0].shape[0]
     me, odd = lax.axis_index("sub"), lax.rem(lax.axis_index("dom"), 2)
@@ -226,7 +226,7 @@
     return blocks
 
 
-def sum_kernel(*refs):
+def sum_kernel(_, *refs):
     total = refs[0][...]
     for ref in refs[1:-1]:
         total = total + ref[...].astype(F32)
@@ -305,7 +305,7 @@
         ),
         name="early_part",
     )(high, low, *[piece for k in first for piece in tiles[k]])
-    return pl.pallas_call(
+    parts = pl.pallas_call(
         functools.partial(late_kernel, subs, rows, last),
         out_shape=[jax.ShapeDtypeStruct((COARSE_ROWS, span), kind) for kind in kinds],
         in_specs=[vmem] * (3 + 2 * len(last) + subs),
@@ -317,6 +317,7 @@
         ),
         name="late_part",
     )(high, low, early, *tiles[-1], *edges)
+    return [*parts, early]
 
 
 def local(a_tiles, a_cols, a_count, p_tiles, p_cols):
@@ -375,16 +376,16 @@
 
     flat = [piece for pieces in tiles for piece in pieces]
     if half == 1:
-        parts = narrow_parts(a_tiles, a_cols, a_count, own, tiles, span)
+        *parts, early = narrow_parts(a_tiles, a_cols, a_count, own, tiles, span)
         to_near, to_far = pl.pallas_call(
             functools.partial(hand_out_pieces_kernel, subs),
             out_shape=[jax.ShapeDtypeStruct(p_tiles.shape, BF16)] * 2,
-            in_specs=[vmem] * (2 * subs),
+            in_specs=[pl.BlockSpec(memory_space=pl.ANY)] + [vmem] * (2 * subs),
             out_specs=[vmem] * 2,
             scratch_shapes=[pltpu.VMEM((2 * rows, tile, 2 * tile), BF16)],
             compiler_params=pltpu.CompilerParams(vmem_limit_bytes=spare),
             name="hand_out",
-        )(*flat)
+        )(early, *flat)
     else:
         flops = 2 * rows * slots * tile * tile * 2 * tile * half
         edges, a_held = pl.pallas_call(
@@ -443,12 +444,12 @@
     sums = pl.pallas_call(
         sum_kernel,
         out_shape=jax.ShapeDtypeStruct((COARSE_ROWS, span), F32),
-        in_specs=[vmem] * (subs - 1),
+        in_specs=[pl.BlockSpec(memory_space=pl.ANY)] + [vmem] * (subs - 1),
         out_specs=vmem,
         compiler_params=pltpu.CompilerParams(vmem_limit_bytes=spare),
         cost_estimate=pl.CostEstimate(flops=3 << 29, bytes_accessed=1 << 20, transcendentals=0),
         name="sum_parts",
-    )(parts[0], *received[:-1])
+    )(near, parts[0], *received[:-1])
     mid, side, terms = pl.pallas_call(
         functools.partial(near_kernel, subs, half),
         out_shape=[

time: 28.4 us -> 28.3 us (level)
  the two profiles are of different devices: /device:TPU:9 before, /device:TPU:1 now
where the time goes in v11:
time: 28.3 us; the launch traced here: 27.8 us
  starting transfers between devices  15.5 us (55%)
  Pallas kernels  6.37 us (23%)
  waiting for transfers between devices  5.83 us (21%)
    ppermute x9, starting transfers between devices, exchange(): return lax.ppermute(value, 'sub', [(s, s ^ k) for s in range(subs)])  8.81 us
    ppermute x9, waiting for transfers between devices, exchange(): return lax.ppermute(value, 'sub', [(s, s ^ k) for s in range(subs)])  5.82 us
    ppermute x1, starting transfers between devices, local(): lax.ppermute(to_far, 'dom', [(d, d - 1 + 2 * (d % 2)) for d in range(1, d...  3.66 us
    pallas_call x1, Pallas kernels, narrow_parts(): pl.pallas_call(functools.partial(terms_kernel, subs), out_shape=[jax.Shap...  3.24 us
    ppermute x1, starting transfers between devices, local(): near = lax.ppermute(to_near, 'dom', [(d, d ^ 1) for d in range(doms)])  3.08 us
    pallas_call x1, Pallas kernels, local(): pl.pallas_call(order_kernel, out_shape=[jax.ShapeDtypeStruct((rows // 2,...  1.02 us
    pallas_call x1, Pallas kernels, local(): pl.pallas_call(functools.partial(finish_kernel, subs, half), out_shape=ja...  0.83 us
    pallas_call x1, Pallas kernels, narrow_parts(): pl.pallas_call(functools.partial(early_kernel, rows, first), out_shape=ja...  0.57 us
  transfers between devices with their start and end apart: 11, of which 5 were waited for; matrix products, arithmetic and copies ran while one was open for 0% of the time, Pallas kernels for 16%

profile of v11, /device:TPU:1, one launch (start us, length us, event | category | flops | bytes accessed | tf_op | source)
XLA Modules:
  0.0 27.8 jit_solution(9053461792949501447)
XLA Ops:
  0.0 0.0 copy-start
  0.0 1.0 %order_columns.1 = (bf16[2,128,256]{2,1,0:T(8,128)(2,1)S(1)}, bf16[2,128,256]{2,1,0:T(8,128)(2,1)S(1)}) custom-call(s32[2,4]{1,0:T(2,128)} %bitcast.1, bf16[4,128,256]{2,1,0:T(8,128)(2,1)} %p_hbm.1), custom_call_target="tpu_custom_call" | custom-call | flops 1073741824 | bytes 524288 | tf_op jit(solution)/shard_map/order_columns/pallas_call | solution.py:340
  1.0 2.1 %collective-permute-start.2 = (bf16[2,128,256]{2,1,0:T(8,128)(2,1)S(1)}, bf16[2,128,256]{2,1,0:T(8,128)(2,1)S(1)}, u32[]{:S(2)}, u32[]{:S(2)}) collective-permute-start(bf16[2,128,256]{2,1,0:T(8,128)(2,1)S(1)} %get-tuple-element.22.own_0.rest_0_.refs_0_), channel_id=1, source_target_pairs={{0,2},{1,3},{2,0},{3,1},{4,6},{5,7},{6,4},{7,5},{8,10},{9,11},{10,... | collective-permute-start | bytes 393224 | tf_op jit(solution)/shard_map/ppermute | solution.py:338
  3.2 1.2 %collective-permute-start.1 = (bf16[2,128,256]{2,1,0:T(8,128)(2,1)S(1)}, bf16[2,128,256]{2,1,0:T(8,128)(2,1)S(1)}, u32[]{:S(2)}, u32[]{:S(2)}) collective-permute-start(bf16[2,128,256]{2,1,0:T(8,128)(2,1)S(1)} %get-tuple-element.23.own_1.rest_1_.refs_1_), channel_id=1, source_target_pairs={{0,1},{1,0},{2,3},{3,2},{4,5},{5,4},{6,7},{7,6},{8,9},{9,8},{10,11... | collective-permute-start | bytes 393224 | tf_op jit(solution)/shard_map/ppermute | solution.py:338
  4.4 0.3 collective-permute-start
  4.6 0.1 collective-permute-start.3
  4.7 1.7 %collective-permute-done.2.rest_4_.refs_4_ = bf16[2,128,256]{2,1,0:T(8,128)(2,1)S(1)} collective-permute-done((bf16[2,128,256]{2,1,0:T(8,128)(2,1)S(1)}, bf16[2,128,256]{2,1,0:T(8,128)(2,1)S(1)}, u32[]{:S(2)}, u32[]{:S(2)}) %collective-permute-start.2) | collective-permute-done | bytes 131104 | tf_op jit(solution)/shard_map/ppermute | solution.py:338
  6.4 1.1 %collective-permute-start.4 = (bf16[2,128,256]{2,1,0:T(8,128)(2,1)S(1)}, bf16[2,128,256]{2,1,0:T(8,128)(2,1)S(1)}, u32[]{:S(2)}, u32[]{:S(2)}) collective-permute-start(bf16[2,128,256]{2,1,0:T(8,128)(2,1)S(1)} %collective-permute-done.2.rest_4_.refs_4_), channel_id=1, source_target_pairs={{0,1},{1,0},{2,3},{3,2},{4,5},{5,4},{6,7},{7,6},{8,9},{9,8},{10,11... | collective-permute-start | bytes 393224 | tf_op jit(solution)/shard_map/ppermute | solution.py:338
  7.5 0.0 collective-permute-done.1.rest_3_.refs_3_
  7.5 1.2 %collective-permute-start.5 = (bf16[2,128,256]{2,1,0:T(8,128)(2,1)S(1)}, bf16[2,128,256]{2,1,0:T(8,128)(2,1)S(1)}, u32[]{:S(2)}, u32[]{:S(2)}) collective-permute-start(bf16[2,128,256]{2,1,0:T(8,128)(2,1)S(1)} %collective-permute-done.1.rest_3_.refs_3_), channel_id=1, source_target_pairs={{0,2},{1,3},{2,0},{3,1},{4,6},{5,7},{6,4},{7,5},{8,10},{9,11},{10,... | collective-permute-start | bytes 393224 | tf_op jit(solution)/shard_map/ppermute | solution.py:338
  8.7 0.0 copy-done
  8.7 0.0 copy-done.1
  8.7 3.2 %terms.1 = (f32[64,1024]{1,0:T(8,128)S(1)}, bf16[64,1024]{1,0:T(8,128)(2,1)S(1)}, bf16[64,1024]{1,0:T(8,128)(2,1)S(1)}, bf16[64,1024]{1,0:T(8,128)(2,1)S(1)}, bf...) custom-call(s32[4,10]{1,0:T(4,128)S(1)} %copy-done, s32[4]{0:T(128)S(1)} %copy-done.1, ...), custom_call_target="tpu_custom_call" | custom-call | flops 2147483648 | bytes 1310720 | tf_op jit(solution)/shard_map/terms/pallas_call | solution.py:276
  12.0 0.0 collective-permute-done.rest_2_.refs_2_
  12.0 0.0 collective-permute-done.3.rest_5_.refs_5_
  12.0 0.6 %early_part.1._.early_ref = f32[256,256]{1,0:T(8,128)S(1)} custom-call(bf16[16,256,128]{2,1,0:T(8,128)(2,1)S(1)} %get-tuple-element.24.high_ref, bf16[16,256,128]{2,1,0:T(8,128)(2,1)S(1)} %get-tuple-element.25.low_ref, bf16[2,128,256]{2,1,0:T(8,128)(2,1)S(1)} %get-tuple-element.22.own_0.rest_0_.refs_0_, ...), custom_call_target="tpu_custom_call" | custom-call | flops 402653184 | bytes 1048576 | tf_op jit(solution)/shard_map/early_part/pallas_call | solution.py:297
  12.6 0.2 collective-permute-done.4.refs_6_.rest_0_
  12.8 0.0 collective-permute-done.5.refs_7_.rest_1_
  12.8 0.1 hand_out.1
  12.9 3.1 %collective-permute-start.7 = (bf16[4,128,256]{2,1,0:T(8,128)(2,1)S(1)}, bf16[4,128,256]{2,1,0:T(8,128)(2,1)S(1)}, u32[]{:S(2)}, u32[]{:S(2)}) collective-permute-start(bf16[4,128,256]{2,1,0:T(8,128)(2,1)S(1)} %get-tuple-element.27), channel_id=1, source_target_pairs={{0,4},{4,0},{8,12},{12,8},{16,20},{20,16},{24,28},{28,24},{1,5},{5... | collective-permute-start | bytes 786440 | tf_op jit(solution)/shard_map/ppermute | solution.py:443
  16.0 0.3 %late_part.1 = (f32[64,1280]{1,0:T(8,128)S(1)}, bf16[64,1280]{1,0:T(8,128)(2,1)S(1)}, bf16[64,1280]{1,0:T(8,128)(2,1)S(1)}, bf16[64,1280]{1,0:T(8,128)(2,1)S(1)}) custom-call(bf16[16,256,128]{2,1,0:T(8,128)(2,1)S(1)} %get-tuple-element.24.high_ref, bf16[16,256,128]{2,1,0:T(8,128)(2,1)S(1)} %get-tuple-element.25.low_ref, ...), custom_call_target="tpu_custom_call" | custom-call | flops 134217728 | bytes 1048576 | tf_op jit(solution)/shard_map/late_part/pallas_call | solution.py:308
  16.3 1.3 %collective-permute-start.8 = (bf16[64,1280]{1,0:T(8,128)(2,1)S(1)}, bf16[64,1280]{1,0:T(8,128)(2,1)S(1)}, u32[]{:S(2)}, u32[]{:S(2)}) collective-permute-start(bf16[64,1280]{1,0:T(8,128)(2,1)S(1)} %get-tuple-element.33), channel_id=1, source_target_pairs={{0,3},{1,2},{2,1},{3,0},{4,7},{5,6},{6,5},{7,4},{8,11},{9,10},{10,... | collective-permute-start | bytes 491528 | tf_op jit(solution)/shard_map/ppermute | solution.py:338
  17.7 0.7 %collective-permute-start.9 = (bf16[64,1280]{1,0:T(8,128)(2,1)S(1)}, bf16[64,1280]{1,0:T(8,128)(2,1)S(1)}, u32[]{:S(2)}, u32[]{:S(2)}) collective-permute-start(bf16[64,1280]{1,0:T(8,128)(2,1)S(1)} %get-tuple-element.34), channel_id=1, source_target_pairs={{0,1},{1,0},{2,3},{3,2},{4,5},{5,4},{6,7},{7,6},{8,9},{9,8},{10,11... | collective-permute-start | bytes 491528 | tf_op jit(solution)/shard_map/ppermute | solution.py:338
  18.4 3.7 %collective-permute-start.6 = (bf16[4,128,256]{2,1,0:T(8,128)(2,1)S(1)}, bf16[4,128,256]{2,1,0:T(8,128)(2,1)S(1)}, u32[]{:S(2)}, u32[]{:S(2)}) collective-permute-start(bf16[4,128,256]{2,1,0:T(8,128)(2,1)S(1)} %get-tuple-element.26), channel_id=1, source_target_pairs={{4,8},{8,4},{12,16},{16,12},{20,24},{24,20},{5,9},{9,5},{13,17},{1... | collective-permute-start | bytes 786440 | tf_op jit(solution)/shard_map/ppermute | solution.py:440
  22.0 0.7 %collective-permute-start.10 = (bf16[64,1280]{1,0:T(8,128)(2,1)S(1)}, bf16[64,1280]{1,0:T(8,128)(2,1)S(1)}, u32[]{:S(2)}, u32[]{:S(2)}) collective-permute-start(bf16[64,1280]{1,0:T(8,128)(2,1)S(1)} %get-tuple-element.35), channel_id=1, source_target_pairs={{0,2},{1,3},{2,0},{3,1},{4,6},{5,7},{6,4},{7,5},{8,10},{9,11},{10,... | collective-permute-start | bytes 491528 | tf_op jit(solution)/shard_map/ppermute | solution.py:338
  22.8 0.3 %collective-permute-done.8.refs_1_ = bf16[64,1280]{1,0:T(8,128)(2,1)S(1)} collective-permute-done((bf16[64,1280]{1,0:T(8,128)(2,1)S(1)}, bf16[64,1280]{1,0:T(8,128)(2,1)S(1)}, u32[]{:S(2)}, u32[]{:S(2)}) %collective-permute-start.8) | collective-permute-done | bytes 163872 | tf_op jit(solution)/shard_map/ppermute | solution.py:338
  23.1 3.1 %collective-permute-done.9.refs_2_ = bf16[64,1280]{1,0:T(8,128)(2,1)S(1)} collective-permute-done((bf16[64,1280]{1,0:T(8,128)(2,1)S(1)}, bf16[64,1280]{1,0:T(8,128)(2,1)S(1)}, u32[]{:S(2)}, u32[]{:S(2)}) %collective-permute-start.9) | collective-permute-done | bytes 163872 | tf_op jit(solution)/shard_map/ppermute | solution.py:338
  26.2 0.0 collective-permute-done.7._.near_ref
  26.3 0.5 %collective-permute-done.10.last_ref = bf16[64,1280]{1,0:T(8,128)(2,1)S(1)} collective-permute-done((bf16[64,1280]{1,0:T(8,128)(2,1)S(1)}, bf16[64,1280]{1,0:T(8,128)(2,1)S(1)}, u32[]{:S(2)}, u32[]{:S(2)}) %collective-permute-start.10) | collective-permute-done | bytes 163872 | tf_op jit(solution)/shard_map/ppermute | solution.py:338
  26.7 0.2 near_part.1
  27.0 0.0 collective-permute-done.6.far_ref
  27.0 0.8 %far_part.1 = bf16[64,768]{1,0:T(8,128)(2,1)} custom-call(s32[1]{0:T(128)} %constant.0.clone.1.pair_ref, bf16[4,128,256]{2,1,0:T(8,128)(2,1)S(1)} %collective-permute-done.6.far_ref, bf16[128,512]{1,0:T(8,128)(2,1)S(1)} %get-tuple-element.36.terms_ref, bf16[64,256]{1,0:T(8,128)(2,1)S(1)} %get-tuple-element.37.mid_ref, ...), custom_call_target="tpu_custom_call" | custom-call | flops 1048576 | bytes 1048576 | tf_op jit(solution)/shard_map/far_part/pallas_call | solution.py:467
  (2 shorter events, 0.0 us)
Async XLA Ops:
  0.0 8.7 %copy-start = (s32[4,10]{1,0:T(4,128)S(1)}, s32[4,10]{1,0:T(4,128)}, u32[]{:S(2)}) copy-start(s32[4,10]{1,0:T(4,128)} %cols_ref.1) | copy-start | bytes 484
  0.0 8.7 %copy-start.1 = (s32[4]{0:T(128)S(1)}, s32[4]{0:T(128)}, u32[]{:S(2)}) copy-start(s32[4]{0:T(128)} %count_ref.1) | copy-start | bytes 52
  1.0 5.4 %collective-permute-start.2 = (bf16[2,128,256]{2,1,0:T(8,128)(2,1)S(1)}, bf16[2,128,256]{2,1,0:T(8,128)(2,1)S(1)}, u32[]{:S(2)}, u32[]{:S(2)}) collective-permute-start(bf16[2,128,256]{2,1,0:T(8,128)(2,1)S(1)} %get-tuple-element.22.own_0.rest_0_.refs_0_), channel_id=1, source_target_pairs={{0,2},{1,3},{2,0},{3,1},{4,6},{5,7},{6,4},{7,5},{8,10},{9,11},{10,... | collective-permute-start | bytes 393224 | tf_op jit(solution)/shard_map/ppermute | solution.py:338
  3.2 4.3 %collective-permute-start.1 = (bf16[2,128,256]{2,1,0:T(8,128)(2,1)S(1)}, bf16[2,128,256]{2,1,0:T(8,128)(2,1)S(1)}, u32[]{:S(2)}, u32[]{:S(2)}) collective-permute-start(bf16[2,128,256]{2,1,0:T(8,128)(2,1)S(1)} %get-tuple-element.23.own_1.rest_1_.refs_1_), channel_id=1, source_target_pairs={{0,1},{1,0},{2,3},{3,2},{4,5},{5,4},{6,7},{7,6},{8,9},{9,8},{10,11... | collective-permute-start | bytes 393224 | tf_op jit(solution)/shard_map/ppermute | solution.py:338
  4.4 7.6 %collective-permute-start = (bf16[2,128,256]{2,1,0:T(8,128)(2,1)S(1)}, bf16[2,128,256]{2,1,0:T(8,128)(2,1)S(1)}, u32[]{:S(2)}, u32[]{:S(2)}) collective-permute-start(bf16[2,128,256]{2,1,0:T(8,128)(2,1)S(1)} %get-tuple-element.22.own_0.rest_0_.refs_0_), channel_id=1, source_target_pairs={{0,1},{1,0},{2,3},{3,2},{4,5},{5,4},{6,7},{7,6},{8,9},{9,8},{10,11... | collective-permute-start | bytes 393224 | tf_op jit(solution)/shard_map/ppermute | solution.py:338
  4.6 7.4 %collective-permute-start.3 = (bf16[2,128,256]{2,1,0:T(8,128)(2,1)S(1)}, bf16[2,128,256]{2,1,0:T(8,128)(2,1)S(1)}, u32[]{:S(2)}, u32[]{:S(2)}) collective-permute-start(bf16[2,128,256]{2,1,0:T(8,128)(2,1)S(1)} %get-tuple-element.23.own_1.rest_1_.refs_1_), channel_id=1, source_target_pairs={{0,2},{1,3},{2,0},{3,1},{4,6},{5,7},{6,4},{7,5},{8,10},{9,11},{10,... | collective-permute-start | bytes 393224 | tf_op jit(solution)/shard_map/ppermute | solution.py:338
  6.4 6.4 %collective-permute-start.4 = (bf16[2,128,256]{2,1,0:T(8,128)(2,1)S(1)}, bf16[2,128,256]{2,1,0:T(8,128)(2,1)S(1)}, u32[]{:S(2)}, u32[]{:S(2)}) collective-permute-start(bf16[2,128,256]{2,1,0:T(8,128)(2,1)S(1)} %collective-permute-done.2.rest_4_.refs_4_), channel_id=1, source_target_pairs={{0,1},{1,0},{2,3},{3,2},{4,5},{5,4},{6,7},{7,6},{8,9},{9,8},{10,11... | collective-permute-start | bytes 393224 | tf_op jit(solution)/shard_map/ppermute | solution.py:338
  7.5 5.3 %collective-permute-start.5 = (bf16[2,128,256]{2,1,0:T(8,128)(2,1)S(1)}, bf16[2,128,256]{2,1,0:T(8,128)(2,1)S(1)}, u32[]{:S(2)}, u32[]{:S(2)}) collective-permute-start(bf16[2,128,256]{2,1,0:T(8,128)(2,1)S(1)} %collective-permute-done.1.rest_3_.refs_3_), channel_id=1, source_target_pairs={{0,2},{1,3},{2,0},{3,1},{4,6},{5,7},{6,4},{7,5},{8,10},{9,11},{10,... | collective-permute-start | bytes 393224 | tf_op jit(solution)/shard_map/ppermute | solution.py:338
  12.9 13.3 %collective-permute-start.7 = (bf16[4,128,256]{2,1,0:T(8,128)(2,1)S(1)}, bf16[4,128,256]{2,1,0:T(8,128)(2,1)S(1)}, u32[]{:S(2)}, u32[]{:S(2)}) collective-permute-start(bf16[4,128,256]{2,1,0:T(8,128)(2,1)S(1)} %get-tuple-element.27), channel_id=1, source_target_pairs={{0,4},{4,0},{8,12},{12,8},{16,20},{20,16},{24,28},{28,24},{1,5},{5... | collective-permute-start | bytes 786440 | tf_op jit(solution)/shard_map/ppermute | solution.py:443
  16.3 6.8 %collective-permute-start.8 = (bf16[64,1280]{1,0:T(8,128)(2,1)S(1)}, bf16[64,1280]{1,0:T(8,128)(2,1)S(1)}, u32[]{:S(2)}, u32[]{:S(2)}) collective-permute-start(bf16[64,1280]{1,0:T(8,128)(2,1)S(1)} %get-tuple-element.33), channel_id=1, source_target_pairs={{0,3},{1,2},{2,1},{3,0},{4,7},{5,6},{6,5},{7,4},{8,11},{9,10},{10,... | collective-permute-start | bytes 491528 | tf_op jit(solution)/shard_map/ppermute | solution.py:338
  17.7 8.6 %collective-permute-start.9 = (bf16[64,1280]{1,0:T(8,128)(2,1)S(1)}, bf16[64,1280]{1,0:T(8,128)(2,1)S(1)}, u32[]{:S(2)}, u32[]{:S(2)}) collective-permute-start(bf16[64,1280]{1,0:T(8,128)(2,1)S(1)} %get-tuple-element.34), channel_id=1, source_target_pairs={{0,1},{1,0},{2,3},{3,2},{4,5},{5,4},{6,7},{7,6},{8,9},{9,8},{10,11... | collective-permute-start | bytes 491528 | tf_op jit(solution)/shard_map/ppermute | solution.py:338
  18.4 8.6 %collective-permute-start.6 = (bf16[4,128,256]{2,1,0:T(8,128)(2,1)S(1)}, bf16[4,128,256]{2,1,0:T(8,128)(2,1)S(1)}, u32[]{:S(2)}, u32[]{:S(2)}) collective-permute-start(bf16[4,128,256]{2,1,0:T(8,128)(2,1)S(1)} %get-tuple-element.26), channel_id=1, source_target_pairs={{4,8},{8,4},{12,16},{16,12},{20,24},{24,20},{5,9},{9,5},{13,17},{1... | collective-permute-start | bytes 786440 | tf_op jit(solution)/shard_map/ppermute | solution.py:440
  22.0 4.7 %collective-permute-start.10 = (bf16[64,1280]{1,0:T(8,128)(2,1)S(1)}, bf16[64,1280]{1,0:T(8,128)(2,1)S(1)}, u32[]{:S(2)}, u32[]{:S(2)}) collective-permute-start(bf16[64,1280]{1,0:T(8,128)(2,1)S(1)} %get-tuple-element.35), channel_id=1, source_target_pairs={{0,2},{1,3},{2,0},{3,1},{4,6},{5,7},{6,4},{7,5},{8,10},{9,11},{10,... | collective-permute-start | bytes 491528 | tf_op jit(solution)/shard_map/ppermute | solution.py:338

commit v12 on v10

--- a/solution.py
+++ b/solution.py
@@ -41,21 +41,36 @@
     return outs
 
 
-def order_kernel(cols_hbm, p_hbm, *rest):
-    outs, (cols_ref, p_ref, sems) = rest[:2], rest[2:]
+def order_kernel(with_a, cols_hbm, p_hbm, *rest):
+    if with_a:
+        (a_hbm, *outs, a_ref), (cols_ref, p_ref, sems) = rest[:-3], rest[-3:]
+    else:
+        outs, (cols_ref, p_ref, sems) = rest[:-3], rest[-3:]
     rows, tile = p_ref.shape[:2]
     piece = rows // 2
+    odd = lax.rem(lax.axis_index("dom"), 2) == 1
     lists = pltpu.make_async_copy(cols_hbm, cols_ref, sems.at[rows])
     lists.start()
     loads = [pltpu.make_async_copy(p_hbm.at[f], p_ref.at[f], sems.at[f]) for f in range(rows)]
     for load in loads:
         load.start()
+    if with_a:
+
+        @pl.when(odd)
+        def _():
+            pltpu.make_async_copy(a_hbm, a_ref, sems.at[rows + 1]).start()
+
     lists.wait()
     for f in range(rows):
         loads[f].wait()
         first = pl.multiple_of(jnp.where(cols_ref[0, f] > cols_ref[1, f], tile, 0), tile)
         for t, start in ((0, first), (1, pl.multiple_of(tile - first, tile))):
             outs[f // piece][f % piece, :, t * tile : (t + 1) * tile] = p_ref[f, :, pl.ds(start, tile)]
+    if with_a:
+
+        @pl.when(odd)
+        def _():
+            pltpu.make_async_copy(a_hbm, a_ref, sems.at[rows + 1]).wait()
 
 
 def hand_out_kernel(subs, pool, near_ref, far_ref):
@@ -95,15 +110,21 @@
                         out_ref[at, pl.ds(pl.multiple_of(start * tile, tile), tile)] += part
 
 
-def terms_kernel(subs, cols_ref, count_ref, a_hbm, own_0, own_1, *rest):
+def terms_kernel(subs, cols_ref, count_ref, a_hbm, a_held, own_0, own_1, *rest):
     edges, (high_ref, low_ref, a_ref, total, turned, sems) = rest[:subs], rest[subs:]
     rows, slots, tile = a_ref.shape[:3]
     tiles = total.shape[0] - 1
     me = lax.axis_index("sub")
     base = lax.axis_index("dom") * (subs * rows) - rows
+    odd = lax.rem(lax.axis_index("dom"), 2)
     loads = [pltpu.make_async_copy(a_hbm.at[f], a_ref.at[f], sems.at[f]) for f in range(rows)]
-    for load in loads:
-        load.start()
+    for source, here in ((a_held, odd == 1), (a_hbm, odd == 0)):
+
+        @pl.when(here)
+        def _():
+            for f in range(rows):
+                pltpu.make_async_copy(source.at[f], a_ref.at[f], sems.at[f]).start()
+
     total[...] = jnp.zeros(total.shape, F32)
     for f in range(rows):
         turned[f] = (own_0, own_1)[f // (rows // 2)][f % (rows // 2)].T
@@ -248,7 +269,7 @@
             out_ref[:, at : at + tile] = blocks[b].astype(BF16)
 
 
-def narrow_parts(a_tiles, a_cols, a_count, own, tiles, span):
+def narrow_parts(a_tiles, a_held, a_cols, a_count, own, tiles, span):
     rows, slots, tile = a_tiles.shape[:3]
     subs = lax.axis_size("sub")
     width = 2 * tile
@@ -261,7 +282,7 @@
         functools.partial(terms_kernel, subs),
         out_shape=[jax.ShapeDtypeStruct((COARSE_ROWS, span - width), kind) for kind in kinds]
         + [jax.ShapeDtypeStruct((subs * rows, width, tile), BF16)] * 2,
-        in_specs=[smem, smem, pl.BlockSpec(memory_space=pltpu.HBM), vmem, vmem],
+        in_specs=[smem, smem, pl.BlockSpec(memory_space=pltpu.HBM), vmem, vmem, vmem],
         out_specs=[vmem] * (subs + 2),
         scratch_shapes=[
             pltpu.VMEM(a_tiles.shape, BF16),
@@ -276,7 +297,7 @@
             flops=1 << 31, bytes_accessed=2 * a_tiles.size, transcendentals=0
         ),
         name="terms",
-    )(a_cols, a_count, pltpu.with_memory_space_constraint(a_tiles, pltpu.HBM), *own)
+    )(a_cols, a_count, pltpu.with_memory_space_constraint(a_tiles, pltpu.HBM), a_held, *own)
     first, last = list(range(subs - 1)), [subs - 1]
     early = pl.pallas_call(
         functools.partial(early_kernel, rows, first),
@@ -324,25 +345,25 @@
     def exchange(value, k):
         return lax.ppermute(value, "sub", [(s, s ^ k) for s in range(subs)])
 
-    own = pl.pallas_call(
-        order_kernel,
-        out_shape=[jax.ShapeDtypeStruct((rows // 2, tile, 2 * tile), BF16)] * 2,
-        in_specs=[pl.BlockSpec(memory_space=pltpu.HBM)] * 2,
-        out_specs=[vmem] * 2,
+    loaded = [p_cols.T, p_tiles] + ([a_tiles] if half == 1 else [])
+    ordered = pl.pallas_call(
+        functools.partial(order_kernel, half == 1),
+        out_shape=[jax.ShapeDtypeStruct((rows // 2, tile, 2 * tile), BF16)] * 2
+        + [jax.ShapeDtypeStruct(array.shape, BF16) for array in loaded[2:]],
+        in_specs=[pl.BlockSpec(memory_space=pltpu.HBM)] * len(loaded),
+        out_specs=[vmem] * len(loaded),
         scratch_shapes=[
             pltpu.SMEM((2, rows), jnp.int32),
             pltpu.VMEM(p_tiles.shape, BF16),
-            pltpu.SemaphoreType.DMA((rows + 1,)),
+            pltpu.SemaphoreType.DMA((rows + 2,)),
         ],
         compiler_params=pltpu.CompilerParams(vmem_limit_bytes=spare),
         cost_estimate=pl.CostEstimate(
             flops=1 << 30, bytes_accessed=2 * p_bytes, transcendentals=0
         ),
         name="order_columns",
-    )(
-        pltpu.with_memory_space_constraint(p_cols.T, pltpu.HBM),
-        pltpu.with_memory_space_constraint(p_tiles, pltpu.HBM),
-    )
+    )(*[pltpu.with_memory_space_constraint(array, pltpu.HBM) for array in loaded])
+    own, a_held = ordered[:2], ordered[-1]
 
     tiles = [list(own)] + [[None, None] for _ in range(subs - 1)]
     for k in range(1, subs):
@@ -363,7 +384,7 @@
 
     flat = [piece for pieces in tiles for piece in pieces]
     if half == 1:
-        *parts, to_near, to_far = narrow_parts(a_tiles, a_cols, a_count, own, tiles, span)
+        *parts, to_near, to_far = narrow_parts(a_tiles, a_held, a_cols, a_count, own, tiles, span)
     else:
         flops = 2 * rows * slots * tile * tile * 2 * tile * half
         edges, a_held = pl.pallas_call(

time: 28.1 us -> 28 us (level)
  starting transfers between devices: 15.7 us -> 14.7 us
  waiting for transfers between devices: 5.76 us -> 6.57 us
    ppermute x9, waiting for transfers between devices: 1.93 us -> 3.85 us  [exchange(): return lax.ppermute(value, 'sub', [(s, s ^ k) for s in range(subs)])]
    ppermute x1, starting transfers between devices: 6.92 us -> 5.78 us  [local(): lax.ppermute(to_far, 'dom', [(d, d - 1 + 2 * (d % 2)) for d in range(1, d...]
    ppermute x1, waiting for transfers between devices: 3.82 us -> 2.72 us  [local(): lax.ppermute(to_far, 'dom', [(d, d - 1 + 2 * (d % 2)) for d in range(1, d...]
    pallas_call x1, Pallas kernels: 1.02 us -> 1.55 us  [local(): pl.pallas_call(functools.partial(order_kernel, half == 1), out_shape=[jax...]
    pallas_call x1, Pallas kernels: 3.23 us -> 2.94 us  [narrow_parts(): pl.pallas_call(functools.partial(terms_kernel, subs), out_shape=[jax.Shap...]
  transfers between devices with their start and end apart: 11 -> 11, of which waited for: 3 -> 4; matrix products, arithmetic and copies ran while one was open for 0% -> 0% of each run, Pallas kernels for 14% -> 13%
where the time goes in v12:
time: 28 us; the launch traced here: 27.9 us
  starting transfers between devices  14.7 us (52%)
  waiting for transfers between devices  6.57 us (23%)
  Pallas kernels  6.49 us (23%)
    ppermute x9, starting transfers between devices, exchange(): return lax.ppermute(value, 'sub', [(s, s ^ k) for s in range(subs)])  8.84 us
    ppermute x1, starting transfers between devices, local(): lax.ppermute(to_far, 'dom', [(d, d - 1 + 2 * (d % 2)) for d in range(1, d...  5.78 us
    ppermute x9, waiting for transfers between devices, exchange(): return lax.ppermute(value, 'sub', [(s, s ^ k) for s in range(subs)])  3.85 us
    pallas_call x1, Pallas kernels, narrow_parts(): pl.pallas_call(functools.partial(terms_kernel, subs), out_shape=[jax.Shap...  2.94 us
    ppermute x1, waiting for transfers between devices, local(): lax.ppermute(to_far, 'dom', [(d, d - 1 + 2 * (d % 2)) for d in range(1, d...  2.72 us
    pallas_call x1, Pallas kernels, local(): pl.pallas_call(functools.partial(order_kernel, half == 1), out_shape=[jax...  1.55 us
    pallas_call x1, Pallas kernels, local(): pl.pallas_call(functools.partial(finish_kernel, subs, half), out_shape=ja...  0.93 us
    pallas_call x1, Pallas kernels, narrow_parts(): pl.pallas_call(functools.partial(early_kernel, rows, first), out_shape=ja...  0.57 us
  transfers between devices with their start and end apart: 11, of which 4 were waited for; matrix products, arithmetic and copies ran while one was open for 0% of the time, Pallas kernels for 13%

profile of v12, /device:TPU:1, one launch (start us, length us, event | category | flops | bytes accessed | tf_op | source)
XLA Modules:
  0.0 27.9 jit_solution(13476434598666840981)
XLA Ops:
  0.0 0.0 copy-start
  0.0 0.0 copy-start.1
  0.0 1.5 %order_columns.1 = (bf16[2,128,256]{2,1,0:T(8,128)(2,1)S(1)}, bf16[2,128,256]{2,1,0:T(8,128)(2,1)S(1)}, bf16[4,10,128,128]{3,2,1,0:T(8,128)(2,1)S(1)}) custom-call(s32[2,4]{1,0:T(2,128)} %bitcast.1, bf16[4,128,256]{2,1,0:T(8,128)(2,1)} %p_hbm.1, bf16[4,10,128,128]{3,2,1,0:T(8,128)(2,1)} %a_hbm.1), custom_call_target="tpu_custom_call" | custom-call | flops 1073741824 | bytes 524288 | tf_op jit(solution)/shard_map/order_columns/pallas_call | solution.py:349
  1.6 2.1 %collective-permute-start.2 = (bf16[2,128,256]{2,1,0:T(8,128)(2,1)S(1)}, bf16[2,128,256]{2,1,0:T(8,128)(2,1)S(1)}, u32[]{:S(2)}, u32[]{:S(2)}) collective-permute-start(bf16[2,128,256]{2,1,0:T(8,128)(2,1)S(1)} %get-tuple-element.23.own_0.rest_0_), channel_id=1, source_target_pairs={{0,2},{1,3},{2,0},{3,1},{4,6},{5,7},{6,4},{7,5},{8,10},{9,11},{10,... | collective-permute-start | bytes 393224 | tf_op jit(solution)/shard_map/ppermute | solution.py:346
  3.7 1.2 %collective-permute-start.1 = (bf16[2,128,256]{2,1,0:T(8,128)(2,1)S(1)}, bf16[2,128,256]{2,1,0:T(8,128)(2,1)S(1)}, u32[]{:S(2)}, u32[]{:S(2)}) collective-permute-start(bf16[2,128,256]{2,1,0:T(8,128)(2,1)S(1)} %get-tuple-element.24.own_1.rest_1_), channel_id=1, source_target_pairs={{0,1},{1,0},{2,3},{3,2},{4,5},{5,4},{6,7},{7,6},{8,9},{9,8},{10,11... | collective-permute-start | bytes 393224 | tf_op jit(solution)/shard_map/ppermute | solution.py:346
  4.9 0.3 collective-permute-start
  5.2 0.1 collective-permute-start.3
  5.2 2.2 %collective-permute-done.2.rest_4_ = bf16[2,128,256]{2,1,0:T(8,128)(2,1)S(1)} collective-permute-done((bf16[2,128,256]{2,1,0:T(8,128)(2,1)S(1)}, bf16[2,128,256]{2,1,0:T(8,128)(2,1)S(1)}, u32[]{:S(2)}, u32[]{:S(2)}) %collective-permute-start.2) | collective-permute-done | bytes 131104 | tf_op jit(solution)/shard_map/ppermute | solution.py:346
  7.4 1.2 %collective-permute-start.4 = (bf16[2,128,256]{2,1,0:T(8,128)(2,1)S(1)}, bf16[2,128,256]{2,1,0:T(8,128)(2,1)S(1)}, u32[]{:S(2)}, u32[]{:S(2)}) collective-permute-start(bf16[2,128,256]{2,1,0:T(8,128)(2,1)S(1)} %collective-permute-done.2.rest_4_), channel_id=1, source_target_pairs={{0,1},{1,0},{2,3},{3,2},{4,5},{5,4},{6,7},{7,6},{8,9},{9,8},{10,11... | collective-permute-start | bytes 393224 | tf_op jit(solution)/shard_map/ppermute | solution.py:346
  8.6 0.0 collective-permute-done.1.rest_3_
  8.6 1.2 %collective-permute-start.5 = (bf16[2,128,256]{2,1,0:T(8,128)(2,1)S(1)}, bf16[2,128,256]{2,1,0:T(8,128)(2,1)S(1)}, u32[]{:S(2)}, u32[]{:S(2)}) collective-permute-start(bf16[2,128,256]{2,1,0:T(8,128)(2,1)S(1)} %collective-permute-done.1.rest_3_), channel_id=1, source_target_pairs={{0,2},{1,3},{2,0},{3,1},{4,6},{5,7},{6,4},{7,5},{8,10},{9,11},{10,... | collective-permute-start | bytes 393224 | tf_op jit(solution)/shard_map/ppermute | solution.py:346
  9.9 0.0 copy-done
  9.9 0.0 copy-done.1
  9.9 2.9 %terms.1 = (f32[64,1024]{1,0:T(8,128)S(1)}, bf16[64,1024]{1,0:T(8,128)(2,1)S(1)}, bf16[64,1024]{1,0:T(8,128)(2,1)S(1)}, bf16[64,1024]{1,0:T(8,128)(2,1)S(1)}, bf...) custom-call(s32[4,10]{1,0:T(4,128)S(1)} %copy-done, s32[4]{0:T(128)S(1)} %copy-done.1, ...), custom_call_target="tpu_custom_call" | custom-call | flops 2147483648 | bytes 1310720 | tf_op jit(solution)/shard_map/terms/pallas_call | solution.py:281
  12.8 0.0 collective-permute-done.rest_2_
  12.8 0.0 collective-permute-done.3.rest_5_
  12.8 0.6 %early_part.1.early_ref = f32[256,256]{1,0:T(8,128)S(1)} custom-call(bf16[16,256,128]{2,1,0:T(8,128)(2,1)S(1)} %get-tuple-element.25.high_ref, bf16[16,256,128]{2,1,0:T(8,128)(2,1)S(1)} %get-tuple-element.26.low_ref, bf16[2,128,256]{2,1,0:T(8,128)(2,1)S(1)} %get-tuple-element.23.own_0.rest_0_, bf16[2,128,256]{2,1,0:T(8,128)(2,1)S(1)} %get-tuple-element.24.own_1.rest_1_, ...), custom_call_target="tpu_custom_call" | custom-call | flops 402653184 | bytes 1048576 | tf_op jit(solution)/shard_map/early_part/pallas_call | solution.py:302
  13.4 0.5 %collective-permute-done.4.rest_6_ = bf16[2,128,256]{2,1,0:T(8,128)(2,1)S(1)} collective-permute-done((bf16[2,128,256]{2,1,0:T(8,128)(2,1)S(1)}, bf16[2,128,256]{2,1,0:T(8,128)(2,1)S(1)}, u32[]{:S(2)}, u32[]{:S(2)}) %collective-permute-start.4) | collective-permute-done | bytes 131104 | tf_op jit(solution)/shard_map/ppermute | solution.py:346
  14.0 0.0 collective-permute-done.5.rest_7_
  14.0 0.4 %late_part.1 = (f32[64,1280]{1,0:T(8,128)S(1)}, bf16[64,1280]{1,0:T(8,128)(2,1)S(1)}, bf16[64,1280]{1,0:T(8,128)(2,1)S(1)}, bf16[64,1280]{1,0:T(8,128)(2,1)S(1)}...) custom-call(bf16[16,256,128]{2,1,0:T(8,128)(2,1)S(1)} %get-tuple-element.25.high_ref, ...), custom_call_target="tpu_custom_call" | custom-call | flops 134217728 | bytes 1048576 | tf_op jit(solution)/shard_map/late_part/pallas_call | solution.py:313
  14.4 1.0 %collective-permute-start.8 = (bf16[64,1280]{1,0:T(8,128)(2,1)S(1)}, bf16[64,1280]{1,0:T(8,128)(2,1)S(1)}, u32[]{:S(2)}, u32[]{:S(2)}) collective-permute-start(bf16[64,1280]{1,0:T(8,128)(2,1)S(1)} %get-tuple-element.34), channel_id=1, source_target_pairs={{0,3},{1,2},{2,1},{3,0},{4,7},{5,6},{6,5},{7,4},{8,11},{9,10},{10,... | collective-permute-start | bytes 491528 | tf_op jit(solution)/shard_map/ppermute | solution.py:346
  15.3 1.5 %collective-permute-start.9 = (bf16[64,1280]{1,0:T(8,128)(2,1)S(1)}, bf16[64,1280]{1,0:T(8,128)(2,1)S(1)}, u32[]{:S(2)}, u32[]{:S(2)}) collective-permute-start(bf16[64,1280]{1,0:T(8,128)(2,1)S(1)} %get-tuple-element.35), channel_id=1, source_target_pairs={{0,2},{1,3},{2,0},{3,1},{4,6},{5,7},{6,4},{7,5},{8,10},{9,11},{10,... | collective-permute-start | bytes 491528 | tf_op jit(solution)/shard_map/ppermute | solution.py:346
  16.8 0.3 collective-permute-start.10
  17.1 5.8 %collective-permute-start.6 = (bf16[4,128,256]{2,1,0:T(8,128)(2,1)S(1)}, bf16[4,128,256]{2,1,0:T(8,128)(2,1)S(1)}, u32[]{:S(2)}, u32[]{:S(2)}) collective-permute-start(bf16[4,128,256]{2,1,0:T(8,128)(2,1)S(1)} %get-tuple-element.31), channel_id=1, source_target_pairs={{4,8},{8,4},{12,16},{16,12},{20,24},{24,20},{5,9},{9,5},{13,17},{1... | collective-permute-start | bytes 786440 | tf_op jit(solution)/shard_map/ppermute | solution.py:439
  22.9 0.1 collective-permute-start.7
  23.0 0.0 collective-permute-done.8.refs_1_
  23.0 1.1 %collective-permute-done.9.refs_2_ = bf16[64,1280]{1,0:T(8,128)(2,1)S(1)} collective-permute-done((bf16[64,1280]{1,0:T(8,128)(2,1)S(1)}, bf16[64,1280]{1,0:T(8,128)(2,1)S(1)}, u32[]{:S(2)}, u32[]{:S(2)}) %collective-permute-start.9) | collective-permute-done | bytes 163872 | tf_op jit(solution)/shard_map/ppermute | solution.py:346
  24.1 0.0 collective-permute-done.10.refs_3_
  24.1 0.1 sum_parts.1
  24.2 2.7 %collective-permute-done.6.refs_0_ = bf16[4,128,256]{2,1,0:T(8,128)(2,1)S(1)} collective-permute-done((bf16[4,128,256]{2,1,0:T(8,128)(2,1)S(1)}, bf16[4,128,256]{2,1,0:T(8,128)(2,1)S(1)}, u32[]{:S(2)}, u32[]{:S(2)}) %collective-permute-start.6) | collective-permute-done | bytes 262176 | tf_op jit(solution)/shard_map/ppermute | solution.py:439
  26.9 0.0 collective-permute-done.7.refs_1_
  26.9 0.9 %finish.1 = bf16[64,768]{1,0:T(8,128)(2,1)} custom-call(bf16[4,128,256]{2,1,0:T(8,128)(2,1)S(1)} %collective-permute-done.6.refs_0_, bf16[4,128,256]{2,1,0:T(8,128)(2,1)S(1)} %collective-permute-done.7.refs_1_, bf16[64,256]{1,0:T(8,128)(2,1)S(1)} %get-tuple-element.37.refs_2_, bf16[128,1024]{1,0:T(8,128)(2,1)S(1)} %get-tuple-element.38.refs_3_), custom_call_target="tpu_custom_call" | custom-call | flops 268435456 | bytes 1048576 | tf_op jit(solution)/shard_map/finish/pallas_call | solution.py:457
Async XLA Ops:
  0.0 9.9 %copy-start = (s32[4,10]{1,0:T(4,128)S(1)}, s32[4,10]{1,0:T(4,128)}, u32[]{:S(2)}) copy-start(s32[4,10]{1,0:T(4,128)} %cols_ref.1) | copy-start | bytes 484
  0.0 9.9 %copy-start.1 = (s32[4]{0:T(128)S(1)}, s32[4]{0:T(128)}, u32[]{:S(2)}) copy-start(s32[4]{0:T(128)} %count_ref.1) | copy-start | bytes 52
  1.6 5.9 %collective-permute-start.2 = (bf16[2,128,256]{2,1,0:T(8,128)(2,1)S(1)}, bf16[2,128,256]{2,1,0:T(8,128)(2,1)S(1)}, u32[]{:S(2)}, u32[]{:S(2)}) collective-permute-start(bf16[2,128,256]{2,1,0:T(8,128)(2,1)S(1)} %get-tuple-element.23.own_0.rest_0_), channel_id=1, source_target_pairs={{0,2},{1,3},{2,0},{3,1},{4,6},{5,7},{6,4},{7,5},{8,10},{9,11},{10,... | collective-permute-start | bytes 393224 | tf_op jit(solution)/shard_map/ppermute | solution.py:346
  3.7 4.9 %collective-permute-start.1 = (bf16[2,128,256]{2,1,0:T(8,128)(2,1)S(1)}, bf16[2,128,256]{2,1,0:T(8,128)(2,1)S(1)}, u32[]{:S(2)}, u32[]{:S(2)}) collective-permute-start(bf16[2,128,256]{2,1,0:T(8,128)(2,1)S(1)} %get-tuple-element.24.own_1.rest_1_), channel_id=1, source_target_pairs={{0,1},{1,0},{2,3},{3,2},{4,5},{5,4},{6,7},{7,6},{8,9},{9,8},{10,11... | collective-permute-start | bytes 393224 | tf_op jit(solution)/shard_map/ppermute | solution.py:346
  4.9 7.9 %collective-permute-start = (bf16[2,128,256]{2,1,0:T(8,128)(2,1)S(1)}, bf16[2,128,256]{2,1,0:T(8,128)(2,1)S(1)}, u32[]{:S(2)}, u32[]{:S(2)}) collective-permute-start(bf16[2,128,256]{2,1,0:T(8,128)(2,1)S(1)} %get-tuple-element.23.own_0.rest_0_), channel_id=1, source_target_pairs={{0,1},{1,0},{2,3},{3,2},{4,5},{5,4},{6,7},{7,6},{8,9},{9,8},{10,11... | collective-permute-start | bytes 393224 | tf_op jit(solution)/shard_map/ppermute | solution.py:346
  5.2 7.7 %collective-permute-start.3 = (bf16[2,128,256]{2,1,0:T(8,128)(2,1)S(1)}, bf16[2,128,256]{2,1,0:T(8,128)(2,1)S(1)}, u32[]{:S(2)}, u32[]{:S(2)}) collective-permute-start(bf16[2,128,256]{2,1,0:T(8,128)(2,1)S(1)} %get-tuple-element.24.own_1.rest_1_), channel_id=1, source_target_pairs={{0,2},{1,3},{2,0},{3,1},{4,6},{5,7},{6,4},{7,5},{8,10},{9,11},{10,... | collective-permute-start | bytes 393224 | tf_op jit(solution)/shard_map/ppermute | solution.py:346
  7.4 6.5 %collective-permute-start.4 = (bf16[2,128,256]{2,1,0:T(8,128)(2,1)S(1)}, bf16[2,128,256]{2,1,0:T(8,128)(2,1)S(1)}, u32[]{:S(2)}, u32[]{:S(2)}) collective-permute-start(bf16[2,128,256]{2,1,0:T(8,128)(2,1)S(1)} %collective-permute-done.2.rest_4_), channel_id=1, source_target_pairs={{0,1},{1,0},{2,3},{3,2},{4,5},{5,4},{6,7},{7,6},{8,9},{9,8},{10,11... | collective-permute-start | bytes 393224 | tf_op jit(solution)/shard_map/ppermute | solution.py:346
  8.6 5.3 %collective-permute-start.5 = (bf16[2,128,256]{2,1,0:T(8,128)(2,1)S(1)}, bf16[2,128,256]{2,1,0:T(8,128)(2,1)S(1)}, u32[]{:S(2)}, u32[]{:S(2)}) collective-permute-start(bf16[2,128,256]{2,1,0:T(8,128)(2,1)S(1)} %collective-permute-done.1.rest_3_), channel_id=1, source_target_pairs={{0,2},{1,3},{2,0},{3,1},{4,6},{5,7},{6,4},{7,5},{8,10},{9,11},{10,... | collective-permute-start | bytes 393224 | tf_op jit(solution)/shard_map/ppermute | solution.py:346
  14.4 8.6 %collective-permute-start.8 = (bf16[64,1280]{1,0:T(8,128)(2,1)S(1)}, bf16[64,1280]{1,0:T(8,128)(2,1)S(1)}, u32[]{:S(2)}, u32[]{:S(2)}) collective-permute-start(bf16[64,1280]{1,0:T(8,128)(2,1)S(1)} %get-tuple-element.34), channel_id=1, source_target_pairs={{0,3},{1,2},{2,1},{3,0},{4,7},{5,6},{6,5},{7,4},{8,11},{9,10},{10,... | collective-permute-start | bytes 491528 | tf_op jit(solution)/shard_map/ppermute | solution.py:346
  15.3 8.8 %collective-permute-start.9 = (bf16[64,1280]{1,0:T(8,128)(2,1)S(1)}, bf16[64,1280]{1,0:T(8,128)(2,1)S(1)}, u32[]{:S(2)}, u32[]{:S(2)}) collective-permute-start(bf16[64,1280]{1,0:T(8,128)(2,1)S(1)} %get-tuple-element.35), channel_id=1, source_target_pairs={{0,2},{1,3},{2,0},{3,1},{4,6},{5,7},{6,4},{7,5},{8,10},{9,11},{10,... | collective-permute-start | bytes 491528 | tf_op jit(solution)/shard_map/ppermute | solution.py:346
  16.8 7.3 %collective-permute-start.10 = (bf16[64,1280]{1,0:T(8,128)(2,1)S(1)}, bf16[64,1280]{1,0:T(8,128)(2,1)S(1)}, u32[]{:S(2)}, u32[]{:S(2)}) collective-permute-start(bf16[64,1280]{1,0:T(8,128)(2,1)S(1)} %get-tuple-element.36), channel_id=1, source_target_pairs={{0,1},{1,0},{2,3},{3,2},{4,5},{5,4},{6,7},{7,6},{8,9},{9,8},{10,11... | collective-permute-start | bytes 491528 | tf_op jit(solution)/shard_map/ppermute | solution.py:346
  17.1 9.8 %collective-permute-start.6 = (bf16[4,128,256]{2,1,0:T(8,128)(2,1)S(1)}, bf16[4,128,256]{2,1,0:T(8,128)(2,1)S(1)}, u32[]{:S(2)}, u32[]{:S(2)}) collective-permute-start(bf16[4,128,256]{2,1,0:T(8,128)(2,1)S(1)} %get-tuple-element.31), channel_id=1, source_target_pairs={{4,8},{8,4},{12,16},{16,12},{20,24},{24,20},{5,9},{9,5},{13,17},{1... | collective-permute-start | bytes 786440 | tf_op jit(solution)/shard_map/ppermute | solution.py:439
  22.9 4.0 %collective-permute-start.7 = (bf16[4,128,256]{2,1,0:T(8,128)(2,1)S(1)}, bf16[4,128,256]{2,1,0:T(8,128)(2,1)S(1)}, u32[]{:S(2)}, u32[]{:S(2)}) collective-permute-start(bf16[4,128,256]{2,1,0:T(8,128)(2,1)S(1)} %get-tuple-element.32), channel_id=1, source_target_pairs={{0,4},{4,0},{8,12},{12,8},{16,20},{20,16},{24,28},{28,24},{1,5},{5... | collective-permute-start | bytes 786440 | tf_op jit(solution)/shard_map/ppermute | solution.py:442

commit v13 on v10

--- a/solution.py
+++ b/solution.py
@@ -122,6 +122,12 @@
         for i, c in enumerate([*range(rows), *range(tiles - rows, tiles)]):
             part = total[c, pl.ds(start, COARSE_ROWS)]
             edges[k][:, i * tile : (i + 1) * tile] = part.astype(edges[k].dtype)
+    k = subs - 1
+    start = pl.multiple_of(lax.bitwise_xor(me, k) * COARSE_ROWS, COARSE_ROWS)
+    for f in range(rows):
+        part = total[rows + lax.bitwise_xor(me, k) * rows + f, pl.ds(start, COARSE_ROWS)]
+        at = (2 * rows + f) * tile
+        edges[k][:, at : at + tile] = part.astype(edges[k].dtype)
 
 
 def terms_product(rows, sources, high_ref, low_ref, p_refs):
@@ -136,18 +142,24 @@
     return out[:height] + out[height:]
 
 
-def early_kernel(rows, sources, high_ref, low_ref, *rest):
-    rest[-1][...] = terms_product(rows, sources, high_ref, low_ref, rest[:-1])
+def early_kernel(subs, rows, sources, high_ref, low_ref, edge_ref, *rest):
+    p_refs, (out_ref, part_ref) = rest[:-2], rest[-2:]
+    out_ref[...] = terms_product(rows, sources, high_ref, low_ref, p_refs)
+    width = out_ref.shape[1]
+    start = lax.bitwise_xor(lax.axis_index("sub"), subs - 1) * COARSE_ROWS
+    at = pl.ds(pl.multiple_of(start, COARSE_ROWS), COARSE_ROWS)
+    part_ref[:, :width] = out_ref[at].astype(BF16)
+    part_ref[:, width:] = edge_ref[...]
 
 
 def late_kernel(subs, rows, sources, high_ref, low_ref, early_ref, *rest):
     p_refs, rest = rest[: 2 * subs], rest[2 * subs :]
-    edges, outs, (near_ref, far_ref, mid, ends) = rest[:subs], rest[subs:-4], rest[-4:]
+    edges, outs, (near_ref, far_ref, mid, ends) = rest[: subs - 1], rest[subs - 1 : -4], rest[-4:]
     width, piece = mid.shape[1], p_refs[0].shape[0]
     me, odd = lax.axis_index("sub"), lax.rem(lax.axis_index("dom"), 2)
     last = [p_refs[2 * k + i] for k in sources for i in range(2)]
     mid[...] = early_ref[...] + terms_product(rows, sources, high_ref, low_ref, last)
-    for k in range(subs):
+    for k in range(subs - 1):
         start = pl.multiple_of(lax.bitwise_xor(me, k) * COARSE_ROWS, COARSE_ROWS)
         outs[k][:, :width] = mid[pl.ds(start, COARSE_ROWS)].astype(outs[k].dtype)
         outs[k][:, width:] = edges[k][...]
@@ -203,10 +215,15 @@
 
 
 def sum_kernel(subs, width, *refs):
-    part_refs, (mid_ref, edge_ref) = refs[:subs], refs[subs:]
-    total = part_refs[0][...]
-    for k in range(1, subs):
-        total = total + part_refs[k][...].astype(F32)
+    part_refs, own_refs, (mid_ref, edge_ref, total_ref) = refs[:subs], refs[subs:-3], refs[-3:]
+    span = total_ref.shape[1]
+    total_ref[...] = part_refs[0][...]
+    for part in part_refs[1:]:
+        total_ref[...] += part[:, :span].astype(F32)
+        if part.shape[1] > span:
+            stacked = jnp.concatenate([ref[i] for ref in own_refs for i in range(ref.shape[0])], axis=0)
+            total_ref[:, :width] += jnp.dot(part[:, span:], stacked, preferred_element_type=F32)
+    total = total_ref[...]
     mid_ref[...] = total[:, :width].astype(BF16)
     sums = total[:, width:]
     high = sums.astype(BF16)
@@ -259,7 +276,10 @@
     products = 2 * width * rows * tile * width
     *edges, high, low = pl.pallas_call(
         functools.partial(terms_kernel, subs),
-        out_shape=[jax.ShapeDtypeStruct((COARSE_ROWS, span - width), kind) for kind in kinds]
+        out_shape=[
+            jax.ShapeDtypeStruct((COARSE_ROWS, span - width + (k == subs - 1) * rows * tile), kind)
+            for k, kind in enumerate(kinds)
+        ]
         + [jax.ShapeDtypeStruct((subs * rows, width, tile), BF16)] * 2,
         in_specs=[smem, smem, pl.BlockSpec(memory_space=pltpu.HBM), vmem, vmem],
         out_specs=[vmem] * (subs + 2),
@@ -278,23 +298,26 @@
         name="terms",
     )(a_cols, a_count, pltpu.with_memory_space_constraint(a_tiles, pltpu.HBM), *own)
     first, last = list(range(subs - 1)), [subs - 1]
-    early = pl.pallas_call(
-        functools.partial(early_kernel, rows, first),
-        out_shape=jax.ShapeDtypeStruct((width, width), F32),
-        in_specs=[vmem] * (2 + 2 * len(first)),
-        out_specs=vmem,
+    early, farthest = pl.pallas_call(
+        functools.partial(early_kernel, subs, rows, first),
+        out_shape=[
+            jax.ShapeDtypeStruct((width, width), F32),
+            jax.ShapeDtypeStruct((COARSE_ROWS, span + rows * tile), BF16),
+        ],
+        in_specs=[vmem] * (3 + 2 * len(first)),
+        out_specs=[vmem] * 2,
         compiler_params=pltpu.CompilerParams(vmem_limit_bytes=spare),
         cost_estimate=pl.CostEstimate(
             flops=2 * len(first) * products, bytes_accessed=1 << 20, transcendentals=0
         ),
         name="early_part",
-    )(high, low, *[piece for k in first for piece in tiles[k]])
-    return pl.pallas_call(
+    )(high, low, edges[-1], *[piece for k in first for piece in tiles[k]])
+    *parts, near, far = pl.pallas_call(
         functools.partial(late_kernel, subs, rows, last),
-        out_shape=[jax.ShapeDtypeStruct((COARSE_ROWS, span), kind) for kind in kinds]
+        out_shape=[jax.ShapeDtypeStruct((COARSE_ROWS, span), kind) for kind in kinds[:-1]]
         + [jax.ShapeDtypeStruct((rows, tile, width), BF16)] * 2,
-        in_specs=[vmem] * (3 + 3 * subs),
-        out_specs=[vmem] * (subs + 2),
+        in_specs=[vmem] * (2 + 3 * subs),
+        out_specs=[vmem] * (subs + 1),
         scratch_shapes=[
             pltpu.VMEM((width, width), F32),
             pltpu.VMEM((2 * rows, tile, width), BF16),
@@ -304,7 +327,8 @@
             flops=2 * products, bytes_accessed=1 << 20, transcendentals=0
         ),
         name="late_part",
-    )(high, low, early, *[piece for pieces in tiles for piece in pieces], *edges)
+    )(high, low, early, *[piece for pieces in tiles for piece in pieces], *edges[:-1])
+    return [*parts, farthest, near, far]
 
 
 def local(a_tiles, a_cols, a_count, p_tiles, p_cols):
@@ -425,14 +449,15 @@
             jax.ShapeDtypeStruct((COARSE_ROWS, width), BF16),
             jax.ShapeDtypeStruct((2 * COARSE_ROWS, span - width), BF16),
         ],
-        in_specs=[vmem] * subs,
+        in_specs=[vmem] * (subs + len(own)),
         out_specs=[vmem] * 2,
+        scratch_shapes=[pltpu.VMEM((COARSE_ROWS, span), F32)],
         compiler_params=pltpu.CompilerParams(vmem_limit_bytes=spare),
         cost_estimate=pl.CostEstimate(
             flops=1 << 31, bytes_accessed=8 * COARSE_ROWS * span, transcendentals=0
         ),
         name="sum_parts",
-    )(parts[0], *received)
+    )(parts[0], *received, *own)
     return pl.pallas_call(
         functools.partial(finish_kernel, subs, half),
         out_shape=jax.ShapeDtypeStruct((COARSE_ROWS, 3 * width), BF16),

time: 28.1 us -> 28.1 us (level)
  waiting for transfers between devices: 5.76 us -> 5.41 us
  starting transfers between devices: 15.7 us -> 16 us
  transfers between devices with their start and end apart: 11 -> 11, of which waited for: 3 -> 2; matrix products, arithmetic and copies ran while one was open for 0% -> 0% of each run, Pallas kernels for 14% -> 16%
where the time goes in v13:
time: 28.1 us; the launch traced here: 27.9 us
  starting transfers between devices  16 us (57%)
  Pallas kernels  6.39 us (23%)
  waiting for transfers between devices  5.41 us (19%)
    ppermute x9, starting transfers between devices, exchange(): return lax.ppermute(value, 'sub', [(s, s ^ k) for s in range(subs)])  8.81 us
    ppermute x1, starting transfers between devices, local(): lax.ppermute(to_far, 'dom', [(d, d - 1 + 2 * (d % 2)) for d in range(1, d...  7.14 us
    ppermute x1, waiting for transfers between devices, local(): lax.ppermute(to_far, 'dom', [(d, d - 1 + 2 * (d % 2)) for d in range(1, d...  3.71 us
    pallas_call x1, Pallas kernels, narrow_parts(): pl.pallas_call(functools.partial(terms_kernel, subs), out_shape=[jax.Shap...  3.24 us
    ppermute x9, waiting for transfers between devices, exchange(): return lax.ppermute(value, 'sub', [(s, s ^ k) for s in range(subs)])  1.7 us
    pallas_call x1, Pallas kernels, local(): pl.pallas_call(order_kernel, out_shape=[jax.ShapeDtypeStruct((rows // 2,...  1.02 us
    pallas_call x1, Pallas kernels, local(): pl.pallas_call(functools.partial(finish_kernel, subs, half), out_shape=ja...  0.93 us
    pallas_call x1, Pallas kernels, narrow_parts(): pl.pallas_call(functools.partial(early_kernel, subs, rows, first), out_sh...  0.58 us
  transfers between devices with their start and end apart: 11, of which 2 were waited for; matrix products, arithmetic and copies ran while one was open for 0% of the time, Pallas kernels for 16%

profile of v13, /device:TPU:1, one launch (start us, length us, event | category | flops | bytes accessed | tf_op | source)
XLA Modules:
  0.0 27.9 jit_solution(149656863608251369)
XLA Ops:
  0.0 0.0 copy-start
  0.0 0.0 copy-start.1
  0.0 1.0 %order_columns.1 = (bf16[2,128,256]{2,1,0:T(8,128)(2,1)S(1)}, bf16[2,128,256]{2,1,0:T(8,128)(2,1)S(1)}) custom-call(s32[2,4]{1,0:T(2,128)} %bitcast.1, bf16[4,128,256]{2,1,0:T(8,128)(2,1)} %p_hbm.1), custom_call_target="tpu_custom_call" | custom-call | flops 1073741824 | bytes 524288 | tf_op jit(solution)/shard_map/order_columns/pallas_call | solution.py:351
  1.0 2.1 %collective-permute-start.2 = (bf16[2,128,256]{2,1,0:T(8,128)(2,1)S(1)}, bf16[2,128,256]{2,1,0:T(8,128)(2,1)S(1)}, u32[]{:S(2)}, u32[]{:S(2)}) collective-permute-start(bf16[2,128,256]{2,1,0:T(8,128)(2,1)S(1)} %get-tuple-element.22.own_0.rest_0_.refs_4_), channel_id=1, source_target_pairs={{0,2},{1,3},{2,0},{3,1},{4,6},{5,7},{6,4},{7,5},{8,10},{9,11},{10,... | collective-permute-start | bytes 393224 | tf_op jit(solution)/shard_map/ppermute | solution.py:349
  3.2 1.2 %collective-permute-start.1 = (bf16[2,128,256]{2,1,0:T(8,128)(2,1)S(1)}, bf16[2,128,256]{2,1,0:T(8,128)(2,1)S(1)}, u32[]{:S(2)}, u32[]{:S(2)}) collective-permute-start(bf16[2,128,256]{2,1,0:T(8,128)(2,1)S(1)} %get-tuple-element.23.own_1.rest_1_.refs_5_), channel_id=1, source_target_pairs={{0,1},{1,0},{2,3},{3,2},{4,5},{5,4},{6,7},{7,6},{8,9},{9,8},{10,11... | collective-permute-start | bytes 393224 | tf_op jit(solution)/shard_map/ppermute | solution.py:349
  4.4 0.3 collective-permute-start
  4.6 0.1 collective-permute-start.3
  4.7 1.7 %collective-permute-done.2.rest_4_ = bf16[2,128,256]{2,1,0:T(8,128)(2,1)S(1)} collective-permute-done((bf16[2,128,256]{2,1,0:T(8,128)(2,1)S(1)}, bf16[2,128,256]{2,1,0:T(8,128)(2,1)S(1)}, u32[]{:S(2)}, u32[]{:S(2)}) %collective-permute-start.2) | collective-permute-done | bytes 131104 | tf_op jit(solution)/shard_map/ppermute | solution.py:349
  6.4 1.1 %collective-permute-start.4 = (bf16[2,128,256]{2,1,0:T(8,128)(2,1)S(1)}, bf16[2,128,256]{2,1,0:T(8,128)(2,1)S(1)}, u32[]{:S(2)}, u32[]{:S(2)}) collective-permute-start(bf16[2,128,256]{2,1,0:T(8,128)(2,1)S(1)} %collective-permute-done.2.rest_4_), channel_id=1, source_target_pairs={{0,1},{1,0},{2,3},{3,2},{4,5},{5,4},{6,7},{7,6},{8,9},{9,8},{10,11... | collective-permute-start | bytes 393224 | tf_op jit(solution)/shard_map/ppermute | solution.py:349
  7.5 0.0 collective-permute-done.1.rest_3_
  7.5 1.2 %collective-permute-start.5 = (bf16[2,128,256]{2,1,0:T(8,128)(2,1)S(1)}, bf16[2,128,256]{2,1,0:T(8,128)(2,1)S(1)}, u32[]{:S(2)}, u32[]{:S(2)}) collective-permute-start(bf16[2,128,256]{2,1,0:T(8,128)(2,1)S(1)} %collective-permute-done.1.rest_3_), channel_id=1, source_target_pairs={{0,2},{1,3},{2,0},{3,1},{4,6},{5,7},{6,4},{7,5},{8,10},{9,11},{10,... | collective-permute-start | bytes 393224 | tf_op jit(solution)/shard_map/ppermute | solution.py:349
  8.7 0.0 copy-done
  8.7 0.0 copy-done.1
  8.7 3.2 %terms.1 = (f32[64,1024]{1,0:T(8,128)S(1)}, bf16[64,1024]{1,0:T(8,128)(2,1)S(1)}, bf16[64,1024]{1,0:T(8,128)(2,1)S(1)}, bf16[64,1536]{1,0:T(8,128)(2,1)S(1)}, bf...) custom-call(s32[4,10]{1,0:T(4,128)S(1)} %copy-done, s32[4]{0:T(128)S(1)} %copy-done.1, ...), custom_call_target="tpu_custom_call" | custom-call | flops 2147483648 | bytes 1310720 | tf_op jit(solution)/shard_map/terms/pallas_call | solution.py:277
  12.0 0.0 collective-permute-done.rest_2_
  12.0 0.0 collective-permute-done.3.rest_5_
  12.0 0.6 %early_part.1 = (f32[256,256]{1,0:T(8,128)S(1)}, bf16[64,1792]{1,0:T(8,128)(2,1)S(1)}) custom-call(bf16[16,256,128]{2,1,0:T(8,128)(2,1)S(1)} %get-tuple-element.24.high_ref, bf16[16,256,128]{2,1,0:T(8,128)(2,1)S(1)} %get-tuple-element.25.low_ref, bf16[64,1536]{1,0:T(8,128)(2,1)S(1)} %get-tuple-element.26.edge_ref, ...), custom_call_target="tpu_custom_call" | custom-call | flops 402653184 | bytes 1048576 | tf_op jit(solution)/shard_map/early_part/pallas_call | solution.py:301
  12.6 1.0 %collective-permute-start.8 = (bf16[64,1792]{1,0:T(8,128)(2,1)S(1)}, bf16[64,1792]{1,0:T(8,128)(2,1)S(1)}, u32[]{:S(2)}, u32[]{:S(2)}) collective-permute-start(bf16[64,1792]{1,0:T(8,128)(2,1)S(1)} %get-tuple-element.34), channel_id=1, source_target_pairs={{0,3},{1,2},{2,1},{3,0},{4,7},{5,6},{6,5},{7,4},{8,11},{9,10},{10,... | collective-permute-start | bytes 688136 | tf_op jit(solution)/shard_map/ppermute | solution.py:349
  13.6 0.0 collective-permute-done.4.rest_6_
  13.6 0.0 collective-permute-done.5.rest_7_
  13.6 0.4 %late_part.1 = (f32[64,1280]{1,0:T(8,128)S(1)}, bf16[64,1280]{1,0:T(8,128)(2,1)S(1)}, bf16[64,1280]{1,0:T(8,128)(2,1)S(1)}, bf16[4,128,256]{2,1,0:T(8,128)(2,1)S(1)}, bf16[4,128,256]{2,1,0:T(8,128)(2,1)S(1)}) custom-call(bf16[16,256,128]{2,1,0:T(8,128)(2,1)S(1)} %get-tuple-element.24.high_ref, bf16[16,256,128]{2,1,0:T(8,128)(2,1)S(1)} %get-tuple-element.25.low_ref, ...), custom_call_target="tpu_custom_call" | custom-call | flops 134217728 | bytes 1048576 | tf_op jit(solution)/shard_map/late_part/pallas_call | solution.py:315
  14.0 0.6 %collective-permute-start.9 = (bf16[64,1280]{1,0:T(8,128)(2,1)S(1)}, bf16[64,1280]{1,0:T(8,128)(2,1)S(1)}, u32[]{:S(2)}, u32[]{:S(2)}) collective-permute-start(bf16[64,1280]{1,0:T(8,128)(2,1)S(1)} %get-tuple-element.35), channel_id=1, source_target_pairs={{0,2},{1,3},{2,0},{3,1},{4,6},{5,7},{6,4},{7,5},{8,10},{9,11},{10,... | collective-permute-start | bytes 491528 | tf_op jit(solution)/shard_map/ppermute | solution.py:349
  14.6 1.2 %collective-permute-start.10 = (bf16[64,1280]{1,0:T(8,128)(2,1)S(1)}, bf16[64,1280]{1,0:T(8,128)(2,1)S(1)}, u32[]{:S(2)}, u32[]{:S(2)}) collective-permute-start(bf16[64,1280]{1,0:T(8,128)(2,1)S(1)} %get-tuple-element.36), channel_id=1, source_target_pairs={{0,1},{1,0},{2,3},{3,2},{4,5},{5,4},{6,7},{7,6},{8,9},{9,8},{10,11... | collective-permute-start | bytes 491528 | tf_op jit(solution)/shard_map/ppermute | solution.py:349
  15.8 7.1 %collective-permute-start.6 = (bf16[4,128,256]{2,1,0:T(8,128)(2,1)S(1)}, bf16[4,128,256]{2,1,0:T(8,128)(2,1)S(1)}, u32[]{:S(2)}, u32[]{:S(2)}) collective-permute-start(bf16[4,128,256]{2,1,0:T(8,128)(2,1)S(1)} %get-tuple-element.31), channel_id=1, source_target_pairs={{4,8},{8,4},{12,16},{16,12},{20,24},{24,20},{5,9},{9,5},{13,17},{1... | collective-permute-start | bytes 786440 | tf_op jit(solution)/shard_map/ppermute | solution.py:442
  23.0 0.1 collective-permute-start.7
  23.0 0.0 collective-permute-done.8.refs_1_
  23.1 0.0 collective-permute-done.9.refs_2_
  23.1 0.0 collective-permute-done.10.refs_3_
  23.1 0.2 sum_parts.1
  23.3 3.7 %collective-permute-done.6.refs_0_ = bf16[4,128,256]{2,1,0:T(8,128)(2,1)S(1)} collective-permute-done((bf16[4,128,256]{2,1,0:T(8,128)(2,1)S(1)}, bf16[4,128,256]{2,1,0:T(8,128)(2,1)S(1)}, u32[]{:S(2)}, u32[]{:S(2)}) %collective-permute-start.6) | collective-permute-done | bytes 262176 | tf_op jit(solution)/shard_map/ppermute | solution.py:442
  27.0 0.0 collective-permute-done.7.refs_1_
  27.0 0.9 %finish.1 = bf16[64,768]{1,0:T(8,128)(2,1)} custom-call(bf16[4,128,256]{2,1,0:T(8,128)(2,1)S(1)} %collective-permute-done.6.refs_0_, bf16[4,128,256]{2,1,0:T(8,128)(2,1)S(1)} %collective-permute-done.7.refs_1_, bf16[64,256]{1,0:T(8,128)(2,1)S(1)} %get-tuple-element.37.refs_2_, bf16[128,1024]{1,0:T(8,128)(2,1)S(1)} %get-tuple-element.38.refs_3_), custom_call_target="tpu_custom_call" | custom-call | flops 268435456 | bytes 1048576 | tf_op jit(solution)/shard_map/finish/pallas_call | solution.py:461
Async XLA Ops:
  0.0 8.7 %copy-start = (s32[4,10]{1,0:T(4,128)S(1)}, s32[4,10]{1,0:T(4,128)}, u32[]{:S(2)}) copy-start(s32[4,10]{1,0:T(4,128)} %cols_ref.1) | copy-start | bytes 484
  0.0 8.7 %copy-start.1 = (s32[4]{0:T(128)S(1)}, s32[4]{0:T(128)}, u32[]{:S(2)}) copy-start(s32[4]{0:T(128)} %count_ref.1) | copy-start | bytes 52
  1.0 5.4 %collective-permute-start.2 = (bf16[2,128,256]{2,1,0:T(8,128)(2,1)S(1)}, bf16[2,128,256]{2,1,0:T(8,128)(2,1)S(1)}, u32[]{:S(2)}, u32[]{:S(2)}) collective-permute-start(bf16[2,128,256]{2,1,0:T(8,128)(2,1)S(1)} %get-tuple-element.22.own_0.rest_0_.refs_4_), channel_id=1, source_target_pairs={{0,2},{1,3},{2,0},{3,1},{4,6},{5,7},{6,4},{7,5},{8,10},{9,11},{10,... | collective-permute-start | bytes 393224 | tf_op jit(solution)/shard_map/ppermute | solution.py:349
  3.2 4.3 %collective-permute-start.1 = (bf16[2,128,256]{2,1,0:T(8,128)(2,1)S(1)}, bf16[2,128,256]{2,1,0:T(8,128)(2,1)S(1)}, u32[]{:S(2)}, u32[]{:S(2)}) collective-permute-start(bf16[2,128,256]{2,1,0:T(8,128)(2,1)S(1)} %get-tuple-element.23.own_1.rest_1_.refs_5_), channel_id=1, source_target_pairs={{0,1},{1,0},{2,3},{3,2},{4,5},{5,4},{6,7},{7,6},{8,9},{9,8},{10,11... | collective-permute-start | bytes 393224 | tf_op jit(solution)/shard_map/ppermute | solution.py:349
  4.4 7.6 %collective-permute-start = (bf16[2,128,256]{2,1,0:T(8,128)(2,1)S(1)}, bf16[2,128,256]{2,1,0:T(8,128)(2,1)S(1)}, u32[]{:S(2)}, u32[]{:S(2)}) collective-permute-start(bf16[2,128,256]{2,1,0:T(8,128)(2,1)S(1)} %get-tuple-element.22.own_0.rest_0_.refs_4_), channel_id=1, source_target_pairs={{0,1},{1,0},{2,3},{3,2},{4,5},{5,4},{6,7},{7,6},{8,9},{9,8},{10,11... | collective-permute-start | bytes 393224 | tf_op jit(solution)/shard_map/ppermute | solution.py:349
  4.6 7.4 %collective-permute-start.3 = (bf16[2,128,256]{2,1,0:T(8,128)(2,1)S(1)}, bf16[2,128,256]{2,1,0:T(8,128)(2,1)S(1)}, u32[]{:S(2)}, u32[]{:S(2)}) collective-permute-start(bf16[2,128,256]{2,1,0:T(8,128)(2,1)S(1)} %get-tuple-element.23.own_1.rest_1_.refs_5_), channel_id=1, source_target_pairs={{0,2},{1,3},{2,0},{3,1},{4,6},{5,7},{6,4},{7,5},{8,10},{9,11},{10,... | collective-permute-start | bytes 393224 | tf_op jit(solution)/shard_map/ppermute | solution.py:349
  6.4 7.2 %collective-permute-start.4 = (bf16[2,128,256]{2,1,0:T(8,128)(2,1)S(1)}, bf16[2,128,256]{2,1,0:T(8,128)(2,1)S(1)}, u32[]{:S(2)}, u32[]{:S(2)}) collective-permute-start(bf16[2,128,256]{2,1,0:T(8,128)(2,1)S(1)} %collective-permute-done.2.rest_4_), channel_id=1, source_target_pairs={{0,1},{1,0},{2,3},{3,2},{4,5},{5,4},{6,7},{7,6},{8,9},{9,8},{10,11... | collective-permute-start | bytes 393224 | tf_op jit(solution)/shard_map/ppermute | solution.py:349
  7.5 6.1 %collective-permute-start.5 = (bf16[2,128,256]{2,1,0:T(8,128)(2,1)S(1)}, bf16[2,128,256]{2,1,0:T(8,128)(2,1)S(1)}, u32[]{:S(2)}, u32[]{:S(2)}) collective-permute-start(bf16[2,128,256]{2,1,0:T(8,128)(2,1)S(1)} %collective-permute-done.1.rest_3_), channel_id=1, source_target_pairs={{0,2},{1,3},{2,0},{3,1},{4,6},{5,7},{6,4},{7,5},{8,10},{9,11},{10,... | collective-permute-start | bytes 393224 | tf_op jit(solution)/shard_map/ppermute | solution.py:349
  12.6 10.4 %collective-permute-start.8 = (bf16[64,1792]{1,0:T(8,128)(2,1)S(1)}, bf16[64,1792]{1,0:T(8,128)(2,1)S(1)}, u32[]{:S(2)}, u32[]{:S(2)}) collective-permute-start(bf16[64,1792]{1,0:T(8,128)(2,1)S(1)} %get-tuple-element.34), channel_id=1, source_target_pairs={{0,3},{1,2},{2,1},{3,0},{4,7},{5,6},{6,5},{7,4},{8,11},{9,10},{10,... | collective-permute-start | bytes 688136 | tf_op jit(solution)/shard_map/ppermute | solution.py:349
  14.0 9.0 %collective-permute-start.9 = (bf16[64,1280]{1,0:T(8,128)(2,1)S(1)}, bf16[64,1280]{1,0:T(8,128)(2,1)S(1)}, u32[]{:S(2)}, u32[]{:S(2)}) collective-permute-start(bf16[64,1280]{1,0:T(8,128)(2,1)S(1)} %get-tuple-element.35), channel_id=1, source_target_pairs={{0,2},{1,3},{2,0},{3,1},{4,6},{5,7},{6,4},{7,5},{8,10},{9,11},{10,... | collective-permute-start | bytes 491528 | tf_op jit(solution)/shard_map/ppermute | solution.py:349
  14.6 8.5 %collective-permute-start.10 = (bf16[64,1280]{1,0:T(8,128)(2,1)S(1)}, bf16[64,1280]{1,0:T(8,128)(2,1)S(1)}, u32[]{:S(2)}, u32[]{:S(2)}) collective-permute-start(bf16[64,1280]{1,0:T(8,128)(2,1)S(1)} %get-tuple-element.36), channel_id=1, source_target_pairs={{0,1},{1,0},{2,3},{3,2},{4,5},{5,4},{6,7},{7,6},{8,9},{9,8},{10,11... | collective-permute-start | bytes 491528 | tf_op jit(solution)/shard_map/ppermute | solution.py:349
  15.8 11.2 %collective-permute-start.6 = (bf16[4,128,256]{2,1,0:T(8,128)(2,1)S(1)}, bf16[4,128,256]{2,1,0:T(8,128)(2,1)S(1)}, u32[]{:S(2)}, u32[]{:S(2)}) collective-permute-start(bf16[4,128,256]{2,1,0:T(8,128)(2,1)S(1)} %get-tuple-element.31), channel_id=1, source_target_pairs={{4,8},{8,4},{12,16},{16,12},{20,24},{24,20},{5,9},{9,5},{13,17},{1... | collective-permute-start | bytes 786440 | tf_op jit(solution)/shard_map/ppermute | solution.py:442
  23.0 4.0 %collective-permute-start.7 = (bf16[4,128,256]{2,1,0:T(8,128)(2,1)S(1)}, bf16[4,128,256]{2,1,0:T(8,128)(2,1)S(1)}, u32[]{:S(2)}, u32[]{:S(2)}) collective-permute-start(bf16[4,128,256]{2,1,0:T(8,128)(2,1)S(1)} %get-tuple-element.32), channel_id=1, source_target_pairs={{0,4},{4,0},{8,12},{12,8},{16,20},{20,16},{24,28},{28,24},{1,5},{5... | collective-permute-start | bytes 786440 | tf_op jit(solution)/shard_map/ppermute | solution.py:445

commit v14 on v13

--- a/solution.py
+++ b/solution.py
@@ -109,9 +109,13 @@
         turned[f] = (own_0, own_1)[f // (rows // 2)][f % (rows // 2)].T
     for f in range(rows):
         loads[f].wait()
-        for k in range(slots):
-            at = jnp.where(k < count_ref[f], cols_ref[f, k] - base, tiles)
-            total[at] += jnp.dot(turned[f], a_ref[f, k], preferred_element_type=F32)
+        for k in range(0, slots, 2):
+            pair = range(k, min(k + 2, slots))
+            side = jnp.concatenate([a_ref[f, i] for i in pair], axis=1)
+            terms = jnp.dot(turned[f], side, preferred_element_type=F32)
+            for i in pair:
+                at = jnp.where(i < count_ref[f], cols_ref[f, i] - base, tiles)
+                total[at] += terms[:, (i - k) * tile : (i - k + 1) * tile]
     for c in range(subs * rows):
         value = total[rows + c]
         high = value.astype(BF16)

time: 28.1 us -> 28.3 us (level)
  no operation moved by 1% of the time
where the time goes in v14:
time: 28.3 us; the launch traced here: 28.1 us
  starting transfers between devices  16 us (57%)
  Pallas kernels  6.55 us (23%)
  waiting for transfers between devices  5.41 us (19%)
    ppermute x9, starting transfers between devices, exchange(): return lax.ppermute(value, 'sub', [(s, s ^ k) for s in range(subs)])  8.82 us
    ppermute x1, starting transfers between devices, local(): lax.ppermute(to_far, 'dom', [(d, d - 1 + 2 * (d % 2)) for d in range(1, d...  7.14 us
    ppermute x1, waiting for transfers between devices, local(): lax.ppermute(to_far, 'dom', [(d, d - 1 + 2 * (d % 2)) for d in range(1, d...  3.71 us
    pallas_call x1, Pallas kernels, narrow_parts(): pl.pallas_call(functools.partial(terms_kernel, subs), out_shape=[jax.Shap...  3.41 us
    ppermute x9, waiting for transfers between devices, exchange(): return lax.ppermute(value, 'sub', [(s, s ^ k) for s in range(subs)])  1.7 us
    pallas_call x1, Pallas kernels, local(): pl.pallas_call(order_kernel, out_shape=[jax.ShapeDtypeStruct((rows // 2,...  1.02 us
    pallas_call x1, Pallas kernels, local(): pl.pallas_call(functools.partial(finish_kernel, subs, half), out_shape=ja...  0.93 us
    pallas_call x1, Pallas kernels, narrow_parts(): pl.pallas_call(functools.partial(early_kernel, subs, rows, first), out_sh...  0.58 us
  transfers between devices with their start and end apart: 11, of which 2 were waited for; matrix products, arithmetic and copies ran while one was open for 0% of the time, Pallas kernels for 16%

profile of v14, /device:TPU:1, one launch (start us, length us, event | category | flops | bytes accessed | tf_op | source)
XLA Modules:
  0.0 28.1 jit_solution(10527993523709522329)
XLA Ops:
  0.0 0.0 copy-start
  0.0 0.0 copy-start.1
  0.0 1.0 %order_columns.1 = (bf16[2,128,256]{2,1,0:T(8,128)(2,1)S(1)}, bf16[2,128,256]{2,1,0:T(8,128)(2,1)S(1)}) custom-call(s32[2,4]{1,0:T(2,128)} %bitcast.1, bf16[4,128,256]{2,1,0:T(8,128)(2,1)} %p_hbm.1), custom_call_target="tpu_custom_call" | custom-call | flops 1073741824 | bytes 524288 | tf_op jit(solution)/shard_map/order_columns/pallas_call | solution.py:355
  1.0 2.1 %collective-permute-start.2 = (bf16[2,128,256]{2,1,0:T(8,128)(2,1)S(1)}, bf16[2,128,256]{2,1,0:T(8,128)(2,1)S(1)}, u32[]{:S(2)}, u32[]{:S(2)}) collective-permute-start(bf16[2,128,256]{2,1,0:T(8,128)(2,1)S(1)} %get-tuple-element.22.own_0.rest_0_.refs_4_), channel_id=1, source_target_pairs={{0,2},{1,3},{2,0},{3,1},{4,6},{5,7},{6,4},{7,5},{8,10},{9,11},{10,... | collective-permute-start | bytes 393224 | tf_op jit(solution)/shard_map/ppermute | solution.py:353
  3.2 1.2 %collective-permute-start.1 = (bf16[2,128,256]{2,1,0:T(8,128)(2,1)S(1)}, bf16[2,128,256]{2,1,0:T(8,128)(2,1)S(1)}, u32[]{:S(2)}, u32[]{:S(2)}) collective-permute-start(bf16[2,128,256]{2,1,0:T(8,128)(2,1)S(1)} %get-tuple-element.23.own_1.rest_1_.refs_5_), channel_id=1, source_target_pairs={{0,1},{1,0},{2,3},{3,2},{4,5},{5,4},{6,7},{7,6},{8,9},{9,8},{10,11... | collective-permute-start | bytes 393224 | tf_op jit(solution)/shard_map/ppermute | solution.py:353
  4.4 0.3 collective-permute-start
  4.6 0.1 collective-permute-start.3
  4.7 1.7 %collective-permute-done.2.rest_4_ = bf16[2,128,256]{2,1,0:T(8,128)(2,1)S(1)} collective-permute-done((bf16[2,128,256]{2,1,0:T(8,128)(2,1)S(1)}, bf16[2,128,256]{2,1,0:T(8,128)(2,1)S(1)}, u32[]{:S(2)}, u32[]{:S(2)}) %collective-permute-start.2) | collective-permute-done | bytes 131104 | tf_op jit(solution)/shard_map/ppermute | solution.py:353
  6.4 1.1 %collective-permute-start.4 = (bf16[2,128,256]{2,1,0:T(8,128)(2,1)S(1)}, bf16[2,128,256]{2,1,0:T(8,128)(2,1)S(1)}, u32[]{:S(2)}, u32[]{:S(2)}) collective-permute-start(bf16[2,128,256]{2,1,0:T(8,128)(2,1)S(1)} %collective-permute-done.2.rest_4_), channel_id=1, source_target_pairs={{0,1},{1,0},{2,3},{3,2},{4,5},{5,4},{6,7},{7,6},{8,9},{9,8},{10,11... | collective-permute-start | bytes 393224 | tf_op jit(solution)/shard_map/ppermute | solution.py:353
  7.5 0.0 collective-permute-done.1.rest_3_
  7.5 1.2 %collective-permute-start.5 = (bf16[2,128,256]{2,1,0:T(8,128)(2,1)S(1)}, bf16[2,128,256]{2,1,0:T(8,128)(2,1)S(1)}, u32[]{:S(2)}, u32[]{:S(2)}) collective-permute-start(bf16[2,128,256]{2,1,0:T(8,128)(2,1)S(1)} %collective-permute-done.1.rest_3_), channel_id=1, source_target_pairs={{0,2},{1,3},{2,0},{3,1},{4,6},{5,7},{6,4},{7,5},{8,10},{9,11},{10,... | collective-permute-start | bytes 393224 | tf_op jit(solution)/shard_map/ppermute | solution.py:353
  8.7 0.0 copy-done
  8.7 0.0 copy-done.1
  8.7 3.4 %terms.1 = (f32[64,1024]{1,0:T(8,128)S(1)}, bf16[64,1024]{1,0:T(8,128)(2,1)S(1)}, bf16[64,1024]{1,0:T(8,128)(2,1)S(1)}, bf16[64,1536]{1,0:T(8,128)(2,1)S(1)}, bf...) custom-call(s32[4,10]{1,0:T(4,128)S(1)} %copy-done, s32[4]{0:T(128)S(1)} %copy-done.1, ...), custom_call_target="tpu_custom_call" | custom-call | flops 2147483648 | bytes 1310720 | tf_op jit(solution)/shard_map/terms/pallas_call | solution.py:281
  12.2 0.0 collective-permute-done.rest_2_
  12.2 0.0 collective-permute-done.3.rest_5_
  12.2 0.6 %early_part.1 = (f32[256,256]{1,0:T(8,128)S(1)}, bf16[64,1792]{1,0:T(8,128)(2,1)S(1)}) custom-call(bf16[16,256,128]{2,1,0:T(8,128)(2,1)S(1)} %get-tuple-element.24.high_ref, bf16[16,256,128]{2,1,0:T(8,128)(2,1)S(1)} %get-tuple-element.25.low_ref, bf16[64,1536]{1,0:T(8,128)(2,1)S(1)} %get-tuple-element.26.edge_ref, ...), custom_call_target="tpu_custom_call" | custom-call | flops 402653184 | bytes 1048576 | tf_op jit(solution)/shard_map/early_part/pallas_call | solution.py:305
  12.8 1.0 %collective-permute-start.8 = (bf16[64,1792]{1,0:T(8,128)(2,1)S(1)}, bf16[64,1792]{1,0:T(8,128)(2,1)S(1)}, u32[]{:S(2)}, u32[]{:S(2)}) collective-permute-start(bf16[64,1792]{1,0:T(8,128)(2,1)S(1)} %get-tuple-element.34), channel_id=1, source_target_pairs={{0,3},{1,2},{2,1},{3,0},{4,7},{5,6},{6,5},{7,4},{8,11},{9,10},{10,... | collective-permute-start | bytes 688136 | tf_op jit(solution)/shard_map/ppermute | solution.py:353
  13.8 0.0 collective-permute-done.4.rest_6_
  13.8 0.0 collective-permute-done.5.rest_7_
  13.8 0.4 %late_part.1 = (f32[64,1280]{1,0:T(8,128)S(1)}, bf16[64,1280]{1,0:T(8,128)(2,1)S(1)}, bf16[64,1280]{1,0:T(8,128)(2,1)S(1)}, bf16[4,128,256]{2,1,0:T(8,128)(2,1)S(1)}, bf16[4,128,256]{2,1,0:T(8,128)(2,1)S(1)}) custom-call(bf16[16,256,128]{2,1,0:T(8,128)(2,1)S(1)} %get-tuple-element.24.high_ref, bf16[16,256,128]{2,1,0:T(8,128)(2,1)S(1)} %get-tuple-element.25.low_ref, ...), custom_call_target="tpu_custom_call" | custom-call | flops 134217728 | bytes 1048576 | tf_op jit(solution)/shard_map/late_part/pallas_call | solution.py:319
  14.2 0.6 %collective-permute-start.9 = (bf16[64,1280]{1,0:T(8,128)(2,1)S(1)}, bf16[64,1280]{1,0:T(8,128)(2,1)S(1)}, u32[]{:S(2)}, u32[]{:S(2)}) collective-permute-start(bf16[64,1280]{1,0:T(8,128)(2,1)S(1)} %get-tuple-element.35), channel_id=1, source_target_pairs={{0,2},{1,3},{2,0},{3,1},{4,6},{5,7},{6,4},{7,5},{8,10},{9,11},{10,... | collective-permute-start | bytes 491528 | tf_op jit(solution)/shard_map/ppermute | solution.py:353
  14.8 1.2 %collective-permute-start.10 = (bf16[64,1280]{1,0:T(8,128)(2,1)S(1)}, bf16[64,1280]{1,0:T(8,128)(2,1)S(1)}, u32[]{:S(2)}, u32[]{:S(2)}) collective-permute-start(bf16[64,1280]{1,0:T(8,128)(2,1)S(1)} %get-tuple-element.36), channel_id=1, source_target_pairs={{0,1},{1,0},{2,3},{3,2},{4,5},{5,4},{6,7},{7,6},{8,9},{9,8},{10,11... | collective-permute-start | bytes 491528 | tf_op jit(solution)/shard_map/ppermute | solution.py:353
  16.0 7.1 %collective-permute-start.6 = (bf16[4,128,256]{2,1,0:T(8,128)(2,1)S(1)}, bf16[4,128,256]{2,1,0:T(8,128)(2,1)S(1)}, u32[]{:S(2)}, u32[]{:S(2)}) collective-permute-start(bf16[4,128,256]{2,1,0:T(8,128)(2,1)S(1)} %get-tuple-element.31), channel_id=1, source_target_pairs={{4,8},{8,4},{12,16},{16,12},{20,24},{24,20},{5,9},{9,5},{13,17},{1... | collective-permute-start | bytes 786440 | tf_op jit(solution)/shard_map/ppermute | solution.py:446
  23.1 0.1 collective-permute-start.7
  23.2 0.0 collective-permute-done.8.refs_1_
  23.2 0.0 collective-permute-done.9.refs_2_
  23.2 0.0 collective-permute-done.10.refs_3_
  23.2 0.2 sum_parts.1
  23.5 3.7 %collective-permute-done.6.refs_0_ = bf16[4,128,256]{2,1,0:T(8,128)(2,1)S(1)} collective-permute-done((bf16[4,128,256]{2,1,0:T(8,128)(2,1)S(1)}, bf16[4,128,256]{2,1,0:T(8,128)(2,1)S(1)}, u32[]{:S(2)}, u32[]{:S(2)}) %collective-permute-start.6) | collective-permute-done | bytes 262176 | tf_op jit(solution)/shard_map/ppermute | solution.py:446
  27.2 0.0 collective-permute-done.7.refs_1_
  27.2 0.9 %finish.1 = bf16[64,768]{1,0:T(8,128)(2,1)} custom-call(bf16[4,128,256]{2,1,0:T(8,128)(2,1)S(1)} %collective-permute-done.6.refs_0_, bf16[4,128,256]{2,1,0:T(8,128)(2,1)S(1)} %collective-permute-done.7.refs_1_, bf16[64,256]{1,0:T(8,128)(2,1)S(1)} %get-tuple-element.37.refs_2_, bf16[128,1024]{1,0:T(8,128)(2,1)S(1)} %get-tuple-element.38.refs_3_), custom_call_target="tpu_custom_call" | custom-call | flops 268435456 | bytes 1048576 | tf_op jit(solution)/shard_map/finish/pallas_call | solution.py:465
Async XLA Ops:
  0.0 8.7 %copy-start = (s32[4,10]{1,0:T(4,128)S(1)}, s32[4,10]{1,0:T(4,128)}, u32[]{:S(2)}) copy-start(s32[4,10]{1,0:T(4,128)} %cols_ref.1) | copy-start | bytes 484
  0.0 8.7 %copy-start.1 = (s32[4]{0:T(128)S(1)}, s32[4]{0:T(128)}, u32[]{:S(2)}) copy-start(s32[4]{0:T(128)} %count_ref.1) | copy-start | bytes 52
  1.0 5.4 %collective-permute-start.2 = (bf16[2,128,256]{2,1,0:T(8,128)(2,1)S(1)}, bf16[2,128,256]{2,1,0:T(8,128)(2,1)S(1)}, u32[]{:S(2)}, u32[]{:S(2)}) collective-permute-start(bf16[2,128,256]{2,1,0:T(8,128)(2,1)S(1)} %get-tuple-element.22.own_0.rest_0_.refs_4_), channel_id=1, source_target_pairs={{0,2},{1,3},{2,0},{3,1},{4,6},{5,7},{6,4},{7,5},{8,10},{9,11},{10,... | collective-permute-start | bytes 393224 | tf_op jit(solution)/shard_map/ppermute | solution.py:353
  3.2 4.3 %collective-permute-start.1 = (bf16[2,128,256]{2,1,0:T(8,128)(2,1)S(1)}, bf16[2,128,256]{2,1,0:T(8,128)(2,1)S(1)}, u32[]{:S(2)}, u32[]{:S(2)}) collective-permute-start(bf16[2,128,256]{2,1,0:T(8,128)(2,1)S(1)} %get-tuple-element.23.own_1.rest_1_.refs_5_), channel_id=1, source_target_pairs={{0,1},{1,0},{2,3},{3,2},{4,5},{5,4},{6,7},{7,6},{8,9},{9,8},{10,11... | collective-permute-start | bytes 393224 | tf_op jit(solution)/shard_map/ppermute | solution.py:353
  4.4 7.8 %collective-permute-start = (bf16[2,128,256]{2,1,0:T(8,128)(2,1)S(1)}, bf16[2,128,256]{2,1,0:T(8,128)(2,1)S(1)}, u32[]{:S(2)}, u32[]{:S(2)}) collective-permute-start(bf16[2,128,256]{2,1,0:T(8,128)(2,1)S(1)} %get-tuple-element.22.own_0.rest_0_.refs_4_), channel_id=1, source_target_pairs={{0,1},{1,0},{2,3},{3,2},{4,5},{5,4},{6,7},{7,6},{8,9},{9,8},{10,11... | collective-permute-start | bytes 393224 | tf_op jit(solution)/shard_map/ppermute | solution.py:353
  4.6 7.5 %collective-permute-start.3 = (bf16[2,128,256]{2,1,0:T(8,128)(2,1)S(1)}, bf16[2,128,256]{2,1,0:T(8,128)(2,1)S(1)}, u32[]{:S(2)}, u32[]{:S(2)}) collective-permute-start(bf16[2,128,256]{2,1,0:T(8,128)(2,1)S(1)} %get-tuple-element.23.own_1.rest_1_.refs_5_), channel_id=1, source_target_pairs={{0,2},{1,3},{2,0},{3,1},{4,6},{5,7},{6,4},{7,5},{8,10},{9,11},{10,... | collective-permute-start | bytes 393224 | tf_op jit(solution)/shard_map/ppermute | solution.py:353
  6.4 7.4 %collective-permute-start.4 = (bf16[2,128,256]{2,1,0:T(8,128)(2,1)S(1)}, bf16[2,128,256]{2,1,0:T(8,128)(2,1)S(1)}, u32[]{:S(2)}, u32[]{:S(2)}) collective-permute-start(bf16[2,128,256]{2,1,0:T(8,128)(2,1)S(1)} %collective-permute-done.2.rest_4_), channel_id=1, source_target_pairs={{0,1},{1,0},{2,3},{3,2},{4,5},{5,4},{6,7},{7,6},{8,9},{9,8},{10,11... | collective-permute-start | bytes 393224 | tf_op jit(solution)/shard_map/ppermute | solution.py:353
  7.5 6.3 %collective-permute-start.5 = (bf16[2,128,256]{2,1,0:T(8,128)(2,1)S(1)}, bf16[2,128,256]{2,1,0:T(8,128)(2,1)S(1)}, u32[]{:S(2)}, u32[]{:S(2)}) collective-permute-start(bf16[2,128,256]{2,1,0:T(8,128)(2,1)S(1)} %collective-permute-done.1.rest_3_), channel_id=1, source_target_pairs={{0,2},{1,3},{2,0},{3,1},{4,6},{5,7},{6,4},{7,5},{8,10},{9,11},{10,... | collective-permute-start | bytes 393224 | tf_op jit(solution)/shard_map/ppermute | solution.py:353
  12.8 10.4 %collective-permute-start.8 = (bf16[64,1792]{1,0:T(8,128)(2,1)S(1)}, bf16[64,1792]{1,0:T(8,128)(2,1)S(1)}, u32[]{:S(2)}, u32[]{:S(2)}) collective-permute-start(bf16[64,1792]{1,0:T(8,128)(2,1)S(1)} %get-tuple-element.34), channel_id=1, source_target_pairs={{0,3},{1,2},{2,1},{3,0},{4,7},{5,6},{6,5},{7,4},{8,11},{9,10},{10,... | collective-permute-start | bytes 688136 | tf_op jit(solution)/shard_map/ppermute | solution.py:353
  14.2 9.0 %collective-permute-start.9 = (bf16[64,1280]{1,0:T(8,128)(2,1)S(1)}, bf16[64,1280]{1,0:T(8,128)(2,1)S(1)}, u32[]{:S(2)}, u32[]{:S(2)}) collective-permute-start(bf16[64,1280]{1,0:T(8,128)(2,1)S(1)} %get-tuple-element.35), channel_id=1, source_target_pairs={{0,2},{1,3},{2,0},{3,1},{4,6},{5,7},{6,4},{7,5},{8,10},{9,11},{10,... | collective-permute-start | bytes 491528 | tf_op jit(solution)/shard_map/ppermute | solution.py:353
  14.8 8.5 %collective-permute-start.10 = (bf16[64,1280]{1,0:T(8,128)(2,1)S(1)}, bf16[64,1280]{1,0:T(8,128)(2,1)S(1)}, u32[]{:S(2)}, u32[]{:S(2)}) collective-permute-start(bf16[64,1280]{1,0:T(8,128)(2,1)S(1)} %get-tuple-element.36), channel_id=1, source_target_pairs={{0,1},{1,0},{2,3},{3,2},{4,5},{5,4},{6,7},{7,6},{8,9},{9,8},{10,11... | collective-permute-start | bytes 491528 | tf_op jit(solution)/shard_map/ppermute | solution.py:353
  16.0 11.2 %collective-permute-start.6 = (bf16[4,128,256]{2,1,0:T(8,128)(2,1)S(1)}, bf16[4,128,256]{2,1,0:T(8,128)(2,1)S(1)}, u32[]{:S(2)}, u32[]{:S(2)}) collective-permute-start(bf16[4,128,256]{2,1,0:T(8,128)(2,1)S(1)} %get-tuple-element.31), channel_id=1, source_target_pairs={{4,8},{8,4},{12,16},{16,12},{20,24},{24,20},{5,9},{9,5},{13,17},{1... | collective-permute-start | bytes 786440 | tf_op jit(solution)/shard_map/ppermute | solution.py:446
  23.1 4.0 %collective-permute-start.7 = (bf16[4,128,256]{2,1,0:T(8,128)(2,1)S(1)}, bf16[4,128,256]{2,1,0:T(8,128)(2,1)S(1)}, u32[]{:S(2)}, u32[]{:S(2)}) collective-permute-start(bf16[4,128,256]{2,1,0:T(8,128)(2,1)S(1)} %get-tuple-element.32), channel_id=1, source_target_pairs={{0,4},{4,0},{8,12},{12,8},{16,20},{20,16},{24,28},{28,24},{1,5},{5... | collective-permute-start | bytes 786440 | tf_op jit(solution)/shard_map/ppermute | solution.py:449

commit v15 on v13

--- a/solution.py
+++ b/solution.py
@@ -96,36 +96,45 @@
 
 
 def terms_kernel(subs, cols_ref, count_ref, a_hbm, own_0, own_1, *rest):
-    edges, (high_ref, low_ref, a_ref, total, turned, sems) = rest[:subs], rest[subs:]
+    edges, (high_ref, low_ref, a_ref, upper, lower, turned, sems) = rest[:subs], rest[subs:]
     rows, slots, tile = a_ref.shape[:3]
-    tiles = total.shape[0] - 1
+    tiles = upper.shape[0] - 1
+    middle = upper.shape[1]
     me = lax.axis_index("sub")
     base = lax.axis_index("dom") * (subs * rows) - rows
     loads = [pltpu.make_async_copy(a_hbm.at[f], a_ref.at[f], sems.at[f]) for f in range(rows)]
     for load in loads:
         load.start()
-    total[...] = jnp.zeros(total.shape, F32)
+    upper[...] = jnp.zeros(upper.shape, F32)
+    lower[...] = jnp.zeros(lower.shape, F32)
     for f in range(rows):
         turned[f] = (own_0, own_1)[f // (rows // 2)][f % (rows // 2)].T
     for f in range(rows):
         loads[f].wait()
         for k in range(slots):
             at = jnp.where(k < count_ref[f], cols_ref[f, k] - base, tiles)
-            total[at] += jnp.dot(turned[f], a_ref[f, k], preferred_element_type=F32)
+            term = jnp.dot(turned[f], a_ref[f, k], preferred_element_type=F32)
+            upper[at] += term[:middle]
+            lower[at] += term[middle:]
     for c in range(subs * rows):
-        value = total[rows + c]
-        high = value.astype(BF16)
-        high_ref[c] = high
-        low_ref[c] = (value - high.astype(F32)).astype(BF16)
+        for at, ref in ((0, upper), (middle, lower)):
+            value = ref[rows + c]
+            high = value.astype(BF16)
+            high_ref[c, at : at + middle] = high
+            low_ref[c, at : at + middle] = (value - high.astype(F32)).astype(BF16)
+
+    def owned(c, k):
+        at = lax.bitwise_xor(me, k) * COARSE_ROWS
+        here = pl.ds(pl.multiple_of(lax.rem(at, middle), COARSE_ROWS), COARSE_ROWS)
+        return jnp.where(at < middle, upper[c, here], lower[c, here])
+
     for k in range(subs):
-        start = pl.multiple_of(lax.bitwise_xor(me, k) * COARSE_ROWS, COARSE_ROWS)
         for i, c in enumerate([*range(rows), *range(tiles - rows, tiles)]):
-            part = total[c, pl.ds(start, COARSE_ROWS)]
+            part = owned(c, k)
             edges[k][:, i * tile : (i + 1) * tile] = part.astype(edges[k].dtype)
     k = subs - 1
-    start = pl.multiple_of(lax.bitwise_xor(me, k) * COARSE_ROWS, COARSE_ROWS)
-    for f in range(rows):
-        part = total[rows + lax.bitwise_xor(me, k) * rows + f, pl.ds(start, COARSE_ROWS)]
+    for f in range(rows):
+        part = owned(rows + lax.bitwise_xor(me, k) * rows + f, k)
         at = (2 * rows + f) * tile
         edges[k][:, at : at + tile] = part.astype(edges[k].dtype)
 
@@ -285,7 +294,8 @@
         out_specs=[vmem] * (subs + 2),
         scratch_shapes=[
             pltpu.VMEM(a_tiles.shape, BF16),
-            pltpu.VMEM(((subs + 2) * rows + 1, width, tile), F32),
+            pltpu.VMEM(((subs + 2) * rows + 1, width // 2, tile), F32),
+            pltpu.VMEM(((subs + 2) * rows + 1, width // 2, tile), F32),
             pltpu.VMEM((rows, width, tile), BF16),
             pltpu.SemaphoreType.DMA((rows,)),
         ],

time: 28.1 us -> 28.1 us (level)
  no operation moved by 1% of the time
where the time goes in v15:
time: 28.1 us; the launch traced here: 27.9 us
  starting transfers between devices  16 us (57%)
  Pallas kernels  6.38 us (23%)
  waiting for transfers between devices  5.41 us (19%)
    ppermute x9, starting transfers between devices, exchange(): return lax.ppermute(value, 'sub', [(s, s ^ k) for s in range(subs)])  8.81 us
    ppermute x1, starting transfers between devices, local(): lax.ppermute(to_far, 'dom', [(d, d - 1 + 2 * (d % 2)) for d in range(1, d...  7.14 us
    ppermute x1, waiting for transfers between devices, local(): lax.ppermute(to_far, 'dom', [(d, d - 1 + 2 * (d % 2)) for d in range(1, d...  3.71 us
    pallas_call x1, Pallas kernels, narrow_parts(): pl.pallas_call(functools.partial(terms_kernel, subs), out_shape=[jax.Shap...  3.24 us
    ppermute x9, waiting for transfers between devices, exchange(): return lax.ppermute(value, 'sub', [(s, s ^ k) for s in range(subs)])  1.7 us
    pallas_call x1, Pallas kernels, local(): pl.pallas_call(order_kernel, out_shape=[jax.ShapeDtypeStruct((rows // 2,...  1.02 us
    pallas_call x1, Pallas kernels, local(): pl.pallas_call(functools.partial(finish_kernel, subs, half), out_shape=ja...  0.93 us
    pallas_call x1, Pallas kernels, narrow_parts(): pl.pallas_call(functools.partial(early_kernel, subs, rows, first), out_sh...  0.58 us
  transfers between devices with their start and end apart: 11, of which 2 were waited for; matrix products, arithmetic and copies ran while one was open for 0% of the time, Pallas kernels for 16%

profile of v15, /device:TPU:1, one launch (start us, length us, event | category | flops | bytes accessed | tf_op | source)
XLA Modules:
  0.0 27.9 jit_solution(14009233742385664967)
XLA Ops:
  0.0 0.0 copy-start
  0.0 0.0 copy-start.1
  0.0 1.0 %order_columns.1 = (bf16[2,128,256]{2,1,0:T(8,128)(2,1)S(1)}, bf16[2,128,256]{2,1,0:T(8,128)(2,1)S(1)}) custom-call(s32[2,4]{1,0:T(2,128)} %bitcast.1, bf16[4,128,256]{2,1,0:T(8,128)(2,1)} %p_hbm.1), custom_call_target="tpu_custom_call" | custom-call | flops 1073741824 | bytes 524288 | tf_op jit(solution)/shard_map/order_columns/pallas_call | solution.py:361
  1.0 2.1 %collective-permute-start.2 = (bf16[2,128,256]{2,1,0:T(8,128)(2,1)S(1)}, bf16[2,128,256]{2,1,0:T(8,128)(2,1)S(1)}, u32[]{:S(2)}, u32[]{:S(2)}) collective-permute-start(bf16[2,128,256]{2,1,0:T(8,128)(2,1)S(1)} %get-tuple-element.22.own_0.rest_0_.refs_4_), channel_id=1, source_target_pairs={{0,2},{1,3},{2,0},{3,1},{4,6},{5,7},{6,4},{7,5},{8,10},{9,11},{10,... | collective-permute-start | bytes 393224 | tf_op jit(solution)/shard_map/ppermute | solution.py:359
  3.2 1.2 %collective-permute-start.1 = (bf16[2,128,256]{2,1,0:T(8,128)(2,1)S(1)}, bf16[2,128,256]{2,1,0:T(8,128)(2,1)S(1)}, u32[]{:S(2)}, u32[]{:S(2)}) collective-permute-start(bf16[2,128,256]{2,1,0:T(8,128)(2,1)S(1)} %get-tuple-element.23.own_1.rest_1_.refs_5_), channel_id=1, source_target_pairs={{0,1},{1,0},{2,3},{3,2},{4,5},{5,4},{6,7},{7,6},{8,9},{9,8},{10,11... | collective-permute-start | bytes 393224 | tf_op jit(solution)/shard_map/ppermute | solution.py:359
  4.4 0.3 collective-permute-start
  4.6 0.1 collective-permute-start.3
  4.7 1.7 %collective-permute-done.2.rest_4_ = bf16[2,128,256]{2,1,0:T(8,128)(2,1)S(1)} collective-permute-done((bf16[2,128,256]{2,1,0:T(8,128)(2,1)S(1)}, bf16[2,128,256]{2,1,0:T(8,128)(2,1)S(1)}, u32[]{:S(2)}, u32[]{:S(2)}) %collective-permute-start.2) | collective-permute-done | bytes 131104 | tf_op jit(solution)/shard_map/ppermute | solution.py:359
  6.4 1.1 %collective-permute-start.4 = (bf16[2,128,256]{2,1,0:T(8,128)(2,1)S(1)}, bf16[2,128,256]{2,1,0:T(8,128)(2,1)S(1)}, u32[]{:S(2)}, u32[]{:S(2)}) collective-permute-start(bf16[2,128,256]{2,1,0:T(8,128)(2,1)S(1)} %collective-permute-done.2.rest_4_), channel_id=1, source_target_pairs={{0,1},{1,0},{2,3},{3,2},{4,5},{5,4},{6,7},{7,6},{8,9},{9,8},{10,11... | collective-permute-start | bytes 393224 | tf_op jit(solution)/shard_map/ppermute | solution.py:359
  7.5 0.0 collective-permute-done.1.rest_3_
  7.5 1.2 %collective-permute-start.5 = (bf16[2,128,256]{2,1,0:T(8,128)(2,1)S(1)}, bf16[2,128,256]{2,1,0:T(8,128)(2,1)S(1)}, u32[]{:S(2)}, u32[]{:S(2)}) collective-permute-start(bf16[2,128,256]{2,1,0:T(8,128)(2,1)S(1)} %collective-permute-done.1.rest_3_), channel_id=1, source_target_pairs={{0,2},{1,3},{2,0},{3,1},{4,6},{5,7},{6,4},{7,5},{8,10},{9,11},{10,... | collective-permute-start | bytes 393224 | tf_op jit(solution)/shard_map/ppermute | solution.py:359
  8.7 0.0 copy-done
  8.7 0.0 copy-done.1
  8.7 3.2 %terms.1 = (f32[64,1024]{1,0:T(8,128)S(1)}, bf16[64,1024]{1,0:T(8,128)(2,1)S(1)}, bf16[64,1024]{1,0:T(8,128)(2,1)S(1)}, bf16[64,1536]{1,0:T(8,128)(2,1)S(1)}, bf...) custom-call(s32[4,10]{1,0:T(4,128)S(1)} %copy-done, s32[4]{0:T(128)S(1)} %copy-done.1, ...), custom_call_target="tpu_custom_call" | custom-call | flops 2147483648 | bytes 1310720 | tf_op jit(solution)/shard_map/terms/pallas_call | solution.py:286
  12.0 0.0 collective-permute-done.rest_2_
  12.0 0.0 collective-permute-done.3.rest_5_
  12.0 0.6 %early_part.1 = (f32[256,256]{1,0:T(8,128)S(1)}, bf16[64,1792]{1,0:T(8,128)(2,1)S(1)}) custom-call(bf16[16,256,128]{2,1,0:T(8,128)(2,1)S(1)} %get-tuple-element.24.high_ref, bf16[16,256,128]{2,1,0:T(8,128)(2,1)S(1)} %get-tuple-element.25.low_ref, bf16[64,1536]{1,0:T(8,128)(2,1)S(1)} %get-tuple-element.26.edge_ref, ...), custom_call_target="tpu_custom_call" | custom-call | flops 402653184 | bytes 1048576 | tf_op jit(solution)/shard_map/early_part/pallas_call | solution.py:311
  12.6 1.0 %collective-permute-start.8 = (bf16[64,1792]{1,0:T(8,128)(2,1)S(1)}, bf16[64,1792]{1,0:T(8,128)(2,1)S(1)}, u32[]{:S(2)}, u32[]{:S(2)}) collective-permute-start(bf16[64,1792]{1,0:T(8,128)(2,1)S(1)} %get-tuple-element.34), channel_id=1, source_target_pairs={{0,3},{1,2},{2,1},{3,0},{4,7},{5,6},{6,5},{7,4},{8,11},{9,10},{10,... | collective-permute-start | bytes 688136 | tf_op jit(solution)/shard_map/ppermute | solution.py:359
  13.6 0.0 collective-permute-done.4.rest_6_
  13.6 0.0 collective-permute-done.5.rest_7_
  13.6 0.4 %late_part.1 = (f32[64,1280]{1,0:T(8,128)S(1)}, bf16[64,1280]{1,0:T(8,128)(2,1)S(1)}, bf16[64,1280]{1,0:T(8,128)(2,1)S(1)}, bf16[4,128,256]{2,1,0:T(8,128)(2,1)S(1)}, bf16[4,128,256]{2,1,0:T(8,128)(2,1)S(1)}) custom-call(bf16[16,256,128]{2,1,0:T(8,128)(2,1)S(1)} %get-tuple-element.24.high_ref, bf16[16,256,128]{2,1,0:T(8,128)(2,1)S(1)} %get-tuple-element.25.low_ref, ...), custom_call_target="tpu_custom_call" | custom-call | flops 134217728 | bytes 1048576 | tf_op jit(solution)/shard_map/late_part/pallas_call | solution.py:325
  14.0 0.6 %collective-permute-start.9 = (bf16[64,1280]{1,0:T(8,128)(2,1)S(1)}, bf16[64,1280]{1,0:T(8,128)(2,1)S(1)}, u32[]{:S(2)}, u32[]{:S(2)}) collective-permute-start(bf16[64,1280]{1,0:T(8,128)(2,1)S(1)} %get-tuple-element.35), channel_id=1, source_target_pairs={{0,2},{1,3},{2,0},{3,1},{4,6},{5,7},{6,4},{7,5},{8,10},{9,11},{10,... | collective-permute-start | bytes 491528 | tf_op jit(solution)/shard_map/ppermute | solution.py:359
  14.6 1.2 %collective-permute-start.10 = (bf16[64,1280]{1,0:T(8,128)(2,1)S(1)}, bf16[64,1280]{1,0:T(8,128)(2,1)S(1)}, u32[]{:S(2)}, u32[]{:S(2)}) collective-permute-start(bf16[64,1280]{1,0:T(8,128)(2,1)S(1)} %get-tuple-element.36), channel_id=1, source_target_pairs={{0,1},{1,0},{2,3},{3,2},{4,5},{5,4},{6,7},{7,6},{8,9},{9,8},{10,11... | collective-permute-start | bytes 491528 | tf_op jit(solution)/shard_map/ppermute | solution.py:359
  15.8 7.1 %collective-permute-start.6 = (bf16[4,128,256]{2,1,0:T(8,128)(2,1)S(1)}, bf16[4,128,256]{2,1,0:T(8,128)(2,1)S(1)}, u32[]{:S(2)}, u32[]{:S(2)}) collective-permute-start(bf16[4,128,256]{2,1,0:T(8,128)(2,1)S(1)} %get-tuple-element.31), channel_id=1, source_target_pairs={{4,8},{8,4},{12,16},{16,12},{20,24},{24,20},{5,9},{9,5},{13,17},{1... | collective-permute-start | bytes 786440 | tf_op jit(solution)/shard_map/ppermute | solution.py:452
  23.0 0.1 collective-permute-start.7
  23.0 0.0 collective-permute-done.8.refs_1_
  23.0 0.0 collective-permute-done.9.refs_2_
  23.1 0.0 collective-permute-done.10.refs_3_
  23.1 0.2 sum_parts.1
  23.3 3.7 %collective-permute-done.6.refs_0_ = bf16[4,128,256]{2,1,0:T(8,128)(2,1)S(1)} collective-permute-done((bf16[4,128,256]{2,1,0:T(8,128)(2,1)S(1)}, bf16[4,128,256]{2,1,0:T(8,128)(2,1)S(1)}, u32[]{:S(2)}, u32[]{:S(2)}) %collective-permute-start.6) | collective-permute-done | bytes 262176 | tf_op jit(solution)/shard_map/ppermute | solution.py:452
  27.0 0.0 collective-permute-done.7.refs_1_
  27.0 0.9 %finish.1 = bf16[64,768]{1,0:T(8,128)(2,1)} custom-call(bf16[4,128,256]{2,1,0:T(8,128)(2,1)S(1)} %collective-permute-done.6.refs_0_, bf16[4,128,256]{2,1,0:T(8,128)(2,1)S(1)} %collective-permute-done.7.refs_1_, bf16[64,256]{1,0:T(8,128)(2,1)S(1)} %get-tuple-element.37.refs_2_, bf16[128,1024]{1,0:T(8,128)(2,1)S(1)} %get-tuple-element.38.refs_3_), custom_call_target="tpu_custom_call" | custom-call | flops 268435456 | bytes 1048576 | tf_op jit(solution)/shard_map/finish/pallas_call | solution.py:471
Async XLA Ops:
  0.0 8.7 %copy-start = (s32[4,10]{1,0:T(4,128)S(1)}, s32[4,10]{1,0:T(4,128)}, u32[]{:S(2)}) copy-start(s32[4,10]{1,0:T(4,128)} %cols_ref.1) | copy-start | bytes 484
  0.0 8.7 %copy-start.1 = (s32[4]{0:T(128)S(1)}, s32[4]{0:T(128)}, u32[]{:S(2)}) copy-start(s32[4]{0:T(128)} %count_ref.1) | copy-start | bytes 52
  1.0 5.4 %collective-permute-start.2 = (bf16[2,128,256]{2,1,0:T(8,128)(2,1)S(1)}, bf16[2,128,256]{2,1,0:T(8,128)(2,1)S(1)}, u32[]{:S(2)}, u32[]{:S(2)}) collective-permute-start(bf16[2,128,256]{2,1,0:T(8,128)(2,1)S(1)} %get-tuple-element.22.own_0.rest_0_.refs_4_), channel_id=1, source_target_pairs={{0,2},{1,3},{2,0},{3,1},{4,6},{5,7},{6,4},{7,5},{8,10},{9,11},{10,... | collective-permute-start | bytes 393224 | tf_op jit(solution)/shard_map/ppermute | solution.py:359
  3.2 4.3 %collective-permute-start.1 = (bf16[2,128,256]{2,1,0:T(8,128)(2,1)S(1)}, bf16[2,128,256]{2,1,0:T(8,128)(2,1)S(1)}, u32[]{:S(2)}, u32[]{:S(2)}) collective-permute-start(bf16[2,128,256]{2,1,0:T(8,128)(2,1)S(1)} %get-tuple-element.23.own_1.rest_1_.refs_5_), channel_id=1, source_target_pairs={{0,1},{1,0},{2,3},{3,2},{4,5},{5,4},{6,7},{7,6},{8,9},{9,8},{10,11... | collective-permute-start | bytes 393224 | tf_op jit(solution)/shard_map/ppermute | solution.py:359
  4.4 7.6 %collective-permute-start = (bf16[2,128,256]{2,1,0:T(8,128)(2,1)S(1)}, bf16[2,128,256]{2,1,0:T(8,128)(2,1)S(1)}, u32[]{:S(2)}, u32[]{:S(2)}) collective-permute-start(bf16[2,128,256]{2,1,0:T(8,128)(2,1)S(1)} %get-tuple-element.22.own_0.rest_0_.refs_4_), channel_id=1, source_target_pairs={{0,1},{1,0},{2,3},{3,2},{4,5},{5,4},{6,7},{7,6},{8,9},{9,8},{10,11... | collective-permute-start | bytes 393224 | tf_op jit(solution)/shard_map/ppermute | solution.py:359
  4.6 7.4 %collective-permute-start.3 = (bf16[2,128,256]{2,1,0:T(8,128)(2,1)S(1)}, bf16[2,128,256]{2,1,0:T(8,128)(2,1)S(1)}, u32[]{:S(2)}, u32[]{:S(2)}) collective-permute-start(bf16[2,128,256]{2,1,0:T(8,128)(2,1)S(1)} %get-tuple-element.23.own_1.rest_1_.refs_5_), channel_id=1, source_target_pairs={{0,2},{1,3},{2,0},{3,1},{4,6},{5,7},{6,4},{7,5},{8,10},{9,11},{10,... | collective-permute-start | bytes 393224 | tf_op jit(solution)/shard_map/ppermute | solution.py:359
  6.4 7.2 %collective-permute-start.4 = (bf16[2,128,256]{2,1,0:T(8,128)(2,1)S(1)}, bf16[2,128,256]{2,1,0:T(8,128)(2,1)S(1)}, u32[]{:S(2)}, u32[]{:S(2)}) collective-permute-start(bf16[2,128,256]{2,1,0:T(8,128)(2,1)S(1)} %collective-permute-done.2.rest_4_), channel_id=1, source_target_pairs={{0,1},{1,0},{2,3},{3,2},{4,5},{5,4},{6,7},{7,6},{8,9},{9,8},{10,11... | collective-permute-start | bytes 393224 | tf_op jit(solution)/shard_map/ppermute | solution.py:359
  7.5 6.1 %collective-permute-start.5 = (bf16[2,128,256]{2,1,0:T(8,128)(2,1)S(1)}, bf16[2,128,256]{2,1,0:T(8,128)(2,1)S(1)}, u32[]{:S(2)}, u32[]{:S(2)}) collective-permute-start(bf16[2,128,256]{2,1,0:T(8,128)(2,1)S(1)} %collective-permute-done.1.rest_3_), channel_id=1, source_target_pairs={{0,2},{1,3},{2,0},{3,1},{4,6},{5,7},{6,4},{7,5},{8,10},{9,11},{10,... | collective-permute-start | bytes 393224 | tf_op jit(solution)/shard_map/ppermute | solution.py:359
  12.6 10.4 %collective-permute-start.8 = (bf16[64,1792]{1,0:T(8,128)(2,1)S(1)}, bf16[64,1792]{1,0:T(8,128)(2,1)S(1)}, u32[]{:S(2)}, u32[]{:S(2)}) collective-permute-start(bf16[64,1792]{1,0:T(8,128)(2,1)S(1)} %get-tuple-element.34), channel_id=1, source_target_pairs={{0,3},{1,2},{2,1},{3,0},{4,7},{5,6},{6,5},{7,4},{8,11},{9,10},{10,... | collective-permute-start | bytes 688136 | tf_op jit(solution)/shard_map/ppermute | solution.py:359
  14.0 9.0 %collective-permute-start.9 = (bf16[64,1280]{1,0:T(8,128)(2,1)S(1)}, bf16[64,1280]{1,0:T(8,128)(2,1)S(1)}, u32[]{:S(2)}, u32[]{:S(2)}) collective-permute-start(bf16[64,1280]{1,0:T(8,128)(2,1)S(1)} %get-tuple-element.35), channel_id=1, source_target_pairs={{0,2},{1,3},{2,0},{3,1},{4,6},{5,7},{6,4},{7,5},{8,10},{9,11},{10,... | collective-permute-start | bytes 491528 | tf_op jit(solution)/shard_map/ppermute | solution.py:359
  14.6 8.5 %collective-permute-start.10 = (bf16[64,1280]{1,0:T(8,128)(2,1)S(1)}, bf16[64,1280]{1,0:T(8,128)(2,1)S(1)}, u32[]{:S(2)}, u32[]{:S(2)}) collective-permute-start(bf16[64,1280]{1,0:T(8,128)(2,1)S(1)} %get-tuple-element.36), channel_id=1, source_target_pairs={{0,1},{1,0},{2,3},{3,2},{4,5},{5,4},{6,7},{7,6},{8,9},{9,8},{10,11... | collective-permute-start | bytes 491528 | tf_op jit(solution)/shard_map/ppermute | solution.py:359
  15.8 11.2 %collective-permute-start.6 = (bf16[4,128,256]{2,1,0:T(8,128)(2,1)S(1)}, bf16[4,128,256]{2,1,0:T(8,128)(2,1)S(1)}, u32[]{:S(2)}, u32[]{:S(2)}) collective-permute-start(bf16[4,128,256]{2,1,0:T(8,128)(2,1)S(1)} %get-tuple-element.31), channel_id=1, source_target_pairs={{4,8},{8,4},{12,16},{16,12},{20,24},{24,20},{5,9},{9,5},{13,17},{1... | collective-permute-start | bytes 786440 | tf_op jit(solution)/shard_map/ppermute | solution.py:452
  23.0 4.0 %collective-permute-start.7 = (bf16[4,128,256]{2,1,0:T(8,128)(2,1)S(1)}, bf16[4,128,256]{2,1,0:T(8,128)(2,1)S(1)}, u32[]{:S(2)}, u32[]{:S(2)}) collective-permute-start(bf16[4,128,256]{2,1,0:T(8,128)(2,1)S(1)} %get-tuple-element.32), channel_id=1, source_target_pairs={{0,4},{4,0},{8,12},{12,8},{16,20},{20,16},{24,28},{28,24},{1,5},{5... | collective-permute-start | bytes 786440 | tf_op jit(solution)/shard_map/ppermute | solution.py:455

commit v16 on v13

--- a/solution.py
+++ b/solution.py
@@ -95,20 +95,16 @@
                         out_ref[at, pl.ds(pl.multiple_of(start * tile, tile), tile)] += part
 
 
-def terms_kernel(subs, cols_ref, count_ref, a_hbm, own_0, own_1, *rest):
-    edges, (high_ref, low_ref, a_ref, total, turned, sems) = rest[:subs], rest[subs:]
+def terms_kernel(subs, cols_ref, count_ref, a_ref, own_0, own_1, *rest):
+    edges, (high_ref, low_ref, total, turned) = rest[:subs], rest[subs:]
     rows, slots, tile = a_ref.shape[:3]
     tiles = total.shape[0] - 1
     me = lax.axis_index("sub")
     base = lax.axis_index("dom") * (subs * rows) - rows
-    loads = [pltpu.make_async_copy(a_hbm.at[f], a_ref.at[f], sems.at[f]) for f in range(rows)]
-    for load in loads:
-        load.start()
     total[...] = jnp.zeros(total.shape, F32)
     for f in range(rows):
         turned[f] = (own_0, own_1)[f // (rows // 2)][f % (rows // 2)].T
     for f in range(rows):
-        loads[f].wait()
         for k in range(slots):
             at = jnp.where(k < count_ref[f], cols_ref[f, k] - base, tiles)
             total[at] += jnp.dot(turned[f], a_ref[f, k], preferred_element_type=F32)
@@ -281,22 +277,20 @@
             for k, kind in enumerate(kinds)
         ]
         + [jax.ShapeDtypeStruct((subs * rows, width, tile), BF16)] * 2,
-        in_specs=[smem, smem, pl.BlockSpec(memory_space=pltpu.HBM), vmem, vmem],
+        in_specs=[smem, smem, vmem, vmem, vmem],
         out_specs=[vmem] * (subs + 2),
         scratch_shapes=[
-            pltpu.VMEM(a_tiles.shape, BF16),
             pltpu.VMEM(((subs + 2) * rows + 1, width, tile), F32),
             pltpu.VMEM((rows, width, tile), BF16),
-            pltpu.SemaphoreType.DMA((rows,)),
         ],
         compiler_params=pltpu.CompilerParams(
-            vmem_limit_bytes=2 * a_tiles.size + 4 * ((subs + 2) * rows + 1) * width * tile + spare
+            vmem_limit_bytes=4 * ((subs + 2) * rows + 1) * width * tile + spare
         ),
         cost_estimate=pl.CostEstimate(
             flops=1 << 31, bytes_accessed=2 * a_tiles.size, transcendentals=0
         ),
         name="terms",
-    )(a_cols, a_count, pltpu.with_memory_space_constraint(a_tiles, pltpu.HBM), *own)
+    )(a_cols, a_count, a_tiles, *own)
     first, last = list(range(subs - 1)), [subs - 1]
     early, farthest = pl.pallas_call(
         functools.partial(early_kernel, subs, rows, first),

time: 28.1 us -> 29 us (1.032)
  starting transfers between devices: 16 us -> 17.7 us
  Pallas kernels: 6.39 us -> 5.2 us
  waiting for transfers between devices: 5.41 us -> 5.9 us
    ppermute x1, starting transfers between devices: 7.14 us -> 9.06 us  [local(): lax.ppermute(to_far, 'dom', [(d, d - 1 + 2 * (d % 2)) for d in range(1, d...]
    pallas_call x1, Pallas kernels: 3.24 us -> 1.98 us  [narrow_parts(): pl.pallas_call(functools.partial(terms_kernel, subs), out_shape=[jax.Shap...]
    ppermute x9, waiting for transfers between devices: 1.7 us -> 2.18 us  [exchange(): return lax.ppermute(value, 'sub', [(s, s ^ k) for s in range(subs)])]
  transfers between devices with their start and end apart: 11 -> 11, of which waited for: 2 -> 3; matrix products, arithmetic and copies ran while one was open for 0% -> 0% of each run, Pallas kernels for 16% -> 11%
where the time goes in v16:
time: 29 us; the launch traced here: 28.9 us
  starting transfers between devices  17.7 us (61%)
  waiting for transfers between devices  5.9 us (20%)
  Pallas kernels  5.2 us (18%)
    ppermute x1, starting transfers between devices, local(): lax.ppermute(to_far, 'dom', [(d, d - 1 + 2 * (d % 2)) for d in range(1, d...  9.06 us
    ppermute x9, starting transfers between devices, exchange(): return lax.ppermute(value, 'sub', [(s, s ^ k) for s in range(subs)])  8.54 us
    ppermute x1, waiting for transfers between devices, local(): lax.ppermute(to_far, 'dom', [(d, d - 1 + 2 * (d % 2)) for d in range(1, d...  3.71 us
    ppermute x9, waiting for transfers between devices, exchange(): return lax.ppermute(value, 'sub', [(s, s ^ k) for s in range(subs)])  2.18 us
    pallas_call x1, Pallas kernels, narrow_parts(): pl.pallas_call(functools.partial(terms_kernel, subs), out_shape=[jax.Shap...  1.98 us
    pallas_call x1, Pallas kernels, local(): pl.pallas_call(order_kernel, out_shape=[jax.ShapeDtypeStruct((rows // 2,...  1.09 us
    pallas_call x1, Pallas kernels, local(): pl.pallas_call(functools.partial(finish_kernel, subs, half), out_shape=ja...  0.93 us
  transfers between devices with their start and end apart: 11, of which 3 were waited for; matrix products, arithmetic and copies ran while one was open for 0% of the time, Pallas kernels for 11%

profile of v16, /device:TPU:1, one launch (start us, length us, event | category | flops | bytes accessed | tf_op | source)
XLA Modules:
  0.0 28.9 jit_solution(1959694036200485923)
XLA Ops:
  0.0 0.0 copy-start
  0.0 1.1 %order_columns.1 = (bf16[2,128,256]{2,1,0:T(8,128)(2,1)S(1)}, bf16[2,128,256]{2,1,0:T(8,128)(2,1)S(1)}) custom-call(s32[2,4]{1,0:T(2,128)} %bitcast.1, bf16[4,128,256]{2,1,0:T(8,128)(2,1)} %p_hbm.1), custom_call_target="tpu_custom_call" | custom-call | flops 1073741824 | bytes 524288 | tf_op jit(solution)/shard_map/order_columns/pallas_call | solution.py:345
  1.1 2.1 %collective-permute-start.2 = (bf16[2,128,256]{2,1,0:T(8,128)(2,1)S(1)}, bf16[2,128,256]{2,1,0:T(8,128)(2,1)S(1)}, u32[]{:S(2)}, u32[]{:S(2)}) collective-permute-start(bf16[2,128,256]{2,1,0:T(8,128)(2,1)S(1)} %get-tuple-element.22.own_0.rest_0_.refs_4_), channel_id=1, source_target_pairs={{0,2},{1,3},{2,0},{3,1},{4,6},{5,7},{6,4},{7,5},{8,10},{9,11},{10,... | collective-permute-start | bytes 393224 | tf_op jit(solution)/shard_map/ppermute | solution.py:343
  3.2 1.2 %collective-permute-start.1 = (bf16[2,128,256]{2,1,0:T(8,128)(2,1)S(1)}, bf16[2,128,256]{2,1,0:T(8,128)(2,1)S(1)}, u32[]{:S(2)}, u32[]{:S(2)}) collective-permute-start(bf16[2,128,256]{2,1,0:T(8,128)(2,1)S(1)} %get-tuple-element.23.own_1.rest_1_.refs_5_), channel_id=1, source_target_pairs={{0,1},{1,0},{2,3},{3,2},{4,5},{5,4},{6,7},{7,6},{8,9},{9,8},{10,11... | collective-permute-start | bytes 393224 | tf_op jit(solution)/shard_map/ppermute | solution.py:343
  4.5 0.3 collective-permute-start
  4.7 0.1 collective-permute-start.3
  4.8 1.7 %collective-permute-done.2.rest_4_ = bf16[2,128,256]{2,1,0:T(8,128)(2,1)S(1)} collective-permute-done((bf16[2,128,256]{2,1,0:T(8,128)(2,1)S(1)}, bf16[2,128,256]{2,1,0:T(8,128)(2,1)S(1)}, u32[]{:S(2)}, u32[]{:S(2)}) %collective-permute-start.2) | collective-permute-done | bytes 131104 | tf_op jit(solution)/shard_map/ppermute | solution.py:343
  6.5 1.1 %collective-permute-start.4 = (bf16[2,128,256]{2,1,0:T(8,128)(2,1)S(1)}, bf16[2,128,256]{2,1,0:T(8,128)(2,1)S(1)}, u32[]{:S(2)}, u32[]{:S(2)}) collective-permute-start(bf16[2,128,256]{2,1,0:T(8,128)(2,1)S(1)} %collective-permute-done.2.rest_4_), channel_id=1, source_target_pairs={{0,1},{1,0},{2,3},{3,2},{4,5},{5,4},{6,7},{7,6},{8,9},{9,8},{10,11... | collective-permute-start | bytes 393224 | tf_op jit(solution)/shard_map/ppermute | solution.py:343
  7.6 0.0 collective-permute-done.1.rest_3_
  7.6 1.2 %collective-permute-start.5 = (bf16[2,128,256]{2,1,0:T(8,128)(2,1)S(1)}, bf16[2,128,256]{2,1,0:T(8,128)(2,1)S(1)}, u32[]{:S(2)}, u32[]{:S(2)}) collective-permute-start(bf16[2,128,256]{2,1,0:T(8,128)(2,1)S(1)} %collective-permute-done.1.rest_3_), channel_id=1, source_target_pairs={{0,2},{1,3},{2,0},{3,1},{4,6},{5,7},{6,4},{7,5},{8,10},{9,11},{10,... | collective-permute-start | bytes 393224 | tf_op jit(solution)/shard_map/ppermute | solution.py:343
  8.8 0.0 copy-done
  8.8 0.0 copy-done.1
  8.8 0.0 copy-done.2
  8.8 2.0 %terms.1 = (f32[64,1024]{1,0:T(8,128)S(1)}, bf16[64,1024]{1,0:T(8,128)(2,1)S(1)}, bf16[64,1024]{1,0:T(8,128)(2,1)S(1)}, bf16[64,1536]{1,0:T(8,128)(2,1)S(1)}, bf...) custom-call(s32[4,10]{1,0:T(4,128)S(1)} %copy-done.1, s32[4]{0:T(128)S(1)} %copy-done.2, ...), custom_call_target="tpu_custom_call" | custom-call | flops 2147483648 | bytes 1310720 | tf_op jit(solution)/shard_map/terms/pallas_call | solution.py:273
  10.8 0.0 collective-permute-done.rest_2_
  10.8 0.0 collective-permute-done.3.rest_5_
  10.8 0.6 %early_part.1 = (f32[256,256]{1,0:T(8,128)S(1)}, bf16[64,1792]{1,0:T(8,128)(2,1)S(1)}) custom-call(bf16[16,256,128]{2,1,0:T(8,128)(2,1)S(1)} %get-tuple-element.24.high_ref, bf16[16,256,128]{2,1,0:T(8,128)(2,1)S(1)} %get-tuple-element.25.low_ref, bf16[64,1536]{1,0:T(8,128)(2,1)S(1)} %get-tuple-element.26.edge_ref, ...), custom_call_target="tpu_custom_call" | custom-call | flops 402653184 | bytes 1048576 | tf_op jit(solution)/shard_map/early_part/pallas_call | solution.py:295
  11.4 1.0 %collective-permute-start.8 = (bf16[64,1792]{1,0:T(8,128)(2,1)S(1)}, bf16[64,1792]{1,0:T(8,128)(2,1)S(1)}, u32[]{:S(2)}, u32[]{:S(2)}) collective-permute-start(bf16[64,1792]{1,0:T(8,128)(2,1)S(1)} %get-tuple-element.34), channel_id=1, source_target_pairs={{0,3},{1,2},{2,1},{3,0},{4,7},{5,6},{6,5},{7,4},{8,11},{9,10},{10,... | collective-permute-start | bytes 688136 | tf_op jit(solution)/shard_map/ppermute | solution.py:343
  12.4 0.5 %collective-permute-done.4.rest_6_ = bf16[2,128,256]{2,1,0:T(8,128)(2,1)S(1)} collective-permute-done((bf16[2,128,256]{2,1,0:T(8,128)(2,1)S(1)}, bf16[2,128,256]{2,1,0:T(8,128)(2,1)S(1)}, u32[]{:S(2)}, u32[]{:S(2)}) %collective-permute-start.4) | collective-permute-done | bytes 131104 | tf_op jit(solution)/shard_map/ppermute | solution.py:343
  12.9 0.0 collective-permute-done.5.rest_7_
  12.9 0.4 %late_part.1 = (f32[64,1280]{1,0:T(8,128)S(1)}, bf16[64,1280]{1,0:T(8,128)(2,1)S(1)}, bf16[64,1280]{1,0:T(8,128)(2,1)S(1)}, bf16[4,128,256]{2,1,0:T(8,128)(2,1)S(1)}, bf16[4,128,256]{2,1,0:T(8,128)(2,1)S(1)}) custom-call(bf16[16,256,128]{2,1,0:T(8,128)(2,1)S(1)} %get-tuple-element.24.high_ref, bf16[16,256,128]{2,1,0:T(8,128)(2,1)S(1)} %get-tuple-element.25.low_ref, ...), custom_call_target="tpu_custom_call" | custom-call | flops 134217728 | bytes 1048576 | tf_op jit(solution)/shard_map/late_part/pallas_call | solution.py:309
  13.3 0.3 %collective-permute-start.9 = (bf16[64,1280]{1,0:T(8,128)(2,1)S(1)}, bf16[64,1280]{1,0:T(8,128)(2,1)S(1)}, u32[]{:S(2)}, u32[]{:S(2)}) collective-permute-start(bf16[64,1280]{1,0:T(8,128)(2,1)S(1)} %get-tuple-element.35), channel_id=1, source_target_pairs={{0,2},{1,3},{2,0},{3,1},{4,6},{5,7},{6,4},{7,5},{8,10},{9,11},{10,... | collective-permute-start | bytes 491528 | tf_op jit(solution)/shard_map/ppermute | solution.py:343
  13.6 1.2 %collective-permute-start.10 = (bf16[64,1280]{1,0:T(8,128)(2,1)S(1)}, bf16[64,1280]{1,0:T(8,128)(2,1)S(1)}, u32[]{:S(2)}, u32[]{:S(2)}) collective-permute-start(bf16[64,1280]{1,0:T(8,128)(2,1)S(1)} %get-tuple-element.36), channel_id=1, source_target_pairs={{0,1},{1,0},{2,3},{3,2},{4,5},{5,4},{6,7},{7,6},{8,9},{9,8},{10,11... | collective-permute-start | bytes 491528 | tf_op jit(solution)/shard_map/ppermute | solution.py:343
  14.8 9.1 %collective-permute-start.6 = (bf16[4,128,256]{2,1,0:T(8,128)(2,1)S(1)}, bf16[4,128,256]{2,1,0:T(8,128)(2,1)S(1)}, u32[]{:S(2)}, u32[]{:S(2)}) collective-permute-start(bf16[4,128,256]{2,1,0:T(8,128)(2,1)S(1)} %get-tuple-element.31), channel_id=1, source_target_pairs={{4,8},{8,4},{12,16},{16,12},{20,24},{24,20},{5,9},{9,5},{13,17},{1... | collective-permute-start | bytes 786440 | tf_op jit(solution)/shard_map/ppermute | solution.py:436
  23.9 0.1 collective-permute-start.7
  24.0 0.0 collective-permute-done.8.refs_1_
  24.0 0.0 collective-permute-done.9.refs_2_
  24.0 0.0 collective-permute-done.10.refs_3_
  24.0 0.2 sum_parts.1
  24.2 3.7 %collective-permute-done.6.refs_0_ = bf16[4,128,256]{2,1,0:T(8,128)(2,1)S(1)} collective-permute-done((bf16[4,128,256]{2,1,0:T(8,128)(2,1)S(1)}, bf16[4,128,256]{2,1,0:T(8,128)(2,1)S(1)}, u32[]{:S(2)}, u32[]{:S(2)}) %collective-permute-start.6) | collective-permute-done | bytes 262176 | tf_op jit(solution)/shard_map/ppermute | solution.py:436
  28.0 0.0 collective-permute-done.7.refs_1_
  28.0 0.9 %finish.1 = bf16[64,768]{1,0:T(8,128)(2,1)} custom-call(bf16[4,128,256]{2,1,0:T(8,128)(2,1)S(1)} %collective-permute-done.6.refs_0_, bf16[4,128,256]{2,1,0:T(8,128)(2,1)S(1)} %collective-permute-done.7.refs_1_, bf16[64,256]{1,0:T(8,128)(2,1)S(1)} %get-tuple-element.37.refs_2_, bf16[128,1024]{1,0:T(8,128)(2,1)S(1)} %get-tuple-element.38.refs_3_), custom_call_target="tpu_custom_call" | custom-call | flops 268435456 | bytes 1048576 | tf_op jit(solution)/shard_map/finish/pallas_call | solution.py:455
  (2 shorter events, 0.0 us)
Async XLA Ops:
  0.0 8.8 %copy-start = (bf16[4,10,128,128]{3,2,1,0:T(8,128)(2,1)S(1)}, bf16[4,10,128,128]{3,2,1,0:T(8,128)(2,1)}, u32[]{:S(2)}) copy-start(bf16[4,10,128,128]{3,2,1,0:T(8,128)(2,1)} %a_ref.1) | copy-start | bytes 3932164
  0.0 8.8 %copy-start.1 = (s32[4,10]{1,0:T(4,128)S(1)}, s32[4,10]{1,0:T(4,128)}, u32[]{:S(2)}) copy-start(s32[4,10]{1,0:T(4,128)} %cols_ref.1) | copy-start | bytes 484
  0.0 8.8 %copy-start.2 = (s32[4]{0:T(128)S(1)}, s32[4]{0:T(128)}, u32[]{:S(2)}) copy-start(s32[4]{0:T(128)} %count_ref.1) | copy-start | bytes 52
  1.1 5.4 %collective-permute-start.2 = (bf16[2,128,256]{2,1,0:T(8,128)(2,1)S(1)}, bf16[2,128,256]{2,1,0:T(8,128)(2,1)S(1)}, u32[]{:S(2)}, u32[]{:S(2)}) collective-permute-start(bf16[2,128,256]{2,1,0:T(8,128)(2,1)S(1)} %get-tuple-element.22.own_0.rest_0_.refs_4_), channel_id=1, source_target_pairs={{0,2},{1,3},{2,0},{3,1},{4,6},{5,7},{6,4},{7,5},{8,10},{9,11},{10,... | collective-permute-start | bytes 393224 | tf_op jit(solution)/shard_map/ppermute | solution.py:343
  3.2 4.3 %collective-permute-start.1 = (bf16[2,128,256]{2,1,0:T(8,128)(2,1)S(1)}, bf16[2,128,256]{2,1,0:T(8,128)(2,1)S(1)}, u32[]{:S(2)}, u32[]{:S(2)}) collective-permute-start(bf16[2,128,256]{2,1,0:T(8,128)(2,1)S(1)} %get-tuple-element.23.own_1.rest_1_.refs_5_), channel_id=1, source_target_pairs={{0,1},{1,0},{2,3},{3,2},{4,5},{5,4},{6,7},{7,6},{8,9},{9,8},{10,11... | collective-permute-start | bytes 393224 | tf_op jit(solution)/shard_map/ppermute | solution.py:343
  4.5 6.4 %collective-permute-start = (bf16[2,128,256]{2,1,0:T(8,128)(2,1)S(1)}, bf16[2,128,256]{2,1,0:T(8,128)(2,1)S(1)}, u32[]{:S(2)}, u32[]{:S(2)}) collective-permute-start(bf16[2,128,256]{2,1,0:T(8,128)(2,1)S(1)} %get-tuple-element.22.own_0.rest_0_.refs_4_), channel_id=1, source_target_pairs={{0,1},{1,0},{2,3},{3,2},{4,5},{5,4},{6,7},{7,6},{8,9},{9,8},{10,11... | collective-permute-start | bytes 393224 | tf_op jit(solution)/shard_map/ppermute | solution.py:343
  4.7 6.1 %collective-permute-start.3 = (bf16[2,128,256]{2,1,0:T(8,128)(2,1)S(1)}, bf16[2,128,256]{2,1,0:T(8,128)(2,1)S(1)}, u32[]{:S(2)}, u32[]{:S(2)}) collective-permute-start(bf16[2,128,256]{2,1,0:T(8,128)(2,1)S(1)} %get-tuple-element.23.own_1.rest_1_.refs_5_), channel_id=1, source_target_pairs={{0,2},{1,3},{2,0},{3,1},{4,6},{5,7},{6,4},{7,5},{8,10},{9,11},{10,... | collective-permute-start | bytes 393224 | tf_op jit(solution)/shard_map/ppermute | solution.py:343
  6.5 6.4 %collective-permute-start.4 = (bf16[2,128,256]{2,1,0:T(8,128)(2,1)S(1)}, bf16[2,128,256]{2,1,0:T(8,128)(2,1)S(1)}, u32[]{:S(2)}, u32[]{:S(2)}) collective-permute-start(bf16[2,128,256]{2,1,0:T(8,128)(2,1)S(1)} %collective-permute-done.2.rest_4_), channel_id=1, source_target_pairs={{0,1},{1,0},{2,3},{3,2},{4,5},{5,4},{6,7},{7,6},{8,9},{9,8},{10,11... | collective-permute-start | bytes 393224 | tf_op jit(solution)/shard_map/ppermute | solution.py:343
  7.6 5.3 %collective-permute-start.5 = (bf16[2,128,256]{2,1,0:T(8,128)(2,1)S(1)}, bf16[2,128,256]{2,1,0:T(8,128)(2,1)S(1)}, u32[]{:S(2)}, u32[]{:S(2)}) collective-permute-start(bf16[2,128,256]{2,1,0:T(8,128)(2,1)S(1)} %collective-permute-done.1.rest_3_), channel_id=1, source_target_pairs={{0,2},{1,3},{2,0},{3,1},{4,6},{5,7},{6,4},{7,5},{8,10},{9,11},{10,... | collective-permute-start | bytes 393224 | tf_op jit(solution)/shard_map/ppermute | solution.py:343
  11.4 12.6 %collective-permute-start.8 = (bf16[64,1792]{1,0:T(8,128)(2,1)S(1)}, bf16[64,1792]{1,0:T(8,128)(2,1)S(1)}, u32[]{:S(2)}, u32[]{:S(2)}) collective-permute-start(bf16[64,1792]{1,0:T(8,128)(2,1)S(1)} %get-tuple-element.34), channel_id=1, source_target_pairs={{0,3},{1,2},{2,1},{3,0},{4,7},{5,6},{6,5},{7,4},{8,11},{9,10},{10,... | collective-permute-start | bytes 688136 | tf_op jit(solution)/shard_map/ppermute | solution.py:343
  13.3 10.7 %collective-permute-start.9 = (bf16[64,1280]{1,0:T(8,128)(2,1)S(1)}, bf16[64,1280]{1,0:T(8,128)(2,1)S(1)}, u32[]{:S(2)}, u32[]{:S(2)}) collective-permute-start(bf16[64,1280]{1,0:T(8,128)(2,1)S(1)} %get-tuple-element.35), channel_id=1, source_target_pairs={{0,2},{1,3},{2,0},{3,1},{4,6},{5,7},{6,4},{7,5},{8,10},{9,11},{10,... | collective-permute-start | bytes 491528 | tf_op jit(solution)/shard_map/ppermute | solution.py:343
  13.6 10.4 %collective-permute-start.10 = (bf16[64,1280]{1,0:T(8,128)(2,1)S(1)}, bf16[64,1280]{1,0:T(8,128)(2,1)S(1)}, u32[]{:S(2)}, u32[]{:S(2)}) collective-permute-start(bf16[64,1280]{1,0:T(8,128)(2,1)S(1)} %get-tuple-element.36), channel_id=1, source_target_pairs={{0,1},{1,0},{2,3},{3,2},{4,5},{5,4},{6,7},{7,6},{8,9},{9,8},{10,11... | collective-permute-start | bytes 491528 | tf_op jit(solution)/shard_map/ppermute | solution.py:343
  14.8 13.1 %collective-permute-start.6 = (bf16[4,128,256]{2,1,0:T(8,128)(2,1)S(1)}, bf16[4,128,256]{2,1,0:T(8,128)(2,1)S(1)}, u32[]{:S(2)}, u32[]{:S(2)}) collective-permute-start(bf16[4,128,256]{2,1,0:T(8,128)(2,1)S(1)} %get-tuple-element.31), channel_id=1, source_target_pairs={{4,8},{8,4},{12,16},{16,12},{20,24},{24,20},{5,9},{9,5},{13,17},{1... | collective-permute-start | bytes 786440 | tf_op jit(solution)/shard_map/ppermute | solution.py:436
  23.9 4.0 %collective-permute-start.7 = (bf16[4,128,256]{2,1,0:T(8,128)(2,1)S(1)}, bf16[4,128,256]{2,1,0:T(8,128)(2,1)S(1)}, u32[]{:S(2)}, u32[]{:S(2)}) collective-permute-start(bf16[4,128,256]{2,1,0:T(8,128)(2,1)S(1)} %get-tuple-element.32), channel_id=1, source_target_pairs={{0,4},{4,0},{8,12},{12,8},{16,20},{20,16},{24,28},{28,24},{1,5},{5... | collective-permute-start | bytes 786440 | tf_op jit(solution)/shard_map/ppermute | solution.py:439
